TPU v7x, 32 devices: a whole 2x2x4 slice. The times are simulated.
32 devices in a mesh: grp: 8 (over z, y), ctx: 4 (over x, core).
Axes of the slice: x: 2, y: 2, z: 4, core: 2. Of those that a mesh axis runs over, the one named last changes fastest.
Arguments:
- latents: bfloat16 [1024, 32, 1024], P(('grp', 'ctx')), may hold values from -6 to 6
- embeds: bfloat16 [1024, 32, 1024], P(('grp', 'ctx')), may hold values from -6 to 6
- cotangent: bfloat16 [1024, 32, 1024], P(('grp', 'ctx')), may hold values from -6 to 6
- counts: int32 [32], replicated, may hold values from 1 to 2, as said below
- w_adapt: bfloat16 [2048, 1024], P(('grp', 'ctx')), may hold values from -0.125 to 0.125
- w_query: bfloat16 [1024, 1024], P(('grp', 'ctx')), may hold values from -0.1875 to 0.1875
- w_key: bfloat16 [1024, 1024], P(('grp', 'ctx')), may hold values from -0.1875 to 0.1875
- w_value: bfloat16 [1024, 1024], P(('grp', 'ctx')), may hold values from -0.1875 to 0.1875
- w_out: bfloat16 [1024, 1024], P(('grp', 'ctx')), may hold values from -0.1875 to 0.1875
- w_gate: bfloat16 [1024, 2816], P(('grp', 'ctx')), may hold values from -0.1875 to 0.1875
- w_up: bfloat16 [1024, 2816], P(('grp', 'ctx')), may hold values from -0.1875 to 0.1875
- w_down: bfloat16 [2816, 1024], P(('grp', 'ctx')), may hold values from -0.109375 to 0.109375
- gains: bfloat16 [4, 1024], P(None, ('grp', 'ctx')), may hold values from 0.099609375 to 1.8984375
Outputs:
- final_latents: bfloat16 [1024, 32, 1024], P(('grp', 'ctx'))
- latent_grad: bfloat16 [1024, 32, 1024], P(('grp', 'ctx'))
- embed_grad: bfloat16 [1024, 32, 1024], P(('grp', 'ctx'))
- adapt_grad: float32 [2048, 1024], P(('grp', 'ctx'))
- query_grad: float32 [1024, 1024], P(('grp', 'ctx'))
- key_grad: float32 [1024, 1024], P(('grp', 'ctx'))
- value_grad: float32 [1024, 1024], P(('grp', 'ctx'))
- out_grad: float32 [1024, 1024], P(('grp', 'ctx'))
- gate_grad: float32 [1024, 2816], P(('grp', 'ctx'))
- up_grad: float32 [1024, 2816], P(('grp', 'ctx'))
- down_grad: float32 [2816, 1024], P(('grp', 'ctx'))
- gain_grad: float32 [4, 1024], P(None, ('grp', 'ctx'))
Inputs may be any that keep to these rules, and one draw needn't show every extreme that they name: `counts`: exactly 16 sequences have count 2, the others count 1.
All inputs are finite; a program needn't handle non-finite values.
Results may differ from a plain program's by a relative error of at most 0.024.
Values may be sent and summed in bfloat16 or wider, within the bound.
A program may use at most 320 MiB of HBM per device.

v0:
```python
import jax
import jax.numpy as jnp
from jax import lax
from jax.sharding import PartitionSpec as P

HEADS = 8
HEAD_DIM = 128


def rms_scale(values):
    return lax.rsqrt(jnp.mean(values * values, -1, keepdims=True) + 1e-06)


def norm_back(values, upstream, gain_vec):
    scale_rows = rms_scale(values)
    normal = values * scale_rows
    gain_part = jnp.sum(upstream * normal, 0)
    scaled = upstream * gain_vec
    return (
        scale_rows * (scaled - normal * jnp.mean(scaled * normal, -1, keepdims=True)),
        gain_part,
    )


def rope_table(positions):
    freq = 10000.0 ** (-2.0 * jnp.arange(HEAD_DIM // 2, dtype=jnp.float32) / HEAD_DIM)
    angle = positions.astype(jnp.float32)[:, None] * freq
    return (jnp.cos(angle), jnp.sin(angle))


def rotate(values, cosine, sine):
    half_dim = HEAD_DIM // 2
    first_half = values[..., :half_dim]
    second_half = values[..., half_dim:]
    cos_b = cosine[:, None, None, :]
    sin_b = sine[:, None, None, :]
    return jnp.concatenate(
        [first_half * cos_b - second_half * sin_b, second_half * cos_b + first_half * sin_b], -1
    )


def unrotate(grads, cosine, sine):
    half_dim = HEAD_DIM // 2
    first_half = grads[..., :half_dim]
    second_half = grads[..., half_dim:]
    cos_b = cosine[:, None, None, :]
    sin_b = sine[:, None, None, :]
    return jnp.concatenate(
        [first_half * cos_b + second_half * sin_b, second_half * cos_b - first_half * sin_b], -1
    )


def score_block(queries, keys_in, query_pos, key_pos_in):
    raw = jnp.einsum(
        "qshd,kshd->qshk", queries, keys_in, preferred_element_type=jnp.float32
    ) * HEAD_DIM ** (-0.5)
    causal = key_pos_in[None, :] <= query_pos[:, None]
    return jnp.where(causal[:, None, None, :], raw, -1e30)


def back_block(queries, keys_in, values_in, d_mixed, log_total, delta, query_pos, key_pos_in):
    scores = score_block(queries, keys_in, query_pos, key_pos_in)
    probs = jnp.exp(scores - log_total[..., None])
    d_probs = jnp.einsum("qshd,kshd->qshk", d_mixed, values_in, preferred_element_type=jnp.float32)
    slopes = (probs * (d_probs - delta[..., None])).astype(jnp.bfloat16)
    return (probs.astype(jnp.bfloat16), slopes)


def on_device(
    latents,
    embeds,
    cotangent,
    counts,
    w_adapt,
    w_query,
    w_key,
    w_value,
    w_out,
    w_gate,
    w_up,
    w_down,
    gains,
):
    groups = lax.axis_size("grp")
    ctx_count = lax.axis_size("ctx")
    seq_total = latents.shape[1]
    seq_group = seq_total // groups
    block_len = latents.shape[0]
    model_width = latents.shape[2]
    group_len = groups * block_len
    adapt_w, query_w, key_w, value_w, output_w, gate_w, up_w, down_w, gain_rows = (
        lax.all_gather(w_adapt, ("grp", "ctx"), axis=0, tiled=True),
        lax.all_gather(w_query, ("grp", "ctx"), axis=0, tiled=True),
        lax.all_gather(w_key, ("grp", "ctx"), axis=0, tiled=True),
        lax.all_gather(w_value, ("grp", "ctx"), axis=0, tiled=True),
        lax.all_gather(w_out, ("grp", "ctx"), axis=0, tiled=True),
        lax.all_gather(w_gate, ("grp", "ctx"), axis=0, tiled=True),
        lax.all_gather(w_up, ("grp", "ctx"), axis=0, tiled=True),
        lax.all_gather(w_down, ("grp", "ctx"), axis=0, tiled=True),
        lax.all_gather(gains, ("grp", "ctx"), axis=1, tiled=True),
    )
    gain_float = gain_rows.astype(jnp.float32)
    seq_order = jnp.arange(seq_total, dtype=jnp.int32)
    latent_in, embed_in, slope_in = (
        lax.all_to_all(
            jnp.take(latents, seq_order, axis=1), "grp", split_axis=1, concat_axis=0, tiled=True
        ),
        lax.all_to_all(
            jnp.take(embeds, seq_order, axis=1), "grp", split_axis=1, concat_axis=0, tiled=True
        ),
        lax.all_to_all(
            jnp.take(cotangent, seq_order, axis=1), "grp", split_axis=1, concat_axis=0, tiled=True
        ),
    )
    ctx_index = lax.axis_index("ctx")

    def key_position(flat_index):
        source = flat_index // group_len
        within = flat_index % group_len
        return (within // block_len * ctx_count + source) * block_len + within % block_len

    query_pos = key_position(ctx_index * group_len + jnp.arange(group_len, dtype=jnp.int32))
    cos_query, sin_query = rope_table(query_pos)

    def attend_forward(queries, keys_in, values_in):
        piece = lax.all_gather(keys_in, "ctx", axis=0, tiled=True)
        scores = score_block(
            queries, piece, query_pos, key_position(jnp.arange(piece.shape[0], dtype=jnp.int32))
        )
        log_total = jax.nn.logsumexp(scores, -1)
        probs = jnp.exp(scores - log_total[..., None]).astype(jnp.bfloat16)
        mixed_raw = jnp.einsum(
            "qshk,kshd->qshd",
            probs,
            lax.all_gather(values_in, "ctx", axis=0, tiled=True),
            preferred_element_type=jnp.float32,
        )
        return (mixed_raw.astype(jnp.bfloat16), (queries, keys_in, values_in, log_total, mixed_raw))

    def core_block(latent, embedding):
        seq_batch = latent.shape[1]
        row_count = group_len * seq_batch
        joined = jnp.concatenate([latent.astype(jnp.bfloat16), embedding], -1).reshape(
            row_count, 2 * model_width
        )
        resid = jnp.dot(joined, adapt_w, preferred_element_type=jnp.float32)
        normed = (resid * rms_scale(resid) * gain_float[0]).astype(jnp.bfloat16)

        def heads_of(matrix):
            return jnp.dot(normed, matrix, preferred_element_type=jnp.float32).reshape(
                group_len, seq_batch, HEADS, HEAD_DIM
            )

        queries = rotate(heads_of(query_w), cos_query, sin_query).astype(jnp.bfloat16)
        keys_in = rotate(heads_of(key_w), cos_query, sin_query).astype(jnp.bfloat16)
        values_in = heads_of(value_w).astype(jnp.bfloat16)
        mixed, kept = attend_forward(queries, keys_in, values_in)
        mixed_flat = mixed.reshape(row_count, model_width)
        branch = jnp.dot(mixed_flat, output_w, preferred_element_type=jnp.float32)
        middle = resid + branch * rms_scale(branch) * gain_float[1]
        mlp_in = (middle * rms_scale(middle) * gain_float[2]).astype(jnp.bfloat16)
        gate_pre = jnp.dot(mlp_in, gate_w, preferred_element_type=jnp.float32)
        up_pre = jnp.dot(mlp_in, up_w, preferred_element_type=jnp.float32)
        hidden = (jax.nn.silu(gate_pre) * up_pre).astype(jnp.bfloat16)
        down_out = jnp.dot(hidden, down_w, preferred_element_type=jnp.float32)
        result = middle + down_out * rms_scale(down_out) * gain_float[3]
        flat_saved = tuple(
            (
                stored.reshape(group_len, seq_batch, stored.shape[-1])
                for stored in (
                    joined,
                    resid,
                    normed,
                    mixed_flat,
                    branch,
                    middle,
                    mlp_in,
                    gate_pre,
                    up_pre,
                    hidden,
                    down_out,
                )
            )
        )
        return (result.reshape(group_len, seq_batch, model_width), (flat_saved, kept))

    group_counts = lax.dynamic_slice_in_dim(
        jnp.take(counts, seq_order), lax.axis_index("grp") * seq_group, seq_group
    )
    first_out, first_saved = core_block(latent_in, embed_in)
    last_in = jnp.where(group_counts[None, :, None] == 2, first_out, latent_in.astype(jnp.float32))
    final_out, saved = core_block(last_in, embed_in)
    upstream = slope_in.astype(jnp.float32)
    flat_saved, kept = saved
    (
        joined,
        resid,
        normed,
        mixed_flat,
        branch,
        middle,
        mlp_in,
        gate_pre,
        up_pre,
        hidden,
        down_out,
    ) = tuple((stored.reshape(-1, stored.shape[-1]) for stored in flat_saved))
    seq_batch = upstream.shape[1]
    d_result = upstream.reshape(-1, model_width)
    d_down, gain_four = norm_back(down_out, d_result, gain_float[3])
    d_down = d_down.astype(jnp.bfloat16)
    down_part = jnp.einsum("rf,rd->fd", hidden, d_down, preferred_element_type=jnp.float32)
    d_hidden = jnp.einsum("rd,fd->rf", d_down, down_w, preferred_element_type=jnp.float32)
    sigma = jax.nn.sigmoid(gate_pre)
    d_gate = (d_hidden * up_pre * sigma * (1.0 + gate_pre * (1.0 - sigma))).astype(jnp.bfloat16)
    d_up = (d_hidden * gate_pre * sigma).astype(jnp.bfloat16)
    gate_part = jnp.einsum("rd,rf->df", mlp_in, d_gate, preferred_element_type=jnp.float32)
    up_part = jnp.einsum("rd,rf->df", mlp_in, d_up, preferred_element_type=jnp.float32)
    d_mlp = jnp.einsum(
        "rf,df->rd", d_gate, gate_w, preferred_element_type=jnp.float32
    ) + jnp.einsum("rf,df->rd", d_up, up_w, preferred_element_type=jnp.float32)
    d_middle, gain_three = norm_back(middle, d_mlp, gain_float[2])
    d_middle = d_middle + d_result
    d_branch, gain_two = norm_back(branch, d_middle, gain_float[1])
    d_branch = d_branch.astype(jnp.bfloat16)
    out_part = jnp.einsum("re,rd->ed", mixed_flat, d_branch, preferred_element_type=jnp.float32)
    d_mixed = jnp.einsum(
        "rd,ed->re", d_branch, output_w, preferred_element_type=jnp.float32
    ).astype(jnp.bfloat16)
    attend_d_mixed = d_mixed.reshape(group_len, seq_batch, HEADS, HEAD_DIM)
    queries, keys_in, values_in, log_total, mixed_raw = kept
    delta = jnp.sum(attend_d_mixed.astype(jnp.float32) * mixed_raw, -1)
    key_part = lax.all_gather(keys_in, "ctx", axis=0, tiled=True)
    value_part = lax.all_gather(values_in, "ctx", axis=0, tiled=True)
    key_pos_in = key_position(jnp.arange(key_part.shape[0], dtype=jnp.int32))
    probs_low, slopes = back_block(
        queries, key_part, value_part, attend_d_mixed, log_total, delta, query_pos, key_pos_in
    )
    d_query = HEAD_DIM ** (-0.5) * jnp.einsum(
        "qshk,kshd->qshd", slopes, key_part, preferred_element_type=jnp.float32
    )
    pull_stacked = jnp.stack([probs_low, slopes])
    d_query, stacked = (d_query, pull_stacked)
    d_key = HEAD_DIM ** (-0.5) * jnp.einsum(
        "qshk,qshd->kshd", stacked[1], queries, preferred_element_type=jnp.float32
    )
    d_value = jnp.einsum(
        "qshk,qshd->kshd", stacked[0], attend_d_mixed, preferred_element_type=jnp.float32
    )
    paired = lax.psum_scatter(
        jnp.concatenate([d_key, d_value], -1).astype(jnp.bfloat16),
        "ctx",
        scatter_dimension=0,
        tiled=True,
    ).astype(jnp.float32)
    d_query, d_key, d_value = (
        unrotate(d_query, cos_query, sin_query).astype(jnp.bfloat16),
        unrotate(paired[..., :HEAD_DIM], cos_query, sin_query).astype(jnp.bfloat16),
        paired[..., HEAD_DIM:].astype(jnp.bfloat16),
    )
    d_query = d_query.reshape(-1, model_width)
    d_key = d_key.reshape(-1, model_width)
    d_value = d_value.reshape(-1, model_width)
    query_part = jnp.einsum("rd,re->de", normed, d_query, preferred_element_type=jnp.float32)
    key_part = jnp.einsum("rd,re->de", normed, d_key, preferred_element_type=jnp.float32)
    value_part = jnp.einsum("rd,re->de", normed, d_value, preferred_element_type=jnp.float32)
    d_normed = (
        jnp.einsum("re,de->rd", d_query, query_w, preferred_element_type=jnp.float32)
        + jnp.einsum("re,de->rd", d_key, key_w, preferred_element_type=jnp.float32)
        + jnp.einsum("re,de->rd", d_value, value_w, preferred_element_type=jnp.float32)
    )
    d_resid, gain_one = norm_back(resid, d_normed, gain_float[0])
    d_resid = (d_resid + d_middle).astype(jnp.bfloat16)
    adapt_part = jnp.einsum("rk,rd->kd", joined, d_resid, preferred_element_type=jnp.float32)
    d_joined = jnp.einsum("rd,kd->rk", d_resid, adapt_w, preferred_element_type=jnp.float32)
    gain_part = jnp.stack([gain_one, gain_two, gain_three, gain_four])
    d_joined, grads = (
        d_joined.reshape(group_len, seq_batch, 2 * model_width),
        (
            adapt_part,
            query_part,
            key_part,
            value_part,
            out_part,
            gate_part,
            up_part,
            down_part,
            gain_part,
        ),
    )
    final_back, latent_back, embed_back = (
        lax.all_to_all(
            final_out.astype(jnp.bfloat16), "grp", split_axis=0, concat_axis=1, tiled=True
        ),
        lax.all_to_all(
            d_joined[..., :model_width].astype(jnp.bfloat16),
            "grp",
            split_axis=0,
            concat_axis=1,
            tiled=True,
        ),
        lax.all_to_all(
            d_joined[..., model_width:].astype(jnp.bfloat16),
            "grp",
            split_axis=0,
            concat_axis=1,
            tiled=True,
        ),
    )
    seq_index = jnp.arange(seq_total, dtype=jnp.int32)
    inverse = jnp.sum(jnp.where(seq_order[:, None] == seq_index[None, :], seq_index[:, None], 0), 0)
    (
        adapt_part,
        query_part,
        key_part,
        value_part,
        out_part,
        gate_part,
        up_part,
        down_part,
        gain_part,
    ) = grads
    summed = (
        lax.psum_scatter(adapt_part, ("grp", "ctx"), scatter_dimension=0, tiled=True),
        lax.psum_scatter(query_part, ("grp", "ctx"), scatter_dimension=0, tiled=True),
        lax.psum_scatter(key_part, ("grp", "ctx"), scatter_dimension=0, tiled=True),
        lax.psum_scatter(value_part, ("grp", "ctx"), scatter_dimension=0, tiled=True),
        lax.psum_scatter(out_part, ("grp", "ctx"), scatter_dimension=0, tiled=True),
        lax.psum_scatter(gate_part, ("grp", "ctx"), scatter_dimension=0, tiled=True),
        lax.psum_scatter(up_part, ("grp", "ctx"), scatter_dimension=0, tiled=True),
        lax.psum_scatter(down_part, ("grp", "ctx"), scatter_dimension=0, tiled=True),
        lax.psum_scatter(gain_part, ("grp", "ctx"), scatter_dimension=1, tiled=True),
    )
    return (
        jnp.take(final_back, inverse, axis=1),
        jnp.take(latent_back, inverse, axis=1),
        jnp.take(embed_back, inverse, axis=1),
        summed[0],
        summed[1],
        summed[2],
        summed[3],
        summed[4],
        summed[5],
        summed[6],
        summed[7],
        summed[8],
    )


def solution(mesh):
    placed = (
        P(("grp", "ctx"), None, None),
        P(("grp", "ctx"), None, None),
        P(("grp", "ctx"), None, None),
        P(),
        P(("grp", "ctx"), None),
        P(("grp", "ctx"), None),
        P(("grp", "ctx"), None),
        P(("grp", "ctx"), None),
        P(("grp", "ctx"), None),
        P(("grp", "ctx"), None),
        P(("grp", "ctx"), None),
        P(("grp", "ctx"), None),
        P(None, ("grp", "ctx")),
    )
    return jax.shard_map(
        on_device,
        mesh=mesh,
        in_specs=placed,
        out_specs=(
            P(("grp", "ctx"), None, None),
            P(("grp", "ctx"), None, None),
            P(("grp", "ctx"), None, None),
            P(("grp", "ctx"), None),
            P(("grp", "ctx"), None),
            P(("grp", "ctx"), None),
            P(("grp", "ctx"), None),
            P(("grp", "ctx"), None),
            P(("grp", "ctx"), None),
            P(("grp", "ctx"), None),
            P(("grp", "ctx"), None),
            P(None, ("grp", "ctx")),
        ),
        check_vma=False,
    )
```

profile of v0, /device:TPU:0, one launch (start us, length us, event | category | flops | bytes accessed | tf_op | source)
XLA Modules:
  0.0 2567.6 jit_solution(7005235177151027575)
XLA Ops:
  49.8 57.6 %all-to-all-done = bf16[32,32,1024]{2,0,1:T(8,128)(2,1)} async-done(((bf16[32,32,1024]{2,0,1:T(8,128)(2,1)}), bf16[32,32,1024]{2,0,1:T(8,128)(2,1)}, u32[]{:S(2)}, u32[]{:S(2)}) %all-to-all-start) | async-done | bytes 2097184 | tf_op jit(solution)/shard_map/all_to_all | solution.py:105
  112.5 70.7 %all-gather = bf16[32,32,4]{1,2,0:T(4,128)(2,1)S(1)} all-gather(bf16[1,32,4]{1,2,0:T(4,128)(2,1)S(1)} %bitcast.279), channel_id=1, replica_groups=mesh['grp'=8,'ctx'=4] {'grp','ctx'}, dimensions={0}, use_global_device_ids=true | all-gather | bytes 8448 | tf_op jit(solution)/shard_map/all_gather | solution.py:100
  218.0 23.9 all-gather.24.cloned.1.call-done
  253.1 17.0 subtract_convert_fusion.4
  272.8 27.1 %all-gather.16.cloned.1.call-done = bf16[1024,1024]{1,0:T(8,128)(2,1)} async-done(((bf16[32,1024]{1,0:T(8,128)(2,1)}), bf16[1024,1024]{1,0:T(8,128)(2,1)}) %all-gather.16.cloned.1.call-update) | async-done | bytes 2097168 | tf_op jit(solution)/shard_map/all_gather | solution.py:95
  323.2 35.2 %all-gather.22.cloned.1.call-done = bf16[1024,4,8,128]{3,0,2,1:T(8,128)(2,1)} async-done(((bf16[256,4,8,128]{3,0,2,1:T(8,128)(2,1)}), bf16[1024,4,8,128]{3,0,2,1:T(8,128)(2,1)}) %all-gather.22.cloned.1.call-update) | async-done | bytes 8388624 | tf_op jit(solution)/shard_map/all_gather | solution.py:126
  358.4 20.3 fusion.3
  378.7 14.6 exponential_reduce_fusion.1
  393.3 25.9 %all-gather.18.cloned.1.call-done = bf16[1024,4,8,128]{0,3,2,1:T(8,128)(2,1)} async-done(((bf16[256,4,8,128]{0,3,2,1:T(8,128)(2,1)}), bf16[1024,4,8,128]{0,3,2,1:T(8,128)(2,1)}) %all-gather.18.cloned.1.call-update) | async-done | bytes 8388624 | tf_op jit(solution)/shard_map/all_gather | solution.py:135
  419.2 18.3 convert_bitcast_fusion.3
  442.2 36.3 %all-gather.26.cloned.1.call-done = bf16[1024,1024]{1,0:T(8,128)(2,1)} async-done(((bf16[32,1024]{1,0:T(8,128)(2,1)}), bf16[1024,1024]{1,0:T(8,128)(2,1)}) %all-gather.26.cloned.1.call-update) | async-done | bytes 2097168 | tf_op jit(solution)/shard_map/all_gather | solution.py:96
  486.2 61.3 %all-gather.28.cloned.1.call-done = bf16[1024,2816]{1,0:T(8,128)(2,1)} async-done(((bf16[32,2816]{1,0:T(8,128)(2,1)}), bf16[1024,2816]{1,0:T(8,128)(2,1)}) %all-gather.28.cloned.1.call-update) | async-done | bytes 5767184 | tf_op jit(solution)/shard_map/all_gather | solution.py:97
  547.5 12.4 fusion.89
  559.9 56.8 %all-gather.30.cloned.1.call-done = bf16[1024,2816]{1,0:T(8,128)(2,1)} async-done(((bf16[32,2816]{1,0:T(8,128)(2,1)}), bf16[1024,2816]{1,0:T(8,128)(2,1)}) %all-gather.30.cloned.1.call-update) | async-done | bytes 5767184 | tf_op jit(solution)/shard_map/all_gather | solution.py:98
  616.6 69.0 %all-gather.32.cloned.1.call-done = bf16[2816,1024]{1,0:T(8,128)(2,1)} async-done(((bf16[88,1024]{1,0:T(8,128)(2,1)}), bf16[2816,1024]{1,0:T(8,128)(2,1)}) %all-gather.32.cloned.1.call-update) | async-done | bytes 5767184 | tf_op jit(solution)/shard_map/all_gather | solution.py:99
  685.6 22.2 multiply_reduce_fusion.12
  740.2 14.5 subtract_convert_fusion.2
  771.2 53.3 %all_to_all.93 = bf16[32,32,1024]{2,0,1:T(8,128)(2,1)S(1)} all-to-all(bf16[32,32,1024]{2,0,1:T(8,128)(2,1)S(1)} %copy.308), channel_id=1, replica_groups=mesh['grp'=8,'ctx'=4] {'grp'}, dimensions={1} | all-to-all | bytes 4194304 | tf_op jit(solution)/shard_map/all_to_all | solution.py:111
  838.8 18.5 fusion.4
  857.3 14.5 exponential_reduce_fusion
  875.4 19.8 bitcast_convert_fusion
  917.7 9.1 fusion.96
  926.9 14.4 multiply_convert_fusion.3
  941.3 10.0 multiply_reduce_fusion.8
  966.8 18.7 multiply_convert_fusion.1
  985.5 10.0 fusion.97
  995.6 10.9 multiply_reduce_fusion.1
  1021.4 18.0 convert_bitcast_fusion
  1043.1 24.9 fusion.1
  1068.0 10.3 fusion.10
  1078.3 13.9 pad_maximum_fusion
  1092.2 15.2 multiply_bitcast_fusion
  1107.4 111.0 %reduce-scatter.13.cloned.1.call-done = bf16[256,4,8,256]{3,0,2,1:T(8,128)(2,1)} async-done(((bf16[1024,4,8,256]{3,0,2,1:T(8,128)(2,1)}), bf16[256,4,8,256]{3,0,2,1:T(8,128)(2,1)}) %reduce-scatter.13.cloned.1.call-update) | async-done | bytes 4194320 | tf_op jit(solution)/shard_map/reduce_scatter | solution.py:250
  1250.7 11.9 fusion.100
  1262.7 11.8 fusion.99
  1274.6 11.9 fusion.98
  1334.0 9.3 convolution_convert_fusion
  1354.9 27.7 %all-to-all-done.2 = bf16[256,4,1024]{2,1,0:T(4,128)(2,1)S(1)} async-done(((bf16[256,4,1024]{2,1,0:T(4,128)(2,1)}), bf16[256,4,1024]{2,1,0:T(4,128)(2,1)S(1)}, u32[]{:S(2)}, u32[]{:S(2)}) %all-to-all-start.2) | async-done | bytes 2097184 | tf_op jit(solution)/shard_map/all_to_all | solution.py:292
  1382.6 60.5 %all_to_all.94 = bf16[256,4,1024]{2,1,0:T(4,128)(2,1)} all-to-all(bf16[256,4,1024]{2,1,0:T(4,128)(2,1)} %get-tuple-element.103), channel_id=1, replica_groups=mesh['grp'=8,'ctx'=4] {'grp'}, dimensions={0} | all-to-all | bytes 4194304 | tf_op jit(solution)/shard_map/all_to_all | solution.py:295
  1460.8 39.8 %all-to-all-done.5 = bf16[256,4,1024]{2,1,0:T(4,128)(2,1)} async-done(((bf16[256,4,1024]{2,1,0:T(4,128)(2,1)}), bf16[256,4,1024]{2,1,0:T(4,128)(2,1)}, u32[]{:S(2)}, u32[]{:S(2)}) %all-to-all-start.5) | async-done | bytes 2097184 | tf_op jit(solution)/shard_map/all_to_all | solution.py:302
  1518.1 10.8 reduce-scatter.23.cloned.1.call-done
  1529.0 157.7 %reduce-scatter.29.cloned.1.call-done = f32[88,1024]{1,0:T(8,128)} async-done(((f32[2816,1024]{1,0:T(8,128)}), f32[88,1024]{1,0:T(8,128)}) %reduce-scatter.29.cloned.1.call-update) | async-done | bytes 360464 | tf_op jit(solution)/shard_map/reduce_scatter | solution.py:331
  1686.7 153.5 %reduce-scatter.27.cloned.1.call-done = f32[32,2816]{1,0:T(8,128)} async-done(((f32[1024,2816]{1,0:T(8,128)}), f32[32,2816]{1,0:T(8,128)}) %reduce-scatter.27.cloned.1.call-update) | async-done | bytes 360464 | tf_op jit(solution)/shard_map/reduce_scatter | solution.py:330
  1840.2 153.4 %reduce-scatter.25.cloned.1.call-done = f32[32,2816]{1,0:T(8,128)} async-done(((f32[1024,2816]{1,0:T(8,128)}), f32[32,2816]{1,0:T(8,128)}) %reduce-scatter.25.cloned.1.call-update) | async-done | bytes 360464 | tf_op jit(solution)/shard_map/reduce_scatter | solution.py:329
  1993.6 139.8 %reduce-scatter.21.cloned.1.call-done = f32[32,1024]{1,0:T(8,128)} async-done(((f32[1024,1024]{1,0:T(8,128)}), f32[32,1024]{1,0:T(8,128)}) %reduce-scatter.21.cloned.1.call-update) | async-done | bytes 131088 | tf_op jit(solution)/shard_map/reduce_scatter | solution.py:327
  2133.4 139.6 %reduce-scatter.19.cloned.1.call-done = f32[32,1024]{1,0:T(8,128)} async-done(((f32[1024,1024]{1,0:T(8,128)}), f32[32,1024]{1,0:T(8,128)}) %reduce-scatter.19.cloned.1.call-update) | async-done | bytes 131088 | tf_op jit(solution)/shard_map/reduce_scatter | solution.py:326
  2273.0 139.6 %reduce-scatter.17.cloned.1.call-done = f32[32,1024]{1,0:T(8,128)} async-done(((f32[1024,1024]{1,0:T(8,128)}), f32[32,1024]{1,0:T(8,128)}) %reduce-scatter.17.cloned.1.call-update) | async-done | bytes 131088 | tf_op jit(solution)/shard_map/reduce_scatter | solution.py:325
  2412.6 147.6 %reduce-scatter.15.cloned.1.call-done = f32[64,1024]{1,0:T(8,128)} async-done(((f32[2048,1024]{1,0:T(8,128)}), f32[64,1024]{1,0:T(8,128)}) %reduce-scatter.15.cloned.1.call-update) | async-done | bytes 262160 | tf_op jit(solution)/shard_map/reduce_scatter | solution.py:324
  (315 shorter events, 381.2 us)
Async XLA Ops:
  7.2 193.6 %all-gather.14.cloned.1.call-start = ((), (), s32[]{:S(2)}) async-start(), calls=%async_computation.16 | async-start | bytes 4325376 | tf_op jit(solution)/shard_map/all_gather | solution.py:92
  7.9 202.3 %all-gather.20.cloned.1.call-start = ((), (), s32[]{:S(2)}) async-start(), calls=%async_computation.19 | async-start | bytes 2162688 | tf_op jit(solution)/shard_map/all_gather | solution.py:94
  39.3 68.1 %all-to-all-start = ((bf16[32,32,1024]{2,0,1:T(8,128)(2,1)}), bf16[32,32,1024]{2,0,1:T(8,128)(2,1)}, u32[]{:S(2)}, u32[]{:S(2)}) async-start(bf16[32,32,1024]{2,0,1:T(8,128)(2,1)} %copy.281), calls=%async_computation | async-start | bytes 4194304 | tf_op jit(solution)/shard_map/all_to_all | solution.py:105
  46.6 195.2 %all-gather.24.cloned.1.call-start = ((), (), s32[]{:S(2)}) async-start(), calls=%async_computation.21 | async-start | bytes 2162688 | tf_op jit(solution)/shard_map/all_gather | solution.py:93
  47.4 65.1 %copy-start.51 = (bf16[4,32]{1,0:T(4,128)(2,1)S(1)}, bf16[4,32]{1,0:T(4,128)(2,1)}, u32[]{:S(2)}) copy-start(bf16[4,32]{1,0:T(4,128)(2,1)} %param.27) | copy-start | bytes 772
  107.5 84.0 %all-to-all-start.1 = ((bf16[32,32,1024]{2,0,1:T(8,128)(2,1)}), bf16[32,32,1024]{2,0,1:T(8,128)(2,1)}, u32[]{:S(2)}, u32[]{:S(2)}) async-start(bf16[32,32,1024]{2,0,1:T(8,128)(2,1)} %copy.283), calls=%async_computation.1 | async-start | bytes 4194304 | tf_op jit(solution)/shard_map/all_to_all | solution.py:108
  111.8 188.0 %all-gather.16.cloned.1.call-start = ((), (), s32[]{:S(2)}) async-start(), calls=%async_computation.17 | async-start | bytes 2162688 | tf_op jit(solution)/shard_map/all_gather | solution.py:95
  112.4 246.0 %all-gather.22.cloned.1.call-start = ((), (), s32[]{:S(2)}) async-start(), calls=%async_computation.20 | async-start | bytes 10485760 | tf_op jit(solution)/shard_map/all_gather | solution.py:126
  183.4 524.4 %copy-start.46 = (f32[1,1024]{1,0:T(1,128)}, f32[1,1024]{1,0:T(1,128)S(1)}, u32[]{:S(2)}) copy-start(f32[1,1024]{1,0:T(1,128)S(1)} %get-tuple-element.118) | copy-start | bytes 12292
  183.4 542.0 %copy-start.44 = (f32[1,1024]{1,0:T(1,128)}, f32[1,1024]{1,0:T(1,128)S(1)}, u32[]{:S(2)}) copy-start(f32[1,1024]{1,0:T(1,128)S(1)} %get-tuple-element.121) | copy-start | bytes 12292
  183.9 556.3 %copy-start.23 = (f32[256,64]{1,0:T(8,128)}, f32[256,64]{1,0:T(8,128)S(1)}, u32[]{:S(2)}) copy-start(f32[256,64]{1,0:T(8,128)S(1)} %get-tuple-element.122) | copy-start | bytes 196612
  183.9 556.3 %copy-start.25 = (f32[256,64]{1,0:T(8,128)}, f32[256,64]{1,0:T(8,128)S(1)}, u32[]{:S(2)}) copy-start(f32[256,64]{1,0:T(8,128)S(1)} %get-tuple-element.123) | copy-start | bytes 196612
  191.5 9.3 copy-start.22
  210.2 31.6 %copy-start.37 = (bf16[1024,1024]{0,1:T(8,128)(2,1)}, bf16[1024,1024]{0,1:T(8,128)(2,1)S(1)}, u32[]{:S(2)}) copy-start(bf16[1024,1024]{0,1:T(8,128)(2,1)S(1)} %multiply_convert_fusion.10) | copy-start | bytes 6291460
  272.7 146.5 %all-gather.18.cloned.1.call-start = ((), (), s32[]{:S(2)}) async-start(), calls=%async_computation.18 | async-start | bytes 10485760 | tf_op jit(solution)/shard_map/all_gather | solution.py:135
  310.8 167.7 %all-gather.26.cloned.1.call-start = ((), (), s32[]{:S(2)}) async-start(), calls=%async_computation.22 | async-start | bytes 2162688 | tf_op jit(solution)/shard_map/all_gather | solution.py:96
  311.6 235.9 %all-gather.28.cloned.1.call-start = ((), (), s32[]{:S(2)}) async-start(), calls=%async_computation.23 | async-start | bytes 5947392 | tf_op jit(solution)/shard_map/all_gather | solution.py:97
  312.3 304.3 %all-gather.30.cloned.1.call-start = ((), (), s32[]{:S(2)}) async-start(), calls=%async_computation.24 | async-start | bytes 5947392 | tf_op jit(solution)/shard_map/all_gather | solution.py:98
  313.1 372.5 %all-gather.32.cloned.1.call-start = ((), (), s32[]{:S(2)}) async-start(), calls=%async_computation.25 | async-start | bytes 5947392 | tf_op jit(solution)/shard_map/all_gather | solution.py:99
  313.7 525.2 %all-gather.36.cloned.1.call-start = ((), (), s32[]{:S(2)}) async-start(), calls=%async_computation.27 | async-start | bytes 10485760 | tf_op jit(solution)/shard_map/all_gather | solution.py:126
  314.9 560.5 %copy-start.14 = (pred[256,1024]{0,1:T(8,128)(4,1)}, pred[256,1024]{0,1:T(8,128)(4,1)S(1)}, u32[]{:S(2)}) copy-start(pred[256,1024]{0,1:T(8,128)(4,1)S(1)} %broadcast_compare_fusion) | copy-start | bytes 786436
  757.2 118.3 %all-gather.34.cloned.1.call-start = ((), (), s32[]{:S(2)}) async-start(), calls=%async_computation.26 | async-start | bytes 10485760 | tf_op jit(solution)/shard_map/all_gather | solution.py:135
  768.2 450.2 %reduce-scatter.13.cloned.1.call-start = ((), (), s32[]{:S(2)}) async-start(), calls=%async_computation.28 | async-start | bytes 20971520 | tf_op jit(solution)/shard_map/reduce_scatter | solution.py:250
  871.9 23.4 copy-start.48
  917.3 9.6 slice-start.3
  917.7 9.1 copy-start.33
  917.7 23.6 slice-start.5
  926.9 14.5 slice-start.6
  966.8 18.7 copy-start.29
  985.5 10.0 copy-start.8
  995.6 10.9 copy-start.5
  995.6 10.9 copy-start.10
  1043.1 24.9 copy-start.18
  1043.1 24.9 copy-start.19
  1092.1 360.0 %reduce-scatter.31.cloned.1.call-start = ((), (), s32[]{:S(2)}) async-start(), calls=%async_computation.37 | async-start | bytes 540672
  1107.4 114.4 %copy-start.24 = (f32[256,64]{1,0:T(8,128)S(1)}, f32[256,64]{1,0:T(8,128)}, u32[]{:S(2)}) copy-start(f32[256,64]{1,0:T(8,128)} %copy-done.23) | copy-start | bytes 196612
  1107.4 114.4 %copy-start.26 = (f32[256,64]{1,0:T(8,128)S(1)}, f32[256,64]{1,0:T(8,128)}, u32[]{:S(2)}) copy-start(f32[256,64]{1,0:T(8,128)} %copy-done.25) | copy-start | bytes 196612
  1243.9 285.1 %reduce-scatter.23.cloned.1.call-start = ((), (), s32[]{:S(2)}) async-start(), calls=%async_computation.33 | async-start | bytes 4325376 | tf_op jit(solution)/shard_map/reduce_scatter | solution.py:328
  1250.6 436.0 %reduce-scatter.29.cloned.1.call-start = ((), (), s32[]{:S(2)}) async-start(), calls=%async_computation.36 | async-start | bytes 11894784 | tf_op jit(solution)/shard_map/reduce_scatter | solution.py:331
  1262.7 577.5 %reduce-scatter.27.cloned.1.call-start = ((), (), s32[]{:S(2)}) async-start(), calls=%async_computation.35 | async-start | bytes 11894784 | tf_op jit(solution)/shard_map/reduce_scatter | solution.py:330
  1274.5 719.0 %reduce-scatter.25.cloned.1.call-start = ((), (), s32[]{:S(2)}) async-start(), calls=%async_computation.34 | async-start | bytes 11894784 | tf_op jit(solution)/shard_map/reduce_scatter | solution.py:329
  1286.5 846.8 %reduce-scatter.21.cloned.1.call-start = ((), (), s32[]{:S(2)}) async-start(), calls=%async_computation.32 | async-start | bytes 4325376 | tf_op jit(solution)/shard_map/reduce_scatter | solution.py:327
  1293.2 979.8 %reduce-scatter.19.cloned.1.call-start = ((), (), s32[]{:S(2)}) async-start(), calls=%async_computation.31 | async-start | bytes 4325376 | tf_op jit(solution)/shard_map/reduce_scatter | solution.py:326
  1299.9 1112.8 %reduce-scatter.17.cloned.1.call-start = ((), (), s32[]{:S(2)}) async-start(), calls=%async_computation.30 | async-start | bytes 4325376 | tf_op jit(solution)/shard_map/reduce_scatter | solution.py:325
  1305.8 1254.4 %reduce-scatter.15.cloned.1.call-start = ((), (), s32[]{:S(2)}) async-start(), calls=%async_computation.29 | async-start | bytes 8650752 | tf_op jit(solution)/shard_map/reduce_scatter | solution.py:324
  1328.2 54.4 %all-to-all-start.2 = ((bf16[256,4,1024]{2,1,0:T(4,128)(2,1)}), bf16[256,4,1024]{2,1,0:T(4,128)(2,1)S(1)}, u32[]{:S(2)}, u32[]{:S(2)}) async-start(bf16[256,4,1024]{2,1,0:T(4,128)(2,1)} %convert_element_type.148), calls=%async_computation.2 | async-start | bytes 4194304 | tf_op jit(solution)/shard_map/all_to_all | solution.py:292
  1443.1 57.5 %all-to-all-start.5 = ((bf16[256,4,1024]{2,1,0:T(4,128)(2,1)}), bf16[256,4,1024]{2,1,0:T(4,128)(2,1)}, u32[]{:S(2)}, u32[]{:S(2)}) async-start(bf16[256,4,1024]{2,1,0:T(4,128)(2,1)} %get-tuple-element.102), calls=%async_computation.6 | async-start | bytes 4194304 | tf_op jit(solution)/shard_map/all_to_all | solution.py:302
  1513.2 1047.1 %copy-start.1 = (bf16[32,32,1024]{2,1,0:T(8,128)(2,1)S(1)}, bf16[32,32,1024]{2,1,0:T(8,128)(2,1)}, u32[]{:S(2)}) copy-start(bf16[32,32,1024]{2,1,0:T(8,128)(2,1)} %param.17) | copy-start | bytes 6291460
  (42 other events, 175.8 us)
Sparse Core Ops, SparseCore 0:
  10.9 93.2 all-gather.13
  107.1 76.5 all-gather.19
  186.6 55.2 all-gather.23
  244.6 55.2 all-gather.15
  301.2 57.1 all-gather.21
  359.8 59.3 all-gather.17
  422.1 56.3 all-gather.25
  481.4 66.1 all-gather.27
  550.4 66.2 all-gather.29
  619.3 66.2 all-gather.31
  757.3 57.2 all-gather.35
  816.0 59.3 all-gather.33
  1092.3 126.0 reduce-scatter.12
  1244.0 135.9 reduce-scatter.30
  1382.7 146.2 reduce-scatter.22
  1531.7 154.9 reduce-scatter.28
  1689.4 150.7 reduce-scatter.26
  1842.9 150.6 reduce-scatter.24
  1996.4 136.8 reduce-scatter.20
  2136.0 136.9 reduce-scatter.18
  2275.9 136.7 reduce-scatter.16
  2415.5 144.7 reduce-scatter.14
where the time goes:
time: 2580 us; the launch traced here: 2570 us
  waiting for transfers between devices  1620 us (63%)
  matrix products  390 us (15%)
  local copies, waits for them, and re-layouts  196 us (8%)
  blocking collectives  184 us (7%)
  other arithmetic  135 us (5%)
    reduce_scatter x1, waiting for transfers between devices, on_device(): lax.psum_scatter(down_part, ('grp', 'ctx'), scatter_dimension=0, tiled=True)  158 us
    reduce_scatter x1, waiting for transfers between devices, on_device(): lax.psum_scatter(up_part, ('grp', 'ctx'), scatter_dimension=0, tiled=True)  153 us
    reduce_scatter x1, waiting for transfers between devices, on_device(): lax.psum_scatter(gate_part, ('grp', 'ctx'), scatter_dimension=0, tiled=True)  153 us
    reduce_scatter x1, waiting for transfers between devices, on_device(): lax.psum_scatter(adapt_part, ('grp', 'ctx'), scatter_dimension=0, tiled=T...  148 us
    reduce_scatter x1, waiting for transfers between devices, on_device(): lax.psum_scatter(value_part, ('grp', 'ctx'), scatter_dimension=0, tiled=T...  140 us
    reduce_scatter x1, waiting for transfers between devices, on_device(): lax.psum_scatter(key_part, ('grp', 'ctx'), scatter_dimension=0, tiled=True)  140 us
    reduce_scatter x1, waiting for transfers between devices, on_device(): lax.psum_scatter(query_part, ('grp', 'ctx'), scatter_dimension=0, tiled=T...  140 us
    reduce_scatter x1, waiting for transfers between devices, on_device(): lax.psum_scatter(jnp.concatenate([d_key, d_value], -1).astype(jnp.bfloat1...  111 us
  transfers between devices with their start and end apart: 26, of which 21 were waited for; matrix products, arithmetic and copies ran while one was open for 16% of the time, Pallas kernels for 0%

commit v1 on v0

--- a/solution.py
+++ b/solution.py
@@ -1,6 +1,10 @@
+import functools
+
 import jax
 import jax.numpy as jnp
 from jax import lax
+from jax.experimental import pallas as pl
+from jax.experimental.pallas import tpu as pltpu
 from jax.sharding import PartitionSpec as P
 
 HEADS = 8
@@ -66,7 +70,7 @@
     return (probs.astype(jnp.bfloat16), slopes)
 
 
-def on_device(
+def spread_on_device(
     latents,
     embeds,
     cotangent,
@@ -347,6 +351,453 @@
     )
 
 
+BOTH = ("grp", "ctx")
+LOG2E = 1.4426950408889634
+SCALE = HEAD_DIM ** (-0.5)
+TILE = 256
+NEG = -1e30
+
+
+def grid_sizes():
+    ctx = lax.axis_size("ctx")
+    x_size = ctx // 2
+    return lax.axis_size("grp") // x_size, x_size, x_size, 2
+
+
+def grid_place():
+    z_size, y_size, x_size, k_size = grid_sizes()
+    g, c = lax.axis_index("grp"), lax.axis_index("ctx")
+    return g // y_size, g % y_size, c // k_size, c % k_size
+
+
+def send(values, axis, shift=None, keep=None):
+    sizes = grid_sizes()
+    pairs = []
+    for flat in range(sizes[0] * sizes[1] * sizes[2] * sizes[3]):
+        rest, spot = flat, [0, 0, 0, 0]
+        for at in (3, 2, 1, 0):
+            spot[at] = rest % sizes[at]
+            rest //= sizes[at]
+        own = spot[axis]
+        other = 1 - own if shift is None else own + shift
+        if 0 <= other < sizes[axis] and (keep is None or keep(own)):
+            spot[axis] = other
+            target = ((spot[0] * sizes[1] + spot[1]) * sizes[2] + spot[2]) * sizes[3] + spot[3]
+            pairs.append((flat, target))
+    return lax.ppermute(values, BOTH, pairs)
+
+
+def join_pair(values, axis, spot, at):
+    other = send(values, axis)
+    first = jnp.where(spot == 0, values, other)
+    second = jnp.where(spot == 0, other, values)
+    return jnp.stack([first, second], at)
+
+
+def gather_rows(shard):
+    z_size = grid_sizes()[0]
+    z, y, x, k = grid_place()
+    rows, width = shard.shape
+    up, down = [shard], [shard]
+    for step in range(1, z_size):
+        up.append(send(up[-1], 0, 1, lambda own, s=step: own >= s - 1))
+        down.append(send(down[-1], 0, -1, lambda own, s=step: own <= z_size - s))
+    line = lax.dynamic_update_index_in_dim(jnp.zeros((z_size, rows, width), shard.dtype), shard, z, 0)
+    for step in range(1, z_size):
+        block = jnp.where(z >= step, up[step], down[z_size - step])
+        line = lax.dynamic_update_index_in_dim(line, block, (z - step + z_size) % z_size, 0)
+    half = z_size // 2
+    low, high = line[:half], line[half:]
+    low = join_pair(low, 2, x, 1)
+    high = join_pair(high, 1, y, 1)
+    low = join_pair(low, 1, y, 1)
+    high = join_pair(high, 2, x, 2)
+    chip = jnp.concatenate([low, high], 0)
+    return join_pair(chip, 3, k, 3).reshape(-1, rows, width)
+
+
+def fold_pair(values, axis, spot, at):
+    leaving = lax.dynamic_index_in_dim(values, 1 - spot, at, keepdims=False).astype(jnp.bfloat16)
+    staying = lax.dynamic_index_in_dim(values, spot, at, keepdims=False).astype(jnp.float32)
+    return (staying + send(leaving, axis).astype(jnp.float32)).astype(jnp.bfloat16)
+
+
+def scatter_rows(blocks):
+    sizes = grid_sizes()
+    z_size = sizes[0]
+    z, y, x, k = grid_place()
+    chip = fold_pair(blocks.reshape(sizes + blocks.shape[1:]), 3, k, 3)
+    half = z_size // 2
+    low, high = chip[:half], chip[half:]
+    low = fold_pair(low, 1, y, 1)
+    high = fold_pair(high, 2, x, 2)
+    low = fold_pair(low, 2, x, 1)
+    high = fold_pair(high, 1, y, 1)
+    line = jnp.concatenate([low, high], 0)
+    up = down = jnp.zeros(line.shape[1:], line.dtype)
+    for step in range(1, z_size):
+        rising = lax.dynamic_index_in_dim(line, (z + z_size - step) % z_size, 0, keepdims=False)
+        rising = (rising.astype(jnp.float32) + up.astype(jnp.float32)).astype(jnp.bfloat16)
+        up = send(rising, 0, 1, lambda own, s=step: own <= s - 1)
+        sinking = lax.dynamic_index_in_dim(line, (z + step) % z_size, 0, keepdims=False)
+        sinking = (sinking.astype(jnp.float32) + down.astype(jnp.float32)).astype(jnp.bfloat16)
+        down = send(sinking, 0, -1, lambda own, s=step: own >= z_size - s)
+    own = lax.dynamic_index_in_dim(line, z, 0, keepdims=False)
+    return own.astype(jnp.float32) + up.astype(jnp.float32) + down.astype(jnp.float32)
+
+
+def dot_t(left, right):
+    return lax.dot_general(left, right, (((1,), (1,)), ((), ())), preferred_element_type=jnp.float32)
+
+
+def dot_n(left, right):
+    return jnp.dot(left, right, preferred_element_type=jnp.float32)
+
+
+def dot_w(left, right):
+    return lax.dot_general(left, right, (((0,), (0,)), ((), ())), preferred_element_type=jnp.float32)
+
+
+def below(rows, columns):
+    at_row = lax.broadcasted_iota(jnp.int32, (rows, columns), 0)
+    at_column = lax.broadcasted_iota(jnp.int32, (rows, columns), 1)
+    return at_column <= at_row
+
+
+def whole_attend(q_ref, k_ref, v_ref, o_ref, log_ref):
+    head = pl.program_id(0)
+    length = q_ref.shape[0]
+    lane = lax.broadcasted_iota(jnp.int32, (TILE, 128), 1)
+    for at in range(length // TILE):
+        rows = pl.ds(at * TILE, TILE)
+        seen = (at + 1) * TILE
+        raw = dot_t(q_ref[rows, :], k_ref[:seen, :]) * (SCALE * LOG2E)
+        last = jnp.where(below(TILE, TILE), raw[:, at * TILE :], NEG)
+        raw = jnp.concatenate([raw[:, : at * TILE], last], 1) if at else last
+        top = jnp.max(raw, 1, keepdims=True)
+        weight = jnp.exp2(raw - top)
+        total = jnp.sum(weight, 1, keepdims=True)
+        mixed = dot_n(weight.astype(jnp.bfloat16), v_ref[:seen, :])
+        o_ref[rows, :] = (mixed / total).astype(o_ref.dtype)
+        log_total = top + jnp.log2(total)
+        log_ref[rows, :] = jnp.where(lane == head, log_total, log_ref[rows, :])
+
+
+def attend_whole(queries, keys_in, values_in):
+    length, width = queries.shape
+    head_block = pl.BlockSpec((length, HEAD_DIM), lambda h: (0, h))
+    return pl.pallas_call(
+        whole_attend,
+        grid=(width // HEAD_DIM,),
+        in_specs=[head_block] * 3,
+        out_specs=[head_block, pl.BlockSpec((length, 128), lambda h: (0, 0))],
+        out_shape=[
+            jax.ShapeDtypeStruct((length, width), jnp.bfloat16),
+            jax.ShapeDtypeStruct((length, 128), jnp.float32),
+        ],
+        compiler_params=pltpu.CompilerParams(vmem_limit_bytes=32 * 2**20),
+        cost_estimate=pl.CostEstimate(
+            flops=2 * length * length * width, bytes_accessed=8 * length * width, transcendentals=0
+        ),
+        name="attend_whole",
+    )(queries, keys_in, values_in)
+
+
+def shared_attend(block_len, core_ref, q_ref, k_ref, v_ref, ok_ref, ov_ref, o_ref):
+    core = core_ref[0]
+    length = q_ref.shape[0]
+    for at in range(length // TILE):
+        rows = pl.ds(at * TILE, TILE)
+        seen = (at + 1) * TILE
+        queries = q_ref[rows, :]
+        raw = dot_t(queries, k_ref[:seen, :]) * (SCALE * LOG2E)
+        far = dot_t(queries, ok_ref[:seen, :]) * (SCALE * LOG2E)
+        at_row = lax.broadcasted_iota(jnp.int32, (TILE, TILE), 0)
+        at_column = lax.broadcasted_iota(jnp.int32, (TILE, TILE), 1)
+        near_last = jnp.where(at_column <= at_row, raw[:, at * TILE :], NEG)
+        far_ok = at_column // block_len < at_row // block_len + core
+        far_last = jnp.where(far_ok, far[:, at * TILE :], NEG)
+        raw = jnp.concatenate([raw[:, : at * TILE], near_last], 1) if at else near_last
+        far = jnp.concatenate([far[:, : at * TILE], far_last], 1) if at else far_last
+        top = jnp.maximum(jnp.max(raw, 1, keepdims=True), jnp.max(far, 1, keepdims=True))
+        weight = jnp.exp2(raw - top)
+        far_weight = jnp.exp2(far - top)
+        total = jnp.sum(weight, 1, keepdims=True) + jnp.sum(far_weight, 1, keepdims=True)
+        mixed = dot_n(weight.astype(jnp.bfloat16), v_ref[:seen, :])
+        mixed = mixed + dot_n(far_weight.astype(jnp.bfloat16), ov_ref[:seen, :])
+        o_ref[rows, :] = (mixed / total).astype(o_ref.dtype)
+
+
+def attend_shared(core, block_len, queries, keys_in, values_in, far_keys, far_values):
+    length, width = queries.shape
+    head_block = pl.BlockSpec((length, HEAD_DIM), lambda h: (0, h))
+    return pl.pallas_call(
+        functools.partial(shared_attend, block_len),
+        grid=(width // HEAD_DIM,),
+        in_specs=[pl.BlockSpec(memory_space=pltpu.SMEM)] + [head_block] * 5,
+        out_specs=head_block,
+        out_shape=jax.ShapeDtypeStruct((length, width), jnp.bfloat16),
+        compiler_params=pltpu.CompilerParams(vmem_limit_bytes=32 * 2**20),
+        cost_estimate=pl.CostEstimate(
+            flops=4 * length * length * width, bytes_accessed=12 * length * width, transcendentals=0
+        ),
+        name="attend_shared",
+    )(core.reshape(1), queries, keys_in, values_in, far_keys, far_values)
+
+
+def whole_attend_back(
+    q_ref, k_ref, v_ref, o_ref, do_ref, log_ref, cos_ref, sin_ref, dq_ref, dk_ref, dv_ref, dk_sum, dv_sum
+):
+    head = pl.program_id(0)
+    length = q_ref.shape[0]
+    lane = lax.broadcasted_iota(jnp.int32, (TILE, 128), 1)
+
+    def unrotated(grads, rows):
+        turned = pltpu.roll(grads, HEAD_DIM // 2, 1)
+        return grads * cos_ref[rows, :] - turned * sin_ref[rows, :]
+
+    for at in range(length // TILE):
+        rows = pl.ds(at * TILE, TILE)
+        seen = (at + 1) * TILE
+        queries, d_mixed = q_ref[rows, :], do_ref[rows, :]
+        log_total = jnp.sum(jnp.where(lane == head, log_ref[rows, :], 0.0), 1, keepdims=True)
+        delta = jnp.sum(d_mixed.astype(jnp.float32) * o_ref[rows, :].astype(jnp.float32), 1, keepdims=True)
+        raw = dot_t(queries, k_ref[:seen, :]) * (SCALE * LOG2E)
+        last = jnp.where(below(TILE, TILE), raw[:, at * TILE :], NEG)
+        raw = jnp.concatenate([raw[:, : at * TILE], last], 1) if at else last
+        probs = jnp.exp2(raw - log_total)
+        d_probs = dot_t(d_mixed, v_ref[:seen, :])
+        slopes = (probs * (d_probs - delta)).astype(jnp.bfloat16)
+        d_query = dot_n(slopes, k_ref[:seen, :]) * SCALE
+        dq_ref[rows, :] = unrotated(d_query, rows).astype(dq_ref.dtype)
+        d_value = dot_w(probs.astype(jnp.bfloat16), d_mixed)
+        d_key = dot_w(slopes, queries)
+        if at:
+            before = pl.ds(0, at * TILE)
+            dv_sum[before, :] += d_value[: at * TILE]
+            dk_sum[before, :] += d_key[: at * TILE]
+        dv_sum[rows, :] = d_value[at * TILE :]
+        dk_sum[rows, :] = d_key[at * TILE :]
+    everything = pl.ds(0, length)
+    dk_ref[...] = unrotated(dk_sum[...] * SCALE, everything).astype(dk_ref.dtype)
+    dv_ref[...] = dv_sum[...].astype(dv_ref.dtype)
+
+
+def attend_whole_back(queries, keys_in, values_in, mixed, d_mixed, log_total, cos_full, sin_full):
+    length, width = queries.shape
+    head_block = pl.BlockSpec((length, HEAD_DIM), lambda h: (0, h))
+    fixed = pl.BlockSpec((length, 128), lambda h: (0, 0))
+    return pl.pallas_call(
+        whole_attend_back,
+        grid=(width // HEAD_DIM,),
+        in_specs=[head_block] * 5 + [fixed] * 3,
+        out_specs=[head_block] * 3,
+        out_shape=[jax.ShapeDtypeStruct((length, width), jnp.bfloat16)] * 3,
+        scratch_shapes=[pltpu.VMEM((length, HEAD_DIM), jnp.float32)] * 2,
+        compiler_params=pltpu.CompilerParams(vmem_limit_bytes=40 * 2**20),
+        cost_estimate=pl.CostEstimate(
+            flops=5 * length * length * width, bytes_accessed=16 * length * width, transcendentals=0
+        ),
+        name="attend_whole_back",
+    )(queries, keys_in, values_in, mixed, d_mixed, log_total, cos_full, sin_full)
+
+
+def rope_full(positions):
+    cosine, sine = rope_table(positions)
+    return jnp.concatenate([cosine, cosine], 1), jnp.concatenate([-sine, sine], 1)
+
+
+def rotate_rows(values, cos_full, sin_full):
+    rows, width = values.shape
+    heads = values.reshape(rows, width // HEAD_DIM, HEAD_DIM)
+    half = HEAD_DIM // 2
+    turned = jnp.concatenate([heads[..., half:], heads[..., :half]], -1)
+    return (heads * cos_full[:, None] + turned * sin_full[:, None]).reshape(rows, width)
+
+
+def paired_on_device(
+    latents, embeds, cotangent, counts, w_adapt, w_query, w_key, w_value, w_out, w_gate, w_up, w_down, gains
+):
+    block_len, seqs, width = latents.shape
+    parts = lax.axis_size("grp") * lax.axis_size("ctx")
+    length = block_len * parts
+    core = grid_place()[3]
+    owner = core == 0
+
+    twice = counts == 2
+    slot = jnp.where(
+        twice,
+        2 * (jnp.cumsum(twice.astype(jnp.int32)) - 1),
+        2 * (jnp.cumsum((~twice).astype(jnp.int32)) - 1) + 1,
+    )
+    row_count = block_len * seqs
+    target = (slot[None, :] * block_len + jnp.arange(block_len, dtype=jnp.int32)[:, None]).reshape(row_count)
+    order = (lax.broadcasted_iota(jnp.int32, (row_count, row_count), 0) == target[None, :]).astype(jnp.bfloat16)
+
+    def to_slots(values):
+        return dot_n(order, values.reshape(row_count, width)).astype(jnp.bfloat16)
+
+    def from_slots(values):
+        return dot_w(order, values.reshape(row_count, width)).astype(jnp.bfloat16)
+
+    def exchange(values):
+        return lax.all_to_all(values, BOTH, split_axis=0, concat_axis=0, tiled=True)
+
+    adapt_w = gather_rows(w_adapt).reshape(-1, width)
+    gain_rows = jnp.pad(gains.reshape(1, -1), ((0, 15), (0, width - gains.size)))
+    side = w_query.shape[0]
+    square = gather_rows(jnp.concatenate([w_query, w_key, w_value, w_out, gain_rows], 0))
+    query_w, key_w, value_w, output_w = (
+        square[:, at * side : (at + 1) * side].reshape(width, width) for at in range(4)
+    )
+    gain_float = (
+        square[:, 4 * side, : gains.size]
+        .reshape(parts, gains.shape[0], gains.shape[1])
+        .transpose(1, 0, 2)
+        .reshape(gains.shape[0], width)
+        .astype(jnp.float32)
+    )
+    gate_w = gather_rows(w_gate).reshape(width, -1)
+    up_w = gather_rows(w_up).reshape(width, -1)
+    down_w = gather_rows(w_down).reshape(-1, width)
+
+    latent_slots, embed_slots = to_slots(latents), to_slots(embeds)
+    upstream = exchange(to_slots(cotangent).reshape(parts, block_len, width)).reshape(length, width)
+    embed_part = dot_n(embed_slots, adapt_w[width:])
+    adapted = (dot_n(latent_slots, adapt_w[:width]) + embed_part).reshape(parts, block_len, width)
+    embed_part = embed_part.reshape(parts, block_len, width)
+    pair_at = lax.broadcasted_iota(jnp.int32, (parts, 1, 1), 0) % 2
+    starting = jnp.where(pair_at == 0, embed_part, adapted).astype(jnp.bfloat16)
+    shared = adapted.reshape(parts // 2, 2, block_len, width)[:, 0].astype(jnp.bfloat16)
+    shared = lax.all_to_all(
+        shared,
+        BOTH,
+        split_axis=0,
+        concat_axis=0,
+        tiled=True,
+        axis_index_groups=[list(range(k, parts, 2)) for k in range(2)],
+    )
+    starting = exchange(starting).reshape(length, width).astype(jnp.float32)
+
+    def before_attention(resid, cos_full, sin_full):
+        normed = (resid * rms_scale(resid) * gain_float[0]).astype(jnp.bfloat16)
+        queries = rotate_rows(dot_n(normed, query_w), cos_full, sin_full).astype(jnp.bfloat16)
+        keys_in = rotate_rows(dot_n(normed, key_w), cos_full, sin_full).astype(jnp.bfloat16)
+        values_in = dot_n(normed, value_w).astype(jnp.bfloat16)
+        return normed, queries, keys_in, values_in
+
+    def after_attention(resid, mixed):
+        branch = dot_n(mixed, output_w)
+        middle = resid + branch * rms_scale(branch) * gain_float[1]
+        mlp_in = (middle * rms_scale(middle) * gain_float[2]).astype(jnp.bfloat16)
+        gate_pre = dot_n(mlp_in, gate_w)
+        up_pre = dot_n(mlp_in, up_w)
+        hidden = (jax.nn.silu(gate_pre) * up_pre).astype(jnp.bfloat16)
+        down_out = dot_n(hidden, down_w)
+        result = middle + down_out * rms_scale(down_out) * gain_float[3]
+        return result.astype(jnp.bfloat16), (branch, middle, mlp_in, gate_pre, up_pre, hidden, down_out)
+
+    resid = shared.reshape(length // 2, width).astype(jnp.float32)
+    local = jnp.arange(length // 2, dtype=jnp.int32)
+    cos_half, sin_half = rope_full((local // block_len * 2 + core) * block_len + local % block_len)
+    normed, queries, keys_in, values_in = before_attention(resid, cos_half, sin_half)
+    far_keys, far_values = send(keys_in, 3), send(values_in, 3)
+    mixed = attend_shared(core, block_len, queries, keys_in, values_in, far_keys, far_values)
+    first_out, _ = after_attention(resid, mixed)
+    far_out = send(first_out, 3, -1)
+    first_out = jnp.stack(
+        [first_out.reshape(-1, block_len, width), far_out.reshape(-1, block_len, width)], 1
+    ).reshape(length, width)
+    first_out = jnp.where(owner, first_out, jnp.zeros_like(first_out))
+
+    cos_full, sin_full = rope_full(jnp.arange(length, dtype=jnp.int32))
+    resid = starting + dot_n(first_out, adapt_w[:width])
+    normed, queries, keys_in, values_in = before_attention(resid, cos_full, sin_full)
+    mixed, log_total = attend_whole(queries, keys_in, values_in)
+    result, saved = after_attention(resid, mixed)
+    branch, middle, mlp_in, gate_pre, up_pre, hidden, down_out = saved
+    final_back = exchange(result.reshape(parts, block_len, width))
+
+    d_result = upstream.astype(jnp.float32)
+    d_down, gain_four = norm_back(down_out, d_result, gain_float[3])
+    d_down = d_down.astype(jnp.bfloat16)
+    down_part = dot_w(hidden, d_down).astype(jnp.bfloat16)
+    d_hidden = dot_t(d_down, down_w)
+    sigma = jax.nn.sigmoid(gate_pre)
+    d_gate = (d_hidden * up_pre * sigma * (1.0 + gate_pre * (1.0 - sigma))).astype(jnp.bfloat16)
+    d_up = (d_hidden * gate_pre * sigma).astype(jnp.bfloat16)
+    gate_part = dot_w(mlp_in, d_gate).astype(jnp.bfloat16)
+    up_part = dot_w(mlp_in, d_up).astype(jnp.bfloat16)
+    d_mlp = dot_t(d_gate, gate_w) + dot_t(d_up, up_w)
+    d_middle, gain_three = norm_back(middle, d_mlp, gain_float[2])
+    d_middle = d_middle + d_result
+    d_branch, gain_two = norm_back(branch, d_middle, gain_float[1])
+    d_branch = d_branch.astype(jnp.bfloat16)
+    out_part = dot_w(mixed, d_branch).astype(jnp.bfloat16)
+    d_mixed = dot_t(d_branch, output_w).astype(jnp.bfloat16)
+    d_query, d_key, d_value = attend_whole_back(
+        queries, keys_in, values_in, mixed, d_mixed, log_total, cos_full, sin_full
+    )
+    query_part = dot_w(normed, d_query).astype(jnp.bfloat16)
+    key_part = dot_w(normed, d_key).astype(jnp.bfloat16)
+    value_part = dot_w(normed, d_value).astype(jnp.bfloat16)
+    d_normed = dot_t(d_query, query_w) + dot_t(d_key, key_w) + dot_t(d_value, value_w)
+    d_resid, gain_one = norm_back(resid, d_normed, gain_float[0])
+    d_resid = (d_resid + d_middle).astype(jnp.bfloat16)
+    d_home = exchange(d_resid.reshape(parts, block_len, width))
+    first_part = dot_w(first_out, d_resid)
+
+    d_home = from_slots(d_home)
+    latent_back = dot_t(d_home, adapt_w[:width]).astype(jnp.bfloat16).reshape(latents.shape)
+    embed_back = dot_t(d_home, adapt_w[width:]).astype(jnp.bfloat16).reshape(latents.shape)
+    once = jnp.where(twice[None, :, None], jnp.zeros_like(latents), latents).reshape(row_count, width)
+    latent_part = first_part + dot_w(once, d_home)
+    embed_part = dot_w(embeds.reshape(row_count, width), d_home)
+    final_back = from_slots(final_back).reshape(latents.shape)
+
+    def blocks(part):
+        return part.reshape(parts, -1, part.shape[-1])
+
+    down_grad = scatter_rows(blocks(down_part))
+    gate_grad = scatter_rows(blocks(gate_part))
+    up_grad = scatter_rows(blocks(up_part))
+    gain_part = jnp.stack([gain_one, gain_two, gain_three, gain_four])
+    gain_part = gain_part.reshape(gains.shape[0], parts, gains.shape[1]).transpose(1, 0, 2)
+    gain_part = jnp.pad(
+        gain_part.reshape(parts, 1, gains.size).astype(jnp.bfloat16), ((0, 0), (0, 15), (0, width - gains.size))
+    )
+    square_grad = scatter_rows(
+        jnp.concatenate(
+            [blocks(query_part), blocks(key_part), blocks(value_part), blocks(out_part), gain_part], 1
+        )
+    )
+    query_grad, key_grad, value_grad, out_grad = (square_grad[at * side : (at + 1) * side] for at in range(4))
+    gain_grad = square_grad[4 * side, : gains.size].reshape(gains.shape)
+    adapt_grad = scatter_rows(blocks(jnp.concatenate([latent_part, embed_part], 0).astype(jnp.bfloat16)))
+    return (
+        final_back,
+        latent_back,
+        embed_back,
+        adapt_grad,
+        query_grad,
+        key_grad,
+        value_grad,
+        out_grad,
+        gate_grad,
+        up_grad,
+        down_grad,
+        gain_grad,
+    )
+
+
+def on_device(latents, *others):
+    ctx = lax.axis_size("ctx")
+    parts = lax.axis_size("grp") * ctx
+    if latents.shape[1] == parts and ctx == 4 and latents.shape[0] % 16 == 0:
+        return paired_on_device(latents, *others)
+    return spread_on_device(latents, *others)
+
+
 def solution(mesh):
     placed = (
         P(("grp", "ctx"), None, None),

time: 2580 us -> 1060 us (0.41)
  waiting for transfers between devices: 1620 us -> 254 us
  starting transfers between devices: 23 us -> 231 us
  blocking collectives: 184 us -> 0 us
  matrix products: 390 us -> 220 us
  local copies, waits for them, and re-layouts: 196 us -> 125 us
  Pallas kernels: 0 us -> 48.4 us
  other arithmetic: 135 us -> 165 us
    reduce_scatter x9 -> x0, waiting for transfers between devices: 1150 us -> none  [the longest x1 158 us: on_device(): lax.psum_scatter(down_part, ('grp', 'ctx'), scatter_dimension=0, tiled=True)]
    all_gather x12 -> x0, waiting for transfers between devices: 339 us -> none  [the longest x1 69 us: on_device(): lax.all_gather(w_down, ('grp', 'ctx'), axis=0, tiled=True)]
    ppermute x0 -> x113, waiting for transfers between devices: none -> 225 us  [send(): return lax.ppermute(values, BOTH, pairs)]
    ppermute x0 -> x113, starting transfers between devices: none -> 201 us  [send(): return lax.ppermute(values, BOTH, pairs)]
    dot_general x39 -> x38, matrix products: 390 us -> 220 us  [the longest x17 99 us: dot_n(): return jnp.dot(left, right, preferred_element_type=jnp.float32)]
    all_to_all x2 -> x0, blocking collectives: 114 us -> none  [the longest x1 60.5 us: on_device(): lax.all_to_all(d_joined[..., :model_width].astype(jnp.bfloat16), 'grp', s...]
    all_to_all x4 -> x5, waiting for transfers between devices: 125 us -> 29.6 us  [the longest x4 25.1 us: exchange(): return lax.all_to_all(values, BOTH, split_axis=0, concat_axis=0, tiled=True)]
    all_gather x1 -> x0, blocking collectives: 70.7 us -> none  [on_device(): lax.all_gather(gains, ('grp', 'ctx'), axis=1, tiled=True)]
  transfers between devices with their start and end apart: 26 -> 118, of which waited for: 21 -> 41; matrix products, arithmetic and copies ran while one was open for 16% -> 37% of each run, Pallas kernels for 0% -> 5%
where the time goes in v1:
time: 1060 us; the launch traced here: 1050 us
  waiting for transfers between devices  254 us (24%)
  starting transfers between devices  231 us (22%)
  matrix products  220 us (21%)
  other arithmetic  165 us (16%)
  local copies, waits for them, and re-layouts  125 us (12%)
  Pallas kernels  48.4 us (5%)
    ppermute x113, waiting for transfers between devices, send(): return lax.ppermute(values, BOTH, pairs)  225 us
    ppermute x113, starting transfers between devices, send(): return lax.ppermute(values, BOTH, pairs)  201 us
    dot_general x17, matrix products, dot_n(): return jnp.dot(left, right, preferred_element_type=jnp.float32)  99 us
    dot_general x9, matrix products, dot_t(): lax.dot_general(left, right, (((1,), (1,)), ((), ())), preferred_element_...  62.4 us
    dot_general x12, matrix products, dot_w(): lax.dot_general(left, right, (((0,), (0,)), ((), ())), preferred_element_...  58.7 us
    another operation x35, other arithmetic, join_pair(): return jnp.stack([first, second], at)  52.6 us
    unnamed x287, local copies, waits for them, and re-layouts  44.9 us
    all_to_all x4, waiting for transfers between devices, exchange(): return lax.all_to_all(values, BOTH, split_axis=0, concat_axis=0, tiled=True)  25.1 us
  transfers between devices with their start and end apart: 118, of which 41 were waited for; matrix products, arithmetic and copies ran while one was open for 37% of the time, Pallas kernels for 5%

profile of v1, /device:TPU:0, one launch (start us, length us, event | category | flops | bytes accessed | tf_op | source)
XLA Modules:
  0.0 1048.9 jit_solution(7519491550482621917)
XLA Ops:
  2.2 6.2 collective-permute-start.24
  62.1 6.5 collective-permute-done.27
  70.6 5.5 collective-permute-start.46
  139.8 9.7 collective-permute-done.7
  152.0 7.4 collective-permute-done.17
  162.7 14.9 %collective-permute-done.42 = bf16[2,2,32,2816]{3,2,0,1:T(8,128)(2,1)S(1)} collective-permute-done((bf16[2,2,32,2816]{3,2,0,1:T(8,128)(2,1)S(1)}, bf16[2,2,32,2816]{3,2,0,1:T(8,128)(2,1)S(1)}, u32[]{:S(2)}, u32[]{:S(2)}) %collective-permute-start.42) | collective-permute-done | bytes 720928 | tf_op jit(solution)/shard_map/ppermute | solution.py:387
  180.2 10.1 collective-permute-done.33
  195.7 12.8 %collective-permute-done.53 = bf16[2,2,88,1024]{3,2,0,1:T(8,128)(2,1)S(1)} collective-permute-done((bf16[2,2,88,1024]{3,2,0,1:T(8,128)(2,1)S(1)}, bf16[2,2,88,1024]{3,2,0,1:T(8,128)(2,1)S(1)}, u32[]{:S(2)}, u32[]{:S(2)}) %collective-permute-start.53) | collective-permute-done | bytes 720928 | tf_op jit(solution)/shard_map/ppermute | solution.py:387
  211.4 15.0 %collective-permute-done.18 = bf16[2,2,144,1024]{3,2,0,1:T(8,128)(2,1)S(1)} collective-permute-done((bf16[2,2,144,1024]{3,2,0,1:T(8,128)(2,1)S(1)}, bf16[2,2,144,1024]{3,2,0,1:T(8,128)(2,1)S(1)}, u32[]{:S(2)}, u32[]{:S(2)}) %collective-permute-start.18) | collective-permute-done | bytes 1179680 | tf_op jit(solution)/shard_map/ppermute | solution.py:387
  226.4 9.7 collective-permute-start.56
  244.1 8.0 fusion.36
  252.1 9.3 fusion.43
  263.7 6.8 all-to-all-start.1
  285.1 5.6 select_bitcast_fusion.7
  295.1 6.2 all-to-all-start
  301.7 9.5 select_bitcast_fusion.1
  311.2 8.3 pad_maximum_fusion
  320.4 6.2 fusion.146
  372.9 9.8 attend_shared.1
  390.5 14.1 %multiply_reduce_fusion.10 = (f32[512]{0:T(512)S(1)}, f32[512,1024]{1,0:T(8,128)}) fusion(bf16[2816,1024]{1,0:T(8,128)(2,1)} %bitcast.579, f32[512,2816]{1,0:T(8,128)} %fusion.140, bf16[1024,2816]{1,0:T(8,128)(2,1)} %bitcast.574, f32[512,1024]{1,0:T(8,128)} %copy-done.46, f32[1024]{0:T(1024)S(1)} %mul.493, f32[512]{0:T(512)S(1)} %add_rsqrt_fusion.6), kind=kOutput, calls=%fused_computation.111 | convolution fusion | flops 5916851712 | bytes 21504000 | tf_op jit(solution)/shard_map/dot_general | solution.py:454
  426.4 8.0 all-to-all-start.3
  434.4 5.3 multiply_reduce_fusion.9
  469.6 16.2 %attend_whole.1 = (bf16[1024,1024]{1,0:T(8,128)(2,1)S(1)}, f32[1024,128]{1,0:T(8,128)S(1)}) custom-call(bf16[1024,1024]{1,0:T(8,128)(2,1)S(1)} %copy-done.2, bf16[1024,1024]{1,0:T(8,128)(2,1)S(1)} %copy-done.4, bf16[1024,1024]{1,0:T(8,128)(2,1)S(1)} %copy-done.6), custom_call_target="tpu_custom_call" | custom-call | flops 2147483648 | bytes 8388608 | tf_op jit(solution)/shard_map/attend_whole/pallas_call | solution.py:489
  493.6 8.8 fusion.164
  502.5 12.7 %multiply_convert_fusion.2 = (bf16[1024,2816]{1,0:T(8,128)(2,1)}, f32[1024,2816]{1,0:T(8,128)}) fusion(f32[1024,2816]{1,0:T(8,128)} %fusion.164, bf16[1024,1024]{1,0:T(8,128)(2,1)S(1)} %multiply_convert_fusion.5, bf16[1024,2816]{1,0:T(8,128)(2,1)S(1)} %bitcast.578), kind=kOutput, calls=%fused_computation.2 | convolution fusion | flops 5922881536 | bytes 36700160 | tf_op jit(solution)/shard_map/dot_general | solution.py:454
  515.2 11.4 %multiply_reduce_fusion.6 = (f32[1024]{0:T(1024)S(1)}, f32[1024,1024]{1,0:T(8,128)}) fusion(bf16[1024,2816]{1,0:T(8,128)(2,1)} %get-tuple-element.182, bf16[2816,1024]{1,0:T(8,128)(2,1)} %bitcast.580), kind=kOutput, calls=%fused_computation.57 | convolution fusion | flops 5907676160 | bytes 15732736 | tf_op jit(solution)/shard_map/dot_general | solution.py:454
  536.2 8.0 convolution_convert_fusion
  544.2 19.5 %multiply_convert_fusion.1 = (bf16[1024,2816]{1,0:T(8,128)(2,1)}, bf16[1024,2816]{1,0:T(8,128)(2,1)}) fusion(f32[1024,2816]{1,0:T(8,128)} %fusion.164, f32[1024,2816]{1,0:T(8,128)} %get-tuple-element.183, bf16[1024,1024]{1,0:T(8,128)(2,1)} %copy-done.90, bf16[2816,1024]{1,0:T(8,128)(2,1)} %bitcast.581), kind=kOutput, calls=%fused_computation.1 | convolution fusion | flops 5943066624 | bytes 42467328 | tf_op jit(solution)/shard_map/dot_general | solution.py:450
  563.7 11.3 %convolution_convert_fusion.1 = bf16[1024,2816]{1,0:T(8,128)(2,1)} fusion(bf16[1024,1024]{1,0:T(8,128)(2,1)} %copy-done.82, bf16[1024,2816]{1,0:T(8,128)(2,1)} %get-tuple-element.50), kind=kOutput, calls=%fused_computation.21 | convolution fusion | flops 5908463616 | bytes 13631488 | tf_op jit(solution)/shard_map/dot_general | solution.py:458
  575.0 9.7 fusion.165
  584.8 6.9 convolution_convert_fusion.2
  591.8 11.9 %multiply_reduce_fusion = (bf16[1024]{0:T(1024)(128)(2,1)S(1)}, f32[1024]{0:T(1024)S(1)}, f32[1024,1024]{1,0:T(8,128)}) fusion(f32[1024,1024]{1,0:T(8,128)S(1)} %copy-done.20, f32[1024]{0:T(1024)S(1)} %add_rsqrt_fusion.2, f32[1024]{0:T(1024)S(1)} %mul.493, f32[1024,1024]{1,0:T(8,128)} %fusion.165, bf16[1024,2816]{1,0:T(8,128)(2,1)} %get-tuple-element.49, ...), kind=kOutput, calls=%fused_computation.46 | convolution fusion | flops 5912918016 | bytes 24131584 | tf_op jit(solution)/shard_map/dot_general | solution.py:450
  633.7 22.4 %attend_whole_back.1 = (bf16[1024,1024]{1,0:T(8,128)(2,1)S(1)}, bf16[1024,1024]{1,0:T(8,128)(2,1)S(1)}, bf16[1024,1024]{1,0:T(8,128)(2,1)S(1)}) custom-call(bf16[1024,1024]{1,0:T(8,128)(2,1)S(1)} %copy-done.3, bf16[1024,1024]{1,0:T(8,128)(2,1)S(1)} %copy-done.5, bf16[1024,1024]{1,0:T(8,128)(2,1)S(1)} %copy-done.7, bf16[1024,1024]{1,0:T(8,128)(2,1)} %copy-done.8, ...), custom_call_target="tpu_custom_call" | custom-call | flops 5368709120 | bytes 16777216 | tf_op jit(solution)/shard_map/attend_whole_back/pallas_call | solution.py:590
  690.6 7.3 constant_dynamic-slice_fusion.7
  706.9 6.1 all-to-all-start.4
  728.5 22.8 %collective-permute-done.105 = bf16[2,2,88,1024]{3,2,0,1:T(8,128)(2,1)S(1)} collective-permute-done((bf16[2,2,88,1024]{3,2,0,1:T(8,128)(2,1)S(1)}, bf16[2,2,88,1024]{3,2,0,1:T(8,128)(2,1)S(1)}, u32[]{:S(2)}, u32[]{:S(2)}) %collective-permute-start.105) | collective-permute-done | bytes 720928 | tf_op jit(solution)/shard_map/ppermute | solution.py:387
  754.1 15.5 %collective-permute-done.94 = bf16[2,2,32,2816]{3,2,0,1:T(8,128)(2,1)S(1)} collective-permute-done((bf16[2,2,32,2816]{3,2,0,1:T(8,128)(2,1)S(1)}, bf16[2,2,32,2816]{3,2,0,1:T(8,128)(2,1)S(1)}, u32[]{:S(2)}, u32[]{:S(2)}) %collective-permute-start.94) | collective-permute-done | bytes 720928 | tf_op jit(solution)/shard_map/ppermute | solution.py:387
  772.1 12.9 %collective-permute-done.83 = bf16[2,2,32,2816]{3,2,0,1:T(8,128)(2,1)S(1)} collective-permute-done((bf16[2,2,32,2816]{3,2,0,1:T(8,128)(2,1)S(1)}, bf16[2,2,32,2816]{3,2,0,1:T(8,128)(2,1)S(1)}, u32[]{:S(2)}, u32[]{:S(2)}) %collective-permute-start.83) | collective-permute-done | bytes 720928 | tf_op jit(solution)/shard_map/ppermute | solution.py:387
  794.5 5.9 collective-permute-done.95
  841.5 25.1 %all-to-all-done.2 = bf16[32,32,1024]{2,1,0:T(8,128)(2,1)} async-done(((bf16[32,32,1024]{2,1,0:T(8,128)(2,1)}), bf16[32,32,1024]{2,1,0:T(8,128)(2,1)}, u32[]{:S(2)}, u32[]{:S(2)}) %all-to-all-start.2) | async-done | bytes 2097184 | tf_op jit(solution)/shard_map/all_to_all | solution.py:644
  866.6 5.5 fusion.46
  905.7 12.7 %collective-permute-start.98 = (bf16[32,2816]{1,0:T(8,128)(2,1)S(1)}, bf16[32,2816]{1,0:T(8,128)(2,1)S(1)}, u32[]{:S(2)}, u32[]{:S(2)}) collective-permute-start(bf16[32,2816]{1,0:T(8,128)(2,1)S(1)} %copy-done.95), channel_id=1, source_target_pairs={{0,8},{1,9},{2,10},{3,11},{4,12},{5,13},{6,14},{7,15},{8,16},{9,17... | collective-permute-start | bytes 540680 | tf_op jit(solution)/shard_map/ppermute | solution.py:387
  919.5 10.1 collective-permute-done.72
  937.4 9.7 collective-permute-done.73
  950.9 8.1 collective-permute-done.61
  959.0 15.1 %collective-permute-start.74 = (bf16[144,1024]{1,0:T(8,128)(2,1)S(1)}, bf16[144,1024]{1,0:T(8,128)(2,1)S(1)}, u32[]{:S(2)}, u32[]{:S(2)}) collective-permute-start(bf16[144,1024]{1,0:T(8,128)(2,1)S(1)} %fusion.80), channel_id=1, source_target_pairs={{0,8},{1,9},{2,10},{3,11},{4,12},{5,13},{6,14},{7,15}} | collective-permute-start | bytes 884744 | tf_op jit(solution)/shard_map/ppermute | solution.py:387
  1005.7 6.6 collective-permute-done.101
  1022.0 9.9 collective-permute-start.76
  (767 shorter events, 537.4 us)
Async XLA Ops:
  0.7 41.4 %collective-permute-start.25 = (bf16[32,2816]{1,0:T(8,128)(2,1)}, bf16[32,2816]{1,0:T(8,128)(2,1)}, u32[]{:S(2)}, u32[]{:S(2)}) collective-permute-start(bf16[32,2816]{1,0:T(8,128)(2,1)} %param.22), channel_id=1, source_target_pairs={{8,0},{9,1},{10,2},{11,3},{12,4},{13,5},{14,6},{15,7},{16,8},{17,9... | collective-permute-start | bytes 540680 | tf_op jit(solution)/shard_map/ppermute | solution.py:387
  2.2 58.0 %collective-permute-start.24 = (bf16[32,2816]{1,0:T(8,128)(2,1)}, bf16[32,2816]{1,0:T(8,128)(2,1)}, u32[]{:S(2)}, u32[]{:S(2)}) collective-permute-start(bf16[32,2816]{1,0:T(8,128)(2,1)} %param.22), channel_id=1, source_target_pairs={{0,8},{1,9},{2,10},{3,11},{4,12},{5,13},{6,14},{7,15},{8,16},{9,17... | collective-permute-start | bytes 540680 | tf_op jit(solution)/shard_map/ppermute | solution.py:387
  14.9 46.6 %collective-permute-start.36 = (bf16[32,2816]{1,0:T(8,128)(2,1)}, bf16[32,2816]{1,0:T(8,128)(2,1)}, u32[]{:S(2)}, u32[]{:S(2)}) collective-permute-start(bf16[32,2816]{1,0:T(8,128)(2,1)} %param.23), channel_id=1, source_target_pairs={{8,0},{9,1},{10,2},{11,3},{12,4},{13,5},{14,6},{15,7},{16,8},{17,9... | collective-permute-start | bytes 540680 | tf_op jit(solution)/shard_map/ppermute | solution.py:387
  42.2 36.8 %collective-permute-start.35 = (bf16[32,2816]{1,0:T(8,128)(2,1)}, bf16[32,2816]{1,0:T(8,128)(2,1)S(1)}, u32[]{:S(2)}, u32[]{:S(2)}) collective-permute-start(bf16[32,2816]{1,0:T(8,128)(2,1)} %param.23), channel_id=1, source_target_pairs={{0,8},{1,9},{2,10},{3,11},{4,12},{5,13},{6,14},{7,15},{8,16},{9,17... | collective-permute-start | bytes 540680 | tf_op jit(solution)/shard_map/ppermute | solution.py:387
  54.9 32.6 %collective-permute-start.12 = (bf16[144,1024]{1,0:T(8,128)(2,1)}, bf16[144,1024]{1,0:T(8,128)(2,1)S(1)}, u32[]{:S(2)}, u32[]{:S(2)}) collective-permute-start(bf16[144,1024]{1,0:T(8,128)(2,1)} %pad_dynamic-update-slice_fusion), channel_id=1, source_target_pairs={{8,0},{9,1},{10,2},{11,3},{12,4},{13,5},{14,6},{15,7},{16,8},{17,9... | collective-permute-start | bytes 884744 | tf_op jit(solution)/shard_map/ppermute | solution.py:387
  60.2 23.3 %collective-permute-start.47 = (bf16[88,1024]{1,0:T(8,128)(2,1)}, bf16[88,1024]{1,0:T(8,128)(2,1)S(1)}, u32[]{:S(2)}, u32[]{:S(2)}) collective-permute-start(bf16[88,1024]{1,0:T(8,128)(2,1)} %param.24), channel_id=1, source_target_pairs={{8,0},{9,1},{10,2},{11,3},{12,4},{13,5},{14,6},{15,7},{16,8},{17,9... | collective-permute-start | bytes 540680 | tf_op jit(solution)/shard_map/ppermute | solution.py:387
  130.6 28.8 %collective-permute-start.17 = (bf16[2,144,1024]{2,1,0:T(8,128)(2,1)S(1)}, bf16[2,144,1024]{2,1,0:T(8,128)(2,1)S(1)}, u32[]{:S(2)}, u32[]{:S(2)}) collective-permute-start(bf16[2,144,1024]{2,1,0:T(8,128)(2,1)S(1)} %get-tuple-element.119), channel_id=1, source_target_pairs={{0,2},{1,3},{2,0},{3,1},{4,6},{5,7},{6,4},{7,5},{8,10},{9,11},{10,... | collective-permute-start | bytes 1769480 | tf_op jit(solution)/shard_map/ppermute | solution.py:387
  135.5 26.6 %collective-permute-start.19 = (bf16[2,144,1024]{2,1,0:T(8,128)(2,1)S(1)}, bf16[2,144,1024]{2,1,0:T(8,128)(2,1)S(1)}, u32[]{:S(2)}, u32[]{:S(2)}) collective-permute-start(bf16[2,144,1024]{2,1,0:T(8,128)(2,1)S(1)} %get-tuple-element.120), channel_id=1, source_target_pairs={{0,4},{1,5},{2,6},{3,7},{4,0},{5,1},{6,2},{7,3},{8,12},{9,13},{10,... | collective-permute-start | bytes 1769480 | tf_op jit(solution)/shard_map/ppermute | solution.py:387
  138.3 39.3 %collective-permute-start.42 = (bf16[2,2,32,2816]{3,2,0,1:T(8,128)(2,1)S(1)}, bf16[2,2,32,2816]{3,2,0,1:T(8,128)(2,1)S(1)}, u32[]{:S(2)}, u32[]{:S(2)}) collective-permute-start(bf16[2,2,32,2816]{3,2,0,1:T(8,128)(2,1)S(1)} %pad_maximum_fusion.16), channel_id=1, source_target_pairs={{0,4},{1,5},{2,6},{3,7},{4,0},{5,1},{6,2},{7,3},{8,12},{9,13},{10,... | collective-permute-start | bytes 2162696 | tf_op jit(solution)/shard_map/ppermute | solution.py:387
  149.5 28.3 %collective-permute-start.44 = (bf16[2,2,32,2816]{3,2,1,0:T(8,128)(2,1)S(1)}, bf16[2,2,32,2816]{3,2,1,0:T(8,128)(2,1)S(1)}, u32[]{:S(2)}, u32[]{:S(2)}) collective-permute-start(bf16[2,2,32,2816]{3,2,1,0:T(8,128)(2,1)S(1)} %pad_maximum_fusion.17), channel_id=1, source_target_pairs={{0,2},{1,3},{2,0},{3,1},{4,6},{5,7},{6,4},{7,5},{8,10},{9,11},{10,... | collective-permute-start | bytes 2162696 | tf_op jit(solution)/shard_map/ppermute | solution.py:387
  149.7 40.6 %collective-permute-start.33 = (bf16[2,2,32,2816]{3,2,1,0:T(8,128)(2,1)S(1)}, bf16[2,2,32,2816]{3,2,1,0:T(8,128)(2,1)S(1)}, u32[]{:S(2)}, u32[]{:S(2)}) collective-permute-start(bf16[2,2,32,2816]{3,2,1,0:T(8,128)(2,1)S(1)} %pad_maximum_fusion.15), channel_id=1, source_target_pairs={{0,2},{1,3},{2,0},{3,1},{4,6},{5,7},{6,4},{7,5},{8,10},{9,11},{10,... | collective-permute-start | bytes 2162696 | tf_op jit(solution)/shard_map/ppermute | solution.py:387
  159.4 33.7 %collective-permute-start.31 = (bf16[2,2,32,2816]{3,2,0,1:T(8,128)(2,1)S(1)}, bf16[2,2,32,2816]{3,2,0,1:T(8,128)(2,1)S(1)}, u32[]{:S(2)}, u32[]{:S(2)}) collective-permute-start(bf16[2,2,32,2816]{3,2,0,1:T(8,128)(2,1)S(1)} %pad_maximum_fusion.14), channel_id=1, source_target_pairs={{0,4},{1,5},{2,6},{3,7},{4,0},{5,1},{6,2},{7,3},{8,12},{9,13},{10,... | collective-permute-start | bytes 2162696 | tf_op jit(solution)/shard_map/ppermute | solution.py:387
  162.2 46.3 %collective-permute-start.53 = (bf16[2,2,88,1024]{3,2,0,1:T(8,128)(2,1)S(1)}, bf16[2,2,88,1024]{3,2,0,1:T(8,128)(2,1)S(1)}, u32[]{:S(2)}, u32[]{:S(2)}) collective-permute-start(bf16[2,2,88,1024]{3,2,0,1:T(8,128)(2,1)S(1)} %pad_maximum_fusion.18), channel_id=1, source_target_pairs={{0,4},{1,5},{2,6},{3,7},{4,0},{5,1},{6,2},{7,3},{8,12},{9,13},{10,... | collective-permute-start | bytes 2162696 | tf_op jit(solution)/shard_map/ppermute | solution.py:387
  177.6 31.0 %collective-permute-start.55 = (bf16[2,2,88,1024]{3,2,1,0:T(8,128)(2,1)S(1)}, bf16[2,2,88,1024]{3,2,1,0:T(8,128)(2,1)S(1)}, u32[]{:S(2)}, u32[]{:S(2)}) collective-permute-start(bf16[2,2,88,1024]{3,2,1,0:T(8,128)(2,1)S(1)} %pad_maximum_fusion.19), channel_id=1, source_target_pairs={{0,2},{1,3},{2,0},{3,1},{4,6},{5,7},{6,4},{7,5},{8,10},{9,11},{10,... | collective-permute-start | bytes 2162696 | tf_op jit(solution)/shard_map/ppermute | solution.py:387
  177.8 62.7 %collective-permute-start.10 = (bf16[4,2,2,64,1024]{4,3,2,1,0:T(8,128)(2,1)S(1)}, bf16[4,2,2,64,1024]{4,3,2,1,0:T(8,128)(2,1)S(1)}, u32[]{:S(2)}, u32[]{:S(2)}) collective-permute-start(bf16[4,2,2,64,1024]{4,3,2,1,0:T(8,128)(2,1)S(1)} %maximum_maximum_fusion.3), channel_id=1, source_target_pairs={{0,1},{1,0},{2,3},{3,2},{4,5},{5,4},{6,7},{7,6},{8,9},{9,8},{10,11... | collective-permute-start | bytes 6291464 | tf_op jit(solution)/shard_map/ppermute | solution.py:387
  190.3 36.1 %collective-permute-start.18 = (bf16[2,2,144,1024]{3,2,0,1:T(8,128)(2,1)S(1)}, bf16[2,2,144,1024]{3,2,0,1:T(8,128)(2,1)S(1)}, u32[]{:S(2)}, u32[]{:S(2)}) collective-permute-start(bf16[2,2,144,1024]{3,2,0,1:T(8,128)(2,1)S(1)} %pad_maximum_fusion.11), channel_id=1, source_target_pairs={{0,4},{1,5},{2,6},{3,7},{4,0},{5,1},{6,2},{7,3},{8,12},{9,13},{10,... | collective-permute-start | bytes 3538952 | tf_op jit(solution)/shard_map/ppermute | solution.py:387
  193.1 43.2 %collective-permute-start.20 = (bf16[2,2,144,1024]{3,2,1,0:T(8,128)(2,1)S(1)}, bf16[2,2,144,1024]{3,2,1,0:T(8,128)(2,1)S(1)}, u32[]{:S(2)}, u32[]{:S(2)}) collective-permute-start(bf16[2,2,144,1024]{3,2,1,0:T(8,128)(2,1)S(1)} %pad_maximum_fusion.12), channel_id=1, source_target_pairs={{0,2},{1,3},{2,0},{3,1},{4,6},{5,7},{6,4},{7,5},{8,10},{9,11},{10,... | collective-permute-start | bytes 3538952 | tf_op jit(solution)/shard_map/ppermute | solution.py:387
  208.5 72.0 %collective-permute-start.45 = (bf16[4,2,2,32,2816]{4,3,2,1,0:T(8,128)(2,1)}, bf16[4,2,2,32,2816]{4,3,2,1,0:T(8,128)(2,1)}, u32[]{:S(2)}, u32[]{:S(2)}) collective-permute-start(bf16[4,2,2,32,2816]{4,3,2,1,0:T(8,128)(2,1)} %maximum_maximum_fusion.1), channel_id=1, source_target_pairs={{0,1},{1,0},{2,3},{3,2},{4,5},{5,4},{6,7},{7,6},{8,9},{9,8},{10,11... | collective-permute-start | bytes 8650760 | tf_op jit(solution)/shard_map/ppermute | solution.py:387
  208.6 76.4 %collective-permute-start.34 = (bf16[4,2,2,32,2816]{4,3,2,1,0:T(8,128)(2,1)}, bf16[4,2,2,32,2816]{4,3,2,1,0:T(8,128)(2,1)}, u32[]{:S(2)}, u32[]{:S(2)}) collective-permute-start(bf16[4,2,2,32,2816]{4,3,2,1,0:T(8,128)(2,1)} %copy_dynamic-update-slice_fusion), channel_id=1, source_target_pairs={{0,1},{1,0},{2,3},{3,2},{4,5},{5,4},{6,7},{7,6},{8,9},{9,8},{10,11... | collective-permute-start | bytes 8650760 | tf_op jit(solution)/shard_map/ppermute | solution.py:387
  226.4 49.3 %collective-permute-start.56 = (bf16[4,2,2,88,1024]{4,3,2,1,0:T(8,128)(2,1)}, bf16[4,2,2,88,1024]{4,3,2,1,0:T(8,128)(2,1)}, u32[]{:S(2)}, u32[]{:S(2)}) collective-permute-start(bf16[4,2,2,88,1024]{4,3,2,1,0:T(8,128)(2,1)} %maximum_maximum_fusion.2), channel_id=1, source_target_pairs={{0,1},{1,0},{2,3},{3,2},{4,5},{5,4},{6,7},{7,6},{8,9},{9,8},{10,11... | collective-permute-start | bytes 8650760 | tf_op jit(solution)/shard_map/ppermute | solution.py:387
  240.1 61.6 %collective-permute-start.21 = (bf16[4,2,2,144,1024]{4,3,2,1,0:T(8,128)(2,1)}, bf16[4,2,2,144,1024]{4,3,2,1,0:T(8,128)(2,1)}, u32[]{:S(2)}, u32[]{:S(2)}) collective-permute-start(bf16[4,2,2,144,1024]{4,3,2,1,0:T(8,128)(2,1)} %maximum_maximum_fusion), channel_id=1, source_target_pairs={{0,1},{1,0},{2,3},{3,2},{4,5},{5,4},{6,7},{7,6},{8,9},{9,8},{10,11... | collective-permute-start | bytes 14155784 | tf_op jit(solution)/shard_map/ppermute | solution.py:387
  263.7 31.5 %all-to-all-start.1 = ((bf16[16,32,1024]{2,1,0:T(8,128)(2,1)}), bf16[16,32,1024]{2,1,0:T(8,128)(2,1)S(1)}, u32[]{:S(2)}, u32[]{:S(2)}) async-start(bf16[16,32,1024]{2,1,0:T(8,128)(2,1)} %slice_bitcast_fusion), calls=%async_computation.1 | async-start | bytes 2097152 | tf_op jit(solution)/shard_map/all_to_all | solution.py:672
  295.1 131.3 %all-to-all-start = ((bf16[32,32,1024]{2,1,0:T(8,128)(2,1)}), bf16[32,32,1024]{2,1,0:T(8,128)(2,1)}, u32[]{:S(2)}, u32[]{:S(2)}) async-start(bf16[32,32,1024]{2,1,0:T(8,128)(2,1)} %select_convert_fusion), calls=%async_computation | async-start | bytes 4194304 | tf_op jit(solution)/shard_map/all_to_all | solution.py:644
  331.2 40.4 %collective-permute-start.23 = (bf16[512,1024]{1,0:T(8,128)(2,1)}, bf16[512,1024]{1,0:T(8,128)(2,1)}, u32[]{:S(2)}, u32[]{:S(2)}) collective-permute-start(bf16[512,1024]{1,0:T(8,128)(2,1)} %convolution_convert_fusion.11.v_ref), channel_id=1, source_target_pairs={{0,1},{1,0},{2,3},{3,2},{4,5},{5,4},{6,7},{7,6},{8,9},{9,8},{10,11... | collective-permute-start | bytes 3145736 | tf_op jit(solution)/shard_map/ppermute | solution.py:387
  426.4 100.2 %all-to-all-start.3 = ((bf16[32,32,1024]{2,1,0:T(8,128)(2,1)}), bf16[32,32,1024]{2,1,0:T(8,128)(2,1)}, u32[]{:S(2)}, u32[]{:S(2)}) async-start(bf16[32,32,1024]{2,1,0:T(8,128)(2,1)} %bitcast.604), calls=%async_computation.3 | async-start | bytes 4194304 | tf_op jit(solution)/shard_map/all_to_all | solution.py:644
  624.0 89.0 %collective-permute-start.102 = (bf16[4,2,2,88,1024]{4,3,0,1,2:T(8,128)(2,1)}, bf16[4,2,2,88,1024]{4,3,0,1,2:T(8,128)(2,1)}, u32[]{:S(2)}, u32[]{:S(2)}) collective-permute-start(bf16[4,2,2,88,1024]{4,3,0,1,2:T(8,128)(2,1)} %bitcast.543), channel_id=1, source_target_pairs={{0,1},{1,0},{2,3},{3,2},{4,5},{5,4},{6,7},{7,6},{8,9},{9,8},{10,11... | collective-permute-start | bytes 8650760 | tf_op jit(solution)/shard_map/ppermute | solution.py:387
  628.2 92.7 %collective-permute-start.91 = (bf16[4,2,2,32,2816]{4,3,0,1,2:T(8,128)(2,1)}, bf16[4,2,2,32,2816]{4,3,0,1,2:T(8,128)(2,1)}, u32[]{:S(2)}, u32[]{:S(2)}) collective-permute-start(bf16[4,2,2,32,2816]{4,3,0,1,2:T(8,128)(2,1)} %bitcast.544), channel_id=1, source_target_pairs={{0,1},{1,0},{2,3},{3,2},{4,5},{5,4},{6,7},{7,6},{8,9},{9,8},{10,11... | collective-permute-start | bytes 8650760 | tf_op jit(solution)/shard_map/ppermute | solution.py:387
  632.1 92.3 %collective-permute-start.80 = (bf16[4,2,2,32,2816]{4,3,0,1,2:T(8,128)(2,1)}, bf16[4,2,2,32,2816]{4,3,0,1,2:T(8,128)(2,1)}, u32[]{:S(2)}, u32[]{:S(2)}) collective-permute-start(bf16[4,2,2,32,2816]{4,3,0,1,2:T(8,128)(2,1)} %bitcast.545), channel_id=1, source_target_pairs={{0,1},{1,0},{2,3},{3,2},{4,5},{5,4},{6,7},{7,6},{8,9},{9,8},{10,11... | collective-permute-start | bytes 8650760 | tf_op jit(solution)/shard_map/ppermute | solution.py:387
  700.8 195.1 %collective-permute-start.69 = (bf16[4,2,2,144,1024]{4,3,0,1,2:T(8,128)(2,1)}, bf16[4,2,2,144,1024]{4,3,0,1,2:T(8,128)(2,1)}, u32[]{:S(2)}, u32[]{:S(2)}) collective-permute-start(bf16[4,2,2,144,1024]{4,3,0,1,2:T(8,128)(2,1)} %bitcast.542), channel_id=1, source_target_pairs={{0,1},{1,0},{2,3},{3,2},{4,5},{5,4},{6,7},{7,6},{8,9},{9,8},{10,11... | collective-permute-start | bytes 14155784 | tf_op jit(solution)/shard_map/ppermute | solution.py:387
  706.9 107.1 %all-to-all-start.4 = ((bf16[32,32,1024]{2,1,0:T(8,128)(2,1)}), bf16[32,32,1024]{2,1,0:T(8,128)(2,1)}, u32[]{:S(2)}, u32[]{:S(2)}) async-start(bf16[32,32,1024]{2,1,0:T(8,128)(2,1)} %bitcast.559), calls=%async_computation.4 | async-start | bytes 4194304 | tf_op jit(solution)/shard_map/all_to_all | solution.py:644
  717.5 33.8 %collective-permute-start.105 = (bf16[2,2,88,1024]{3,2,0,1:T(8,128)(2,1)S(1)}, bf16[2,2,88,1024]{3,2,0,1:T(8,128)(2,1)S(1)}, u32[]{:S(2)}, u32[]{:S(2)}) collective-permute-start(bf16[2,2,88,1024]{3,2,0,1:T(8,128)(2,1)S(1)} %dynamic-slice_bitcast_fusion.2), channel_id=1, source_target_pairs={{0,2},{1,3},{2,0},{3,1},{4,6},{5,7},{6,4},{7,5},{8,10},{9,11},{10,... | collective-permute-start | bytes 2162696 | tf_op jit(solution)/shard_map/ppermute | solution.py:387
  719.3 32.4 %collective-permute-start.103 = (bf16[2,2,88,1024]{3,2,0,1:T(8,128)(2,1)S(1)}, bf16[2,2,88,1024]{3,2,0,1:T(8,128)(2,1)S(1)}, u32[]{:S(2)}, u32[]{:S(2)}) collective-permute-start(bf16[2,2,88,1024]{3,2,0,1:T(8,128)(2,1)S(1)} %dynamic-slice_bitcast_fusion.3), channel_id=1, source_target_pairs={{0,4},{1,5},{2,6},{3,7},{4,0},{5,1},{6,2},{7,3},{8,12},{9,13},{10,... | collective-permute-start | bytes 2162696 | tf_op jit(solution)/shard_map/ppermute | solution.py:387
  723.8 45.8 %collective-permute-start.94 = (bf16[2,2,32,2816]{3,2,0,1:T(8,128)(2,1)S(1)}, bf16[2,2,32,2816]{3,2,0,1:T(8,128)(2,1)S(1)}, u32[]{:S(2)}, u32[]{:S(2)}) collective-permute-start(bf16[2,2,32,2816]{3,2,0,1:T(8,128)(2,1)S(1)} %dynamic-slice_bitcast_fusion.4), channel_id=1, source_target_pairs={{0,2},{1,3},{2,0},{3,1},{4,6},{5,7},{6,4},{7,5},{8,10},{9,11},{10,... | collective-permute-start | bytes 2162696 | tf_op jit(solution)/shard_map/ppermute | solution.py:387
  724.5 46.8 %collective-permute-start.92 = (bf16[2,2,32,2816]{3,2,0,1:T(8,128)(2,1)S(1)}, bf16[2,2,32,2816]{3,2,0,1:T(8,128)(2,1)S(1)}, u32[]{:S(2)}, u32[]{:S(2)}) collective-permute-start(bf16[2,2,32,2816]{3,2,0,1:T(8,128)(2,1)S(1)} %dynamic-slice_bitcast_fusion.5), channel_id=1, source_target_pairs={{0,4},{1,5},{2,6},{3,7},{4,0},{5,1},{6,2},{7,3},{8,12},{9,13},{10,... | collective-permute-start | bytes 2162696 | tf_op jit(solution)/shard_map/ppermute | solution.py:387
  751.3 33.7 %collective-permute-start.83 = (bf16[2,2,32,2816]{3,2,0,1:T(8,128)(2,1)S(1)}, bf16[2,2,32,2816]{3,2,0,1:T(8,128)(2,1)S(1)}, u32[]{:S(2)}, u32[]{:S(2)}) collective-permute-start(bf16[2,2,32,2816]{3,2,0,1:T(8,128)(2,1)S(1)} %dynamic-slice_bitcast_fusion.6), channel_id=1, source_target_pairs={{0,2},{1,3},{2,0},{3,1},{4,6},{5,7},{6,4},{7,5},{8,10},{9,11},{10,... | collective-permute-start | bytes 2162696 | tf_op jit(solution)/shard_map/ppermute | solution.py:387
  751.8 34.9 %collective-permute-start.81 = (bf16[2,2,32,2816]{3,2,0,1:T(8,128)(2,1)S(1)}, bf16[2,2,32,2816]{3,2,0,1:T(8,128)(2,1)S(1)}, u32[]{:S(2)}, u32[]{:S(2)}) collective-permute-start(bf16[2,2,32,2816]{3,2,0,1:T(8,128)(2,1)S(1)} %dynamic-slice_bitcast_fusion.7), channel_id=1, source_target_pairs={{0,4},{1,5},{2,6},{3,7},{4,0},{5,1},{6,2},{7,3},{8,12},{9,13},{10,... | collective-permute-start | bytes 2162696 | tf_op jit(solution)/shard_map/ppermute | solution.py:387
  800.5 71.6 %collective-permute-start.107 = (bf16[88,1024]{1,0:T(8,128)(2,1)S(1)}, bf16[88,1024]{1,0:T(8,128)(2,1)}, u32[]{:S(2)}, u32[]{:S(2)}) collective-permute-start(bf16[88,1024]{1,0:T(8,128)(2,1)S(1)} %fusion.91), channel_id=1, source_target_pairs={{0,8},{1,9},{2,10},{3,11},{4,12},{5,13},{6,14},{7,15}} | collective-permute-start | bytes 540680 | tf_op jit(solution)/shard_map/ppermute | solution.py:387
  805.8 68.8 %collective-permute-start.96 = (bf16[32,2816]{1,0:T(8,128)(2,1)}, bf16[32,2816]{1,0:T(8,128)(2,1)}, u32[]{:S(2)}, u32[]{:S(2)}) collective-permute-start(bf16[32,2816]{1,0:T(8,128)(2,1)} %fusion.99), channel_id=1, source_target_pairs={{0,8},{1,9},{2,10},{3,11},{4,12},{5,13},{6,14},{7,15}} | collective-permute-start | bytes 540680 | tf_op jit(solution)/shard_map/ppermute | solution.py:387
  809.5 68.7 %collective-permute-start.85 = (bf16[32,2816]{1,0:T(8,128)(2,1)}, bf16[32,2816]{1,0:T(8,128)(2,1)}, u32[]{:S(2)}, u32[]{:S(2)}) collective-permute-start(bf16[32,2816]{1,0:T(8,128)(2,1)} %fusion.107), channel_id=1, source_target_pairs={{0,8},{1,9},{2,10},{3,11},{4,12},{5,13},{6,14},{7,15}} | collective-permute-start | bytes 540680 | tf_op jit(solution)/shard_map/ppermute | solution.py:387
  814.1 52.5 %all-to-all-start.2 = ((bf16[32,32,1024]{2,1,0:T(8,128)(2,1)}), bf16[32,32,1024]{2,1,0:T(8,128)(2,1)}, u32[]{:S(2)}, u32[]{:S(2)}) async-start(bf16[32,32,1024]{2,1,0:T(8,128)(2,1)} %bitcast.554), calls=%async_computation.2 | async-start | bytes 4194304 | tf_op jit(solution)/shard_map/all_to_all | solution.py:644
  833.1 100.4 %collective-permute-start.58 = (bf16[4,2,2,64,1024]{4,3,0,1,2:T(8,128)(2,1)}, bf16[4,2,2,64,1024]{4,3,0,1,2:T(8,128)(2,1)}, u32[]{:S(2)}, u32[]{:S(2)}) collective-permute-start(bf16[4,2,2,64,1024]{4,3,0,1,2:T(8,128)(2,1)} %bitcast.546), channel_id=1, source_target_pairs={{0,1},{1,0},{2,3},{3,2},{4,5},{5,4},{6,7},{7,6},{8,9},{9,8},{10,11... | collective-permute-start | bytes 6291464 | tf_op jit(solution)/shard_map/ppermute | solution.py:387
  883.0 154.5 %collective-permute-start.109 = (bf16[88,1024]{1,0:T(8,128)(2,1)}, bf16[88,1024]{1,0:T(8,128)(2,1)}, u32[]{:S(2)}, u32[]{:S(2)}) collective-permute-start(bf16[88,1024]{1,0:T(8,128)(2,1)} %get-tuple-element.34), channel_id=1, source_target_pairs={{0,8},{1,9},{2,10},{3,11},{4,12},{5,13},{6,14},{7,15},{8,16},{9,17... | collective-permute-start | bytes 540680 | tf_op jit(solution)/shard_map/ppermute | solution.py:387
  901.5 28.1 %collective-permute-start.72 = (bf16[2,2,144,1024]{3,2,0,1:T(8,128)(2,1)S(1)}, bf16[2,2,144,1024]{3,2,0,1:T(8,128)(2,1)S(1)}, u32[]{:S(2)}, u32[]{:S(2)}) collective-permute-start(bf16[2,2,144,1024]{3,2,0,1:T(8,128)(2,1)S(1)} %dynamic-slice_bitcast_fusion), channel_id=1, source_target_pairs={{0,2},{1,3},{2,0},{3,1},{4,6},{5,7},{6,4},{7,5},{8,10},{9,11},{10,... | collective-permute-start | bytes 3538952 | tf_op jit(solution)/shard_map/ppermute | solution.py:387
  904.0 28.8 %collective-permute-start.70 = (bf16[2,2,144,1024]{3,2,0,1:T(8,128)(2,1)S(1)}, bf16[2,2,144,1024]{3,2,0,1:T(8,128)(2,1)S(1)}, u32[]{:S(2)}, u32[]{:S(2)}) collective-permute-start(bf16[2,2,144,1024]{3,2,0,1:T(8,128)(2,1)S(1)} %dynamic-slice_bitcast_fusion.1), channel_id=1, source_target_pairs={{0,4},{1,5},{2,6},{3,7},{4,0},{5,1},{6,2},{7,3},{8,12},{9,13},{10,... | collective-permute-start | bytes 3538952 | tf_op jit(solution)/shard_map/ppermute | solution.py:387
  905.7 99.3 %collective-permute-start.98 = (bf16[32,2816]{1,0:T(8,128)(2,1)S(1)}, bf16[32,2816]{1,0:T(8,128)(2,1)S(1)}, u32[]{:S(2)}, u32[]{:S(2)}) collective-permute-start(bf16[32,2816]{1,0:T(8,128)(2,1)S(1)} %copy-done.95), channel_id=1, source_target_pairs={{0,8},{1,9},{2,10},{3,11},{4,12},{5,13},{6,14},{7,15},{8,16},{9,17... | collective-permute-start | bytes 540680 | tf_op jit(solution)/shard_map/ppermute | solution.py:387
  929.7 86.4 %collective-permute-start.87 = (bf16[32,2816]{1,0:T(8,128)(2,1)S(1)}, bf16[32,2816]{1,0:T(8,128)(2,1)S(1)}, u32[]{:S(2)}, u32[]{:S(2)}) collective-permute-start(bf16[32,2816]{1,0:T(8,128)(2,1)S(1)} %copy-done.94), channel_id=1, source_target_pairs={{0,8},{1,9},{2,10},{3,11},{4,12},{5,13},{6,14},{7,15},{8,16},{9,17... | collective-permute-start | bytes 540680 | tf_op jit(solution)/shard_map/ppermute | solution.py:387
  947.7 26.7 %collective-permute-start.59 = (bf16[2,2,64,1024]{3,2,0,1:T(8,128)(2,1)S(1)}, bf16[2,2,64,1024]{3,2,0,1:T(8,128)(2,1)S(1)}, u32[]{:S(2)}, u32[]{:S(2)}) collective-permute-start(bf16[2,2,64,1024]{3,2,0,1:T(8,128)(2,1)S(1)} %dynamic-slice_bitcast_fusion.11), channel_id=1, source_target_pairs={{0,4},{1,5},{2,6},{3,7},{4,0},{5,1},{6,2},{7,3},{8,12},{9,13},{10,... | collective-permute-start | bytes 1572872 | tf_op jit(solution)/shard_map/ppermute | solution.py:387
  994.7 44.1 %collective-permute-start.112 = (bf16[88,1024]{1,0:T(8,128)(2,1)S(1)}, bf16[88,1024]{1,0:T(8,128)(2,1)S(1)}, u32[]{:S(2)}, u32[]{:S(2)}) collective-permute-start(bf16[88,1024]{1,0:T(8,128)(2,1)S(1)} %add_convert_fusion.6), channel_id=1, source_target_pairs={{8,0},{9,1},{10,2},{11,3},{12,4},{13,5},{14,6},{15,7},{16,8},{17,9... | collective-permute-start | bytes 540680 | tf_op jit(solution)/shard_map/ppermute | solution.py:387
  (209 other events, 2622.3 us)

commit v2 on v1

--- a/solution.py
+++ b/solution.py
@@ -387,63 +387,365 @@
     return lax.ppermute(values, BOTH, pairs)
 
 
-def join_pair(values, axis, spot, at):
-    other = send(values, axis)
-    first = jnp.where(spot == 0, values, other)
-    second = jnp.where(spot == 0, other, values)
-    return jnp.stack([first, second], at)
-
-
-def gather_rows(shard):
-    z_size = grid_sizes()[0]
+MESH = pl.DeviceIdType.MESH
+
+
+def device_at(z, y, x, k):
+    _, y_size, _, k_size = grid_sizes()
+    return (z * y_size + y, x * k_size + k)
+
+
+def order_of(z, y, x, half, slot_z):
+    high = slot_z // half
+    first = (y + high * (1 - 2 * y), x + (1 - high) * (1 - 2 * x))
+    second = (y + (1 - high) * (1 - 2 * y), x + high * (1 - 2 * x))
+    return first, second
+
+
+def greet(devices):
+    barrier = pltpu.get_barrier_semaphore()
+    for device in devices:
+        pl.semaphore_signal(barrier, inc=1, device_id=device, device_id_type=MESH)
+    pl.semaphore_wait(barrier, len(devices))
+
+
+def greet_line(z, y, x, k, z_size):
+    barrier = pltpu.get_barrier_semaphore()
+    for device in (device_at(z, 1 - y, x, k), device_at(z, y, 1 - x, k), device_at(z, y, x, 1 - k)):
+        pl.semaphore_signal(barrier, inc=1, device_id=device, device_id_type=MESH)
+
+    @pl.when(z > 0)
+    def _():
+        pl.semaphore_signal(barrier, inc=1, device_id=device_at(z - 1, y, x, k), device_id_type=MESH)
+
+    @pl.when(z < z_size - 1)
+    def _():
+        pl.semaphore_signal(barrier, inc=1, device_id=device_at(z + 1, y, x, k), device_id_type=MESH)
+
+    pl.semaphore_wait(barrier, 3 + jnp.minimum(z, 1) + jnp.minimum(z_size - 1 - z, 1))
+
+
+def remote(source, target, send_sem, recv_sem, device):
+    return pltpu.make_async_remote_copy(
+        src_ref=source,
+        dst_ref=target,
+        send_sem=send_sem,
+        recv_sem=recv_sem,
+        device_id=device,
+        device_id_type=MESH,
+    )
+
+
+def gather_kernel(count, *refs):
+    z_size, _, _, _ = grid_sizes()
     z, y, x, k = grid_place()
-    rows, width = shard.shape
-    up, down = [shard], [shard]
+    half = z_size // 2
+    shards, outs = refs[:count], refs[count : 2 * count]
+    local_sem, z_send, z_recv, p_send, p_recv, k_send, k_recv = refs[2 * count :]
+    greet_line(z, y, x, k, z_size)
+
+    def z_copy(g, slot_z, way):
+        spot = outs[g].at[slot_z, y, x, k]
+        side = z + 1 - 2 * way
+        return remote(spot, spot, z_send.at[g, slot_z, way], z_recv.at[g, slot_z], device_at(side, y, x, k))
+
+    def plane_copy(g, slot_z, kind):
+        first, second = order_of(z, y, x, half, slot_z)
+        from_at = first if kind == 2 else (y, x)
+        to_at = first if kind == 0 else second
+        spot = outs[g].at[slot_z, from_at[0], from_at[1], k]
+        return remote(
+            spot, spot, p_send.at[g, slot_z, kind], p_recv.at[g, slot_z, kind], device_at(z, to_at[0], to_at[1], k)
+        )
+
+    def core_copy(g, slot_z):
+        spot = outs[g].at[slot_z, :, :, k]
+        return remote(spot, spot, k_send.at[g, slot_z], k_recv.at[g, slot_z], device_at(z, y, x, 1 - k))
+
+    def spread_z(g, slot_z, up, down):
+        if up:
+
+            @pl.when(z < z_size - 1)
+            def _():
+                z_copy(g, slot_z, 0).start()
+
+        if down:
+
+            @pl.when(z > 0)
+            def _():
+                z_copy(g, slot_z, 1).start()
+
+    def at_offsets(step, body):
+        if step == 0:
+            body(z, True, True)
+            return
+
+        @pl.when(z >= step)
+        def _():
+            body(z - step, True, False)
+
+        @pl.when(z + step < z_size)
+        def _():
+            body(z + step, False, True)
+
+    own = [pltpu.make_async_copy(shards[g], outs[g].at[z, y, x, k], local_sem.at[g]) for g in range(count)]
+    for copy in own:
+        copy.start()
+    for step in range(z_size):
+        for g in range(count):
+            if step == 0:
+                own[g].wait()
+
+            def arrive(slot_z, up, down, g=g):
+                if not (up and down):
+                    z_copy(g, slot_z, 1 if up else 0).wait_recv()
+                spread_z(g, slot_z, up, down)
+                plane_copy(g, slot_z, 0).start()
+                plane_copy(g, slot_z, 1).start()
+
+            at_offsets(step, arrive)
+        for g in range(count):
+
+            def pass_on(slot_z, up, down, g=g):
+                plane_copy(g, slot_z, 0).wait_recv()
+                plane_copy(g, slot_z, 2).start()
+
+            at_offsets(step, pass_on)
+        if step > 0:
+            for g in range(count):
+
+                def cross(slot_z, up, down, g=g):
+                    plane_copy(g, slot_z, 1).wait_recv()
+                    plane_copy(g, slot_z, 2).wait_recv()
+                    core_copy(g, slot_z).start()
+
+                at_offsets(step - 1, cross)
+    for g in range(count):
+
+        def cross_last(slot_z, up, down, g=g):
+            plane_copy(g, slot_z, 1).wait_recv()
+            plane_copy(g, slot_z, 2).wait_recv()
+            core_copy(g, slot_z).start()
+
+        at_offsets(z_size - 1, cross_last)
+    for g in range(count):
+        for slot_z in range(z_size):
+            core_copy(g, slot_z).wait()
+            for kind in range(3):
+                plane_copy(g, slot_z, kind).wait_send()
+    for step in range(z_size):
+        for g in range(count):
+
+            def settle(slot_z, up, down, g=g):
+                if up:
+
+                    @pl.when(z < z_size - 1)
+                    def _():
+                        z_copy(g, slot_z, 0).wait_send()
+
+                if down:
+
+                    @pl.when(z > 0)
+                    def _():
+                        z_copy(g, slot_z, 1).wait_send()
+
+            at_offsets(step, settle)
+
+
+def gather_all(shards, collective_id):
+    sizes = grid_sizes()
+    count, z_size = len(shards), sizes[0]
+    anywhere = pl.BlockSpec(memory_space=pl.ANY)
+    dma = pltpu.SemaphoreType.DMA
+    return pl.pallas_call(
+        functools.partial(gather_kernel, count),
+        in_specs=[anywhere] * count,
+        out_specs=[anywhere] * count,
+        out_shape=[jax.ShapeDtypeStruct(sizes + shard.shape, shard.dtype) for shard in shards],
+        scratch_shapes=[
+            dma((count,)),
+            dma((count, z_size, 2)),
+            dma((count, z_size)),
+            dma((count, z_size, 3)),
+            dma((count, z_size, 3)),
+            dma((count, z_size)),
+            dma((count, z_size)),
+        ],
+        compiler_params=pltpu.CompilerParams(collective_id=collective_id, has_side_effects=True),
+        name="gather_weights",
+    )(*shards)
+
+
+def scatter_kernel(count, *refs):
+    z_size, _, _, _ = grid_sizes()
+    z, y, x, k = grid_place()
+    half = z_size // 2
+    parts, outs = refs[:count], refs[count : 2 * count]
+    held, from_core = refs[2 * count : 3 * count], refs[3 * count : 4 * count]
+    from_second, from_first = refs[4 * count : 5 * count], refs[5 * count : 6 * count]
+    from_z = refs[6 * count : 7 * count]
+    local_sem, k_send, k_recv, p_send, p_recv, z_send, z_recv = refs[7 * count :]
+    greet_line(z, y, x, k, z_size)
+
+    def core_copy(g, slot_z):
+        return remote(
+            parts[g].at[slot_z, :, :, 1 - k],
+            from_core[g].at[slot_z],
+            k_send.at[g, slot_z],
+            k_recv.at[g, slot_z],
+            device_at(z, y, x, 1 - k),
+        )
+
+    def own_copy(g, slot_z):
+        return pltpu.make_async_copy(parts[g].at[slot_z, :, :, k], held[g].at[slot_z], local_sem.at[g, slot_z])
+
+    def second_copy(g, slot_z, kind):
+        _, second = order_of(z, y, x, half, slot_z)
+        at = second if kind == 0 else (1 - y, 1 - x)
+        return remote(
+            held[g].at[slot_z, at[0], at[1]],
+            from_second[g].at[slot_z, kind],
+            p_send.at[g, slot_z, kind],
+            p_recv.at[g, slot_z, kind],
+            device_at(z, second[0], second[1], k),
+        )
+
+    def first_copy(g, slot_z):
+        first, _ = order_of(z, y, x, half, slot_z)
+        return remote(
+            held[g].at[slot_z, first[0], first[1]],
+            from_first[g].at[slot_z],
+            p_send.at[g, slot_z, 2],
+            p_recv.at[g, slot_z, 2],
+            device_at(z, first[0], first[1], k),
+        )
+
+    def z_copy(g, step, way):
+        slot_z = z + (1 - 2 * way) * (z_size - step)
+        return remote(
+            held[g].at[slot_z, y, x],
+            from_z[g].at[step - 1, way],
+            z_send.at[g, step - 1, way],
+            z_recv.at[g, step - 1, way],
+            device_at(z + 1 - 2 * way, y, x, k),
+        )
+
+    def z_wait(g, step, way):
+        remote(
+            held[g].at[z, y, x],
+            from_z[g].at[step - 1, way],
+            z_send.at[g, step - 1, way],
+            z_recv.at[g, step - 1, way],
+            device_at(z - 1 + 2 * way, y, x, k),
+        ).wait_recv()
+
+    def add(ref, at, other, other_at):
+        total = ref[at].astype(jnp.float32) + other[other_at].astype(jnp.float32)
+        ref[at] = total.astype(ref.dtype)
+
+    for slot_z in range(z_size):
+        for g in range(count):
+            core_copy(g, slot_z).start()
+            own_copy(g, slot_z).start()
+    for slot_z in range(z_size):
+        first, second = order_of(z, y, x, half, slot_z)
+        for g in range(count):
+            own_copy(g, slot_z).wait()
+            core_copy(g, slot_z).wait_recv()
+            for at in (second, (1 - y, 1 - x)):
+                add(held[g], (slot_z, at[0], at[1]), from_core[g], (slot_z, at[0], at[1]))
+            second_copy(g, slot_z, 0).start()
+            second_copy(g, slot_z, 1).start()
+            for at in (first, (y, x)):
+                add(held[g], (slot_z, at[0], at[1]), from_core[g], (slot_z, at[0], at[1]))
+    for slot_z in range(z_size):
+        first, second = order_of(z, y, x, half, slot_z)
+        for g in range(count):
+            second_copy(g, slot_z, 1).wait_recv()
+            add(held[g], (slot_z, first[0], first[1]), from_second[g], (slot_z, 1))
+            first_copy(g, slot_z).start()
+    for slot_z in range(z_size):
+        for g in range(count):
+            second_copy(g, slot_z, 0).wait_recv()
+            add(held[g], (slot_z, y, x), from_second[g], (slot_z, 0))
+            first_copy(g, slot_z).wait_recv()
+            add(held[g], (slot_z, y, x), from_first[g], (slot_z,))
     for step in range(1, z_size):
-        up.append(send(up[-1], 0, 1, lambda own, s=step: own >= s - 1))
-        down.append(send(down[-1], 0, -1, lambda own, s=step: own <= z_size - s))
-    line = lax.dynamic_update_index_in_dim(jnp.zeros((z_size, rows, width), shard.dtype), shard, z, 0)
-    for step in range(1, z_size):
-        block = jnp.where(z >= step, up[step], down[z_size - step])
-        line = lax.dynamic_update_index_in_dim(line, block, (z - step + z_size) % z_size, 0)
-    half = z_size // 2
-    low, high = line[:half], line[half:]
-    low = join_pair(low, 2, x, 1)
-    high = join_pair(high, 1, y, 1)
-    low = join_pair(low, 1, y, 1)
-    high = join_pair(high, 2, x, 2)
-    chip = jnp.concatenate([low, high], 0)
-    return join_pair(chip, 3, k, 3).reshape(-1, rows, width)
-
-
-def fold_pair(values, axis, spot, at):
-    leaving = lax.dynamic_index_in_dim(values, 1 - spot, at, keepdims=False).astype(jnp.bfloat16)
-    staying = lax.dynamic_index_in_dim(values, spot, at, keepdims=False).astype(jnp.float32)
-    return (staying + send(leaving, axis).astype(jnp.float32)).astype(jnp.bfloat16)
-
-
-def scatter_rows(blocks):
+        for way in range(2):
+            for g in range(count):
+                goes = z <= step - 1 if way == 0 else z >= z_size - step
+                came = (z >= 1) & (z <= step - 1) if way == 0 else (z <= z_size - 2) & (z >= z_size - step)
+
+                @pl.when(goes)
+                def _(g=g, step=step, way=way, came=came):
+                    slot_z = z + (1 - 2 * way) * (z_size - step)
+                    if step > 1:
+
+                        @pl.when(came)
+                        def _():
+                            z_wait(g, step - 1, way)
+                            add(held[g], (slot_z, y, x), from_z[g], (step - 2, way))
+
+                    z_copy(g, step, way).start()
+
+    for g in range(count):
+        total = held[g][z, y, x].astype(jnp.float32)
+        outs[g][...] = total
+        for way in range(2):
+
+            @pl.when(z > 0 if way == 0 else z < z_size - 1)
+            def _(g=g, way=way):
+                z_wait(g, z_size - 1, way)
+                outs[g][...] += from_z[g][z_size - 2, way].astype(jnp.float32)
+
+    for g in range(count):
+        for slot_z in range(z_size):
+            core_copy(g, slot_z).wait_send()
+            second_copy(g, slot_z, 0).wait_send()
+            second_copy(g, slot_z, 1).wait_send()
+            first_copy(g, slot_z).wait_send()
+        for step in range(1, z_size):
+            for way in range(2):
+
+                @pl.when(z <= step - 1 if way == 0 else z >= z_size - step)
+                def _(g=g, step=step, way=way):
+                    z_copy(g, step, way).wait_send()
+
+
+def scatter_all(parts, collective_id):
     sizes = grid_sizes()
-    z_size = sizes[0]
-    z, y, x, k = grid_place()
-    chip = fold_pair(blocks.reshape(sizes + blocks.shape[1:]), 3, k, 3)
-    half = z_size // 2
-    low, high = chip[:half], chip[half:]
-    low = fold_pair(low, 1, y, 1)
-    high = fold_pair(high, 2, x, 2)
-    low = fold_pair(low, 2, x, 1)
-    high = fold_pair(high, 1, y, 1)
-    line = jnp.concatenate([low, high], 0)
-    up = down = jnp.zeros(line.shape[1:], line.dtype)
-    for step in range(1, z_size):
-        rising = lax.dynamic_index_in_dim(line, (z + z_size - step) % z_size, 0, keepdims=False)
-        rising = (rising.astype(jnp.float32) + up.astype(jnp.float32)).astype(jnp.bfloat16)
-        up = send(rising, 0, 1, lambda own, s=step: own <= s - 1)
-        sinking = lax.dynamic_index_in_dim(line, (z + step) % z_size, 0, keepdims=False)
-        sinking = (sinking.astype(jnp.float32) + down.astype(jnp.float32)).astype(jnp.bfloat16)
-        down = send(sinking, 0, -1, lambda own, s=step: own >= z_size - s)
-    own = lax.dynamic_index_in_dim(line, z, 0, keepdims=False)
-    return own.astype(jnp.float32) + up.astype(jnp.float32) + down.astype(jnp.float32)
+    count, (z_size, y_size, x_size, _) = len(parts), sizes
+    shapes = [part.shape[1:] for part in parts]
+    dma = pltpu.SemaphoreType.DMA
+    plane = (z_size, y_size, x_size)
+
+    def buffers(lead):
+        return [pltpu.VMEM(lead + shape, jnp.bfloat16) for shape in shapes]
+
+    return pl.pallas_call(
+        functools.partial(scatter_kernel, count),
+        in_specs=[pl.BlockSpec(memory_space=pl.ANY)] * count,
+        out_specs=[pl.BlockSpec(memory_space=pltpu.VMEM)] * count,
+        out_shape=[jax.ShapeDtypeStruct(shape, jnp.float32) for shape in shapes],
+        scratch_shapes=buffers(plane)
+        + buffers(plane)
+        + buffers((z_size, 2))
+        + buffers((z_size,))
+        + buffers((z_size - 1, 2))
+        + [
+            dma((count, z_size)),
+            dma((count, z_size)),
+            dma((count, z_size)),
+            dma((count, z_size, 3)),
+            dma((count, z_size, 3)),
+            dma((count, z_size - 1, 2)),
+            dma((count, z_size - 1, 2)),
+        ],
+        compiler_params=pltpu.CompilerParams(
+            collective_id=collective_id, has_side_effects=True, vmem_limit_bytes=56 * 2**20
+        ),
+        name="scatter_sums",
+    )(*(part.reshape(sizes + part.shape[1:]) for part in parts))
 
 
 def dot_t(left, right):
@@ -643,32 +945,19 @@
     def exchange(values):
         return lax.all_to_all(values, BOTH, split_axis=0, concat_axis=0, tiled=True)
 
-    adapt_w = gather_rows(w_adapt).reshape(-1, width)
-    gain_rows = jnp.pad(gains.reshape(1, -1), ((0, 15), (0, width - gains.size)))
-    side = w_query.shape[0]
-    square = gather_rows(jnp.concatenate([w_query, w_key, w_value, w_out, gain_rows], 0))
-    query_w, key_w, value_w, output_w = (
-        square[:, at * side : (at + 1) * side].reshape(width, width) for at in range(4)
-    )
-    gain_float = (
-        square[:, 4 * side, : gains.size]
-        .reshape(parts, gains.shape[0], gains.shape[1])
-        .transpose(1, 0, 2)
-        .reshape(gains.shape[0], width)
-        .astype(jnp.float32)
-    )
-    gate_w = gather_rows(w_gate).reshape(width, -1)
-    up_w = gather_rows(w_up).reshape(width, -1)
-    down_w = gather_rows(w_down).reshape(-1, width)
-
+    adapt_w = gather_all([w_adapt], 0)[0].reshape(-1, width)
     latent_slots, embed_slots = to_slots(latents), to_slots(embeds)
-    upstream = exchange(to_slots(cotangent).reshape(parts, block_len, width)).reshape(length, width)
+    upstream = to_slots(cotangent).reshape(parts, block_len, width)
     embed_part = dot_n(embed_slots, adapt_w[width:])
     adapted = (dot_n(latent_slots, adapt_w[:width]) + embed_part).reshape(parts, block_len, width)
     embed_part = embed_part.reshape(parts, block_len, width)
     pair_at = lax.broadcasted_iota(jnp.int32, (parts, 1, 1), 0) % 2
     starting = jnp.where(pair_at == 0, embed_part, adapted).astype(jnp.bfloat16)
     shared = adapted.reshape(parts // 2, 2, block_len, width)[:, 0].astype(jnp.bfloat16)
+    gain_rows = jnp.pad(gains.reshape(1, -1), ((0, 15), (0, 0)))
+    shared, *shards = lax.optimization_barrier(
+        (shared, w_query, w_key, w_value, w_out, w_gate, w_up, w_down, gain_rows)
+    )
     shared = lax.all_to_all(
         shared,
         BOTH,
@@ -677,7 +966,15 @@
         tiled=True,
         axis_index_groups=[list(range(k, parts, 2)) for k in range(2)],
     )
+    *matrices, gain_float = gather_all(shards, 1)
+    query_w, key_w, value_w, output_w, gate_w, up_w, down_w = (
+        matrix.reshape(-1, matrix.shape[-1]) for matrix in matrices
+    )
+    gain_float = gain_float.reshape((parts,) + gain_rows.shape)[:, 0].reshape((parts,) + gains.shape)
+    gain_float = gain_float.transpose(1, 0, 2).reshape(gains.shape[0], width).astype(jnp.float32)
+    gate_w, starting, upstream = lax.optimization_barrier((gate_w, starting, upstream))
     starting = exchange(starting).reshape(length, width).astype(jnp.float32)
+    upstream = exchange(upstream).reshape(length, width)
 
     def before_attention(resid, cos_full, sin_full):
         normed = (resid * rms_scale(resid) * gain_float[0]).astype(jnp.bfloat16)
@@ -747,6 +1044,26 @@
     d_home = exchange(d_resid.reshape(parts, block_len, width))
     first_part = dot_w(first_out, d_resid)
 
+    def blocks(part):
+        return part.reshape(parts, -1, part.shape[-1])
+
+    gain_part = jnp.stack([gain_one, gain_two, gain_three, gain_four])
+    gain_part = gain_part.reshape(gains.shape[0], parts, gains.shape[1]).transpose(1, 0, 2)
+    gain_part = jnp.pad(
+        gain_part.reshape(parts, 1, gains.size).astype(jnp.bfloat16), ((0, 0), (0, 15), (0, 0))
+    )
+    sums = scatter_all(
+        [
+            blocks(part)
+            for part in (query_part, key_part, value_part, out_part, gate_part, up_part, down_part)
+        ]
+        + [gain_part],
+        2,
+    )
+    query_grad, key_grad, value_grad, out_grad, gate_grad, up_grad, down_grad, gain_grad = sums
+    gain_grad = gain_grad[0].reshape(gains.shape)
+    d_home, gate_grad = lax.optimization_barrier((d_home, gate_grad))
+
     d_home = from_slots(d_home)
     latent_back = dot_t(d_home, adapt_w[:width]).astype(jnp.bfloat16).reshape(latents.shape)
     embed_back = dot_t(d_home, adapt_w[width:]).astype(jnp.bfloat16).reshape(latents.shape)
@@ -755,25 +1072,8 @@
     embed_part = dot_w(embeds.reshape(row_count, width), d_home)
     final_back = from_slots(final_back).reshape(latents.shape)
 
-    def blocks(part):
-        return part.reshape(parts, -1, part.shape[-1])
-
-    down_grad = scatter_rows(blocks(down_part))
-    gate_grad = scatter_rows(blocks(gate_part))
-    up_grad = scatter_rows(blocks(up_part))
-    gain_part = jnp.stack([gain_one, gain_two, gain_three, gain_four])
-    gain_part = gain_part.reshape(gains.shape[0], parts, gains.shape[1]).transpose(1, 0, 2)
-    gain_part = jnp.pad(
-        gain_part.reshape(parts, 1, gains.size).astype(jnp.bfloat16), ((0, 0), (0, 15), (0, width - gains.size))
-    )
-    square_grad = scatter_rows(
-        jnp.concatenate(
-            [blocks(query_part), blocks(key_part), blocks(value_part), blocks(out_part), gain_part], 1
-        )
-    )
-    query_grad, key_grad, value_grad, out_grad = (square_grad[at * side : (at + 1) * side] for at in range(4))
-    gain_grad = square_grad[4 * side, : gains.size].reshape(gains.shape)
-    adapt_grad = scatter_rows(blocks(jnp.concatenate([latent_part, embed_part], 0).astype(jnp.bfloat16)))
+    adapt_part = jnp.concatenate([latent_part, embed_part], 0).astype(jnp.bfloat16)
+    (adapt_grad,) = scatter_all([blocks(adapt_part)], 3)
     return (
         final_back,
         latent_back,

time: 1060 us -> 855 us (0.81)
  Pallas kernels: 48.4 us -> 462 us
  waiting for transfers between devices: 254 us -> 22.7 us
  starting transfers between devices: 231 us -> 29 us
  other arithmetic: 165 us -> 44.8 us
  local copies, waits for them, and re-layouts: 125 us -> 60.5 us
    pallas_call x0 -> x4, Pallas kernels: none -> 414 us  [the longest x2 225 us: scatter_all(): pl.pallas_call(functools.partial(scatter_kernel, count), in_specs=[pl.Blo...]
    ppermute x113 -> x3, waiting for transfers between devices: 225 us -> 0.01 us  [send(): return lax.ppermute(values, BOTH, pairs)]
    ppermute x113 -> x3, starting transfers between devices: 201 us -> 1.86 us  [send(): return lax.ppermute(values, BOTH, pairs)]
    another operation x37 -> x2, other arithmetic: 52.7 us -> 0.11 us  [the longest x35 52.6 us: join_pair(): return jnp.stack([first, second], at)]
    convert_element_type x46 -> x1, other arithmetic: 32.2 us -> 0.88 us  [paired_on_device(): gain_float.transpose(1, 0, 2).reshape(gains.shape[0], width)]
    dynamic_slice x9 -> x0, local copies, waits for them, and re-layouts: 22.7 us -> none  [the longest x5 15.6 us: fold_pair(): lax.dynamic_index_in_dim(values, spot, at, keepdims=False)]
    unnamed x287 -> x162, local copies, waits for them, and re-layouts: 44.9 us -> 25.7 us
    dynamic_update_slice x14 -> x0, other arithmetic: 11.9 us -> none  [gather_rows(): lax.dynamic_update_index_in_dim(line, block, (z - step + z_size) % z_size...]
  transfers between devices with their start and end apart: 118 -> 8, of which waited for: 41 -> 1; matrix products, arithmetic and copies ran while one was open for 37% -> 21% of each run, Pallas kernels for 5% -> 43%
where the time goes in v2:
time: 855 us; the launch traced here: 845 us
  Pallas kernels  462 us (54%)
  matrix products  224 us (26%)
  local copies, waits for them, and re-layouts  60.5 us (7%)
  other arithmetic  44.8 us (5%)
  starting transfers between devices  29 us (3%)
  waiting for transfers between devices  22.7 us (3%)
    pallas_call x2, Pallas kernels, scatter_all(): pl.pallas_call(functools.partial(scatter_kernel, count), in_specs=[pl.Blo...  225 us
    pallas_call x2, Pallas kernels, gather_all(): pl.pallas_call(functools.partial(gather_kernel, count), in_specs=[anywher...  189 us
    dot_general x17, matrix products, dot_n(): return jnp.dot(left, right, preferred_element_type=jnp.float32)  97.3 us
    dot_general x12, matrix products, dot_w(): lax.dot_general(left, right, (((0,), (0,)), ((), ())), preferred_element_...  65.8 us
    dot_general x9, matrix products, dot_t(): lax.dot_general(left, right, (((1,), (1,)), ((), ())), preferred_element_...  61.2 us
    unnamed x162, local copies, waits for them, and re-layouts  25.7 us
    all_to_all x4, starting transfers between devices, exchange(): return lax.all_to_all(values, BOTH, split_axis=0, concat_axis=0, tiled=True)  23.3 us
    all_to_all x4, waiting for transfers between devices, exchange(): return lax.all_to_all(values, BOTH, split_axis=0, concat_axis=0, tiled=True)  22.7 us
  transfers between devices with their start and end apart: 8, of which 1 were waited for; matrix products, arithmetic and copies ran while one was open for 21% of the time, Pallas kernels for 43%

profile of v2, /device:TPU:0, one launch (start us, length us, event | category | flops | bytes accessed | tf_op | source)
XLA Modules:
  0.0 845.4 jit_solution(4388116867074628578)
XLA Ops:
  0.7 39.7 %gather_weights.2 = bf16[4,2,2,2,64,1024]{5,4,3,2,1,0:T(8,128)(2,1)} custom-call(bf16[64,1024]{1,0:T(8,128)(2,1)} %refs_0_.1), custom_call_target="tpu_custom_call" | custom-call | tf_op jit(solution)/shard_map/gather_weights/pallas_call | solution.py:560
  40.4 4.9 fusion.60
  45.8 8.1 fusion.23
  53.9 9.3 %fusion.33 = bf16[1024,1024]{1,0:T(8,128)(2,1)} fusion(f32[1024,1024]{1,0:T(8,128)} %fusion.23, bf16[1024,1024]{1,0:T(8,128)(2,1)} %bitcast.188, bf16[1024,1024]{1,0:T(8,128)(2,1)} %bitcast.173, s32[1024]{0:T(1024)S(1)} %add.214), kind=kOutput, calls=%fused_computation.82 | convolution fusion | flops 4299161600 | bytes 10489856 | tf_op jit(solution)/shard_map/dot_general | solution.py:756
  66.1 3.9 all-to-all-start.1
  70.1 149.1 %gather_weights.3 = (bf16[4,2,2,2,32,1024]{5,4,3,2,1,0:T(8,128)(2,1)}, bf16[4,2,2,2,32,1024]{5,4,3,2,1,0:T(8,128)(2,1)}, bf16[4,2,2,2,32,1024]{5,4,3,2,1,0:T(8,1...) custom-call(bf16[32,1024]{1,0:T(8,128)(2,1)} %refs_0_.2, ...), custom_call_target="tpu_custom_call" | custom-call | tf_op jit(solution)/shard_map/gather_weights/pallas_call | solution.py:560
  220.5 4.4 copy.39
  224.9 3.9 copy.37
  242.1 4.3 convolution_convert_fusion.11.v_ref
  248.8 3.7 fusion.36
  252.5 4.8 all-to-all-start
  261.1 9.7 %attend_shared.1 = bf16[512,1024]{1,0:T(8,128)(2,1)S(1)} custom-call(s32[1]{0:T(128)} %bitcast.15.core_ref, bf16[512,1024]{1,0:T(8,128)(2,1)S(1)} %copy-done.1, bf16[512,1024]{1,0:T(8,128)(2,1)S(1)} %copy.50.k_ref, bf16[512,1024]{1,0:T(8,128)(2,1)} %convolution_convert_fusion.11.v_ref, bf16[512,1024]{1,0:T(8,128)(2,1)} %collective-permute-done.ok_ref, ...), custom_call_target="tpu_custom_call" | custom-call | flops 1073741824 | bytes 6291456 | tf_op jit(solution)/shard_map/attend_shared/pallas_call | solution.py:836
  273.3 5.1 fusion.57
  278.4 14.1 %multiply_reduce_fusion.10 = (f32[512]{0:T(512)S(1)}, f32[512,1024]{1,0:T(8,128)}) fusion(bf16[2816,1024]{1,0:T(8,128)(2,1)} %bitcast.212, f32[512,2816]{1,0:T(8,128)} %fusion.57, bf16[1024,2816]{1,0:T(8,128)(2,1)} %bitcast.200, f32[512,1024]{1,0:T(8,128)} %copy-done.21, f32[1024]{0:T(1024)S(1)} %mul.493, f32[512]{0:T(512)S(1)} %add_rsqrt_fusion.6), kind=kOutput, calls=%fused_computation.64 | convolution fusion | flops 5916851712 | bytes 21504000 | tf_op jit(solution)/shard_map/dot_general | solution.py:756
  307.9 8.0 all-to-all-start.3
  315.9 5.4 multiply_reduce_fusion.9
  334.7 3.9 fusion.9
  338.6 3.9 copy.51.q_ref
  342.5 3.9 copy.52.k_ref
  351.2 16.2 %attend_whole.1 = (bf16[1024,1024]{1,0:T(8,128)(2,1)S(1)}, f32[1024,128]{1,0:T(8,128)S(1)}) custom-call(bf16[1024,1024]{1,0:T(8,128)(2,1)S(1)} %copy-done.2, bf16[1024,1024]{1,0:T(8,128)(2,1)S(1)} %copy-done.4, bf16[1024,1024]{1,0:T(8,128)(2,1)S(1)} %copy-done.7), custom_call_target="tpu_custom_call" | custom-call | flops 2147483648 | bytes 8388608 | tf_op jit(solution)/shard_map/attend_whole/pallas_call | solution.py:791
  375.3 8.8 %fusion.65 = f32[1024,2816]{1,0:T(8,128)} fusion(bf16[1024,1024]{1,0:T(8,128)(2,1)S(1)} %multiply_convert_fusion.5, bf16[1024,2816]{1,0:T(8,128)(2,1)S(1)} %bitcast.211), kind=kOutput, calls=%fused_computation.163 | convolution fusion | flops 5905580032 | bytes 19398656 | tf_op jit(solution)/shard_map/dot_general | solution.py:756
  384.1 11.9 %multiply_convert_fusion.2 = (bf16[1024,2816]{1,0:T(8,128)(2,1)S(1)}, f32[1024,2816]{1,0:T(8,128)}) fusion(f32[1024,2816]{1,0:T(8,128)} %fusion.65, bf16[1024,1024]{1,0:T(8,128)(2,1)S(1)} %multiply_convert_fusion.5, bf16[1024,2816]{1,0:T(8,128)(2,1)S(1)} %bitcast.204), kind=kOutput, calls=%fused_computation.2 | convolution fusion | flops 5922881536 | bytes 36700160 | tf_op jit(solution)/shard_map/dot_general | solution.py:756
  396.1 11.8 %multiply_reduce_fusion.6 = (f32[1024]{0:T(1024)S(1)}, f32[1024,1024]{1,0:T(8,128)}) fusion(bf16[1024,2816]{1,0:T(8,128)(2,1)S(1)} %get-tuple-element.134, bf16[2816,1024]{1,0:T(8,128)(2,1)} %bitcast.213), kind=kOutput, calls=%fused_computation.36 | convolution fusion | flops 5907676160 | bytes 15732736 | tf_op jit(solution)/shard_map/dot_general | solution.py:756
  407.9 4.3 fusion.5
  412.2 4.8 fusion.4
  417.1 19.6 %multiply_convert_fusion = (bf16[1024,2816]{1,0:T(8,128)(2,1)}, bf16[1024,2816]{1,0:T(8,128)(2,1)}) fusion(f32[1024,2816]{1,0:T(8,128)} %fusion.65, f32[1024,2816]{1,0:T(8,128)} %get-tuple-element.135, bf16[1024,1024]{1,0:T(8,128)(2,1)} %get-tuple-element.101, bf16[2816,1024]{1,0:T(8,128)(2,1)} %bitcast.214), kind=kOutput, calls=%fused_computation | convolution fusion | flops 5943066624 | bytes 42467328 | tf_op jit(solution)/shard_map/dot_general | solution.py:752
  436.7 10.0 %fusion.66 = f32[1024,1024]{1,0:T(8,128)S(1)} fusion(bf16[1024,2816]{1,0:T(8,128)(2,1)} %get-tuple-element.100, bf16[1024,2816]{1,0:T(8,128)(2,1)} %bitcast.205), kind=kOutput, calls=%fused_computation.164 | convolution fusion | flops 5905580032 | bytes 15728640 | tf_op jit(solution)/shard_map/dot_general | solution.py:752
  446.7 10.7 %multiply_reduce_fusion = (bf16[1024]{0:T(1024)(128)(2,1)S(1)}, f32[1024]{0:T(1024)S(1)}, f32[1024,1024]{1,0:T(8,128)S(1)}) fusion(f32[1024,1024]{1,0:T(8,128)S(1)} %copy-done.16, f32[1024]{0:T(1024)S(1)} %add_rsqrt_fusion.2, f32[1024]{0:T(1024)S(1)} %mul.493, f32[1024,1024]{1,0:T(8,128)S(1)} %fusion.66, bf16[1024,2816]{1,0:T(8,128)(2,1)} %get-tuple-element.99, ...), kind=kOutput, calls=%fused_computation.26 | convolution fusion | flops 5912918016 | bytes 24131584 | tf_op jit(solution)/shard_map/dot_general | solution.py:752
  457.4 3.9 multiply_reduce_fusion.1
  467.4 22.6 %attend_whole_back.1 = (bf16[1024,1024]{1,0:T(8,128)(2,1)S(1)}, bf16[1024,1024]{1,0:T(8,128)(2,1)S(1)}, bf16[1024,1024]{1,0:T(8,128)(2,1)S(1)}) custom-call(bf16[1024,1024]{1,0:T(8,128)(2,1)S(1)} %copy-done.3, bf16[1024,1024]{1,0:T(8,128)(2,1)S(1)} %copy-done.5, bf16[1024,1024]{1,0:T(8,128)(2,1)S(1)} %copy-done.8, bf16[1024,1024]{1,0:T(8,128)(2,1)} %copy-done.6, ...), custom_call_target="tpu_custom_call" | custom-call | flops 5368709120 | bytes 16777216 | tf_op jit(solution)/shard_map/attend_whole_back/pallas_call | solution.py:892
  490.0 3.7 convolution_convert_fusion.8
  496.1 3.8 convolution_convert_fusion.7
  502.3 3.7 convolution_convert_fusion.6
  506.0 5.1 multiply_reduce_fusion.2
  513.5 6.1 all-to-all-start.4
  520.8 6.1 convolution_convert_fusion.5
  526.9 10.9 %convolution_convert_fusion.2 = bf16[1024,2816]{1,0:T(8,128)(2,1)} fusion(bf16[1024,1024]{1,0:T(8,128)(2,1)S(1)} %copy-done.36, bf16[1024,2816]{1,0:T(8,128)(2,1)} %get-tuple-element.100), kind=kOutput, calls=%fused_computation.10 | convolution fusion | flops 5908463616 | bytes 13631488 | tf_op jit(solution)/shard_map/dot_general | solution.py:760
  537.8 8.1 convolution_convert_fusion
  545.8 22.6 %all-to-all-done.4 = bf16[32,32,1024]{2,1,0:T(8,128)(2,1)} async-done(((bf16[32,32,1024]{2,1,0:T(8,128)(2,1)}), bf16[32,32,1024]{2,1,0:T(8,128)(2,1)}, u32[]{:S(2)}, u32[]{:S(2)}) %all-to-all-start.4) | async-done | bytes 2097184 | tf_op jit(solution)/shard_map/all_to_all | solution.py:946
  568.5 4.4 all-to-all-start.2
  572.8 10.9 %convolution_convert_fusion.1 = bf16[1024,2816]{1,0:T(8,128)(2,1)} fusion(bf16[1024,1024]{1,0:T(8,128)(2,1)} %copy-done.35, bf16[1024,2816]{1,0:T(8,128)(2,1)} %get-tuple-element.99), kind=kOutput, calls=%fused_computation.9 | convolution fusion | flops 5908463616 | bytes 13631488 | tf_op jit(solution)/shard_map/dot_general | solution.py:760
  583.8 185.4 %scatter_sums.2 = (f32[32,1024]{1,0:T(8,128)}, f32[32,1024]{1,0:T(8,128)}, f32[32,1024]{1,0:T(8,128)}, f32[32,1024]{1,0:T(8,128)}, f32[32,2816]{1,0:T(8,128)}, /...) custom-call(bf16[4,2,2,2,32,1024]{5,4,3,2,1,0:T(8,128)(2,1)} %bitcast.169, ...), custom_call_target="tpu_custom_call" | custom-call | tf_op jit(solution)/shard_map/scatter_sums/pallas_call | solution.py:725
  770.5 4.1 fusion.38
  774.7 3.7 convolution_convert_fusion.4
  778.4 3.7 convolution_convert_fusion.3
  782.1 3.8 convert_bitcast_fusion
  785.9 5.6 fusion.37
  799.0 39.6 %scatter_sums.3 = f32[64,1024]{1,0:T(8,128)} custom-call(bf16[4,2,2,2,64,1024]{5,4,3,2,1,0:T(8,128)(2,1)} %bitcast.156), custom_call_target="tpu_custom_call" | custom-call | tf_op jit(solution)/shard_map/scatter_sums/pallas_call | solution.py:725
  (259 shorter events, 97.2 us)
Async XLA Ops:
  0.6 45.2 %copy-start = (bf16[32,32,1024]{2,1,0:T(8,128)(2,1)S(1)}, bf16[32,32,1024]{2,1,0:T(8,128)(2,1)}, u32[]{:S(2)}) copy-start(bf16[32,32,1024]{2,1,0:T(8,128)(2,1)} %param.14) | copy-start | bytes 6291460
  40.3 5.0 copy-start.60
  45.8 203.0 %copy-start.58 = (s32[1024]{0:T(1024)}, s32[1024]{0:T(1024)S(1)}, u32[]{:S(2)}) copy-start(s32[1024]{0:T(1024)S(1)} %add.214) | copy-start | bytes 12292
  66.1 164.0 %all-to-all-start.1 = ((bf16[16,32,1024]{2,1,0:T(8,128)(2,1)}), bf16[16,32,1024]{2,1,0:T(8,128)(2,1)S(1)}, u32[]{:S(2)}, u32[]{:S(2)}) async-start(bf16[16,32,1024]{2,1,0:T(8,128)(2,1)} %slice_bitcast_fusion), calls=%async_computation.1 | async-start | bytes 2097152 | tf_op jit(solution)/shard_map/all_to_all | solution.py:961
  220.5 100.9 %copy-start.54 = (f32[1024]{0:T(1024)}, f32[1024]{0:T(1024)S(1)}, u32[]{:S(2)}) copy-start(f32[1024]{0:T(1024)S(1)} %mul.469) | copy-start | bytes 12292
  241.7 18.2 %collective-permute-start = (bf16[512,1024]{1,0:T(8,128)(2,1)S(1)}, bf16[512,1024]{1,0:T(8,128)(2,1)}, u32[]{:S(2)}, u32[]{:S(2)}) collective-permute-start(bf16[512,1024]{1,0:T(8,128)(2,1)S(1)} %copy.50.k_ref), channel_id=1, source_target_pairs={{0,1},{1,0},{2,3},{3,2},{4,5},{5,4},{6,7},{7,6},{8,9},{9,8},{10,11... | collective-permute-start | bytes 3145736 | tf_op jit(solution)/shard_map/ppermute | solution.py:387
  242.1 4.4 copy-start.23
  242.1 4.4 copy-start.24
  246.4 13.5 %collective-permute-start.1 = (bf16[512,1024]{1,0:T(8,128)(2,1)}, bf16[512,1024]{1,0:T(8,128)(2,1)}, u32[]{:S(2)}, u32[]{:S(2)}) collective-permute-start(bf16[512,1024]{1,0:T(8,128)(2,1)} %convolution_convert_fusion.11.v_ref), channel_id=1, source_target_pairs={{0,1},{1,0},{2,3},{3,2},{4,5},{5,4},{6,7},{7,6},{8,9},{9,8},{10,11... | collective-permute-start | bytes 3145736 | tf_op jit(solution)/shard_map/ppermute | solution.py:387
  252.5 55.4 %all-to-all-start = ((bf16[32,32,1024]{2,1,0:T(8,128)(2,1)}), bf16[32,32,1024]{2,1,0:T(8,128)(2,1)}, u32[]{:S(2)}, u32[]{:S(2)}) async-start(bf16[32,32,1024]{2,1,0:T(8,128)(2,1)} %select_convert_fusion), calls=%async_computation | async-start | bytes 4194304 | tf_op jit(solution)/shard_map/all_to_all | solution.py:946
  261.1 9.7 %copy-start.62 = (bf16[4,2,2,2,32,1024]{5,4,3,2,1,0:T(8,128)(2,1)S(1)}, bf16[4,2,2,2,32,1024]{5,4,3,2,1,0:T(8,128)(2,1)}, u32[]{:S(2)}) copy-start(bf16[4,2,2,2,32,1024]{5,4,3,2,1,0:T(8,128)(2,1)} %get-tuple-element.62) | copy-start | bytes 6291460
  261.1 11.7 %slice-start.2 = ((s8[5767168]{0:T(1024)(128)(4,1)}), s8[1572864]{0:T(1024)(128)(4,1)S(1)}, s32[]{:S(2)}) async-start(s8[5767168]{0:T(1024)(128)(4,1)} %bitcast.206), calls=%async_computation.7 | async-start | bytes 3145728
  272.8 5.6 copy-start.21
  296.1 8.6 %collective-permute-start.2 = (bf16[512,1024]{1,0:T(8,128)(2,1)}, bf16[512,1024]{1,0:T(8,128)(2,1)}, u32[]{:S(2)}, u32[]{:S(2)}) collective-permute-start(bf16[512,1024]{1,0:T(8,128)(2,1)} %add_convert_fusion.3), channel_id=1, source_target_pairs={{1,0},{3,2},{5,4},{7,6},{9,8},{11,10},{13,12},{15,14},{17,16},{19,... | collective-permute-start | bytes 3145736 | tf_op jit(solution)/shard_map/ppermute | solution.py:387
  307.9 100.0 %all-to-all-start.3 = ((bf16[32,32,1024]{2,1,0:T(8,128)(2,1)}), bf16[32,32,1024]{2,1,0:T(8,128)(2,1)}, u32[]{:S(2)}, u32[]{:S(2)}) async-start(bf16[32,32,1024]{2,1,0:T(8,128)(2,1)} %bitcast.185), calls=%async_computation.3 | async-start | bytes 4194304 | tf_op jit(solution)/shard_map/all_to_all | solution.py:946
  324.5 4.8 copy-start.37
  351.2 16.2 %copy-start.63 = (bf16[4,2,2,2,32,1024]{5,4,3,2,1,0:T(8,128)(2,1)S(1)}, bf16[4,2,2,2,32,1024]{5,4,3,2,1,0:T(8,128)(2,1)}, u32[]{:S(2)}) copy-start(bf16[4,2,2,2,32,1024]{5,4,3,2,1,0:T(8,128)(2,1)} %get-tuple-element.62) | copy-start | bytes 6291460
  367.5 6.7 slice-start.4
  370.6 4.7 slice-start.5
  372.1 12.0 %slice-start = ((s8[5767168]{0:T(1024)(128)(4,1)}), s8[4194304]{0:T(1024)(128)(4,1)S(1)}, s32[]{:S(2)}) async-start(s8[5767168]{0:T(1024)(128)(4,1)} %bitcast.202), calls=%async_computation.5 | async-start | bytes 8388608
  375.3 8.8 %copy-start.35 = (bf16[1024,1024]{1,0:T(8,128)(2,1)}, bf16[1024,1024]{1,0:T(8,128)(2,1)S(1)}, u32[]{:S(2)}) copy-start(bf16[1024,1024]{1,0:T(8,128)(2,1)S(1)} %multiply_convert_fusion.5) | copy-start | bytes 6291460
  375.3 8.8 %slice-start.1 = ((s8[5767168]{0:T(1024)(128)(4,1)}), s8[1572864]{0:T(1024)(128)(4,1)S(1)}, s32[]{:S(2)}) async-start(s8[5767168]{0:T(1024)(128)(4,1)} %bitcast.202), calls=%async_computation.6 | async-start | bytes 3145728
  396.1 11.8 %copy-start.68 = (bf16[1024,2816]{1,0:T(8,128)(2,1)}, bf16[1024,2816]{1,0:T(8,128)(2,1)S(1)}, u32[]{:S(2)}) copy-start(bf16[1024,2816]{1,0:T(8,128)(2,1)S(1)} %get-tuple-element.134) | copy-start | bytes 17301508
  407.9 4.3 copy-start.15
  436.7 10.0 %copy-start.16 = (f32[1024,1024]{1,0:T(8,128)S(1)}, f32[1024,1024]{1,0:T(8,128)}, u32[]{:S(2)}) copy-start(f32[1024,1024]{1,0:T(8,128)} %copy-done.14) | copy-start | bytes 12582916
  446.7 10.7 %copy-start.18 = (f32[1024,1024]{1,0:T(8,128)S(1)}, f32[1024,1024]{1,0:T(8,128)}, u32[]{:S(2)}) copy-start(f32[1024,1024]{1,0:T(8,128)} %copy-done.17) | copy-start | bytes 12582916
  462.9 4.1 copy-start.8
  462.9 4.4 copy-start.10
  467.4 22.6 %copy-start.38 = (bf16[1024,1024]{1,0:T(8,128)(2,1)S(1)}, bf16[1024,1024]{1,0:T(8,128)(2,1)}, u32[]{:S(2)}) copy-start(bf16[1024,1024]{1,0:T(8,128)(2,1)} %copy-done.37) | copy-start | bytes 6291460
  496.1 3.8 copy-start.27
  513.5 55.0 %all-to-all-start.4 = ((bf16[32,32,1024]{2,1,0:T(8,128)(2,1)}), bf16[32,32,1024]{2,1,0:T(8,128)(2,1)}, u32[]{:S(2)}, u32[]{:S(2)}) async-start(bf16[32,32,1024]{2,1,0:T(8,128)(2,1)} %bitcast.158), calls=%async_computation.4 | async-start | bytes 4194304 | tf_op jit(solution)/shard_map/all_to_all | solution.py:946
  520.7 6.1 copy-start.36
  520.7 17.0 %slice-start.6 = ((s8[5767168]{0:T(1024)(128)(4,1)}), s8[4194304]{0:T(1024)(128)(4,1)S(1)}, s32[]{:S(2)}) async-start(s8[5767168]{0:T(1024)(128)(4,1)} %bitcast.222), calls=%async_computation.11 | async-start | bytes 8388608
  526.9 10.9 %copy-start.44 = (bf16[1024,1024]{1,0:T(8,128)(2,1)S(1)}, bf16[1024,1024]{1,0:T(8,128)(2,1)}, u32[]{:S(2)}) copy-start(bf16[1024,1024]{1,0:T(8,128)(2,1)} %get-tuple-element.101) | copy-start | bytes 6291460
  526.9 10.9 %slice-start.7 = ((s8[5767168]{0:T(1024)(128)(4,1)}), s8[1572864]{0:T(1024)(128)(4,1)S(1)}, s32[]{:S(2)}) async-start(s8[5767168]{0:T(1024)(128)(4,1)} %bitcast.222), calls=%async_computation.12 | async-start | bytes 3145728
  568.5 217.4 %all-to-all-start.2 = ((bf16[32,32,1024]{2,1,0:T(8,128)(2,1)}), bf16[32,32,1024]{2,1,0:T(8,128)(2,1)}, u32[]{:S(2)}, u32[]{:S(2)}) async-start(bf16[32,32,1024]{2,1,0:T(8,128)(2,1)} %bitcast.157), calls=%async_computation.2 | async-start | bytes 4194304 | tf_op jit(solution)/shard_map/all_to_all | solution.py:946
  583.8 186.7 %copy-start.59 = (s32[1024]{0:T(1024)S(1)}, s32[1024]{0:T(1024)}, u32[]{:S(2)}) copy-start(s32[1024]{0:T(1024)} %copy-done.58) | copy-start | bytes 12292
  770.5 4.1 copy-start.40
  774.7 7.4 copy-start.66
  785.9 5.6 copy-start.29
  785.9 5.6 copy-start.67
  799.0 41.4 %copy-start.53 = (f32[32,1024]{1,0:T(8,128)S(1)}, f32[32,1024]{1,0:T(8,128)}, u32[]{:S(2)}) copy-start(f32[32,1024]{1,0:T(8,128)} %get-tuple-element.162) | copy-start | bytes 393220
  799.0 42.1 %copy-start.52 = (f32[32,1024]{1,0:T(8,128)S(1)}, f32[32,1024]{1,0:T(8,128)}, u32[]{:S(2)}) copy-start(f32[32,1024]{1,0:T(8,128)} %get-tuple-element.163) | copy-start | bytes 393220
  799.0 42.7 %copy-start.51 = (f32[32,1024]{1,0:T(8,128)S(1)}, f32[32,1024]{1,0:T(8,128)}, u32[]{:S(2)}) copy-start(f32[32,1024]{1,0:T(8,128)} %get-tuple-element.164) | copy-start | bytes 393220
  799.0 43.4 %copy-start.50 = (f32[32,1024]{1,0:T(8,128)S(1)}, f32[32,1024]{1,0:T(8,128)}, u32[]{:S(2)}) copy-start(f32[32,1024]{1,0:T(8,128)} %get-tuple-element.165) | copy-start | bytes 393220
  799.0 44.0 %copy-start.49 = (f32[32,2816]{1,0:T(8,128)S(1)}, f32[32,2816]{1,0:T(8,128)}, u32[]{:S(2)}) copy-start(f32[32,2816]{1,0:T(8,128)} %get-tuple-element.166) | copy-start | bytes 1081348
  838.6 5.1 copy-start.48
  838.7 5.9 copy-start.47
  (37 other events, 91.9 us)

commit v3 on v2

--- a/solution.py
+++ b/solution.py
@@ -395,18 +395,10 @@
     return (z * y_size + y, x * k_size + k)
 
 
-def order_of(z, y, x, half, slot_z):
-    high = slot_z // half
-    first = (y + high * (1 - 2 * y), x + (1 - high) * (1 - 2 * x))
-    second = (y + (1 - high) * (1 - 2 * y), x + high * (1 - 2 * x))
+def order_of(y, x, turn):
+    first = (y + turn * (1 - 2 * y), x + (1 - turn) * (1 - 2 * x))
+    second = (y + (1 - turn) * (1 - 2 * y), x + turn * (1 - 2 * x))
     return first, second
-
-
-def greet(devices):
-    barrier = pltpu.get_barrier_semaphore()
-    for device in devices:
-        pl.semaphore_signal(barrier, inc=1, device_id=device, device_id_type=MESH)
-    pl.semaphore_wait(barrier, len(devices))
 
 
 def greet_line(z, y, x, k, z_size):
@@ -436,138 +428,135 @@
     )
 
 
-def gather_kernel(count, *refs):
+def row_views(shapes):
+    views = []
+    for at, (rows, width) in enumerate(shapes):
+        if rows % 32 == 0 and rows * width >= 2**16:
+            views += [(at, 0, rows // 2, 0), (at, rows // 2, rows // 2, 1)]
+        else:
+            views.append((at, 0, rows, at % 2))
+    return views
+
+
+def at_offsets(z, z_size, step, body):
+    if step == 0:
+        body(z, True, True)
+        return
+
+    @pl.when(z >= step)
+    def _():
+        body(z - step, True, False)
+
+    @pl.when(z + step < z_size)
+    def _():
+        body(z + step, False, True)
+
+
+def gather_kernel(views, count, *refs):
     z_size, _, _, _ = grid_sizes()
     z, y, x, k = grid_place()
-    half = z_size // 2
     shards, outs = refs[:count], refs[count : 2 * count]
     local_sem, z_send, z_recv, p_send, p_recv, k_send, k_recv = refs[2 * count :]
     greet_line(z, y, x, k, z_size)
+    everyone = range(len(views))
+
+    def spot(g, slot_z, at_y, at_x):
+        at, first_row, rows, _ = views[g]
+        return outs[at].at[slot_z, at_y, at_x, k, pl.ds(first_row, rows)]
 
     def z_copy(g, slot_z, way):
-        spot = outs[g].at[slot_z, y, x, k]
+        block = spot(g, slot_z, y, x)
         side = z + 1 - 2 * way
-        return remote(spot, spot, z_send.at[g, slot_z, way], z_recv.at[g, slot_z], device_at(side, y, x, k))
+        return remote(block, block, z_send.at[g, slot_z, way], z_recv.at[g, slot_z], device_at(side, y, x, k))
 
     def plane_copy(g, slot_z, kind):
-        first, second = order_of(z, y, x, half, slot_z)
+        first, second = order_of(y, x, (views[g][3] + slot_z) % 2)
         from_at = first if kind == 2 else (y, x)
         to_at = first if kind == 0 else second
-        spot = outs[g].at[slot_z, from_at[0], from_at[1], k]
-        return remote(
-            spot, spot, p_send.at[g, slot_z, kind], p_recv.at[g, slot_z, kind], device_at(z, to_at[0], to_at[1], k)
-        )
-
-    def core_copy(g, slot_z):
-        spot = outs[g].at[slot_z, :, :, k]
-        return remote(spot, spot, k_send.at[g, slot_z], k_recv.at[g, slot_z], device_at(z, y, x, 1 - k))
-
-    def spread_z(g, slot_z, up, down):
+        block = spot(g, slot_z, from_at[0], from_at[1])
+        device = device_at(z, to_at[0], to_at[1], k)
+        return remote(block, block, p_send.at[g, slot_z, kind], p_recv.at[g, slot_z, kind], device)
+
+    def core_copy(at, slot_z):
+        block = outs[at].at[slot_z, :, :, k]
+        return remote(block, block, k_send.at[at, slot_z], k_recv.at[at, slot_z], device_at(z, y, x, 1 - k))
+
+    def each_way(g, slot_z, up, down, act):
         if up:
 
             @pl.when(z < z_size - 1)
             def _():
-                z_copy(g, slot_z, 0).start()
+                act(z_copy(g, slot_z, 0))
 
         if down:
 
             @pl.when(z > 0)
             def _():
-                z_copy(g, slot_z, 1).start()
-
-    def at_offsets(step, body):
-        if step == 0:
-            body(z, True, True)
-            return
-
-        @pl.when(z >= step)
-        def _():
-            body(z - step, True, False)
-
-        @pl.when(z + step < z_size)
-        def _():
-            body(z + step, False, True)
-
-    own = [pltpu.make_async_copy(shards[g], outs[g].at[z, y, x, k], local_sem.at[g]) for g in range(count)]
+                act(z_copy(g, slot_z, 1))
+
+    own = [pltpu.make_async_copy(shards[at], outs[at].at[z, y, x, k], local_sem.at[at]) for at in range(count)]
     for copy in own:
         copy.start()
-    for step in range(z_size):
-        for g in range(count):
-            if step == 0:
-                own[g].wait()
-
-            def arrive(slot_z, up, down, g=g):
-                if not (up and down):
-                    z_copy(g, slot_z, 1 if up else 0).wait_recv()
-                spread_z(g, slot_z, up, down)
-                plane_copy(g, slot_z, 0).start()
-                plane_copy(g, slot_z, 1).start()
-
-            at_offsets(step, arrive)
-        for g in range(count):
-
-            def pass_on(slot_z, up, down, g=g):
-                plane_copy(g, slot_z, 0).wait_recv()
-                plane_copy(g, slot_z, 2).start()
-
-            at_offsets(step, pass_on)
-        if step > 0:
-            for g in range(count):
-
-                def cross(slot_z, up, down, g=g):
-                    plane_copy(g, slot_z, 1).wait_recv()
-                    plane_copy(g, slot_z, 2).wait_recv()
-                    core_copy(g, slot_z).start()
-
-                at_offsets(step - 1, cross)
-    for g in range(count):
-
-        def cross_last(slot_z, up, down, g=g):
+    for copy in own:
+        copy.wait()
+
+    def arrive(slot_z, up, down):
+        for g in everyone:
+            if not (up and down):
+                z_copy(g, slot_z, 1 if up else 0).wait_recv()
+            each_way(g, slot_z, up, down, lambda copy: copy.start())
+            plane_copy(g, slot_z, 0).start()
+            plane_copy(g, slot_z, 1).start()
+
+    def pass_on(slot_z, up, down):
+        for g in everyone:
+            plane_copy(g, slot_z, 0).wait_recv()
+            plane_copy(g, slot_z, 2).start()
+
+    def cross(slot_z, up, down):
+        for g in everyone:
             plane_copy(g, slot_z, 1).wait_recv()
             plane_copy(g, slot_z, 2).wait_recv()
-            core_copy(g, slot_z).start()
-
-        at_offsets(z_size - 1, cross_last)
-    for g in range(count):
-        for slot_z in range(z_size):
-            core_copy(g, slot_z).wait()
+        for at in range(count):
+            core_copy(at, slot_z).start()
+
+    def settle(slot_z, up, down):
+        for g in everyone:
+            each_way(g, slot_z, up, down, lambda copy: copy.wait_send())
             for kind in range(3):
                 plane_copy(g, slot_z, kind).wait_send()
+
+    for step in range(z_size + 1):
+        if step < z_size:
+            at_offsets(z, z_size, step, arrive)
+            at_offsets(z, z_size, step, pass_on)
+        if step > 0:
+            at_offsets(z, z_size, step - 1, cross)
     for step in range(z_size):
-        for g in range(count):
-
-            def settle(slot_z, up, down, g=g):
-                if up:
-
-                    @pl.when(z < z_size - 1)
-                    def _():
-                        z_copy(g, slot_z, 0).wait_send()
-
-                if down:
-
-                    @pl.when(z > 0)
-                    def _():
-                        z_copy(g, slot_z, 1).wait_send()
-
-            at_offsets(step, settle)
+        at_offsets(z, z_size, step, settle)
+    for slot_z in range(z_size):
+        for at in range(count):
+            core_copy(at, slot_z).wait()
 
 
 def gather_all(shards, collective_id):
     sizes = grid_sizes()
     count, z_size = len(shards), sizes[0]
+    views = row_views([shard.shape for shard in shards])
+    series = len(views)
     anywhere = pl.BlockSpec(memory_space=pl.ANY)
     dma = pltpu.SemaphoreType.DMA
     return pl.pallas_call(
-        functools.partial(gather_kernel, count),
+        functools.partial(gather_kernel, views, count),
         in_specs=[anywhere] * count,
         out_specs=[anywhere] * count,
         out_shape=[jax.ShapeDtypeStruct(sizes + shard.shape, shard.dtype) for shard in shards],
         scratch_shapes=[
             dma((count,)),
-            dma((count, z_size, 2)),
-            dma((count, z_size)),
-            dma((count, z_size, 3)),
-            dma((count, z_size, 3)),
+            dma((series, z_size, 2)),
+            dma((series, z_size)),
+            dma((series, z_size, 3)),
+            dma((series, z_size, 3)),
             dma((count, z_size)),
             dma((count, z_size)),
         ],
@@ -576,146 +565,154 @@
     )(*shards)
 
 
-def scatter_kernel(count, *refs):
+def scatter_kernel(views, count, *refs):
     z_size, _, _, _ = grid_sizes()
     z, y, x, k = grid_place()
-    half = z_size // 2
     parts, outs = refs[:count], refs[count : 2 * count]
     held, from_core = refs[2 * count : 3 * count], refs[3 * count : 4 * count]
     from_second, from_first = refs[4 * count : 5 * count], refs[5 * count : 6 * count]
     from_z = refs[6 * count : 7 * count]
     local_sem, k_send, k_recv, p_send, p_recv, z_send, z_recv = refs[7 * count :]
     greet_line(z, y, x, k, z_size)
-
-    def core_copy(g, slot_z):
+    everyone = range(len(views))
+
+    def rows_of(g):
+        return pl.ds(views[g][1], views[g][2])
+
+    def core_copy(at, slot_z):
         return remote(
-            parts[g].at[slot_z, :, :, 1 - k],
-            from_core[g].at[slot_z],
-            k_send.at[g, slot_z],
-            k_recv.at[g, slot_z],
+            parts[at].at[slot_z, :, :, 1 - k],
+            from_core[at].at[slot_z],
+            k_send.at[at, slot_z],
+            k_recv.at[at, slot_z],
             device_at(z, y, x, 1 - k),
         )
 
-    def own_copy(g, slot_z):
-        return pltpu.make_async_copy(parts[g].at[slot_z, :, :, k], held[g].at[slot_z], local_sem.at[g, slot_z])
+    def own_copy(at, slot_z):
+        return pltpu.make_async_copy(parts[at].at[slot_z, :, :, k], held[at].at[slot_z], local_sem.at[at, slot_z])
+
+    def turns(g, slot_z):
+        return order_of(y, x, (views[g][3] + slot_z) % 2)
 
     def second_copy(g, slot_z, kind):
-        _, second = order_of(z, y, x, half, slot_z)
-        at = second if kind == 0 else (1 - y, 1 - x)
+        at, (_, second) = views[g][0], turns(g, slot_z)
+        block = second if kind == 0 else (1 - y, 1 - x)
         return remote(
-            held[g].at[slot_z, at[0], at[1]],
-            from_second[g].at[slot_z, kind],
+            held[at].at[slot_z, block[0], block[1], rows_of(g)],
+            from_second[at].at[slot_z, kind, rows_of(g)],
             p_send.at[g, slot_z, kind],
             p_recv.at[g, slot_z, kind],
             device_at(z, second[0], second[1], k),
         )
 
     def first_copy(g, slot_z):
-        first, _ = order_of(z, y, x, half, slot_z)
+        at, (first, _) = views[g][0], turns(g, slot_z)
         return remote(
-            held[g].at[slot_z, first[0], first[1]],
-            from_first[g].at[slot_z],
+            held[at].at[slot_z, first[0], first[1], rows_of(g)],
+            from_first[at].at[slot_z, rows_of(g)],
             p_send.at[g, slot_z, 2],
             p_recv.at[g, slot_z, 2],
             device_at(z, first[0], first[1], k),
         )
 
-    def z_copy(g, step, way):
-        slot_z = z + (1 - 2 * way) * (z_size - step)
+    def z_copy(at, slot_z, way, here=None):
+        side = z + 1 - 2 * way if here is None else here
         return remote(
-            held[g].at[slot_z, y, x],
-            from_z[g].at[step - 1, way],
-            z_send.at[g, step - 1, way],
-            z_recv.at[g, step - 1, way],
-            device_at(z + 1 - 2 * way, y, x, k),
+            held[at].at[slot_z, y, x],
+            from_z[at].at[slot_z, way],
+            z_send.at[at, slot_z, way],
+            z_recv.at[at, slot_z, way],
+            device_at(side, y, x, k),
         )
 
-    def z_wait(g, step, way):
-        remote(
-            held[g].at[z, y, x],
-            from_z[g].at[step - 1, way],
-            z_send.at[g, step - 1, way],
-            z_recv.at[g, step - 1, way],
-            device_at(z - 1 + 2 * way, y, x, k),
-        ).wait_recv()
-
     def add(ref, at, other, other_at):
-        total = ref[at].astype(jnp.float32) + other[other_at].astype(jnp.float32)
-        ref[at] = total.astype(ref.dtype)
-
-    for slot_z in range(z_size):
-        for g in range(count):
-            core_copy(g, slot_z).start()
-            own_copy(g, slot_z).start()
-    for slot_z in range(z_size):
-        first, second = order_of(z, y, x, half, slot_z)
-        for g in range(count):
-            own_copy(g, slot_z).wait()
-            core_copy(g, slot_z).wait_recv()
-            for at in (second, (1 - y, 1 - x)):
-                add(held[g], (slot_z, at[0], at[1]), from_core[g], (slot_z, at[0], at[1]))
+        ref[at] = ref[at] + other[other_at]
+
+    def begin(slot_z, below, above):
+        for at in range(count):
+            core_copy(at, slot_z).start()
+            own_copy(at, slot_z).start()
+
+    def fold_core(slot_z, below, above):
+        for at in range(count):
+            own_copy(at, slot_z).wait()
+            core_copy(at, slot_z).wait_recv()
+        for g in everyone:
+            at, rows = views[g][0], rows_of(g)
+            first, second = turns(g, slot_z)
+            for spot in (second, (1 - y, 1 - x)):
+                add(held[at], (slot_z, spot[0], spot[1], rows), from_core[at], (slot_z, spot[0], spot[1], rows))
             second_copy(g, slot_z, 0).start()
             second_copy(g, slot_z, 1).start()
-            for at in (first, (y, x)):
-                add(held[g], (slot_z, at[0], at[1]), from_core[g], (slot_z, at[0], at[1]))
-    for slot_z in range(z_size):
-        first, second = order_of(z, y, x, half, slot_z)
-        for g in range(count):
+            for spot in (first, (y, x)):
+                add(held[at], (slot_z, spot[0], spot[1], rows), from_core[at], (slot_z, spot[0], spot[1], rows))
+
+    def fold_second(slot_z, below, above):
+        for g in everyone:
+            at, rows = views[g][0], rows_of(g)
+            first, _ = turns(g, slot_z)
             second_copy(g, slot_z, 1).wait_recv()
-            add(held[g], (slot_z, first[0], first[1]), from_second[g], (slot_z, 1))
+            add(held[at], (slot_z, first[0], first[1], rows), from_second[at], (slot_z, 1, rows))
             first_copy(g, slot_z).start()
-    for slot_z in range(z_size):
-        for g in range(count):
+
+    def fold_first(slot_z, below, above):
+        for g in everyone:
+            at, rows = views[g][0], rows_of(g)
             second_copy(g, slot_z, 0).wait_recv()
-            add(held[g], (slot_z, y, x), from_second[g], (slot_z, 0))
+            add(held[at], (slot_z, y, x, rows), from_second[at], (slot_z, 0, rows))
             first_copy(g, slot_z).wait_recv()
-            add(held[g], (slot_z, y, x), from_first[g], (slot_z,))
-    for step in range(1, z_size):
-        for way in range(2):
-            for g in range(count):
-                goes = z <= step - 1 if way == 0 else z >= z_size - step
-                came = (z >= 1) & (z <= step - 1) if way == 0 else (z <= z_size - 2) & (z >= z_size - step)
-
-                @pl.when(goes)
-                def _(g=g, step=step, way=way, came=came):
-                    slot_z = z + (1 - 2 * way) * (z_size - step)
-                    if step > 1:
-
-                        @pl.when(came)
-                        def _():
-                            z_wait(g, step - 1, way)
-                            add(held[g], (slot_z, y, x), from_z[g], (step - 2, way))
-
-                    z_copy(g, step, way).start()
-
-    for g in range(count):
-        total = held[g][z, y, x].astype(jnp.float32)
-        outs[g][...] = total
-        for way in range(2):
-
-            @pl.when(z > 0 if way == 0 else z < z_size - 1)
-            def _(g=g, way=way):
-                z_wait(g, z_size - 1, way)
-                outs[g][...] += from_z[g][z_size - 2, way].astype(jnp.float32)
-
-    for g in range(count):
-        for slot_z in range(z_size):
-            core_copy(g, slot_z).wait_send()
+            add(held[at], (slot_z, y, x, rows), from_first[at], (slot_z, rows))
+        if below and above:
+            for at in range(count):
+                outs[at][...] = held[at][slot_z, y, x].astype(jnp.float32)
+        for way, use in ((0, above), (1, below)):
+            if not use:
+                continue
+            came, source = (z > 0, z - 1) if way == 0 else (z < z_size - 1, z + 1)
+
+            @pl.when(came)
+            def _(way=way, source=source):
+                for at in range(count):
+                    z_copy(at, slot_z, way, source).wait_recv()
+                    if below and above:
+                        outs[at][...] += from_z[at][slot_z, way].astype(jnp.float32)
+                    else:
+                        add(held[at], (slot_z, y, x), from_z[at], (slot_z, way))
+
+            if not (below and above):
+                for at in range(count):
+                    z_copy(at, slot_z, way).start()
+
+    def settle(slot_z, below, above):
+        for at in range(count):
+            core_copy(at, slot_z).wait_send()
+            if not (below and above):
+                z_copy(at, slot_z, 0 if above else 1).wait_send()
+        for g in everyone:
             second_copy(g, slot_z, 0).wait_send()
             second_copy(g, slot_z, 1).wait_send()
             first_copy(g, slot_z).wait_send()
-        for step in range(1, z_size):
-            for way in range(2):
-
-                @pl.when(z <= step - 1 if way == 0 else z >= z_size - step)
-                def _(g=g, step=step, way=way):
-                    z_copy(g, step, way).wait_send()
+
+    far = z_size - 1
+    for step in range(far, -1, -1):
+        at_offsets(z, z_size, step, begin)
+    for step in range(far, -3, -1):
+        if step >= 0:
+            at_offsets(z, z_size, step, fold_core)
+        if 0 <= step + 1 <= far:
+            at_offsets(z, z_size, step + 1, fold_second)
+        if 0 <= step + 2 <= far:
+            at_offsets(z, z_size, step + 2, fold_first)
+    for step in range(z_size):
+        at_offsets(z, z_size, step, settle)
 
 
 def scatter_all(parts, collective_id):
     sizes = grid_sizes()
     count, (z_size, y_size, x_size, _) = len(parts), sizes
     shapes = [part.shape[1:] for part in parts]
+    views = row_views(shapes)
+    series = len(views)
     dma = pltpu.SemaphoreType.DMA
     plane = (z_size, y_size, x_size)
 
@@ -723,7 +720,7 @@
         return [pltpu.VMEM(lead + shape, jnp.bfloat16) for shape in shapes]
 
     return pl.pallas_call(
-        functools.partial(scatter_kernel, count),
+        functools.partial(scatter_kernel, views, count),
         in_specs=[pl.BlockSpec(memory_space=pl.ANY)] * count,
         out_specs=[pl.BlockSpec(memory_space=pltpu.VMEM)] * count,
         out_shape=[jax.ShapeDtypeStruct(shape, jnp.float32) for shape in shapes],
@@ -731,15 +728,15 @@
         + buffers(plane)
         + buffers((z_size, 2))
         + buffers((z_size,))
-        + buffers((z_size - 1, 2))
+        + buffers((z_size, 2))
         + [
             dma((count, z_size)),
             dma((count, z_size)),
             dma((count, z_size)),
-            dma((count, z_size, 3)),
-            dma((count, z_size, 3)),
-            dma((count, z_size - 1, 2)),
-            dma((count, z_size - 1, 2)),
+            dma((series, z_size, 3)),
+            dma((series, z_size, 3)),
+            dma((count, z_size, 2)),
+            dma((count, z_size, 2)),
         ],
         compiler_params=pltpu.CompilerParams(
             collective_id=collective_id, has_side_effects=True, vmem_limit_bytes=56 * 2**20
@@ -909,12 +906,361 @@
     return jnp.concatenate([cosine, cosine], 1), jnp.concatenate([-sine, sine], 1)
 
 
-def rotate_rows(values, cos_full, sin_full):
-    rows, width = values.shape
-    heads = values.reshape(rows, width // HEAD_DIM, HEAD_DIM)
-    half = HEAD_DIM // 2
-    turned = jnp.concatenate([heads[..., half:], heads[..., :half]], -1)
-    return (heads * cos_full[:, None] + turned * sin_full[:, None]).reshape(rows, width)
+def whole_block(array):
+    return pl.BlockSpec(array.shape, lambda *_: (0,) * array.ndim, pipeline_mode=pl.Buffered(1))
+
+
+def row_block(rows, width):
+    return pl.BlockSpec((rows, width), lambda i: (i, 0))
+
+
+def compute_params(megabytes=58):
+    return pltpu.CompilerParams(vmem_limit_bytes=megabytes * 2**20)
+
+
+def cost(flops, nbytes):
+    return pl.CostEstimate(flops=int(flops), bytes_accessed=int(nbytes), transcendentals=0)
+
+
+def unit_rows(values):
+    scale_rows = rms_scale(values)
+    return scale_rows, values * scale_rows
+
+
+def pull_norm(values, upstream, gain_row):
+    scale_rows, normal = unit_rows(values)
+    gain_part = jnp.sum(upstream * normal, 0, keepdims=True)
+    scaled = upstream * gain_row
+    return scale_rows * (scaled - normal * jnp.mean(scaled * normal, -1, keepdims=True)), gain_part
+
+
+def home_kernel(block_len, target_ref, s_ref, e_ref, c_ref, w_ref, start_ref, shared_ref, up_ref):
+    rows, width = start_ref.shape
+    count = s_ref.shape[0]
+    at_row = lax.broadcasted_iota(jnp.int32, (rows, count), 0) + pl.program_id(0) * rows
+    order = (at_row == target_ref[...]).astype(jnp.bfloat16)
+    up_ref[...] = dot_n(order, c_ref[...]).astype(jnp.bfloat16)
+    latent = dot_n(order, s_ref[...]).astype(jnp.bfloat16)
+    embed = dot_n(order, e_ref[...]).astype(jnp.bfloat16)
+    embed_part = dot_n(embed, w_ref[width:, :])
+    adapted = dot_n(jnp.concatenate([latent, embed], 1), w_ref[...])
+    shared_ref[...] = adapted.astype(jnp.bfloat16)
+    pair_at = lax.broadcasted_iota(jnp.int32, (rows, 1), 0) // block_len % 2
+    start_ref[...] = jnp.where(pair_at == 0, embed_part, adapted).astype(jnp.bfloat16)
+
+
+def adapt_at_home(target, latents, embeds, cotangent, adapt_w, block_len):
+    count, width = latents.shape
+    like = jax.ShapeDtypeStruct((count, width), jnp.bfloat16)
+    return pl.pallas_call(
+        functools.partial(home_kernel, block_len),
+        grid=(count // TILE,),
+        in_specs=[whole_block(a) for a in (target, latents, embeds, cotangent, adapt_w)],
+        out_specs=[
+            row_block(TILE, width),
+            row_block(TILE, width),
+            row_block(TILE, width),
+        ],
+        out_shape=[like, like, like],
+        compiler_params=compute_params(),
+        cost_estimate=cost(10 * count * width * width, 14 * count * width),
+        name="adapt_at_home",
+    )(target, latents, embeds, cotangent, adapt_w)
+
+
+def turned_heads(values, cos, sin):
+    parts = []
+    for head in range(values.shape[1] // HEAD_DIM):
+        one = values[:, head * HEAD_DIM : (head + 1) * HEAD_DIM]
+        parts.append(one * cos + pltpu.roll(one, HEAD_DIM // 2, 1) * sin)
+    return jnp.concatenate(parts, 1)
+
+
+def project_heads(resid, gain_ref, wq_ref, wk_ref, wv_ref, cos_ref, sin_ref, q_ref, k_ref, v_ref):
+    normed = (unit_rows(resid)[1] * gain_ref[0:1, :]).astype(jnp.bfloat16)
+    cos, sin = cos_ref[...], sin_ref[...]
+    q_ref[...] = turned_heads(dot_n(normed, wq_ref[...]), cos, sin).astype(jnp.bfloat16)
+    k_ref[...] = turned_heads(dot_n(normed, wk_ref[...]), cos, sin).astype(jnp.bfloat16)
+    v_ref[...] = dot_n(normed, wv_ref[...]).astype(jnp.bfloat16)
+    return normed
+
+
+def first_heads_kernel(r_ref, gain_ref, wq_ref, wk_ref, wv_ref, cos_ref, sin_ref, q_ref, k_ref, v_ref):
+    resid = r_ref[...].astype(jnp.float32)
+    project_heads(resid, gain_ref, wq_ref, wk_ref, wv_ref, cos_ref, sin_ref, q_ref, k_ref, v_ref)
+
+
+def first_heads(resid, gain_float, query_w, key_w, value_w, cos, sin):
+    rows, width = resid.shape
+    tile = min(TILE, rows)
+    fixed = (gain_float, query_w, key_w, value_w)
+    return pl.pallas_call(
+        first_heads_kernel,
+        grid=(rows // tile,),
+        in_specs=[row_block(tile, width)] + [whole_block(a) for a in fixed] + [row_block(tile, HEAD_DIM)] * 2,
+        out_specs=[row_block(tile, width)] * 3,
+        out_shape=[jax.ShapeDtypeStruct((rows, width), jnp.bfloat16)] * 3,
+        compiler_params=compute_params(),
+        cost_estimate=cost(6 * rows * width * width, 8 * rows * width + 6 * width * width),
+        name="first_heads",
+    )(resid, *fixed, cos, sin)
+
+
+def last_heads_kernel(
+    start_ref, first_ref, wa_ref, gain_ref, wq_ref, wk_ref, wv_ref, cos_ref, sin_ref, r_ref, n_ref, q_ref, k_ref, v_ref
+):
+    resid = start_ref[...].astype(jnp.float32) + dot_n(first_ref[...], wa_ref[...])
+    r_ref[...] = resid
+    n_ref[...] = project_heads(resid, gain_ref, wq_ref, wk_ref, wv_ref, cos_ref, sin_ref, q_ref, k_ref, v_ref)
+
+
+def last_heads(starting, first_out, adapt_w, gain_float, query_w, key_w, value_w, cos, sin):
+    rows, width = starting.shape
+    upper = pl.BlockSpec((width, width), lambda i: (0, 0), pipeline_mode=pl.Buffered(1))
+    fixed = (gain_float, query_w, key_w, value_w)
+    like = jax.ShapeDtypeStruct((rows, width), jnp.bfloat16)
+    return pl.pallas_call(
+        last_heads_kernel,
+        grid=(rows // TILE,),
+        in_specs=[row_block(TILE, width)] * 2
+        + [upper]
+        + [whole_block(a) for a in fixed]
+        + [row_block(TILE, HEAD_DIM)] * 2,
+        out_specs=[row_block(TILE, width)] * 5,
+        out_shape=[jax.ShapeDtypeStruct((rows, width), jnp.float32)] + [like] * 4,
+        compiler_params=compute_params(),
+        cost_estimate=cost(8 * rows * width * width, 16 * rows * width + 8 * width * width),
+        name="last_heads",
+    )(starting, first_out, adapt_w, *fixed, cos, sin)
+
+
+def column_chunks(total, chunk=768):
+    return [(at, min(chunk, total - at)) for at in range(0, total, chunk)]
+
+
+def forward_rows(resid, mixed, gain_ref, wo_ref, wg_ref, wu_ref, wd_ref, keep):
+    branch = dot_n(mixed, wo_ref[...])
+    middle = resid + unit_rows(branch)[1] * gain_ref[1:2, :]
+    mlp_in = (unit_rows(middle)[1] * gain_ref[2:3, :]).astype(jnp.bfloat16)
+    down_out = None
+    for at, size in column_chunks(wg_ref.shape[1]):
+        columns = slice(at, at + size)
+        gate_pre = dot_n(mlp_in, wg_ref[:, columns])
+        up_pre = dot_n(mlp_in, wu_ref[:, columns])
+        sigma = 1.0 / (1.0 + jnp.exp(-gate_pre))
+        hidden = (gate_pre * sigma * up_pre).astype(jnp.bfloat16)
+        keep(columns, gate_pre, up_pre, hidden)
+        part = dot_n(hidden, wd_ref[columns, :])
+        down_out = part if down_out is None else down_out + part
+    return branch, middle, mlp_in, down_out
+
+
+def first_rows_kernel(r_ref, mixed_ref, gain_ref, wo_ref, wg_ref, wu_ref, wd_ref, out_ref):
+    resid = r_ref[...].astype(jnp.float32)
+    _, middle, _, down_out = forward_rows(
+        resid, mixed_ref[...], gain_ref, wo_ref, wg_ref, wu_ref, wd_ref, lambda *_: None
+    )
+    out_ref[...] = (middle + unit_rows(down_out)[1] * gain_ref[3:4, :]).astype(jnp.bfloat16)
+
+
+def first_rows(resid, mixed, gain_float, output_w, gate_w, up_w, down_w):
+    rows, width = resid.shape
+    tile = min(TILE, rows)
+    fixed = (gain_float, output_w, gate_w, up_w, down_w)
+    weights = output_w.size + gate_w.size + up_w.size + down_w.size
+    return pl.pallas_call(
+        first_rows_kernel,
+        grid=(rows // tile,),
+        in_specs=[row_block(tile, width)] * 2 + [whole_block(a) for a in fixed],
+        out_specs=row_block(tile, width),
+        out_shape=jax.ShapeDtypeStruct((rows, width), jnp.bfloat16),
+        compiler_params=compute_params(),
+        cost_estimate=cost(2 * rows * weights, 6 * rows * width + 2 * weights),
+        name="first_rows",
+    )(resid, mixed, *fixed)
+
+
+def last_rows_kernel(
+    r_ref,
+    mixed_ref,
+    up_ref,
+    gain_ref,
+    wo_ref,
+    wg_ref,
+    wu_ref,
+    wd_ref,
+    out_ref,
+    hidden_ref,
+    dd_ref,
+    mlp_ref,
+    dg_ref,
+    du_ref,
+    dmid_ref,
+    db_ref,
+    dmix_ref,
+    gains_ref,
+    gate_sc,
+    up_sc,
+):
+    def keep(columns, gate_pre, up_pre, hidden):
+        gate_sc[:, columns] = gate_pre
+        up_sc[:, columns] = up_pre
+        hidden_ref[:, columns] = hidden
+
+    branch, middle, mlp_in, down_out = forward_rows(
+        r_ref[...], mixed_ref[...], gain_ref, wo_ref, wg_ref, wu_ref, wd_ref, keep
+    )
+    mlp_ref[...] = mlp_in
+    out_ref[...] = (middle + unit_rows(down_out)[1] * gain_ref[3:4, :]).astype(jnp.bfloat16)
+    d_result = up_ref[...].astype(jnp.float32)
+    d_down, gain_four = pull_norm(down_out, d_result, gain_ref[3:4, :])
+    d_down = d_down.astype(jnp.bfloat16)
+    dd_ref[...] = d_down
+    d_mlp = None
+    for at, size in column_chunks(wg_ref.shape[1]):
+        columns = slice(at, at + size)
+        d_hidden = dot_t(d_down, wd_ref[columns, :])
+        gate_pre, up_pre = gate_sc[:, columns], up_sc[:, columns]
+        sigma = 1.0 / (1.0 + jnp.exp(-gate_pre))
+        d_gate = (d_hidden * up_pre * sigma * (1.0 + gate_pre * (1.0 - sigma))).astype(jnp.bfloat16)
+        d_up = (d_hidden * gate_pre * sigma).astype(jnp.bfloat16)
+        dg_ref[:, columns] = d_gate
+        du_ref[:, columns] = d_up
+        part = dot_t(d_gate, wg_ref[:, columns]) + dot_t(d_up, wu_ref[:, columns])
+        d_mlp = part if d_mlp is None else d_mlp + part
+    d_middle, gain_three = pull_norm(middle, d_mlp, gain_ref[2:3, :])
+    d_middle = d_middle + d_result
+    dmid_ref[...] = d_middle
+    d_branch, gain_two = pull_norm(branch, d_middle, gain_ref[1:2, :])
+    d_branch = d_branch.astype(jnp.bfloat16)
+    db_ref[...] = d_branch
+    dmix_ref[...] = dot_t(d_branch, wo_ref[...]).astype(jnp.bfloat16)
+
+    @pl.when(pl.program_id(0) == 0)
+    def _():
+        gains_ref[...] = jnp.zeros_like(gains_ref)
+
+    gains_ref[0:1, :] += gain_two
+    gains_ref[1:2, :] += gain_three
+    gains_ref[2:3, :] += gain_four
+
+
+def last_rows(resid, mixed, upstream, gain_float, output_w, gate_w, up_w, down_w):
+    rows, width = resid.shape
+    inner = gate_w.shape[1]
+    fixed = (gain_float, output_w, gate_w, up_w, down_w)
+    weights = output_w.size + gate_w.size + up_w.size + down_w.size
+    narrow, wide = (jax.ShapeDtypeStruct((rows, w), jnp.bfloat16) for w in (width, inner))
+    tall = jax.ShapeDtypeStruct((rows, width), jnp.float32)
+    outs = [narrow, wide, narrow, narrow, wide, wide, tall, narrow, narrow]
+    return pl.pallas_call(
+        last_rows_kernel,
+        grid=(rows // TILE,),
+        in_specs=[row_block(TILE, width)] * 3 + [whole_block(a) for a in fixed],
+        out_specs=[row_block(TILE, one.shape[1]) for one in outs]
+        + [pl.BlockSpec((8, width), lambda i: (0, 0))],
+        out_shape=outs + [jax.ShapeDtypeStruct((8, width), jnp.float32)],
+        scratch_shapes=[pltpu.VMEM((TILE, inner), jnp.float32)] * 2,
+        compiler_params=compute_params(),
+        cost_estimate=cost(4 * rows * weights, 30 * rows * width + 2 * weights),
+        name="last_rows",
+    )(resid, mixed, upstream, *fixed)
+
+
+def weight_grad_kernel(left_ref, right_ref, out_ref):
+    out_ref[...] = dot_w(left_ref[...], right_ref[...]).astype(out_ref.dtype)
+
+
+def weight_grad(left, right, tile=256):
+    rows, height = left.shape
+    width = right.shape[1]
+    return pl.pallas_call(
+        weight_grad_kernel,
+        grid=(height // tile,),
+        in_specs=[pl.BlockSpec((rows, tile), lambda i: (0, i)), whole_block(right)],
+        out_specs=row_block(tile, width),
+        out_shape=jax.ShapeDtypeStruct((height, width), jnp.bfloat16),
+        compiler_params=compute_params(),
+        cost_estimate=cost(2 * rows * height * width, 2 * (rows * (height + width) + height * width)),
+        name="weight_grad",
+    )(left, right)
+
+
+def back_heads_kernel(dq_ref, dk_ref, dv_ref, r_ref, dmid_ref, gain_ref, wq_ref, wk_ref, wv_ref, out_ref, gains_ref):
+    d_normed = dot_t(dq_ref[...], wq_ref[...]) + dot_t(dk_ref[...], wk_ref[...]) + dot_t(dv_ref[...], wv_ref[...])
+    d_resid, gain_one = pull_norm(r_ref[...], d_normed, gain_ref[0:1, :])
+    out_ref[...] = (d_resid + dmid_ref[...]).astype(jnp.bfloat16)
+
+    @pl.when(pl.program_id(0) == 0)
+    def _():
+        gains_ref[...] = jnp.zeros_like(gains_ref)
+
+    gains_ref[0:1, :] += gain_one
+
+
+def back_heads(d_query, d_key, d_value, resid, d_middle, gain_float, query_w, key_w, value_w):
+    rows, width = resid.shape
+    fixed = (gain_float, query_w, key_w, value_w)
+    return pl.pallas_call(
+        back_heads_kernel,
+        grid=(rows // TILE,),
+        in_specs=[row_block(TILE, width)] * 5 + [whole_block(a) for a in fixed],
+        out_specs=[row_block(TILE, width), pl.BlockSpec((8, width), lambda i: (0, 0))],
+        out_shape=[
+            jax.ShapeDtypeStruct((rows, width), jnp.bfloat16),
+            jax.ShapeDtypeStruct((8, width), jnp.float32),
+        ],
+        compiler_params=compute_params(),
+        cost_estimate=cost(6 * rows * width * width, 16 * rows * width + 6 * width * width),
+        name="back_heads",
+    )(d_query, d_key, d_value, resid, d_middle, *fixed)
+
+
+def home_back_kernel(
+    target_ref, d_ref, final_ref, s_ref, e_ref, w_ref, first_ref, out_ref, ds_ref, de_ref, grad_ref, sum_ref
+):
+    step = pl.program_id(0)
+    rows, width = ds_ref.shape
+    count = d_ref.shape[0]
+    at_column = lax.broadcasted_iota(jnp.int32, (rows, count), 1)
+    order = (at_column == target_ref[...]).astype(jnp.bfloat16)
+    out_ref[...] = dot_n(order, final_ref[...]).astype(jnp.bfloat16)
+    d_home = dot_n(order, d_ref[...]).astype(jnp.bfloat16)
+    ds_ref[...] = dot_t(d_home, w_ref[:width, :]).astype(jnp.bfloat16)
+    de_ref[...] = dot_t(d_home, w_ref[width:, :]).astype(jnp.bfloat16)
+    upper, lower = dot_w(s_ref[...], d_home), dot_w(e_ref[...], d_home)
+
+    @pl.when(step == 0)
+    def _():
+        sum_ref[:width, :] = upper + first_ref[...]
+        sum_ref[width:, :] = lower
+
+    @pl.when(step > 0)
+    def _():
+        sum_ref[:width, :] += upper
+        sum_ref[width:, :] += lower
+
+    @pl.when(step == pl.num_programs(0) - 1)
+    def _():
+        grad_ref[...] = sum_ref[...].astype(jnp.bfloat16)
+
+
+def back_at_home(target, d_home, final_slots, once, embeds, adapt_w, first_part):
+    count, width = d_home.shape
+    like = jax.ShapeDtypeStruct((count, width), jnp.bfloat16)
+    return pl.pallas_call(
+        home_back_kernel,
+        grid=(count // TILE,),
+        in_specs=[row_block(TILE, 1), whole_block(d_home), whole_block(final_slots)]
+        + [row_block(TILE, width)] * 2
+        + [whole_block(adapt_w), whole_block(first_part)],
+        out_specs=[row_block(TILE, width)] * 3 + [pl.BlockSpec(adapt_w.shape, lambda i: (0, 0))],
+        out_shape=[like] * 3 + [jax.ShapeDtypeStruct(adapt_w.shape, jnp.bfloat16)],
+        scratch_shapes=[pltpu.VMEM(adapt_w.shape, jnp.float32)],
+        compiler_params=compute_params(),
+        cost_estimate=cost(12 * count * width * width, 20 * count * width),
+        name="back_at_home",
+    )(target, d_home, final_slots, once, embeds, adapt_w, first_part)
 
 
 def paired_on_device(
@@ -934,120 +1280,78 @@
     )
     row_count = block_len * seqs
     target = (slot[None, :] * block_len + jnp.arange(block_len, dtype=jnp.int32)[:, None]).reshape(row_count)
-    order = (lax.broadcasted_iota(jnp.int32, (row_count, row_count), 0) == target[None, :]).astype(jnp.bfloat16)
-
-    def to_slots(values):
-        return dot_n(order, values.reshape(row_count, width)).astype(jnp.bfloat16)
-
-    def from_slots(values):
-        return dot_w(order, values.reshape(row_count, width)).astype(jnp.bfloat16)
+    latent_rows, embed_rows, slope_rows = (a.reshape(row_count, width) for a in (latents, embeds, cotangent))
 
     def exchange(values):
         return lax.all_to_all(values, BOTH, split_axis=0, concat_axis=0, tiled=True)
 
     adapt_w = gather_all([w_adapt], 0)[0].reshape(-1, width)
-    latent_slots, embed_slots = to_slots(latents), to_slots(embeds)
-    upstream = to_slots(cotangent).reshape(parts, block_len, width)
-    embed_part = dot_n(embed_slots, adapt_w[width:])
-    adapted = (dot_n(latent_slots, adapt_w[:width]) + embed_part).reshape(parts, block_len, width)
-    embed_part = embed_part.reshape(parts, block_len, width)
-    pair_at = lax.broadcasted_iota(jnp.int32, (parts, 1, 1), 0) % 2
-    starting = jnp.where(pair_at == 0, embed_part, adapted).astype(jnp.bfloat16)
-    shared = adapted.reshape(parts // 2, 2, block_len, width)[:, 0].astype(jnp.bfloat16)
+    starting, shared, upstream = adapt_at_home(
+        target.reshape(1, row_count), latent_rows, embed_rows, slope_rows, adapt_w, block_len
+    )
+
+    half = block_len // 2
+    shared = shared.reshape(parts // 2, 2, block_len, width)[:, 0].reshape(parts, half, width)
+    leaving = jnp.concatenate([starting.reshape(parts, block_len, width), shared], 1)
     gain_rows = jnp.pad(gains.reshape(1, -1), ((0, 15), (0, 0)))
-    shared, *shards = lax.optimization_barrier(
-        (shared, w_query, w_key, w_value, w_out, w_gate, w_up, w_down, gain_rows)
-    )
-    shared = lax.all_to_all(
-        shared,
-        BOTH,
-        split_axis=0,
-        concat_axis=0,
-        tiled=True,
-        axis_index_groups=[list(range(k, parts, 2)) for k in range(2)],
-    )
+    leaving, *shards = lax.optimization_barrier(
+        (leaving, w_query, w_key, w_value, w_out, w_gate, w_up, w_down, gain_rows)
+    )
+    arrived = exchange(leaving)
     *matrices, gain_float = gather_all(shards, 1)
     query_w, key_w, value_w, output_w, gate_w, up_w, down_w = (
         matrix.reshape(-1, matrix.shape[-1]) for matrix in matrices
     )
     gain_float = gain_float.reshape((parts,) + gain_rows.shape)[:, 0].reshape((parts,) + gains.shape)
     gain_float = gain_float.transpose(1, 0, 2).reshape(gains.shape[0], width).astype(jnp.float32)
-    gate_w, starting, upstream = lax.optimization_barrier((gate_w, starting, upstream))
-    starting = exchange(starting).reshape(length, width).astype(jnp.float32)
-    upstream = exchange(upstream).reshape(length, width)
-
-    def before_attention(resid, cos_full, sin_full):
-        normed = (resid * rms_scale(resid) * gain_float[0]).astype(jnp.bfloat16)
-        queries = rotate_rows(dot_n(normed, query_w), cos_full, sin_full).astype(jnp.bfloat16)
-        keys_in = rotate_rows(dot_n(normed, key_w), cos_full, sin_full).astype(jnp.bfloat16)
-        values_in = dot_n(normed, value_w).astype(jnp.bfloat16)
-        return normed, queries, keys_in, values_in
-
-    def after_attention(resid, mixed):
-        branch = dot_n(mixed, output_w)
-        middle = resid + branch * rms_scale(branch) * gain_float[1]
-        mlp_in = (middle * rms_scale(middle) * gain_float[2]).astype(jnp.bfloat16)
-        gate_pre = dot_n(mlp_in, gate_w)
-        up_pre = dot_n(mlp_in, up_w)
-        hidden = (jax.nn.silu(gate_pre) * up_pre).astype(jnp.bfloat16)
-        down_out = dot_n(hidden, down_w)
-        result = middle + down_out * rms_scale(down_out) * gain_float[3]
-        return result.astype(jnp.bfloat16), (branch, middle, mlp_in, gate_pre, up_pre, hidden, down_out)
-
-    resid = shared.reshape(length // 2, width).astype(jnp.float32)
+    gate_w, arrived, upstream = lax.optimization_barrier((gate_w, arrived, upstream))
+    starting = arrived[:, :block_len].reshape(length, width)
+    shared = arrived[:, block_len:].reshape(length // 2, width)
+    upstream = exchange(upstream.reshape(parts, block_len, width)).reshape(length, width)
+
+    resid = shared
     local = jnp.arange(length // 2, dtype=jnp.int32)
-    cos_half, sin_half = rope_full((local // block_len * 2 + core) * block_len + local % block_len)
-    normed, queries, keys_in, values_in = before_attention(resid, cos_half, sin_half)
+    cos_half, sin_half = rope_full((local // half * 2 + core) * half + local % half)
+    queries, keys_in, values_in = first_heads(resid, gain_float, query_w, key_w, value_w, cos_half, sin_half)
     far_keys, far_values = send(keys_in, 3), send(values_in, 3)
-    mixed = attend_shared(core, block_len, queries, keys_in, values_in, far_keys, far_values)
-    first_out, _ = after_attention(resid, mixed)
+    mixed = attend_shared(core, half, queries, keys_in, values_in, far_keys, far_values)
+    first_out = first_rows(resid, mixed, gain_float, output_w, gate_w, up_w, down_w)
     far_out = send(first_out, 3, -1)
     first_out = jnp.stack(
-        [first_out.reshape(-1, block_len, width), far_out.reshape(-1, block_len, width)], 1
+        [first_out.reshape(-1, half, width), far_out.reshape(-1, half, width)], 1
     ).reshape(length, width)
     first_out = jnp.where(owner, first_out, jnp.zeros_like(first_out))
 
     cos_full, sin_full = rope_full(jnp.arange(length, dtype=jnp.int32))
-    resid = starting + dot_n(first_out, adapt_w[:width])
-    normed, queries, keys_in, values_in = before_attention(resid, cos_full, sin_full)
+    resid, normed, queries, keys_in, values_in = last_heads(
+        starting, first_out, adapt_w, gain_float, query_w, key_w, value_w, cos_full, sin_full
+    )
     mixed, log_total = attend_whole(queries, keys_in, values_in)
-    result, saved = after_attention(resid, mixed)
-    branch, middle, mlp_in, gate_pre, up_pre, hidden, down_out = saved
+    result, hidden, d_down, mlp_in, d_gate, d_up, d_middle, d_branch, d_mixed, gain_rest = last_rows(
+        resid, mixed, upstream, gain_float, output_w, gate_w, up_w, down_w
+    )
     final_back = exchange(result.reshape(parts, block_len, width))
-
-    d_result = upstream.astype(jnp.float32)
-    d_down, gain_four = norm_back(down_out, d_result, gain_float[3])
-    d_down = d_down.astype(jnp.bfloat16)
-    down_part = dot_w(hidden, d_down).astype(jnp.bfloat16)
-    d_hidden = dot_t(d_down, down_w)
-    sigma = jax.nn.sigmoid(gate_pre)
-    d_gate = (d_hidden * up_pre * sigma * (1.0 + gate_pre * (1.0 - sigma))).astype(jnp.bfloat16)
-    d_up = (d_hidden * gate_pre * sigma).astype(jnp.bfloat16)
-    gate_part = dot_w(mlp_in, d_gate).astype(jnp.bfloat16)
-    up_part = dot_w(mlp_in, d_up).astype(jnp.bfloat16)
-    d_mlp = dot_t(d_gate, gate_w) + dot_t(d_up, up_w)
-    d_middle, gain_three = norm_back(middle, d_mlp, gain_float[2])
-    d_middle = d_middle + d_result
-    d_branch, gain_two = norm_back(branch, d_middle, gain_float[1])
-    d_branch = d_branch.astype(jnp.bfloat16)
-    out_part = dot_w(mixed, d_branch).astype(jnp.bfloat16)
-    d_mixed = dot_t(d_branch, output_w).astype(jnp.bfloat16)
     d_query, d_key, d_value = attend_whole_back(
         queries, keys_in, values_in, mixed, d_mixed, log_total, cos_full, sin_full
     )
-    query_part = dot_w(normed, d_query).astype(jnp.bfloat16)
-    key_part = dot_w(normed, d_key).astype(jnp.bfloat16)
-    value_part = dot_w(normed, d_value).astype(jnp.bfloat16)
-    d_normed = dot_t(d_query, query_w) + dot_t(d_key, key_w) + dot_t(d_value, value_w)
-    d_resid, gain_one = norm_back(resid, d_normed, gain_float[0])
-    d_resid = (d_resid + d_middle).astype(jnp.bfloat16)
+    d_resid, gain_one = back_heads(
+        d_query, d_key, d_value, resid, d_middle, gain_float, query_w, key_w, value_w
+    )
+    final_back, d_resid = lax.optimization_barrier((final_back, d_resid))
     d_home = exchange(d_resid.reshape(parts, block_len, width))
+    down_part = weight_grad(hidden, d_down)
+    gate_part = weight_grad(mlp_in, d_gate)
+    up_part = weight_grad(mlp_in, d_up)
+    out_part = weight_grad(mixed, d_branch)
+    query_part = weight_grad(normed, d_query)
+    key_part = weight_grad(normed, d_key)
+    value_part = weight_grad(normed, d_value)
     first_part = dot_w(first_out, d_resid)
 
     def blocks(part):
         return part.reshape(parts, -1, part.shape[-1])
 
-    gain_part = jnp.stack([gain_one, gain_two, gain_three, gain_four])
+    gain_part = jnp.concatenate([gain_one[:1], gain_rest[:3]], 0)
     gain_part = gain_part.reshape(gains.shape[0], parts, gains.shape[1]).transpose(1, 0, 2)
     gain_part = jnp.pad(
         gain_part.reshape(parts, 1, gains.size).astype(jnp.bfloat16), ((0, 0), (0, 15), (0, 0))
@@ -1064,20 +1368,21 @@
     gain_grad = gain_grad[0].reshape(gains.shape)
     d_home, gate_grad = lax.optimization_barrier((d_home, gate_grad))
 
-    d_home = from_slots(d_home)
-    latent_back = dot_t(d_home, adapt_w[:width]).astype(jnp.bfloat16).reshape(latents.shape)
-    embed_back = dot_t(d_home, adapt_w[width:]).astype(jnp.bfloat16).reshape(latents.shape)
     once = jnp.where(twice[None, :, None], jnp.zeros_like(latents), latents).reshape(row_count, width)
-    latent_part = first_part + dot_w(once, d_home)
-    embed_part = dot_w(embeds.reshape(row_count, width), d_home)
-    final_back = from_slots(final_back).reshape(latents.shape)
-
-    adapt_part = jnp.concatenate([latent_part, embed_part], 0).astype(jnp.bfloat16)
+    final_back, latent_back, embed_back, adapt_part = back_at_home(
+        target.reshape(row_count, 1),
+        d_home.reshape(row_count, width),
+        final_back.reshape(row_count, width),
+        once,
+        embed_rows,
+        adapt_w,
+        first_part,
+    )
     (adapt_grad,) = scatter_all([blocks(adapt_part)], 3)
     return (
-        final_back,
-        latent_back,
-        embed_back,
+        final_back.reshape(latents.shape),
+        latent_back.reshape(latents.shape),
+        embed_back.reshape(latents.shape),
         adapt_grad,
         query_grad,
         key_grad,

time: 855 us -> 729 us (0.85)
  matrix products: 224 us -> 5.94 us
  Pallas kernels: 462 us -> 627 us
  other arithmetic: 44.8 us -> 11.9 us
  local copies, waits for them, and re-layouts: 60.5 us -> 35.5 us
  waiting for transfers between devices: 22.7 us -> 4.74 us
    pallas_call x4 -> x18, Pallas kernels: 414 us -> 579 us  [the longest x2 195 us: gather_all(): pl.pallas_call(functools.partial(gather_kernel, views, count), in_specs=[...]
    dot_general x26 -> x0, matrix products: 158 us -> none  [the longest x17 97.3 us: dot_n(): return jnp.dot(left, right, preferred_element_type=jnp.float32)]
    dot_general x12 -> x1, matrix products: 65.8 us -> 5.94 us  [dot_w(): lax.dot_general(left, right, (((0,), (0,)), ((), ())), preferred_element_...]
    convert_element_type x11 -> x0, other arithmetic: 21.4 us -> none  [the longest x2 6.43 us: before_attention(): rotate_rows(dot_n(normed, key_w), cos_full, sin_full).astype(jnp.bfloat16)]
    all_to_all x4, waiting for transfers between devices: 22.7 us -> 4.74 us  [exchange(): return lax.all_to_all(values, BOTH, split_axis=0, concat_axis=0, tiled=True)]
    convert_element_type x5 -> x0, local copies, waits for them, and re-layouts: 13.9 us -> none  [the longest x2 6.2 us: before_attention(): rotate_rows(dot_n(normed, query_w), cos_full, sin_full).astype(jnp.bfloat16)]
    reduce_sum x5 -> x0, other arithmetic: 10.1 us -> none  [the longest x2 8.18 us: norm_back(): gain_part = jnp.sum(upstream * normal, 0)]
    all_to_all x4, starting transfers between devices: 23.3 us -> 32 us  [exchange(): return lax.all_to_all(values, BOTH, split_axis=0, concat_axis=0, tiled=True)]
  transfers between devices with their start and end apart: 8 -> 7, of which waited for: 1 -> 1; matrix products, arithmetic and copies ran while one was open for 21% -> 3% of each run, Pallas kernels for 43% -> 62%
where the time goes in v3:
time: 729 us; the launch traced here: 720 us
  Pallas kernels  627 us (86%)
  local copies, waits for them, and re-layouts  35.5 us (5%)
  starting transfers between devices  33.9 us (5%)
  other arithmetic  11.9 us (2%)
    pallas_call x2, Pallas kernels, gather_all(): pl.pallas_call(functools.partial(gather_kernel, views, count), in_specs=[...  195 us
    pallas_call x2, Pallas kernels, scatter_all(): pl.pallas_call(functools.partial(scatter_kernel, views, count), in_specs=...  159 us
    pallas_call x1, Pallas kernels, last_rows(): pl.pallas_call(last_rows_kernel, grid=(rows // TILE,), in_specs=[row_bloc...  63.6 us
    pallas_call x7, Pallas kernels, weight_grad(): pl.pallas_call(weight_grad_kernel, grid=(height // tile,), in_specs=[pl.B...  59.4 us
    all_to_all x4, starting transfers between devices, exchange(): return lax.all_to_all(values, BOTH, split_axis=0, concat_axis=0, tiled=True)  32 us
    pallas_call x1, Pallas kernels, back_at_home(): pl.pallas_call(home_back_kernel, grid=(count // TILE,), in_specs=[row_blo...  25.3 us
    unnamed x72, local copies, waits for them, and re-layouts  23.1 us
    pallas_call x1, Pallas kernels, attend_whole_back(): pl.pallas_call(whole_attend_back, grid=(width // HEAD_DIM,), in_specs=[he...  22.1 us
  transfers between devices with their start and end apart: 7, of which 1 were waited for; matrix products, arithmetic and copies ran while one was open for 3% of the time, Pallas kernels for 62%

profile of v3, /device:TPU:0, one launch (start us, length us, event | category | flops | bytes accessed | tf_op | source)
XLA Modules:
  0.0 720.0 jit_solution(15397011561614704050)
XLA Ops:
  3.1 38.2 %gather_weights.2 = bf16[4,2,2,2,64,1024]{5,4,3,2,1,0:T(8,128)(2,1)} custom-call(bf16[64,1024]{1,0:T(8,128)(2,1)} %refs_0_.1), custom_call_target="tpu_custom_call" | custom-call | tf_op jit(solution)/shard_map/gather_weights/pallas_call | solution.py:549
  41.3 19.1 %adapt_at_home.1 = (bf16[1024,1024]{1,0:T(8,128)(2,1)}, bf16[1024,1024]{1,0:T(8,128)(2,1)}, bf16[1024,1024]{1,0:T(8,128)(2,1)}) custom-call(s32[1,1024]{1,0:T(1,128)} %add.89.target_ref, bf16[1024,1024]{1,0:T(8,128)(2,1)} %bitcast.69, bf16[1024,1024]{1,0:T(8,128)(2,1)} %bitcast.93, bf16[1024,1024]{1,0:T(8,128)(2,1)} %bitcast.92, bf16[2048,1024]{1,0:T(8,128)(2,1)} %bitcast.59), custom_call_target="tpu_custom_call" | custom-call | flops 10737418240 | bytes 14680064 | tf_op jit(solution)/shard_map/adapt_at_home/pallas_call | solution.py:955
  60.4 1.5 slice.30
  62.3 2.0 pad_maximum_fusion
  64.9 4.5 all-to-all-start
  69.4 157.0 %gather_weights.3 = (bf16[4,2,2,2,32,1024]{5,4,3,2,1,0:T(8,128)(2,1)}, bf16[4,2,2,2,32,1024]{5,4,3,2,1,0:T(8,128)(2,1)}, bf16[4,2,2,2,32,1024]{5,4,3,2,1,0:T(8,1...) custom-call(bf16[32,1024]{1,0:T(8,128)(2,1)} %refs_0_.2, ...), custom_call_target="tpu_custom_call" | custom-call | tf_op jit(solution)/shard_map/gather_weights/pallas_call | solution.py:549
  230.1 1.1 slice.25
  231.2 8.1 %first_heads.1 = (bf16[512,1024]{1,0:T(8,128)(2,1)}, bf16[512,1024]{1,0:T(8,128)(2,1)}, bf16[512,1024]{1,0:T(8,128)(2,1)}) custom-call(bf16[512,1024]{1,0:T(8,128)(2,1)} %bitcast.79, f32[4,1024]{1,0:T(4,128)} %reshape.310.gain_ref, bf16[1024,1024]{1,0:T(8,128)(2,1)} %bitcast.95, bf16[1024,1024]{1,0:T(8,128)(2,1)} %bitcast.98, bf16[1024,1024]{1,0:T(8,128)(2,1)} %bitcast.101, ...), custom_call_target="tpu_custom_call" | custom-call | flops 3221225472 | bytes 10485760 | tf_op jit(solution)/shard_map/first_heads/pallas_call | solution.py:997
  239.9 16.4 %all-to-all-start.1 = ((bf16[32,32,1024]{2,1,0:T(8,128)(2,1)}), bf16[32,32,1024]{2,1,0:T(8,128)(2,1)}, u32[]{:S(2)}, u32[]{:S(2)}) async-start(bf16[32,32,1024]{2,1,0:T(8,128)(2,1)} %bitcast.70), calls=%async_computation.1 | async-start | bytes 4194304 | tf_op jit(solution)/shard_map/all_to_all | solution.py:1286
  256.3 9.7 %attend_shared.1.mixed_ref = bf16[512,1024]{1,0:T(8,128)(2,1)S(1)} custom-call(s32[1]{0:T(128)} %bitcast.12.core_ref, bf16[512,1024]{1,0:T(8,128)(2,1)S(1)} %copy-done, bf16[512,1024]{1,0:T(8,128)(2,1)S(1)} %copy-done.1, bf16[512,1024]{1,0:T(8,128)(2,1)S(1)} %copy-done.2, bf16[512,1024]{1,0:T(8,128)(2,1)} %collective-permute-done.ok_ref, ...), custom_call_target="tpu_custom_call" | custom-call | flops 1073741824 | bytes 6291456 | tf_op jit(solution)/shard_map/attend_shared/pallas_call | solution.py:833
  266.9 19.5 %first_rows.1 = bf16[512,1024]{1,0:T(8,128)(2,1)} custom-call(bf16[512,1024]{1,0:T(8,128)(2,1)} %bitcast.80, bf16[512,1024]{1,0:T(8,128)(2,1)} %copy-done.3, f32[4,1024]{1,0:T(4,128)} %reshape.310.gain_ref, bf16[1024,1024]{1,0:T(8,128)(2,1)} %bitcast.104, bf16[1024,2816]{1,0:T(8,128)(2,1)} %bitcast.86, bf16[1024,2816]{1,0:T(8,128)(2,1)} %bitcast.88, ...), custom_call_target="tpu_custom_call" | custom-call | flops 9932111872 | bytes 22544384 | tf_op jit(solution)/shard_map/first_rows/pallas_call | solution.py:1071
  286.5 1.3 collective-permute-start.2
  287.8 1.9 fusion
  289.7 1.4 pad_maximum_fusion.1
  291.1 1.5 slice.24
  292.6 1.6 maximum_select_fusion
  294.2 15.5 %last_heads.1 = (f32[1024,1024]{1,0:T(8,128)}, bf16[1024,1024]{1,0:T(8,128)(2,1)}, bf16[1024,1024]{1,0:T(8,128)(2,1)}, bf16[1024,1024]{1,0:T(8,128)(2,1)}, bf16[1024,1024]{1,0:T(8,128)(2,1)}) custom-call(bf16[1024,1024]{1,0:T(8,128)(2,1)} %bitcast.76, bf16[1024,1024]{1,0:T(8,128)(2,1)} %bitcast.71, bf16[2048,1024]{1,0:T(8,128)(2,1)} %bitcast.60, ...), custom_call_target="tpu_custom_call" | custom-call | flops 8589934592 | bytes 25165824 | tf_op jit(solution)/shard_map/last_heads/pallas_call | solution.py:1022
  309.6 1.6 copy-done.10
  311.2 1.6 copy-done.12
  312.8 1.6 copy-done.14
  314.4 15.7 %attend_whole.1 = (bf16[1024,1024]{1,0:T(8,128)(2,1)S(1)}, f32[1024,128]{1,0:T(8,128)S(1)}) custom-call(bf16[1024,1024]{1,0:T(8,128)(2,1)S(1)} %copy-done.10, bf16[1024,1024]{1,0:T(8,128)(2,1)S(1)} %copy-done.12, bf16[1024,1024]{1,0:T(8,128)(2,1)S(1)} %copy-done.14), custom_call_target="tpu_custom_call" | custom-call | flops 2147483648 | bytes 8388608 | tf_op jit(solution)/shard_map/attend_whole/pallas_call | solution.py:788
  330.2 1.3 copy-done.6
  332.3 63.6 %last_rows.1 = (bf16[1024,1024]{1,0:T(8,128)(2,1)}, bf16[1024,2816]{1,0:T(8,128)(2,1)}, bf16[1024,1024]{1,0:T(8,128)(2,1)}, bf16[1024,1024]{1,0:T(8,128)(2,1)}, ...) custom-call(f32[1024,1024]{1,0:T(8,128)} %get-tuple-element.101.r_re, ...), custom_call_target="tpu_custom_call" | custom-call | flops 39728447488 | bytes 50855936 | tf_op jit(solution)/shard_map/last_rows/pallas_call | solution.py:1156
  396.0 7.1 all-to-all-start.2
  403.1 1.6 copy-done.13
  404.7 1.6 copy-done.15
  406.3 1.0 copy-done.17
  407.3 22.1 %attend_whole_back.1 = (bf16[1024,1024]{1,0:T(8,128)(2,1)S(1)}, bf16[1024,1024]{1,0:T(8,128)(2,1)S(1)}, bf16[1024,1024]{1,0:T(8,128)(2,1)S(1)}) custom-call(bf16[1024,1024]{1,0:T(8,128)(2,1)S(1)} %copy-done.11, bf16[1024,1024]{1,0:T(8,128)(2,1)S(1)} %copy-done.13, bf16[1024,1024]{1,0:T(8,128)(2,1)S(1)} %copy-done.15, bf16[1024,1024]{1,0:T(8,128)(2,1)} %copy-done.6, ...), custom_call_target="tpu_custom_call" | custom-call | flops 5368709120 | bytes 16777216 | tf_op jit(solution)/shard_map/attend_whole_back/pallas_call | solution.py:889
  429.4 1.3 copy-done.7
  430.7 1.4 copy-done.8
  432.1 1.3 copy-done.9
  433.4 13.8 %back_heads.1 = (bf16[1024,1024]{1,0:T(8,128)(2,1)}, f32[8,1024]{1,0:T(8,128)}) custom-call(bf16[1024,1024]{1,0:T(8,128)(2,1)} %copy-done.7, bf16[1024,1024]{1,0:T(8,128)(2,1)} %copy-done.8, bf16[1024,1024]{1,0:T(8,128)(2,1)} %copy-done.9, f32[1024,1024]{1,0:T(8,128)} %get-tuple-element.101.r_ref, f32[1024,1024]{1,0:T(8,128)} %get-tuple-element.113.dmid_ref, ...), custom_call_target="tpu_custom_call" | custom-call | flops 6442450944 | bytes 23068672 | tf_op jit(solution)/shard_map/back_heads/pallas_call | solution.py:1204
  447.2 4.7 all-to-all-done.2
  451.9 4.1 all-to-all-start.3
  456.1 1.4 add.95.target_ref
  457.5 1.5 broadcast_select_fusion
  461.4 6.1 weight_grad.9
  467.5 6.1 weight_grad.8
  473.6 6.1 weight_grad.7
  479.7 6.1 weight_grad.10
  485.8 10.8 %weight_grad.12 = bf16[1024,2816]{1,0:T(8,128)(2,1)} custom-call(bf16[1024,1024]{1,0:T(8,128)(2,1)} %get-tuple-element.118.left_ref, bf16[1024,2816]{1,0:T(8,128)(2,1)} %get-tuple-element.120.right_ref), custom_call_target="tpu_custom_call" | custom-call | flops 5905580032 | bytes 13631488 | tf_op jit(solution)/shard_map/weight_grad/pallas_call | solution.py:1177
  496.7 10.8 %weight_grad.11 = bf16[1024,2816]{1,0:T(8,128)(2,1)} custom-call(bf16[1024,1024]{1,0:T(8,128)(2,1)} %get-tuple-element.118.left_ref, bf16[1024,2816]{1,0:T(8,128)(2,1)} %get-tuple-element.119.right_ref), custom_call_target="tpu_custom_call" | custom-call | flops 5905580032 | bytes 13631488 | tf_op jit(solution)/shard_map/weight_grad/pallas_call | solution.py:1177
  507.5 13.3 %weight_grad.13 = bf16[2816,1024]{1,0:T(8,128)(2,1)} custom-call(bf16[1024,2816]{1,0:T(8,128)(2,1)} %get-tuple-element.121.left_ref, bf16[1024,1024]{1,0:T(8,128)(2,1)} %get-tuple-element.122.right_ref), custom_call_target="tpu_custom_call" | custom-call | flops 5905580032 | bytes 13631488 | tf_op jit(solution)/shard_map/weight_grad/pallas_call | solution.py:1177
  520.8 130.5 %scatter_sums.2 = (f32[32,1024]{1,0:T(8,128)}, f32[32,1024]{1,0:T(8,128)}, f32[32,1024]{1,0:T(8,128)}, f32[32,1024]{1,0:T(8,128)}, f32[32,2816]{1,0:T(8,128)}, /...) custom-call(bf16[4,2,2,2,32,1024]{5,4,3,2,1,0:T(8,128)(2,1)} %bitcast.66, ...), custom_call_target="tpu_custom_call" | custom-call | tf_op jit(solution)/shard_map/scatter_sums/pallas_call | solution.py:722
  652.6 5.9 fusion.15.first_ref
  658.6 25.3 %back_at_home.1 = (bf16[1024,1024]{1,0:T(8,128)(2,1)}, bf16[1024,1024]{1,0:T(8,128)(2,1)}, bf16[1024,1024]{1,0:T(8,128)(2,1)}, bf16[2048,1024]{1,0:T(8,128)(2,1)}) custom-call(s32[1024,1]{1,0:T(8,128)} %add.95.target_ref, bf16[1024,1024]{1,0:T(8,128)(2,1)} %bitcast.39.d_ref, bf16[1024,1024]{1,0:T(8,128)(2,1)} %bitcast.40.final_ref, ...), custom_call_target="tpu_custom_call" | custom-call | flops 12884901888 | bytes 20971520 | tf_op jit(solution)/shard_map/back_at_home/pallas_call | solution.py:1251
  684.0 29.0 %scatter_sums.3 = f32[64,1024]{1,0:T(8,128)} custom-call(bf16[4,2,2,2,64,1024]{5,4,3,2,1,0:T(8,128)(2,1)} %bitcast.62), custom_call_target="tpu_custom_call" | custom-call | tf_op jit(solution)/shard_map/scatter_sums/pallas_call | solution.py:722
  713.0 1.7 copy.52
  (99 shorter events, 18.2 us)
Async XLA Ops:
  60.3 1.5 copy-start.31
  60.3 1.9 copy-start.20
  64.9 165.1 %all-to-all-start = ((bf16[32,48,1024]{2,1,0:T(8,128)(2,1)}), bf16[32,48,1024]{2,1,0:T(8,128)(2,1)S(1)}, u32[]{:S(2)}, u32[]{:S(2)}) async-start(bf16[32,48,1024]{2,1,0:T(8,128)(2,1)} %pad_maximum_fusion), calls=%async_computation | async-start | bytes 6291456 | tf_op jit(solution)/shard_map/all_to_all | solution.py:1286
  230.0 9.2 %copy-start.18 = (bf16[32,48,1024]{2,1,0:T(8,128)(2,1)}, bf16[32,48,1024]{2,1,0:T(8,128)(2,1)S(1)}, u32[]{:S(2)}) copy-start(bf16[32,48,1024]{2,1,0:T(8,128)(2,1)S(1)} %all-to-all-done) | copy-start | bytes 9437188
  239.3 17.0 %collective-permute-start = (bf16[512,1024]{1,0:T(8,128)(2,1)}, bf16[512,1024]{1,0:T(8,128)(2,1)}, u32[]{:S(2)}, u32[]{:S(2)}) collective-permute-start(bf16[512,1024]{1,0:T(8,128)(2,1)} %get-tuple-element.95.k_ref), channel_id=1, source_target_pairs={{0,1},{1,0},{2,3},{3,2},{4,5},{5,4},{6,7},{7,6},{8,9},{9,8},{10,11... | collective-permute-start | bytes 3145736 | tf_op jit(solution)/shard_map/ppermute | solution.py:387
  239.7 16.5 %collective-permute-start.1 = (bf16[512,1024]{1,0:T(8,128)(2,1)}, bf16[512,1024]{1,0:T(8,128)(2,1)}, u32[]{:S(2)}, u32[]{:S(2)}) collective-permute-start(bf16[512,1024]{1,0:T(8,128)(2,1)} %get-tuple-element.96.v_ref), channel_id=1, source_target_pairs={{0,1},{1,0},{2,3},{3,2},{4,5},{5,4},{6,7},{7,6},{8,9},{9,8},{10,11... | collective-permute-start | bytes 3145736 | tf_op jit(solution)/shard_map/ppermute | solution.py:387
  239.9 16.4 %copy-start = (bf16[512,1024]{1,0:T(8,128)(2,1)S(1)}, bf16[512,1024]{1,0:T(8,128)(2,1)}, u32[]{:S(2)}) copy-start(bf16[512,1024]{1,0:T(8,128)(2,1)} %get-tuple-element.94.q_ref) | copy-start | bytes 3145732
  239.9 16.4 %copy-start.1 = (bf16[512,1024]{1,0:T(8,128)(2,1)S(1)}, bf16[512,1024]{1,0:T(8,128)(2,1)}, u32[]{:S(2)}) copy-start(bf16[512,1024]{1,0:T(8,128)(2,1)} %get-tuple-element.95.k_ref) | copy-start | bytes 3145732
  239.9 16.4 %copy-start.2 = (bf16[512,1024]{1,0:T(8,128)(2,1)S(1)}, bf16[512,1024]{1,0:T(8,128)(2,1)}, u32[]{:S(2)}) copy-start(bf16[512,1024]{1,0:T(8,128)(2,1)} %get-tuple-element.96.v_ref) | copy-start | bytes 3145732
  239.9 92.4 %all-to-all-start.1 = ((bf16[32,32,1024]{2,1,0:T(8,128)(2,1)}), bf16[32,32,1024]{2,1,0:T(8,128)(2,1)}, u32[]{:S(2)}, u32[]{:S(2)}) async-start(bf16[32,32,1024]{2,1,0:T(8,128)(2,1)} %bitcast.70), calls=%async_computation.1 | async-start | bytes 4194304 | tf_op jit(solution)/shard_map/all_to_all | solution.py:1286
  266.0 1.0 copy-start.3
  286.5 6.1 collective-permute-start.2
  287.8 3.3 copy-start.19
  291.1 1.5 copy-start.23
  309.6 1.6 copy-start.10
  311.2 1.6 copy-start.12
  312.8 1.6 copy-start.14
  330.1 1.3 copy-start.6
  331.5 0.8 copy-start.16
  396.0 7.1 copy-start.4
  396.0 7.1 copy-start.5
  396.0 7.1 copy-start.11
  396.0 56.0 %all-to-all-start.2 = ((bf16[32,32,1024]{2,1,0:T(8,128)(2,1)}), bf16[32,32,1024]{2,1,0:T(8,128)(2,1)}, u32[]{:S(2)}, u32[]{:S(2)}) async-start(bf16[32,32,1024]{2,1,0:T(8,128)(2,1)} %bitcast.75), calls=%async_computation.2 | async-start | bytes 4194304 | tf_op jit(solution)/shard_map/all_to_all | solution.py:1286
  403.1 1.6 copy-start.13
  404.7 1.6 copy-start.15
  406.3 1.0 copy-start.17
  429.4 1.3 copy-start.7
  430.7 1.4 copy-start.8
  432.1 1.3 copy-start.9
  451.9 5.5 copy-start.21
  451.9 206.6 %all-to-all-start.3 = ((bf16[32,32,1024]{2,1,0:T(8,128)(2,1)}), bf16[32,32,1024]{2,1,0:T(8,128)(2,1)}, u32[]{:S(2)}, u32[]{:S(2)}) async-start(bf16[32,32,1024]{2,1,0:T(8,128)(2,1)} %bitcast.73), calls=%async_computation.3 | async-start | bytes 4194304 | tf_op jit(solution)/shard_map/all_to_all | solution.py:1286
  520.8 131.9 %copy-start.22 = (bf16[32,2,16,1024]{3,2,1,0:T(8,128)(2,1)S(1)}, bf16[32,2,16,1024]{3,2,1,0:T(8,128)(2,1)}, u32[]{:S(2)}) copy-start(bf16[32,2,16,1024]{3,2,1,0:T(8,128)(2,1)} %maximum_select_fusion) | copy-start | bytes 6291460
  683.9 30.8 %copy-start.30 = (f32[32,1024]{1,0:T(8,128)S(1)}, f32[32,1024]{1,0:T(8,128)}, u32[]{:S(2)}) copy-start(f32[32,1024]{1,0:T(8,128)} %get-tuple-element.171) | copy-start | bytes 393220
  683.9 31.5 %copy-start.29 = (f32[32,1024]{1,0:T(8,128)S(1)}, f32[32,1024]{1,0:T(8,128)}, u32[]{:S(2)}) copy-start(f32[32,1024]{1,0:T(8,128)} %get-tuple-element.172) | copy-start | bytes 393220
  683.9 32.1 %copy-start.28 = (f32[32,1024]{1,0:T(8,128)S(1)}, f32[32,1024]{1,0:T(8,128)}, u32[]{:S(2)}) copy-start(f32[32,1024]{1,0:T(8,128)} %get-tuple-element.173) | copy-start | bytes 393220
  684.0 32.8 %copy-start.27 = (f32[32,1024]{1,0:T(8,128)S(1)}, f32[32,1024]{1,0:T(8,128)}, u32[]{:S(2)}) copy-start(f32[32,1024]{1,0:T(8,128)} %get-tuple-element.174) | copy-start | bytes 393220
  684.0 33.4 %copy-start.26 = (f32[32,2816]{1,0:T(8,128)S(1)}, f32[32,2816]{1,0:T(8,128)}, u32[]{:S(2)}) copy-start(f32[32,2816]{1,0:T(8,128)} %get-tuple-element.175) | copy-start | bytes 1081348
  713.0 5.1 copy-start.25
  713.0 5.9 copy-start.24

commit v4 on v3

--- a/solution.py
+++ b/solution.py
@@ -452,106 +452,273 @@
         body(z + step, False, True)
 
 
-def gather_kernel(views, count, *refs):
-    z_size, _, _, _ = grid_sizes()
-    z, y, x, k = grid_place()
-    shards, outs = refs[:count], refs[count : 2 * count]
-    local_sem, z_send, z_recv, p_send, p_recv, k_send, k_recv = refs[2 * count :]
-    greet_line(z, y, x, k, z_size)
-    everyone = range(len(views))
-
-    def spot(g, slot_z, at_y, at_x):
-        at, first_row, rows, _ = views[g]
-        return outs[at].at[slot_z, at_y, at_x, k, pl.ds(first_row, rows)]
-
-    def z_copy(g, slot_z, way):
-        block = spot(g, slot_z, y, x)
-        side = z + 1 - 2 * way
-        return remote(block, block, z_send.at[g, slot_z, way], z_recv.at[g, slot_z], device_at(side, y, x, k))
-
-    def plane_copy(g, slot_z, kind):
-        first, second = order_of(y, x, (views[g][3] + slot_z) % 2)
+def flat_device(at, ctx):
+    return (at // ctx, at % ctx)
+
+
+class Gather:
+    def __init__(self, views, count, shards, outs, sems):
+        self.z_size = grid_sizes()[0]
+        self.place = grid_place()
+        self.views, self.count, self.shards, self.outs = views, count, shards, outs
+        self.local_sem, self.z_send, self.z_recv, self.p_send, self.p_recv, self.k_send, self.k_recv = sems
+
+    def at(self, step, body):
+        at_offsets(self.place[0], self.z_size, step, body)
+
+    def spot(self, g, slot_z, at_y, at_x):
+        at, first_row, rows, _ = self.views[g]
+        return self.outs[at].at[slot_z, at_y, at_x, self.place[3], pl.ds(first_row, rows)]
+
+    def z_copy(self, g, slot_z, way):
+        z, y, x, k = self.place
+        block = self.spot(g, slot_z, y, x)
+        device = device_at(z + 1 - 2 * way, y, x, k)
+        return remote(block, block, self.z_send.at[g, slot_z, way], self.z_recv.at[g, slot_z], device)
+
+    def plane_copy(self, g, slot_z, kind):
+        z, y, x, k = self.place
+        first, second = order_of(y, x, (self.views[g][3] + slot_z) % 2)
         from_at = first if kind == 2 else (y, x)
         to_at = first if kind == 0 else second
-        block = spot(g, slot_z, from_at[0], from_at[1])
+        block = self.spot(g, slot_z, from_at[0], from_at[1])
         device = device_at(z, to_at[0], to_at[1], k)
-        return remote(block, block, p_send.at[g, slot_z, kind], p_recv.at[g, slot_z, kind], device)
-
-    def core_copy(at, slot_z):
-        block = outs[at].at[slot_z, :, :, k]
-        return remote(block, block, k_send.at[at, slot_z], k_recv.at[at, slot_z], device_at(z, y, x, 1 - k))
-
-    def each_way(g, slot_z, up, down, act):
+        return remote(block, block, self.p_send.at[g, slot_z, kind], self.p_recv.at[g, slot_z, kind], device)
+
+    def core_copy(self, at, slot_z):
+        z, y, x, k = self.place
+        block = self.outs[at].at[slot_z, :, :, k]
+        return remote(block, block, self.k_send.at[at, slot_z], self.k_recv.at[at, slot_z], device_at(z, y, x, 1 - k))
+
+    def own_copy(self, at):
+        z, y, x, k = self.place
+        return pltpu.make_async_copy(self.shards[at], self.outs[at].at[z, y, x, k], self.local_sem.at[at])
+
+    def each_way(self, g, slot_z, up, down, act):
+        z = self.place[0]
         if up:
 
-            @pl.when(z < z_size - 1)
+            @pl.when(z < self.z_size - 1)
             def _():
-                act(z_copy(g, slot_z, 0))
+                act(self.z_copy(g, slot_z, 0))
 
         if down:
 
             @pl.when(z > 0)
             def _():
-                act(z_copy(g, slot_z, 1))
-
-    own = [pltpu.make_async_copy(shards[at], outs[at].at[z, y, x, k], local_sem.at[at]) for at in range(count)]
-    for copy in own:
-        copy.start()
-    for copy in own:
-        copy.wait()
-
-    def arrive(slot_z, up, down):
-        for g in everyone:
-            if not (up and down):
-                z_copy(g, slot_z, 1 if up else 0).wait_recv()
-            each_way(g, slot_z, up, down, lambda copy: copy.start())
-            plane_copy(g, slot_z, 0).start()
-            plane_copy(g, slot_z, 1).start()
-
-    def pass_on(slot_z, up, down):
-        for g in everyone:
-            plane_copy(g, slot_z, 0).wait_recv()
-            plane_copy(g, slot_z, 2).start()
-
-    def cross(slot_z, up, down):
-        for g in everyone:
-            plane_copy(g, slot_z, 1).wait_recv()
-            plane_copy(g, slot_z, 2).wait_recv()
-        for at in range(count):
-            core_copy(at, slot_z).start()
-
-    def settle(slot_z, up, down):
-        for g in everyone:
-            each_way(g, slot_z, up, down, lambda copy: copy.wait_send())
-            for kind in range(3):
-                plane_copy(g, slot_z, kind).wait_send()
-
-    for step in range(z_size + 1):
-        if step < z_size:
-            at_offsets(z, z_size, step, arrive)
-            at_offsets(z, z_size, step, pass_on)
+                act(self.z_copy(g, slot_z, 1))
+
+    def series(self, arrays):
+        return [g for g, view in enumerate(self.views) if view[0] in arrays]
+
+    def arrive(self, arrays, step):
+        def body(slot_z, up, down):
+            for g in self.series(arrays):
+                if step > 0:
+                    self.z_copy(g, slot_z, 1 if up else 0).wait_recv()
+                self.each_way(g, slot_z, up, down, lambda copy: copy.start())
+
+        self.at(step, body)
+
+    def spread(self, arrays, step):
+        def body(slot_z, up, down):
+            for g in self.series(arrays):
+                self.plane_copy(g, slot_z, 0).start()
+                self.plane_copy(g, slot_z, 1).start()
+
+        self.at(step, body)
+
+    def pass_on(self, arrays, step):
+        def body(slot_z, up, down):
+            for g in self.series(arrays):
+                self.plane_copy(g, slot_z, 0).wait_recv()
+                self.plane_copy(g, slot_z, 2).start()
+
+        self.at(step, body)
+
+    def cross(self, arrays, step):
+        def body(slot_z, up, down):
+            for g in self.series(arrays):
+                self.plane_copy(g, slot_z, 1).wait_recv()
+                self.plane_copy(g, slot_z, 2).wait_recv()
+            for at in arrays:
+                self.core_copy(at, slot_z).start()
+
+        self.at(step, body)
+
+    def complete(self, arrays):
+        for slot_z in range(self.z_size):
+            for at in arrays:
+                self.core_copy(at, slot_z).wait_recv()
+
+    def settle(self, arrays):
+        def body(slot_z, up, down):
+            for g in self.series(arrays):
+                self.each_way(g, slot_z, up, down, lambda copy: copy.wait_send())
+                for kind in range(3):
+                    self.plane_copy(g, slot_z, kind).wait_send()
+
+        for step in range(self.z_size):
+            self.at(step, body)
+        for slot_z in range(self.z_size):
+            for at in arrays:
+                self.core_copy(at, slot_z).wait_send()
+
+
+def open_kernel(views, count, block_len, *refs):
+    z_size, _, x_size, k_size = grid_sizes()
+    z, y, x, k = grid_place()
+    ctx = x_size * k_size
+    parts = lax.axis_size("grp") * ctx
+    me = lax.axis_index("grp") * ctx + lax.axis_index("ctx")
+    target_ref, s_ref, e_ref, c_ref = refs[:4]
+    shards, refs = refs[4 : 4 + count], refs[4 + count :]
+    outs, refs = refs[:count], refs[count:]
+    shared_out, start_ref, up_ref, joined, shared_held = refs[:5]
+    gather = Gather(views, count, shards, outs, refs[5:12])
+    send_sem, recv_sem, own_sem = refs[12:]
+    width = s_ref.shape[1]
+    count_rows = s_ref.shape[0]
+    half = block_len // 2
+    tiles = count_rows // TILE
+    slots = TILE // block_len
+    adapt, early, late = (0,), (1, 2, 3, 4, 8), (5, 6, 7)
+
+    barrier = pltpu.get_barrier_semaphore()
+
+    def greet(at, carry):
+        @pl.when(at != me)
+        def _():
+            pl.semaphore_signal(barrier, inc=1, device_id=flat_device(at, ctx), device_id_type=MESH)
+
+        return carry
+
+    lax.fori_loop(0, parts, greet, 0)
+    pl.semaphore_wait(barrier, parts - 1)
+
+    def half_copy(at):
+        device = flat_device(at, ctx)
+        return remote(shared_held.at[at], shared_out.at[me], send_sem.at[at], recv_sem.at[me], device)
+
+    own_half = pltpu.make_async_copy(shared_held.at[me], shared_out.at[me], own_sem)
+
+    def reorder(tile):
+        rows = pl.ds(pl.multiple_of(tile * TILE, TILE), TILE)
+        at_row = lax.broadcasted_iota(jnp.int32, (TILE, count_rows), 0) + tile * TILE
+        order = (at_row == target_ref[...]).astype(jnp.bfloat16)
+        joined[rows, :width] = dot_n(order, s_ref[...]).astype(jnp.bfloat16)
+        joined[rows, width:] = dot_n(order, e_ref[...]).astype(jnp.bfloat16)
+        up_ref[rows, :] = dot_n(order, c_ref[...]).astype(jnp.bfloat16)
+
+    def apply(tile):
+        rows = pl.ds(pl.multiple_of(tile * TILE, TILE), TILE)
+        weight = outs[0][...].reshape(2 * width, width)
+        embed_part = dot_n(joined[rows, width:], weight[width:]).astype(jnp.bfloat16)
+        adapted = dot_n(joined[rows, :], weight).astype(jnp.bfloat16)
+        for pair in range(slots // 2):
+            at = tile * slots + 2 * pair
+            even = slice(2 * pair * block_len, (2 * pair + 1) * block_len)
+            odd = slice((2 * pair + 1) * block_len, (2 * pair + 2) * block_len)
+            start_ref[at] = embed_part[even]
+            start_ref[at + 1] = adapted[odd]
+            shared_held[at] = adapted[even][:half]
+            shared_held[at + 1] = adapted[even][half:]
+
+        def leave(at, carry):
+            @pl.when(at != me)
+            def _():
+                half_copy(at).start()
+
+            return carry
+
+        lax.fori_loop(tile * slots, (tile + 1) * slots, leave, 0)
+
+    for at in range(count):
+        gather.own_copy(at).start()
+    gather.own_copy(0).wait()
+    for step in range(z_size):
+        gather.arrive(adapt, step)
+        gather.spread(adapt, step)
+        if step == 0:
+            for at in early + late:
+                gather.own_copy(at).wait()
+        gather.arrive(early, step)
+        if step < tiles:
+            reorder(step)
+        gather.spread(early, step)
+        gather.pass_on(adapt, step)
         if step > 0:
-            at_offsets(z, z_size, step - 1, cross)
+            gather.cross(adapt, step - 1)
+            gather.pass_on(early, step - 1)
+        if step == z_size - 2:
+            gather.arrive(late, 0)
+    gather.spread(late, 0)
+    gather.cross(adapt, z_size - 1)
+    for tile in range(z_size, tiles):
+        reorder(tile)
+    gather.arrive(late, 1)
+    gather.pass_on(early, z_size - 1)
+    gather.spread(late, 1)
+    gather.complete(adapt)
+    for tile in range(tiles):
+        apply(tile)
+        if tile == 0:
+            gather.pass_on(late, 0)
+        if tile == 1:
+            gather.arrive(late, 2)
+            gather.spread(late, 2)
+        if tile == 2:
+            gather.pass_on(late, 1)
+    own_half.start()
+    gather.arrive(late, 3)
+    gather.spread(late, 3)
     for step in range(z_size):
-        at_offsets(z, z_size, step, settle)
-    for slot_z in range(z_size):
-        for at in range(count):
-            core_copy(at, slot_z).wait()
-
-
-def gather_all(shards, collective_id):
+        gather.cross(early, step)
+    gather.cross(late, 0)
+    gather.pass_on(late, 2)
+    gather.cross(late, 1)
+    gather.pass_on(late, 3)
+    gather.cross(late, 2)
+    gather.cross(late, 3)
+    gather.complete(early + late)
+    gather.settle(adapt + early + late)
+
+    def finish(at, carry):
+        @pl.when(at != me)
+        def _():
+            device = flat_device(at, ctx)
+            remote(shared_held.at[at], shared_out.at[at], send_sem.at[at], recv_sem.at[at], device).wait()
+
+        return carry
+
+    lax.fori_loop(0, parts, finish, 0)
+    own_half.wait()
+
+
+def open_all(target, latents, embeds, cotangent, shards, block_len, collective_id):
     sizes = grid_sizes()
+    parts = lax.axis_size("grp") * lax.axis_size("ctx")
     count, z_size = len(shards), sizes[0]
+    rows, width = latents.shape
     views = row_views([shard.shape for shard in shards])
     series = len(views)
     anywhere = pl.BlockSpec(memory_space=pl.ANY)
+    near = pl.BlockSpec(memory_space=pltpu.VMEM)
     dma = pltpu.SemaphoreType.DMA
+    half = block_len // 2
     return pl.pallas_call(
-        functools.partial(gather_kernel, views, count),
-        in_specs=[anywhere] * count,
-        out_specs=[anywhere] * count,
-        out_shape=[jax.ShapeDtypeStruct(sizes + shard.shape, shard.dtype) for shard in shards],
+        functools.partial(open_kernel, views, count, block_len),
+        in_specs=[near] * 4 + [anywhere] * count,
+        out_specs=[near] + [anywhere] * count + [near] * 2,
+        out_shape=[jax.ShapeDtypeStruct(sizes + shard.shape, shard.dtype) for shard in shards]
+        + [
+            jax.ShapeDtypeStruct((parts, half, width), jnp.bfloat16),
+            jax.ShapeDtypeStruct((parts, block_len, width), jnp.bfloat16),
+            jax.ShapeDtypeStruct((rows, width), jnp.bfloat16),
+        ],
         scratch_shapes=[
+            pltpu.VMEM((rows, 2 * width), jnp.bfloat16),
+            pltpu.VMEM((parts, half, width), jnp.bfloat16),
             dma((count,)),
             dma((series, z_size, 2)),
             dma((series, z_size)),
@@ -559,190 +726,214 @@
             dma((series, z_size, 3)),
             dma((count, z_size)),
             dma((count, z_size)),
-        ],
-        compiler_params=pltpu.CompilerParams(collective_id=collective_id, has_side_effects=True),
-        name="gather_weights",
-    )(*shards)
-
-
-def scatter_kernel(views, count, *refs):
-    z_size, _, _, _ = grid_sizes()
-    z, y, x, k = grid_place()
-    parts, outs = refs[:count], refs[count : 2 * count]
-    held, from_core = refs[2 * count : 3 * count], refs[3 * count : 4 * count]
-    from_second, from_first = refs[4 * count : 5 * count], refs[5 * count : 6 * count]
-    from_z = refs[6 * count : 7 * count]
-    local_sem, k_send, k_recv, p_send, p_recv, z_send, z_recv = refs[7 * count :]
-    greet_line(z, y, x, k, z_size)
-    everyone = range(len(views))
-
-    def rows_of(g):
-        return pl.ds(views[g][1], views[g][2])
-
-    def core_copy(at, slot_z):
-        return remote(
-            parts[at].at[slot_z, :, :, 1 - k],
-            from_core[at].at[slot_z],
-            k_send.at[at, slot_z],
-            k_recv.at[at, slot_z],
-            device_at(z, y, x, 1 - k),
-        )
-
-    def own_copy(at, slot_z):
-        return pltpu.make_async_copy(parts[at].at[slot_z, :, :, k], held[at].at[slot_z], local_sem.at[at, slot_z])
-
-    def turns(g, slot_z):
-        return order_of(y, x, (views[g][3] + slot_z) % 2)
-
-    def second_copy(g, slot_z, kind):
-        at, (_, second) = views[g][0], turns(g, slot_z)
-        block = second if kind == 0 else (1 - y, 1 - x)
-        return remote(
-            held[at].at[slot_z, block[0], block[1], rows_of(g)],
-            from_second[at].at[slot_z, kind, rows_of(g)],
-            p_send.at[g, slot_z, kind],
-            p_recv.at[g, slot_z, kind],
-            device_at(z, second[0], second[1], k),
-        )
-
-    def first_copy(g, slot_z):
-        at, (first, _) = views[g][0], turns(g, slot_z)
-        return remote(
-            held[at].at[slot_z, first[0], first[1], rows_of(g)],
-            from_first[at].at[slot_z, rows_of(g)],
-            p_send.at[g, slot_z, 2],
-            p_recv.at[g, slot_z, 2],
-            device_at(z, first[0], first[1], k),
-        )
-
-    def z_copy(at, slot_z, way, here=None):
-        side = z + 1 - 2 * way if here is None else here
-        return remote(
-            held[at].at[slot_z, y, x],
-            from_z[at].at[slot_z, way],
-            z_send.at[at, slot_z, way],
-            z_recv.at[at, slot_z, way],
-            device_at(side, y, x, k),
-        )
-
-    def add(ref, at, other, other_at):
-        ref[at] = ref[at] + other[other_at]
-
-    def begin(slot_z, below, above):
-        for at in range(count):
-            core_copy(at, slot_z).start()
-            own_copy(at, slot_z).start()
-
-    def fold_core(slot_z, below, above):
-        for at in range(count):
-            own_copy(at, slot_z).wait()
-            core_copy(at, slot_z).wait_recv()
-        for g in everyone:
-            at, rows = views[g][0], rows_of(g)
-            first, second = turns(g, slot_z)
-            for spot in (second, (1 - y, 1 - x)):
-                add(held[at], (slot_z, spot[0], spot[1], rows), from_core[at], (slot_z, spot[0], spot[1], rows))
-            second_copy(g, slot_z, 0).start()
-            second_copy(g, slot_z, 1).start()
-            for spot in (first, (y, x)):
-                add(held[at], (slot_z, spot[0], spot[1], rows), from_core[at], (slot_z, spot[0], spot[1], rows))
-
-    def fold_second(slot_z, below, above):
-        for g in everyone:
-            at, rows = views[g][0], rows_of(g)
-            first, _ = turns(g, slot_z)
-            second_copy(g, slot_z, 1).wait_recv()
-            add(held[at], (slot_z, first[0], first[1], rows), from_second[at], (slot_z, 1, rows))
-            first_copy(g, slot_z).start()
-
-    def fold_first(slot_z, below, above):
-        for g in everyone:
-            at, rows = views[g][0], rows_of(g)
-            second_copy(g, slot_z, 0).wait_recv()
-            add(held[at], (slot_z, y, x, rows), from_second[at], (slot_z, 0, rows))
-            first_copy(g, slot_z).wait_recv()
-            add(held[at], (slot_z, y, x, rows), from_first[at], (slot_z, rows))
-        if below and above:
-            for at in range(count):
-                outs[at][...] = held[at][slot_z, y, x].astype(jnp.float32)
-        for way, use in ((0, above), (1, below)):
-            if not use:
-                continue
-            came, source = (z > 0, z - 1) if way == 0 else (z < z_size - 1, z + 1)
-
-            @pl.when(came)
-            def _(way=way, source=source):
-                for at in range(count):
-                    z_copy(at, slot_z, way, source).wait_recv()
-                    if below and above:
-                        outs[at][...] += from_z[at][slot_z, way].astype(jnp.float32)
-                    else:
-                        add(held[at], (slot_z, y, x), from_z[at], (slot_z, way))
-
-            if not (below and above):
-                for at in range(count):
-                    z_copy(at, slot_z, way).start()
-
-    def settle(slot_z, below, above):
-        for at in range(count):
-            core_copy(at, slot_z).wait_send()
-            if not (below and above):
-                z_copy(at, slot_z, 0 if above else 1).wait_send()
-        for g in everyone:
-            second_copy(g, slot_z, 0).wait_send()
-            second_copy(g, slot_z, 1).wait_send()
-            first_copy(g, slot_z).wait_send()
-
-    far = z_size - 1
-    for step in range(far, -1, -1):
-        at_offsets(z, z_size, step, begin)
-    for step in range(far, -3, -1):
-        if step >= 0:
-            at_offsets(z, z_size, step, fold_core)
-        if 0 <= step + 1 <= far:
-            at_offsets(z, z_size, step + 1, fold_second)
-        if 0 <= step + 2 <= far:
-            at_offsets(z, z_size, step + 2, fold_first)
-    for step in range(z_size):
-        at_offsets(z, z_size, step, settle)
-
-
-def scatter_all(parts, collective_id):
-    sizes = grid_sizes()
-    count, (z_size, y_size, x_size, _) = len(parts), sizes
-    shapes = [part.shape[1:] for part in parts]
-    views = row_views(shapes)
-    series = len(views)
-    dma = pltpu.SemaphoreType.DMA
-    plane = (z_size, y_size, x_size)
-
-    def buffers(lead):
-        return [pltpu.VMEM(lead + shape, jnp.bfloat16) for shape in shapes]
-
-    return pl.pallas_call(
-        functools.partial(scatter_kernel, views, count),
-        in_specs=[pl.BlockSpec(memory_space=pl.ANY)] * count,
-        out_specs=[pl.BlockSpec(memory_space=pltpu.VMEM)] * count,
-        out_shape=[jax.ShapeDtypeStruct(shape, jnp.float32) for shape in shapes],
-        scratch_shapes=buffers(plane)
-        + buffers(plane)
-        + buffers((z_size, 2))
-        + buffers((z_size,))
-        + buffers((z_size, 2))
-        + [
-            dma((count, z_size)),
-            dma((count, z_size)),
-            dma((count, z_size)),
-            dma((series, z_size, 3)),
-            dma((series, z_size, 3)),
-            dma((count, z_size, 2)),
-            dma((count, z_size, 2)),
+            dma((parts,)),
+            dma((parts,)),
+            dma,
         ],
         compiler_params=pltpu.CompilerParams(
             collective_id=collective_id, has_side_effects=True, vmem_limit_bytes=56 * 2**20
         ),
-        name="scatter_sums",
-    )(*(part.reshape(sizes + part.shape[1:]) for part in parts))
+        name="open_all",
+    )(target, latents, embeds, cotangent, *shards)
+
+
+class Scatter:
+    def __init__(self, views, parts, outs, buffers, sems):
+        self.z_size = grid_sizes()[0]
+        self.place = grid_place()
+        self.views, self.parts, self.outs = views, parts, outs
+        count = len(parts)
+        self.held, self.mine, self.from_second, self.from_first, self.from_z = (
+            buffers[at * count : (at + 1) * count] for at in range(5)
+        )
+        self.local_sem, self.k_send, self.k_recv, self.p_send, self.p_recv, self.z_send, self.z_recv = sems
+
+    def at(self, step, body):
+        if 0 <= step < self.z_size:
+            at_offsets(self.place[0], self.z_size, step, body)
+
+    def series(self, arrays):
+        return [g for g, view in enumerate(self.views) if view[0] in arrays]
+
+    def rows_of(self, g):
+        return pl.ds(self.views[g][1], self.views[g][2])
+
+    def turns(self, g, slot_z):
+        return order_of(self.place[1], self.place[2], (self.views[g][3] + slot_z) % 2)
+
+    def core_copy(self, at, slot_z):
+        z, y, x, k = self.place
+        return remote(
+            self.parts[at].at[slot_z, :, :, 1 - k],
+            self.held[at].at[slot_z],
+            self.k_send.at[at, slot_z],
+            self.k_recv.at[at, slot_z],
+            device_at(z, y, x, 1 - k),
+        )
+
+    def own_copy(self, at, slot_z, side):
+        return pltpu.make_async_copy(
+            self.parts[at].at[slot_z, :, :, self.place[3]], self.mine[at].at[side], self.local_sem.at[at, side]
+        )
+
+    def second_copy(self, g, slot_z, kind):
+        z, y, x, k = self.place
+        at, (_, second) = self.views[g][0], self.turns(g, slot_z)
+        block = second if kind == 0 else (1 - y, 1 - x)
+        return remote(
+            self.held[at].at[slot_z, block[0], block[1], self.rows_of(g)],
+            self.from_second[at].at[slot_z, kind, self.rows_of(g)],
+            self.p_send.at[g, slot_z, kind],
+            self.p_recv.at[g, slot_z, kind],
+            device_at(z, second[0], second[1], k),
+        )
+
+    def first_copy(self, g, slot_z):
+        z, y, x, k = self.place
+        at, (first, _) = self.views[g][0], self.turns(g, slot_z)
+        return remote(
+            self.held[at].at[slot_z, first[0], first[1], self.rows_of(g)],
+            self.from_first[at].at[slot_z, self.rows_of(g)],
+            self.p_send.at[g, slot_z, 2],
+            self.p_recv.at[g, slot_z, 2],
+            device_at(z, first[0], first[1], k),
+        )
+
+    def z_copy(self, at, slot_z, way, lands_home, here=None):
+        z, y, x, k = self.place
+        side = z + 1 - 2 * way if here is None else here
+        buffer = self.z_size if way == 1 and lands_home else slot_z
+        return remote(
+            self.held[at].at[slot_z, y, x],
+            self.from_z[at].at[buffer],
+            self.z_send.at[at, slot_z, way],
+            self.z_recv.at[at, slot_z, way],
+            device_at(side, y, x, k),
+        )
+
+    def begin(self, arrays):
+        def body(slot_z, below, above):
+            for at in arrays:
+                self.core_copy(at, slot_z).start()
+
+        for step in range(self.z_size - 1, -1, -1):
+            self.at(step, body)
+
+    def fold_core(self, arrays, step):
+        def fetch(slot_z, below, above):
+            for at in arrays:
+                self.own_copy(at, slot_z, 0 if below else 1).start()
+
+        def body(slot_z, below, above):
+            _, y, x, _ = self.place
+            side = 0 if below else 1
+            for at in arrays:
+                self.own_copy(at, slot_z, side).wait()
+                self.core_copy(at, slot_z).wait_recv()
+            for g in self.series(arrays):
+                at, rows = self.views[g][0], self.rows_of(g)
+                held, mine = self.held[at], self.mine[at]
+                first, second = self.turns(g, slot_z)
+                for spot in (second, (1 - y, 1 - x)):
+                    here = (slot_z, spot[0], spot[1], rows)
+                    held[here] = held[here] + mine[(side,) + here[1:]]
+                self.second_copy(g, slot_z, 0).start()
+                self.second_copy(g, slot_z, 1).start()
+                for spot in (first, (y, x)):
+                    here = (slot_z, spot[0], spot[1], rows)
+                    held[here] = held[here] + mine[(side,) + here[1:]]
+
+        self.at(step, fetch)
+        self.at(step, body)
+
+    def fold_second(self, arrays, step):
+        def body(slot_z, below, above):
+            for g in self.series(arrays):
+                at, rows = self.views[g][0], self.rows_of(g)
+                held, come = self.held[at], self.from_second[at]
+                first, _ = self.turns(g, slot_z)
+                self.second_copy(g, slot_z, 1).wait_recv()
+                here = (slot_z, first[0], first[1], rows)
+                held[here] = held[here] + come[slot_z, 1, rows]
+                self.first_copy(g, slot_z).start()
+
+        self.at(step, body)
+
+    def fold_first(self, arrays, step):
+        z, y, x, _ = self.place
+        home = step == 0
+
+        def body(slot_z, below, above):
+            for g in self.series(arrays):
+                at, rows = self.views[g][0], self.rows_of(g)
+                held = self.held[at]
+                here = (slot_z, y, x, rows)
+                self.second_copy(g, slot_z, 0).wait_recv()
+                self.first_copy(g, slot_z).wait_recv()
+                held[here] = held[here] + self.from_second[at][slot_z, 0, rows] + self.from_first[at][slot_z, rows]
+            if home:
+                for at in arrays:
+                    self.outs[at][...] = self.held[at][slot_z, y, x].astype(jnp.float32)
+            for way, use in ((0, above), (1, below)):
+                if not use:
+                    continue
+                came, source = (z > 0, z - 1) if way == 0 else (z < self.z_size - 1, z + 1)
+
+                @pl.when(came)
+                def _(way=way, source=source):
+                    for at in arrays:
+                        self.z_copy(at, slot_z, way, home, source).wait_recv()
+                        come = self.from_z[at][self.z_size if way == 1 and home else slot_z]
+                        if home:
+                            self.outs[at][...] += come.astype(jnp.float32)
+                        else:
+                            self.held[at][slot_z, y, x] = self.held[at][slot_z, y, x] + come
+
+                if not home:
+                    for at in arrays:
+                        self.z_copy(at, slot_z, way, step == 1).start()
+
+        self.at(step, body)
+
+    def settle(self, arrays):
+        for step in range(self.z_size):
+
+            def body(slot_z, below, above, step=step):
+                for at in arrays:
+                    self.core_copy(at, slot_z).wait_send()
+                    if step > 0:
+                        self.z_copy(at, slot_z, 0 if above else 1, step == 1).wait_send()
+                for g in self.series(arrays):
+                    self.second_copy(g, slot_z, 0).wait_send()
+                    self.second_copy(g, slot_z, 1).wait_send()
+                    self.first_copy(g, slot_z).wait_send()
+
+            self.at(step, body)
+
+    def stage(self, arrays, number):
+        far = self.z_size - 1
+        self.fold_core(arrays, far - number)
+        self.fold_second(arrays, far - number + 1)
+        self.fold_first(arrays, far - number + 2)
+
+    def stages(self):
+        return self.z_size + 2
+
+
+def scatter_scratch(shapes):
+    z_size, y_size, x_size, _ = grid_sizes()
+    count, series = len(shapes), len(row_views(shapes))
+    leads = ((z_size, y_size, x_size), (2, y_size, x_size), (z_size, 2), (z_size,), (z_size + 1,))
+    dma = pltpu.SemaphoreType.DMA
+    return [pltpu.VMEM(lead + shape, jnp.bfloat16) for lead in leads for shape in shapes] + [
+        dma((count, 2)),
+        dma((count, z_size)),
+        dma((count, z_size)),
+        dma((series, z_size, 3)),
+        dma((series, z_size, 3)),
+        dma((count, z_size, 2)),
+        dma((count, z_size, 2)),
+    ]
 
 
 def dot_t(left, right):
@@ -844,61 +1035,211 @@
     )(core.reshape(1), queries, keys_in, values_in, far_keys, far_values)
 
 
-def whole_attend_back(
-    q_ref, k_ref, v_ref, o_ref, do_ref, log_ref, cos_ref, sin_ref, dq_ref, dk_ref, dv_ref, dk_sum, dv_sum
+def middle_kernel(
+    shapes,
+    heads,
+    q_ref,
+    k_ref,
+    v_ref,
+    o_ref,
+    do_ref,
+    log_ref,
+    cos_ref,
+    sin_ref,
+    r_ref,
+    dmid_ref,
+    gain_ref,
+    wq_ref,
+    wk_ref,
+    wv_ref,
+    normed_ref,
+    mixed_ref,
+    first_ref,
+    db_ref,
+    *refs,
 ):
-    head = pl.program_id(0)
+    count = len(shapes)
+    parts, refs = refs[:count], refs[count:]
+    dr_ref, gains_ref, grad_ref = refs[:3]
+    outs, refs = refs[3 : 3 + count], refs[3 + count :]
+    dq_all, dk_all, dv_all, dk_sum, dv_sum = refs[:5]
+    scatter = Scatter(row_views(shapes), parts, outs, refs[5 : 5 + 5 * count], refs[5 + 5 * count :])
+    arrays = tuple(range(count))
+    step = pl.program_id(0)
     length = q_ref.shape[0]
-    lane = lax.broadcasted_iota(jnp.int32, (TILE, 128), 1)
-
-    def unrotated(grads, rows):
-        turned = pltpu.roll(grads, HEAD_DIM // 2, 1)
-        return grads * cos_ref[rows, :] - turned * sin_ref[rows, :]
-
-    for at in range(length // TILE):
-        rows = pl.ds(at * TILE, TILE)
-        seen = (at + 1) * TILE
-        queries, d_mixed = q_ref[rows, :], do_ref[rows, :]
-        log_total = jnp.sum(jnp.where(lane == head, log_ref[rows, :], 0.0), 1, keepdims=True)
-        delta = jnp.sum(d_mixed.astype(jnp.float32) * o_ref[rows, :].astype(jnp.float32), 1, keepdims=True)
-        raw = dot_t(queries, k_ref[:seen, :]) * (SCALE * LOG2E)
-        last = jnp.where(below(TILE, TILE), raw[:, at * TILE :], NEG)
-        raw = jnp.concatenate([raw[:, : at * TILE], last], 1) if at else last
-        probs = jnp.exp2(raw - log_total)
-        d_probs = dot_t(d_mixed, v_ref[:seen, :])
-        slopes = (probs * (d_probs - delta)).astype(jnp.bfloat16)
-        d_query = dot_n(slopes, k_ref[:seen, :]) * SCALE
-        dq_ref[rows, :] = unrotated(d_query, rows).astype(dq_ref.dtype)
-        d_value = dot_w(probs.astype(jnp.bfloat16), d_mixed)
-        d_key = dot_w(slopes, queries)
-        if at:
-            before = pl.ds(0, at * TILE)
-            dv_sum[before, :] += d_value[: at * TILE]
-            dk_sum[before, :] += d_key[: at * TILE]
-        dv_sum[rows, :] = d_value[at * TILE :]
-        dk_sum[rows, :] = d_key[at * TILE :]
-    everything = pl.ds(0, length)
-    dk_ref[...] = unrotated(dk_sum[...] * SCALE, everything).astype(dk_ref.dtype)
-    dv_ref[...] = dv_sum[...].astype(dv_ref.dtype)
-
-
-def attend_whole_back(queries, keys_in, values_in, mixed, d_mixed, log_total, cos_full, sin_full):
+    tiles = length // TILE
+    rest = heads + tiles
+    total = rest + 5 * tiles
+
+    @pl.when(step == 0)
+    def _():
+        greet_line(*scatter.place, scatter.z_size)
+        scatter.begin(arrays)
+        gains_ref[...] = jnp.zeros_like(gains_ref)
+
+    for number in range(scatter.stages()):
+
+        @pl.when(step == 2 + number * (total - 3) // scatter.stages())
+        def _(number=number):
+            scatter.stage(arrays, number)
+
+    @pl.when(step < heads)
+    def _():
+        head = step
+        columns = pl.ds(pl.multiple_of(head * HEAD_DIM, HEAD_DIM), HEAD_DIM)
+        lane = lax.broadcasted_iota(jnp.int32, (TILE, 128), 1)
+
+        def unrotated(grads, rows):
+            turned = pltpu.roll(grads, HEAD_DIM // 2, 1)
+            return grads * cos_ref[rows, :] - turned * sin_ref[rows, :]
+
+        for at in range(tiles):
+            rows = pl.ds(at * TILE, TILE)
+            seen = (at + 1) * TILE
+            queries, d_mixed = q_ref[rows, :], do_ref[rows, :]
+            log_total = jnp.sum(jnp.where(lane == head, log_ref[rows, :], 0.0), 1, keepdims=True)
+            delta = jnp.sum(d_mixed.astype(jnp.float32) * o_ref[rows, :].astype(jnp.float32), 1, keepdims=True)
+            raw = dot_t(queries, k_ref[:seen, :]) * (SCALE * LOG2E)
+            last = jnp.where(below(TILE, TILE), raw[:, at * TILE :], NEG)
+            raw = jnp.concatenate([raw[:, : at * TILE], last], 1) if at else last
+            probs = jnp.exp2(raw - log_total)
+            d_probs = dot_t(d_mixed, v_ref[:seen, :])
+            slopes = (probs * (d_probs - delta)).astype(jnp.bfloat16)
+            d_query = dot_n(slopes, k_ref[:seen, :]) * SCALE
+            dq_all[rows, columns] = unrotated(d_query, rows).astype(dq_all.dtype)
+            d_value = dot_w(probs.astype(jnp.bfloat16), d_mixed)
+            d_key = dot_w(slopes, queries)
+            if at:
+                before = pl.ds(0, at * TILE)
+                dv_sum[before, :] += d_value[: at * TILE]
+                dk_sum[before, :] += d_key[: at * TILE]
+            dv_sum[rows, :] = d_value[at * TILE :]
+            dk_sum[rows, :] = d_key[at * TILE :]
+        dk_all[:, columns] = unrotated(dk_sum[...] * SCALE, pl.ds(0, length)).astype(dk_all.dtype)
+        dv_all[:, columns] = dv_sum[...].astype(dv_all.dtype)
+
+    @pl.when((step >= heads) & (step < rest))
+    def _():
+        rows = pl.ds(pl.multiple_of((step - heads) * TILE, TILE), TILE)
+        d_normed = (
+            dot_t(dq_all[rows, :], wq_ref[...])
+            + dot_t(dk_all[rows, :], wk_ref[...])
+            + dot_t(dv_all[rows, :], wv_ref[...])
+        )
+        d_resid, gain_one = pull_norm(r_ref[...], d_normed, gain_ref[0:1, :])
+        dr_ref[rows, :] = (d_resid + dmid_ref[...]).astype(jnp.bfloat16)
+        gains_ref[0:1, :] += gain_one
+
+    pairs = (
+        (normed_ref, dq_all),
+        (normed_ref, dk_all),
+        (normed_ref, dv_all),
+        (mixed_ref, db_ref),
+        (first_ref, dr_ref),
+    )
+    for at, (left, right) in enumerate(pairs):
+
+        @pl.when((step >= rest + at * tiles) & (step < rest + (at + 1) * tiles))
+        def _(left=left, right=right):
+            grad_ref[...] = dot_w(left[...], right[...]).astype(grad_ref.dtype)
+
+    @pl.when(step == total - 1)
+    def _():
+        scatter.settle(arrays)
+
+
+def middle_all(
+    queries,
+    keys_in,
+    values_in,
+    mixed,
+    d_mixed,
+    log_total,
+    cos_full,
+    sin_full,
+    resid,
+    d_middle,
+    gain_float,
+    query_w,
+    key_w,
+    value_w,
+    normed,
+    first_out,
+    d_branch,
+    sums,
+    collective_id,
+):
+    sizes = grid_sizes()
     length, width = queries.shape
-    head_block = pl.BlockSpec((length, HEAD_DIM), lambda h: (0, h))
-    fixed = pl.BlockSpec((length, 128), lambda h: (0, 0))
+    heads, tiles = width // HEAD_DIM, length // TILE
+    rest = heads + tiles
+    shapes = [part.shape[1:] for part in sums]
+    head_block = pl.BlockSpec((length, HEAD_DIM), lambda i: (0, jnp.minimum(i, heads - 1)))
+    tall_block = pl.BlockSpec((TILE, width), lambda i: (jnp.clip(i - heads, 0, tiles - 1), 0))
+
+    def left_block(first, repeats=1):
+        def place(i):
+            inside = jnp.clip(i - rest - first * tiles, 0, repeats * tiles - 1)
+            return (0, inside % tiles)
+
+        return pl.BlockSpec((length, TILE), place)
+
+    fixed = pl.BlockSpec((length, 128), lambda i: (0, 0), pipeline_mode=pl.Buffered(1))
+    anywhere = pl.BlockSpec(memory_space=pl.ANY)
+    near = pl.BlockSpec(memory_space=pltpu.VMEM)
+    once = pl.Buffered(1)
+    weights = sum(shape[0] * shape[1] for shape in shapes)
     return pl.pallas_call(
-        whole_attend_back,
-        grid=(width // HEAD_DIM,),
-        in_specs=[head_block] * 5 + [fixed] * 3,
-        out_specs=[head_block] * 3,
-        out_shape=[jax.ShapeDtypeStruct((length, width), jnp.bfloat16)] * 3,
-        scratch_shapes=[pltpu.VMEM((length, HEAD_DIM), jnp.float32)] * 2,
-        compiler_params=pltpu.CompilerParams(vmem_limit_bytes=40 * 2**20),
-        cost_estimate=pl.CostEstimate(
-            flops=5 * length * length * width, bytes_accessed=16 * length * width, transcendentals=0
+        functools.partial(middle_kernel, shapes, heads),
+        grid=(rest + 5 * tiles,),
+        in_specs=[head_block] * 5
+        + [fixed] * 3
+        + [tall_block] * 2
+        + [whole_block(a) for a in (gain_float, query_w, key_w, value_w)]
+        + [left_block(0, 3), left_block(3), left_block(4)]
+        + [whole_block(d_branch)]
+        + [anywhere] * len(sums),
+        out_specs=[
+            pl.BlockSpec((length, width), lambda i: (0, 0), pipeline_mode=once),
+            pl.BlockSpec((8, width), lambda i: (0, 0), pipeline_mode=once),
+            pl.BlockSpec((TILE, width), lambda i: (jnp.clip(i - rest, 0, 5 * tiles - 1), 0)),
+        ]
+        + [near] * len(sums),
+        out_shape=[
+            jax.ShapeDtypeStruct((length, width), jnp.bfloat16),
+            jax.ShapeDtypeStruct((8, width), jnp.float32),
+            jax.ShapeDtypeStruct((5 * width, width), jnp.bfloat16),
+        ]
+        + [jax.ShapeDtypeStruct(shape, jnp.float32) for shape in shapes],
+        scratch_shapes=[pltpu.VMEM((length, width), jnp.bfloat16)] * 3
+        + [pltpu.VMEM((length, HEAD_DIM), jnp.float32)] * 2
+        + scatter_scratch(shapes),
+        compiler_params=pltpu.CompilerParams(
+            collective_id=collective_id, has_side_effects=True, vmem_limit_bytes=62 * 2**20
         ),
-        name="attend_whole_back",
-    )(queries, keys_in, values_in, mixed, d_mixed, log_total, cos_full, sin_full)
+        cost_estimate=cost(24 * length * width * width, 64 * length * width + 64 * weights),
+        name="middle_all",
+    )(
+        queries,
+        keys_in,
+        values_in,
+        mixed,
+        d_mixed,
+        log_total,
+        cos_full,
+        sin_full,
+        resid,
+        d_middle,
+        gain_float,
+        query_w,
+        key_w,
+        value_w,
+        normed,
+        mixed,
+        first_out,
+        d_branch,
+        *(part.reshape(sizes + part.shape[1:]) for part in sums),
+    )
 
 
 def rope_full(positions):
@@ -932,40 +1273,6 @@
     gain_part = jnp.sum(upstream * normal, 0, keepdims=True)
     scaled = upstream * gain_row
     return scale_rows * (scaled - normal * jnp.mean(scaled * normal, -1, keepdims=True)), gain_part
-
-
-def home_kernel(block_len, target_ref, s_ref, e_ref, c_ref, w_ref, start_ref, shared_ref, up_ref):
-    rows, width = start_ref.shape
-    count = s_ref.shape[0]
-    at_row = lax.broadcasted_iota(jnp.int32, (rows, count), 0) + pl.program_id(0) * rows
-    order = (at_row == target_ref[...]).astype(jnp.bfloat16)
-    up_ref[...] = dot_n(order, c_ref[...]).astype(jnp.bfloat16)
-    latent = dot_n(order, s_ref[...]).astype(jnp.bfloat16)
-    embed = dot_n(order, e_ref[...]).astype(jnp.bfloat16)
-    embed_part = dot_n(embed, w_ref[width:, :])
-    adapted = dot_n(jnp.concatenate([latent, embed], 1), w_ref[...])
-    shared_ref[...] = adapted.astype(jnp.bfloat16)
-    pair_at = lax.broadcasted_iota(jnp.int32, (rows, 1), 0) // block_len % 2
-    start_ref[...] = jnp.where(pair_at == 0, embed_part, adapted).astype(jnp.bfloat16)
-
-
-def adapt_at_home(target, latents, embeds, cotangent, adapt_w, block_len):
-    count, width = latents.shape
-    like = jax.ShapeDtypeStruct((count, width), jnp.bfloat16)
-    return pl.pallas_call(
-        functools.partial(home_kernel, block_len),
-        grid=(count // TILE,),
-        in_specs=[whole_block(a) for a in (target, latents, embeds, cotangent, adapt_w)],
-        out_specs=[
-            row_block(TILE, width),
-            row_block(TILE, width),
-            row_block(TILE, width),
-        ],
-        out_shape=[like, like, like],
-        compiler_params=compute_params(),
-        cost_estimate=cost(10 * count * width * width, 14 * count * width),
-        name="adapt_at_home",
-    )(target, latents, embeds, cotangent, adapt_w)
 
 
 def turned_heads(values, cos, sin):
@@ -1186,81 +1493,127 @@
     )(left, right)
 
 
-def back_heads_kernel(dq_ref, dk_ref, dv_ref, r_ref, dmid_ref, gain_ref, wq_ref, wk_ref, wv_ref, out_ref, gains_ref):
-    d_normed = dot_t(dq_ref[...], wq_ref[...]) + dot_t(dk_ref[...], wk_ref[...]) + dot_t(dv_ref[...], wv_ref[...])
-    d_resid, gain_one = pull_norm(r_ref[...], d_normed, gain_ref[0:1, :])
-    out_ref[...] = (d_resid + dmid_ref[...]).astype(jnp.bfloat16)
-
-    @pl.when(pl.program_id(0) == 0)
-    def _():
-        gains_ref[...] = jnp.zeros_like(gains_ref)
-
-    gains_ref[0:1, :] += gain_one
-
-
-def back_heads(d_query, d_key, d_value, resid, d_middle, gain_float, query_w, key_w, value_w):
-    rows, width = resid.shape
-    fixed = (gain_float, query_w, key_w, value_w)
-    return pl.pallas_call(
-        back_heads_kernel,
-        grid=(rows // TILE,),
-        in_specs=[row_block(TILE, width)] * 5 + [whole_block(a) for a in fixed],
-        out_specs=[row_block(TILE, width), pl.BlockSpec((8, width), lambda i: (0, 0))],
-        out_shape=[
-            jax.ShapeDtypeStruct((rows, width), jnp.bfloat16),
-            jax.ShapeDtypeStruct((8, width), jnp.float32),
-        ],
-        compiler_params=compute_params(),
-        cost_estimate=cost(6 * rows * width * width, 16 * rows * width + 6 * width * width),
-        name="back_heads",
-    )(d_query, d_key, d_value, resid, d_middle, *fixed)
-
-
-def home_back_kernel(
-    target_ref, d_ref, final_ref, s_ref, e_ref, w_ref, first_ref, out_ref, ds_ref, de_ref, grad_ref, sum_ref
+def close_kernel(target_ref, final_ref, w_ref, s_ref, e_ref, dr_ref, grad_ref, gain_ref, *refs):
+    _, _, x_size, k_size = grid_sizes()
+    ctx = x_size * k_size
+    parts_count = lax.axis_size("grp") * ctx
+    me = lax.axis_index("grp") * ctx + lax.axis_index("ctx")
+    final_out, ds_ref, de_ref = refs[:3]
+    outs, refs = refs[3:9], refs[9:]
+    home, first, total, adapt_part = refs[:4]
+    buffers, refs = refs[4:34], refs[34:]
+    sems, (send_sem, recv_sem, own_sem) = refs[:7], refs[7:]
+    parts = [grad_ref.at[at] for at in range(4)] + [adapt_part, gain_ref]
+    scatter = Scatter(row_views([out.shape for out in outs]), parts, outs, buffers, sems)
+    early, late = (0, 1, 2, 3, 5), (4,)
+    count, width = ds_ref.shape
+    tiles = count // TILE
+
+    barrier = pltpu.get_barrier_semaphore()
+
+    def greet(at, carry):
+        @pl.when(at != me)
+        def _():
+            pl.semaphore_signal(barrier, inc=1, device_id=flat_device(at, ctx), device_id_type=MESH)
+
+        return carry
+
+    lax.fori_loop(0, parts_count, greet, 0)
+    pl.semaphore_wait(barrier, parts_count - 1)
+
+    def leave(at, carry):
+        @pl.when(at != me)
+        def _():
+            remote(dr_ref.at[at], home.at[me], send_sem.at[at], recv_sem.at[me], flat_device(at, ctx)).start()
+
+        return carry
+
+    lax.fori_loop(0, parts_count, leave, 0)
+    own = pltpu.make_async_copy(dr_ref.at[me], home.at[me], own_sem.at[0])
+    own_first = pltpu.make_async_copy(grad_ref.at[4], first, own_sem.at[1])
+    own.start()
+    own_first.start()
+    scatter.begin(early)
+
+    def order_rows(tile):
+        rows = pl.ds(pl.multiple_of(tile * TILE, TILE), TILE)
+        at_column = lax.broadcasted_iota(jnp.int32, (TILE, count), 1)
+        return rows, (at_column == target_ref[rows, :]).astype(jnp.bfloat16)
+
+    def at_home(tile):
+        rows, order = order_rows(tile)
+        d_home = dot_n(order, home[...].reshape(count, width)).astype(jnp.bfloat16)
+        ds_ref[rows, :] = dot_t(d_home, w_ref[:width, :]).astype(jnp.bfloat16)
+        de_ref[rows, :] = dot_t(d_home, w_ref[width:, :]).astype(jnp.bfloat16)
+        upper, lower = dot_w(s_ref[rows, :], d_home), dot_w(e_ref[rows, :], d_home)
+        if tile == 0:
+            total[:width, :] = upper + first[...].reshape(width, width).astype(jnp.float32)
+            total[width:, :] = lower
+        else:
+            total[:width, :] += upper
+            total[width:, :] += lower
+
+    for number in range(4):
+        scatter.stage(early, number)
+        if number < tiles:
+            rows, order = order_rows(number)
+            final_out[rows, :] = dot_n(order, final_ref[...]).astype(jnp.bfloat16)
+
+    def arrive(at, carry):
+        @pl.when(at != me)
+        def _():
+            remote(dr_ref.at[at], home.at[at], send_sem.at[at], recv_sem.at[at], flat_device(at, ctx)).wait()
+
+        return carry
+
+    lax.fori_loop(0, parts_count, arrive, 0)
+    own.wait()
+    own_first.wait()
+    for tile in range(tiles):
+        at_home(tile)
+        if tile < scatter.stages() - 4:
+            scatter.stage(early, 4 + tile)
+    adapt_part[...] = total[...].reshape(adapt_part.shape).astype(adapt_part.dtype)
+    scatter.begin(late)
+    for number in range(scatter.stages()):
+        scatter.stage(late, number)
+    scatter.settle(early)
+    scatter.settle(late)
+
+
+def close_all(
+    target, final_slots, adapt_w, once, embeds, d_resid, weight_parts, gain_part, block_len, collective_id
 ):
-    step = pl.program_id(0)
-    rows, width = ds_ref.shape
-    count = d_ref.shape[0]
-    at_column = lax.broadcasted_iota(jnp.int32, (rows, count), 1)
-    order = (at_column == target_ref[...]).astype(jnp.bfloat16)
-    out_ref[...] = dot_n(order, final_ref[...]).astype(jnp.bfloat16)
-    d_home = dot_n(order, d_ref[...]).astype(jnp.bfloat16)
-    ds_ref[...] = dot_t(d_home, w_ref[:width, :]).astype(jnp.bfloat16)
-    de_ref[...] = dot_t(d_home, w_ref[width:, :]).astype(jnp.bfloat16)
-    upper, lower = dot_w(s_ref[...], d_home), dot_w(e_ref[...], d_home)
-
-    @pl.when(step == 0)
-    def _():
-        sum_ref[:width, :] = upper + first_ref[...]
-        sum_ref[width:, :] = lower
-
-    @pl.when(step > 0)
-    def _():
-        sum_ref[:width, :] += upper
-        sum_ref[width:, :] += lower
-
-    @pl.when(step == pl.num_programs(0) - 1)
-    def _():
-        grad_ref[...] = sum_ref[...].astype(jnp.bfloat16)
-
-
-def back_at_home(target, d_home, final_slots, once, embeds, adapt_w, first_part):
-    count, width = d_home.shape
+    sizes = grid_sizes()
+    parts = lax.axis_size("grp") * lax.axis_size("ctx")
+    width = weight_parts.shape[1]
+    count = target.shape[0]
+    side = width // parts
+    square = weight_parts.reshape((5,) + sizes + (side, width))
+    gain = gain_part.reshape(sizes + gain_part.shape[1:])
+    shapes = [(side, width)] * 4 + [(2 * side, width), gain_part.shape[1:]]
+    anywhere = pl.BlockSpec(memory_space=pl.ANY)
+    near = pl.BlockSpec(memory_space=pltpu.VMEM)
+    dma = pltpu.SemaphoreType.DMA
     like = jax.ShapeDtypeStruct((count, width), jnp.bfloat16)
     return pl.pallas_call(
-        home_back_kernel,
-        grid=(count // TILE,),
-        in_specs=[row_block(TILE, 1), whole_block(d_home), whole_block(final_slots)]
-        + [row_block(TILE, width)] * 2
-        + [whole_block(adapt_w), whole_block(first_part)],
-        out_specs=[row_block(TILE, width)] * 3 + [pl.BlockSpec(adapt_w.shape, lambda i: (0, 0))],
-        out_shape=[like] * 3 + [jax.ShapeDtypeStruct(adapt_w.shape, jnp.bfloat16)],
-        scratch_shapes=[pltpu.VMEM(adapt_w.shape, jnp.float32)],
-        compiler_params=compute_params(),
-        cost_estimate=cost(12 * count * width * width, 20 * count * width),
-        name="back_at_home",
-    )(target, d_home, final_slots, once, embeds, adapt_w, first_part)
+        close_kernel,
+        in_specs=[near] * 5 + [anywhere] * 3,
+        out_specs=[near] * (3 + len(shapes)),
+        out_shape=[like] * 3 + [jax.ShapeDtypeStruct(shape, jnp.float32) for shape in shapes],
+        scratch_shapes=[
+            pltpu.VMEM((parts, block_len, width), jnp.bfloat16),
+            pltpu.VMEM(sizes + (side, width), jnp.bfloat16),
+            pltpu.VMEM((2 * width, width), jnp.float32),
+            pltpu.VMEM(sizes + (2 * side, width), jnp.bfloat16),
+        ]
+        + scatter_scratch(shapes)
+        + [dma((parts,)), dma((parts,)), dma((2,))],
+        compiler_params=pltpu.CompilerParams(
+            collective_id=collective_id, has_side_effects=True, vmem_limit_bytes=62 * 2**20
+        ),
+        name="close_all",
+    )(target, final_slots, adapt_w, once, embeds, d_resid, square, gain)
 
 
 def paired_on_device(
@@ -1285,29 +1638,24 @@
     def exchange(values):
         return lax.all_to_all(values, BOTH, split_axis=0, concat_axis=0, tiled=True)
 
-    adapt_w = gather_all([w_adapt], 0)[0].reshape(-1, width)
-    starting, shared, upstream = adapt_at_home(
-        target.reshape(1, row_count), latent_rows, embed_rows, slope_rows, adapt_w, block_len
-    )
-
     half = block_len // 2
-    shared = shared.reshape(parts // 2, 2, block_len, width)[:, 0].reshape(parts, half, width)
-    leaving = jnp.concatenate([starting.reshape(parts, block_len, width), shared], 1)
     gain_rows = jnp.pad(gains.reshape(1, -1), ((0, 15), (0, 0)))
-    leaving, *shards = lax.optimization_barrier(
-        (leaving, w_query, w_key, w_value, w_out, w_gate, w_up, w_down, gain_rows)
-    )
-    arrived = exchange(leaving)
-    *matrices, gain_float = gather_all(shards, 1)
-    query_w, key_w, value_w, output_w, gate_w, up_w, down_w = (
+    *matrices, gain_float, shared, starting, upstream = open_all(
+        target.reshape(1, row_count),
+        latent_rows,
+        embed_rows,
+        slope_rows,
+        [w_adapt, w_query, w_key, w_value, w_out, w_gate, w_up, w_down, gain_rows],
+        block_len,
+        0,
+    )
+    adapt_w, query_w, key_w, value_w, output_w, gate_w, up_w, down_w = (
         matrix.reshape(-1, matrix.shape[-1]) for matrix in matrices
     )
     gain_float = gain_float.reshape((parts,) + gain_rows.shape)[:, 0].reshape((parts,) + gains.shape)
     gain_float = gain_float.transpose(1, 0, 2).reshape(gains.shape[0], width).astype(jnp.float32)
-    gate_w, arrived, upstream = lax.optimization_barrier((gate_w, arrived, upstream))
-    starting = arrived[:, :block_len].reshape(length, width)
-    shared = arrived[:, block_len:].reshape(length // 2, width)
-    upstream = exchange(upstream.reshape(parts, block_len, width)).reshape(length, width)
+    shared = shared.reshape(length // 2, width)
+    starting = exchange(starting).reshape(length, width)
 
     resid = shared
     local = jnp.arange(length // 2, dtype=jnp.int32)
@@ -1316,6 +1664,8 @@
     far_keys, far_values = send(keys_in, 3), send(values_in, 3)
     mixed = attend_shared(core, half, queries, keys_in, values_in, far_keys, far_values)
     first_out = first_rows(resid, mixed, gain_float, output_w, gate_w, up_w, down_w)
+    first_out, upstream = lax.optimization_barrier((first_out, upstream))
+    upstream = exchange(upstream.reshape(parts, block_len, width)).reshape(length, width)
     far_out = send(first_out, 3, -1)
     first_out = jnp.stack(
         [first_out.reshape(-1, half, width), far_out.reshape(-1, half, width)], 1
@@ -1331,54 +1681,52 @@
         resid, mixed, upstream, gain_float, output_w, gate_w, up_w, down_w
     )
     final_back = exchange(result.reshape(parts, block_len, width))
-    d_query, d_key, d_value = attend_whole_back(
-        queries, keys_in, values_in, mixed, d_mixed, log_total, cos_full, sin_full
-    )
-    d_resid, gain_one = back_heads(
-        d_query, d_key, d_value, resid, d_middle, gain_float, query_w, key_w, value_w
-    )
-    final_back, d_resid = lax.optimization_barrier((final_back, d_resid))
-    d_home = exchange(d_resid.reshape(parts, block_len, width))
     down_part = weight_grad(hidden, d_down)
     gate_part = weight_grad(mlp_in, d_gate)
     up_part = weight_grad(mlp_in, d_up)
-    out_part = weight_grad(mixed, d_branch)
-    query_part = weight_grad(normed, d_query)
-    key_part = weight_grad(normed, d_key)
-    value_part = weight_grad(normed, d_value)
-    first_part = dot_w(first_out, d_resid)
 
     def blocks(part):
         return part.reshape(parts, -1, part.shape[-1])
 
+    d_resid, gain_one, weight_parts, gate_grad, up_grad, down_grad = middle_all(
+        queries,
+        keys_in,
+        values_in,
+        mixed,
+        d_mixed,
+        log_total,
+        cos_full,
+        sin_full,
+        resid,
+        d_middle,
+        gain_float,
+        query_w,
+        key_w,
+        value_w,
+        normed,
+        first_out,
+        d_branch,
+        [blocks(part) for part in (gate_part, up_part, down_part)],
+        1,
+    )
     gain_part = jnp.concatenate([gain_one[:1], gain_rest[:3]], 0)
     gain_part = gain_part.reshape(gains.shape[0], parts, gains.shape[1]).transpose(1, 0, 2)
     gain_part = jnp.pad(
         gain_part.reshape(parts, 1, gains.size).astype(jnp.bfloat16), ((0, 0), (0, 15), (0, 0))
     )
-    sums = scatter_all(
-        [
-            blocks(part)
-            for part in (query_part, key_part, value_part, out_part, gate_part, up_part, down_part)
-        ]
-        + [gain_part],
+    final_back, latent_back, embed_back, query_grad, key_grad, value_grad, out_grad, adapt_grad, gain_grad = close_all(
+        target.reshape(row_count, 1),
+        final_back.reshape(row_count, width),
+        adapt_w,
+        jnp.where(twice[None, :, None], jnp.zeros_like(latents), latents).reshape(row_count, width),
+        embed_rows,
+        blocks(d_resid),
+        weight_parts,
+        gain_part,
+        block_len,
         2,
     )
-    query_grad, key_grad, value_grad, out_grad, gate_grad, up_grad, down_grad, gain_grad = sums
     gain_grad = gain_grad[0].reshape(gains.shape)
-    d_home, gate_grad = lax.optimization_barrier((d_home, gate_grad))
-
-    once = jnp.where(twice[None, :, None], jnp.zeros_like(latents), latents).reshape(row_count, width)
-    final_back, latent_back, embed_back, adapt_part = back_at_home(
-        target.reshape(row_count, 1),
-        d_home.reshape(row_count, width),
-        final_back.reshape(row_count, width),
-        once,
-        embed_rows,
-        adapt_w,
-        first_part,
-    )
-    (adapt_grad,) = scatter_all([blocks(adapt_part)], 3)
     return (
         final_back.reshape(latents.shape),
         latent_back.reshape(latents.shape),

time: 729 us -> 659 us (0.904)
  Pallas kernels: 627 us -> 575 us
    pallas_call x8 -> x3, Pallas kernels: 435 us -> 409 us  [the longest x1 181 us: open_all(): pl.pallas_call(functools.partial(open_kernel, views, count, block_len), i...]
    pallas_call x7 -> x3, Pallas kernels: 59.4 us -> 35 us  [weight_grad(): pl.pallas_call(weight_grad_kernel, grid=(height // tile,), in_specs=[pl.B...]
    all_to_all x4 -> x3, starting transfers between devices: 32 us -> 15.2 us  [exchange(): return lax.all_to_all(values, BOTH, split_axis=0, concat_axis=0, tiled=True)]
    ppermute x3, starting transfers between devices: 1.85 us -> 16.5 us  [send(): return lax.ppermute(values, BOTH, pairs)]
    unnamed x72 -> x55, local copies, waits for them, and re-layouts: 23.1 us -> 25.4 us
  transfers between devices with their start and end apart: 7 -> 6, of which waited for: 1 -> 2; matrix products, arithmetic and copies ran while one was open for 3% -> 2% of each run, Pallas kernels for 62% -> 33%
where the time goes in v4:
time: 659 us; the launch traced here: 656 us
  Pallas kernels  575 us (87%)
  local copies, waits for them, and re-layouts  34.4 us (5%)
  starting transfers between devices  31.7 us (5%)
  other arithmetic  9.99 us (2%)
    pallas_call x1, Pallas kernels, open_all(): pl.pallas_call(functools.partial(open_kernel, views, count, block_len), i...  181 us
    pallas_call x1, Pallas kernels, middle_all(): pl.pallas_call(functools.partial(middle_kernel, shapes, heads), grid=(res...  115 us
    pallas_call x1, Pallas kernels, close_all(): pl.pallas_call(close_kernel, in_specs=[near] * 5 + [anywhere] * 3, out_sp...  113 us
    pallas_call x1, Pallas kernels, last_rows(): pl.pallas_call(last_rows_kernel, grid=(rows // TILE,), in_specs=[row_bloc...  63.2 us
    pallas_call x3, Pallas kernels, weight_grad(): pl.pallas_call(weight_grad_kernel, grid=(height // tile,), in_specs=[pl.B...  35 us
    unnamed x55, local copies, waits for them, and re-layouts  25.4 us
    pallas_call x1, Pallas kernels, first_rows(): pl.pallas_call(first_rows_kernel, grid=(rows // tile,), in_specs=[row_blo...  19.5 us
    ppermute x3, starting transfers between devices, send(): return lax.ppermute(values, BOTH, pairs)  16.5 us
  transfers between devices with their start and end apart: 6, of which 2 were waited for; matrix products, arithmetic and copies ran while one was open for 2% of the time, Pallas kernels for 33%

profile of v4, /device:TPU:0, one launch (start us, length us, event | category | flops | bytes accessed | tf_op | source)
XLA Modules:
  0.0 655.9 jit_solution(10657674786579739396)
XLA Ops:
  3.1 0.8 reshape.276
  4.4 181.1 %open_all.1 = (bf16[4,2,2,2,64,1024]{5,4,3,2,1,0:T(8,128)(2,1)}, bf16[4,2,2,2,32,1024]{5,4,3,2,1,0:T(8,128)(2,1)}, bf16[4,2,2,2,32,1024]{5,4,3,2,1,0:T(8,128)(2,...) custom-call(s32[1,1024]{1,0:T(1,128)} %add.89.refs_0_, ...), custom_call_target="tpu_custom_call" | custom-call | tf_op jit(solution)/shard_map/open_all/pallas_call | solution.py:709
  185.5 2.7 all-to-all-start
  188.3 0.9 slice.18
  189.2 0.7 reshape.302.gain_ref
  190.0 1.0 fusion.1
  191.0 1.0 pad_maximum_fusion.2
  192.0 7.8 %first_heads.1 = (bf16[512,1024]{1,0:T(8,128)(2,1)}, bf16[512,1024]{1,0:T(8,128)(2,1)}, bf16[512,1024]{1,0:T(8,128)(2,1)}) custom-call(bf16[512,1024]{1,0:T(8,128)(2,1)} %bitcast.85, f32[4,1024]{1,0:T(4,128)} %reshape.302.gain_ref, bf16[1024,1024]{1,0:T(8,128)(2,1)} %bitcast.74, bf16[1024,1024]{1,0:T(8,128)(2,1)} %bitcast.77, bf16[1024,1024]{1,0:T(8,128)(2,1)} %bitcast.80, ...), custom_call_target="tpu_custom_call" | custom-call | flops 3221225472 | bytes 10485760 | tf_op jit(solution)/shard_map/first_heads/pallas_call | solution.py:1304
  200.4 2.4 collective-permute-done.ok_ref
  202.8 1.5 collective-permute-done.1.ov_ref
  204.3 1.2 copy-done
  205.5 1.2 copy-done.1
  206.7 1.2 copy-done.2
  208.0 9.3 %attend_shared.1.mixed_ref = bf16[512,1024]{1,0:T(8,128)(2,1)S(1)} custom-call(s32[1]{0:T(128)} %bitcast.7.core_ref, bf16[512,1024]{1,0:T(8,128)(2,1)S(1)} %copy-done, bf16[512,1024]{1,0:T(8,128)(2,1)S(1)} %copy-done.1, bf16[512,1024]{1,0:T(8,128)(2,1)S(1)} %copy-done.2, bf16[512,1024]{1,0:T(8,128)(2,1)S(1)} %collective-permute-done.ok_ref, ...), custom_call_target="tpu_custom_call" | custom-call | flops 1073741824 | bytes 6291456 | tf_op jit(solution)/shard_map/attend_shared/pallas_call | solution.py:1024
  217.3 1.0 copy-done.3
  218.3 19.5 %first_rows.1 = bf16[512,1024]{1,0:T(8,128)(2,1)} custom-call(bf16[512,1024]{1,0:T(8,128)(2,1)} %bitcast.86, bf16[512,1024]{1,0:T(8,128)(2,1)} %copy-done.3, f32[4,1024]{1,0:T(4,128)} %reshape.302.gain_ref, bf16[1024,1024]{1,0:T(8,128)(2,1)} %bitcast.83, bf16[1024,2816]{1,0:T(8,128)(2,1)} %bitcast.68, bf16[1024,2816]{1,0:T(8,128)(2,1)} %bitcast.70, ...), custom_call_target="tpu_custom_call" | custom-call | flops 9932111872 | bytes 22544384 | tf_op jit(solution)/shard_map/first_rows/pallas_call | solution.py:1378
  237.8 1.3 copy-done.10
  239.1 5.8 all-to-all-start.1
  244.9 15.9 %collective-permute-start.2 = (bf16[512,1024]{1,0:T(8,128)(2,1)S(1)}, bf16[512,1024]{1,0:T(8,128)(2,1)S(1)}, u32[]{:S(2)}, u32[]{:S(2)}) collective-permute-start(bf16[512,1024]{1,0:T(8,128)(2,1)S(1)} %copy-done.13), channel_id=1, source_target_pairs={{1,0},{3,2},{5,4},{7,6},{9,8},{11,10},{13,12},{15,14},{17,16},{19,... | collective-permute-start | bytes 3145736 | tf_op jit(solution)/shard_map/ppermute | solution.py:387
  260.8 1.4 add.95.target_ref
  262.2 1.9 fusion
  264.1 1.4 pad_maximum_fusion
  265.5 1.6 broadcast_select_fusion
  267.1 1.5 maximum_select_fusion
  268.6 15.5 %last_heads.1 = (f32[1024,1024]{1,0:T(8,128)}, bf16[1024,1024]{1,0:T(8,128)(2,1)}, bf16[1024,1024]{1,0:T(8,128)(2,1)}, bf16[1024,1024]{1,0:T(8,128)(2,1)}, bf16[1024,1024]{1,0:T(8,128)(2,1)}) custom-call(bf16[1024,1024]{1,0:T(8,128)(2,1)} %bitcast.54, bf16[1024,1024]{1,0:T(8,128)(2,1)} %bitcast.55, bf16[2048,1024]{1,0:T(8,128)(2,1)} %bitcast.51, ...), custom_call_target="tpu_custom_call" | custom-call | flops 8589934592 | bytes 25165824 | tf_op jit(solution)/shard_map/last_heads/pallas_call | solution.py:1329
  284.1 1.6 copy-done.4
  285.7 1.6 copy-done.5
  287.3 1.6 copy-done.6
  288.9 15.8 %attend_whole.1 = (bf16[1024,1024]{1,0:T(8,128)(2,1)S(1)}, f32[1024,128]{1,0:T(8,128)S(1)}) custom-call(bf16[1024,1024]{1,0:T(8,128)(2,1)S(1)} %copy-done.4, bf16[1024,1024]{1,0:T(8,128)(2,1)S(1)} %copy-done.5, bf16[1024,1024]{1,0:T(8,128)(2,1)S(1)} %copy-done.6), custom_call_target="tpu_custom_call" | custom-call | flops 2147483648 | bytes 8388608 | tf_op jit(solution)/shard_map/attend_whole/pallas_call | solution.py:979
  304.6 1.3 copy-done.7
  305.9 0.8 copy-done.8
  306.7 63.2 %last_rows.1 = (bf16[1024,1024]{1,0:T(8,128)(2,1)}, bf16[1024,2816]{1,0:T(8,128)(2,1)}, bf16[1024,1024]{1,0:T(8,128)(2,1)}, bf16[1024,1024]{1,0:T(8,128)(2,1)}, ...) custom-call(f32[1024,1024]{1,0:T(8,128)} %get-tuple-element.77.r_ref, ...), custom_call_target="tpu_custom_call" | custom-call | flops 39728447488 | bytes 50855936 | tf_op jit(solution)/shard_map/last_rows/pallas_call | solution.py:1463
  369.9 6.7 %all-to-all-start.2 = ((bf16[32,32,1024]{2,1,0:T(8,128)(2,1)}), bf16[32,32,1024]{2,1,0:T(8,128)(2,1)}, u32[]{:S(2)}, u32[]{:S(2)}) async-start(bf16[32,32,1024]{2,1,0:T(8,128)(2,1)} %bitcast.57), calls=%async_computation.2 | async-start | bytes 4194304 | tf_op jit(solution)/shard_map/all_to_all | solution.py:1639
  376.6 10.9 %weight_grad.4 = bf16[1024,2816]{1,0:T(8,128)(2,1)} custom-call(bf16[1024,1024]{1,0:T(8,128)(2,1)} %get-tuple-element.89.left_ref, bf16[1024,2816]{1,0:T(8,128)(2,1)} %get-tuple-element.91.right_ref), custom_call_target="tpu_custom_call" | custom-call | flops 5905580032 | bytes 13631488 | tf_op jit(solution)/shard_map/weight_grad/pallas_call | solution.py:1484
  387.5 10.8 %weight_grad.3 = bf16[1024,2816]{1,0:T(8,128)(2,1)} custom-call(bf16[1024,1024]{1,0:T(8,128)(2,1)} %get-tuple-element.89.left_ref, bf16[1024,2816]{1,0:T(8,128)(2,1)} %get-tuple-element.90.right_ref), custom_call_target="tpu_custom_call" | custom-call | flops 5905580032 | bytes 13631488 | tf_op jit(solution)/shard_map/weight_grad/pallas_call | solution.py:1484
  398.3 13.3 %weight_grad.5 = bf16[2816,1024]{1,0:T(8,128)(2,1)} custom-call(bf16[1024,2816]{1,0:T(8,128)(2,1)} %get-tuple-element.92.left_ref, bf16[1024,1024]{1,0:T(8,128)(2,1)} %get-tuple-element.93.right_ref), custom_call_target="tpu_custom_call" | custom-call | flops 5905580032 | bytes 13631488 | tf_op jit(solution)/shard_map/weight_grad/pallas_call | solution.py:1484
  411.6 114.9 %middle_all.1 = (bf16[1024,1024]{1,0:T(8,128)(2,1)}, f32[8,1024]{1,0:T(8,128)}, bf16[5120,1024]{1,0:T(8,128)(2,1)}, f32[32,2816]{1,0:T(8,128)}, f32[32,2816]{1,0:T(8,128)}, /*index=5*/f32[88,1024]{1,0:T(8,128)}) custom-call(bf16[1024,1024]{1,0:T(8,128)(2,1)} %get-tuple-element.78.q_ref, bf16[1024,1024]{1,0:T(8,128)(2,1)} %get-tuple-element.79.k_ref, ...), custom_call_target="tpu_custom_call" | custom-call | flops 25769803776 | bytes 84410368 | tf_op jit(solution)/shard_map/middle_all/pallas_call | solution.py:1192
  526.6 0.8 slice.25
  527.4 0.8 slice.24
  529.0 112.7 %close_all.1 = (bf16[1024,1024]{1,0:T(8,128)(2,1)}, bf16[1024,1024]{1,0:T(8,128)(2,1)}, bf16[1024,1024]{1,0:T(8,128)(2,1)}, f32[32,1024]{1,0:T(8,128)}, f32[32,1...) custom-call(s32[1024,1]{1,0:T(8,128)} %add.95.target_ref, ...), custom_call_target="tpu_custom_call" | custom-call | tf_op jit(solution)/shard_map/close_all/pallas_call | solution.py:1599
  643.1 3.3 copy.55
  646.5 1.3 copy.56
  647.8 1.0 copy-done.11
  648.8 1.3 copy.57
  650.2 0.7 copy.58
  653.5 0.7 copy.63
  654.2 0.7 copy.64
  655.0 0.7 copy.65
  (66 shorter events, 8.7 us)
Async XLA Ops:
  185.5 52.3 %all-to-all-start = ((bf16[32,32,1024]{2,1,0:T(8,128)(2,1)}), bf16[32,32,1024]{2,1,0:T(8,128)(2,1)S(1)}, u32[]{:S(2)}, u32[]{:S(2)}) async-start(bf16[32,32,1024]{2,1,0:T(8,128)(2,1)} %get-tuple-element.61), calls=%async_computation | async-start | bytes 4194304 | tf_op jit(solution)/shard_map/all_to_all | solution.py:1639
  199.8 3.0 collective-permute-start
  200.3 4.0 collective-permute-start.1
  204.3 1.2 copy-start
  205.5 1.2 copy-start.1
  206.7 1.2 copy-start.2
  217.3 1.0 copy-start.3
  237.8 1.3 copy-start.10
  237.8 7.1 %copy-start.13 = (bf16[512,1024]{1,0:T(8,128)(2,1)S(1)}, bf16[512,1024]{1,0:T(8,128)(2,1)}, u32[]{:S(2)}) copy-start(bf16[512,1024]{1,0:T(8,128)(2,1)} %first_rows.1) | copy-start | bytes 3145732
  239.1 67.6 %all-to-all-start.1 = ((bf16[32,32,1024]{2,1,0:T(8,128)(2,1)}), bf16[32,32,1024]{2,1,0:T(8,128)(2,1)}, u32[]{:S(2)}, u32[]{:S(2)}) async-start(bf16[32,32,1024]{2,1,0:T(8,128)(2,1)} %bitcast.23), calls=%async_computation.1 | async-start | bytes 4194304 | tf_op jit(solution)/shard_map/all_to_all | solution.py:1639
  244.9 22.1 %collective-permute-start.2 = (bf16[512,1024]{1,0:T(8,128)(2,1)S(1)}, bf16[512,1024]{1,0:T(8,128)(2,1)S(1)}, u32[]{:S(2)}, u32[]{:S(2)}) collective-permute-start(bf16[512,1024]{1,0:T(8,128)(2,1)S(1)} %copy-done.13), channel_id=1, source_target_pairs={{1,0},{3,2},{5,4},{7,6},{9,8},{11,10},{13,12},{15,14},{17,16},{19,... | collective-permute-start | bytes 3145736 | tf_op jit(solution)/shard_map/ppermute | solution.py:387
  262.2 3.3 copy-start.9
  284.1 1.6 copy-start.4
  285.7 1.6 copy-start.5
  287.3 1.6 copy-start.6
  304.6 1.3 copy-start.7
  305.9 0.8 copy-start.8
  369.9 159.1 %all-to-all-start.2 = ((bf16[32,32,1024]{2,1,0:T(8,128)(2,1)}), bf16[32,32,1024]{2,1,0:T(8,128)(2,1)}, u32[]{:S(2)}, u32[]{:S(2)}) async-start(bf16[32,32,1024]{2,1,0:T(8,128)(2,1)} %bitcast.57), calls=%async_computation.2 | async-start | bytes 4194304 | tf_op jit(solution)/shard_map/all_to_all | solution.py:1639
  643.1 3.3 copy-start.12
  646.4 2.3 copy-start.11
  648.8 1.4 copy-start.17
  648.8 2.1 copy-start.21
  648.8 2.7 copy-start.20
  648.8 3.4 copy-start.19
  648.8 4.0 copy-start.18
  648.8 4.7 copy-start.16
  650.2 4.1 copy-start.15
  650.2 4.8 copy-start.14

commit v5 on v4

--- a/solution.py
+++ b/solution.py
@@ -2,6 +2,7 @@
 
 import jax
 import jax.numpy as jnp
+import numpy as np
 from jax import lax
 from jax.experimental import pallas as pl
 from jax.experimental.pallas import tpu as pltpu
@@ -452,6 +453,31 @@
         body(z + step, False, True)
 
 
+def greet_all(parts, me, ctx):
+    barrier = pltpu.get_barrier_semaphore()
+
+    def greet(at, carry):
+        @pl.when(at != me)
+        def _():
+            pl.semaphore_signal(barrier, inc=1, device_id=flat_device(at, ctx), device_id_type=MESH)
+
+        return carry
+
+    lax.fori_loop(0, parts, greet, 0)
+    pl.semaphore_wait(barrier, parts - 1)
+
+
+def each_other(first, last, me, act):
+    def body(at, carry):
+        @pl.when(at != me)
+        def _():
+            act(at)
+
+        return carry
+
+    lax.fori_loop(first, last, body, 0)
+
+
 def flat_device(at, ctx):
     return (at // ctx, at % ctx)
 
@@ -470,20 +496,25 @@
         at, first_row, rows, _ = self.views[g]
         return self.outs[at].at[slot_z, at_y, at_x, self.place[3], pl.ds(first_row, rows)]
 
-    def z_copy(self, g, slot_z, way):
+    def source(self, g, block, own):
+        at, first_row, rows, _ = self.views[g]
+        return self.shards[at].at[pl.ds(first_row, rows)] if own else block
+
+    def z_copy(self, g, slot_z, way, own=False):
         z, y, x, k = self.place
         block = self.spot(g, slot_z, y, x)
         device = device_at(z + 1 - 2 * way, y, x, k)
-        return remote(block, block, self.z_send.at[g, slot_z, way], self.z_recv.at[g, slot_z], device)
-
-    def plane_copy(self, g, slot_z, kind):
+        return remote(self.source(g, block, own), block, self.z_send.at[g, slot_z, way], self.z_recv.at[g, slot_z], device)
+
+    def plane_copy(self, g, slot_z, kind, own=False):
         z, y, x, k = self.place
         first, second = order_of(y, x, (self.views[g][3] + slot_z) % 2)
         from_at = first if kind == 2 else (y, x)
         to_at = first if kind == 0 else second
         block = self.spot(g, slot_z, from_at[0], from_at[1])
         device = device_at(z, to_at[0], to_at[1], k)
-        return remote(block, block, self.p_send.at[g, slot_z, kind], self.p_recv.at[g, slot_z, kind], device)
+        source = self.source(g, block, own)
+        return remote(source, block, self.p_send.at[g, slot_z, kind], self.p_recv.at[g, slot_z, kind], device)
 
     def core_copy(self, at, slot_z):
         z, y, x, k = self.place
@@ -495,18 +526,18 @@
         return pltpu.make_async_copy(self.shards[at], self.outs[at].at[z, y, x, k], self.local_sem.at[at])
 
     def each_way(self, g, slot_z, up, down, act):
-        z = self.place[0]
+        z, own = self.place[0], up and down
         if up:
 
             @pl.when(z < self.z_size - 1)
             def _():
-                act(self.z_copy(g, slot_z, 0))
+                act(self.z_copy(g, slot_z, 0, own))
 
         if down:
 
             @pl.when(z > 0)
             def _():
-                act(self.z_copy(g, slot_z, 1))
+                act(self.z_copy(g, slot_z, 1, own))
 
     def series(self, arrays):
         return [g for g, view in enumerate(self.views) if view[0] in arrays]
@@ -523,8 +554,8 @@
     def spread(self, arrays, step):
         def body(slot_z, up, down):
             for g in self.series(arrays):
-                self.plane_copy(g, slot_z, 0).start()
-                self.plane_copy(g, slot_z, 1).start()
+                self.plane_copy(g, slot_z, 0, step == 0).start()
+                self.plane_copy(g, slot_z, 1, step == 0).start()
 
         self.at(step, body)
 
@@ -542,6 +573,8 @@
                 self.plane_copy(g, slot_z, 1).wait_recv()
                 self.plane_copy(g, slot_z, 2).wait_recv()
             for at in arrays:
+                if step == 0:
+                    self.own_copy(at).wait()
                 self.core_copy(at, slot_z).start()
 
         self.at(step, body)
@@ -584,17 +617,7 @@
     slots = TILE // block_len
     adapt, early, late = (0,), (1, 2, 3, 4, 8), (5, 6, 7)
 
-    barrier = pltpu.get_barrier_semaphore()
-
-    def greet(at, carry):
-        @pl.when(at != me)
-        def _():
-            pl.semaphore_signal(barrier, inc=1, device_id=flat_device(at, ctx), device_id_type=MESH)
-
-        return carry
-
-    lax.fori_loop(0, parts, greet, 0)
-    pl.semaphore_wait(barrier, parts - 1)
+    greet_all(parts, me, ctx)
 
     def half_copy(at):
         device = flat_device(at, ctx)
@@ -624,24 +647,14 @@
             shared_held[at] = adapted[even][:half]
             shared_held[at + 1] = adapted[even][half:]
 
-        def leave(at, carry):
-            @pl.when(at != me)
-            def _():
-                half_copy(at).start()
-
-            return carry
-
-        lax.fori_loop(tile * slots, (tile + 1) * slots, leave, 0)
-
-    for at in range(count):
-        gather.own_copy(at).start()
-    gather.own_copy(0).wait()
+        each_other(tile * slots, (tile + 1) * slots, me, lambda at: half_copy(at).start())
+
     for step in range(z_size):
         gather.arrive(adapt, step)
         gather.spread(adapt, step)
         if step == 0:
-            for at in early + late:
-                gather.own_copy(at).wait()
+            for at in range(count):
+                gather.own_copy(at).start()
         gather.arrive(early, step)
         if step < tiles:
             reorder(step)
@@ -683,15 +696,11 @@
     gather.complete(early + late)
     gather.settle(adapt + early + late)
 
-    def finish(at, carry):
-        @pl.when(at != me)
-        def _():
-            device = flat_device(at, ctx)
-            remote(shared_held.at[at], shared_out.at[at], send_sem.at[at], recv_sem.at[at], device).wait()
-
-        return carry
-
-    lax.fori_loop(0, parts, finish, 0)
+    def settle_half(at):
+        device = flat_device(at, ctx)
+        remote(shared_held.at[at], shared_out.at[at], send_sem.at[at], recv_sem.at[at], device).wait()
+
+    each_other(0, parts, me, settle_half)
     own_half.wait()
 
 
@@ -985,7 +994,7 @@
             jax.ShapeDtypeStruct((length, width), jnp.bfloat16),
             jax.ShapeDtypeStruct((length, 128), jnp.float32),
         ],
-        compiler_params=pltpu.CompilerParams(vmem_limit_bytes=32 * 2**20),
+        compiler_params=pltpu.CompilerParams(vmem_limit_bytes=60 * 2**20),
         cost_estimate=pl.CostEstimate(
             flops=2 * length * length * width, bytes_accessed=8 * length * width, transcendentals=0
         ),
@@ -1027,12 +1036,28 @@
         in_specs=[pl.BlockSpec(memory_space=pltpu.SMEM)] + [head_block] * 5,
         out_specs=head_block,
         out_shape=jax.ShapeDtypeStruct((length, width), jnp.bfloat16),
-        compiler_params=pltpu.CompilerParams(vmem_limit_bytes=32 * 2**20),
+        compiler_params=pltpu.CompilerParams(vmem_limit_bytes=60 * 2**20),
         cost_estimate=pl.CostEstimate(
             flops=4 * length * length * width, bytes_accessed=12 * length * width, transcendentals=0
         ),
         name="attend_shared",
     )(core.reshape(1), queries, keys_in, values_in, far_keys, far_values)
+
+
+def middle_plan(z_size, total):
+    last = total - 1
+    places = {
+        "fold_core": [1 + 2 * at for at in range(z_size)],
+        "fold_second": ([6, 9, 12, 20] + [last] * z_size)[:z_size],
+        "fold_first": ([12, 20] + [last] * z_size)[:z_size],
+    }
+    plan = {}
+    for number in range(z_size + 2):
+        for delay, act in enumerate(places):
+            if 0 <= number - delay < z_size:
+                at = min(places[act][number - delay], last)
+                plan.setdefault(at, []).append((act, z_size - 1 - number + delay))
+    return plan
 
 
 def middle_kernel(
@@ -1060,12 +1085,32 @@
 ):
     count = len(shapes)
     parts, refs = refs[:count], refs[count:]
-    dr_ref, gains_ref, grad_ref = refs[:3]
+    home_out, gains_ref, grad_ref = refs[:3]
     outs, refs = refs[3 : 3 + count], refs[3 + count :]
-    dq_all, dk_all, dv_all, dk_sum, dv_sum = refs[:5]
-    scatter = Scatter(row_views(shapes), parts, outs, refs[5 : 5 + 5 * count], refs[5 + 5 * count :])
+    dq_all, dk_all, dv_all, dr_ref, dk_sum, dv_sum = refs[:6]
+    sems, (send_sem, recv_sem, own_sem) = refs[6 + 5 * count : -3], refs[-3:]
+    scatter = Scatter(row_views(shapes), parts, outs, refs[6 : 6 + 5 * count], sems)
     arrays = tuple(range(count))
     step = pl.program_id(0)
+    ctx = lax.axis_size("ctx")
+    devices = lax.axis_size("grp") * ctx
+    me = lax.axis_index("grp") * ctx + lax.axis_index("ctx")
+    block_len = dr_ref.shape[0] // devices
+    near_home = TILE // block_len
+
+    def home_copy(at):
+        rows = pl.ds(pl.multiple_of(at * block_len, block_len), block_len)
+        device = flat_device(at, ctx)
+        return remote(dr_ref.at[rows], home_out.at[me], send_sem.at[at], recv_sem.at[me], device)
+
+    def own_home():
+        rows = pl.ds(pl.multiple_of(me * block_len, block_len), block_len)
+        return pltpu.make_async_copy(dr_ref.at[rows], home_out.at[me], own_sem)
+
+    def settle_home(at):
+        rows = pl.ds(pl.multiple_of(at * block_len, block_len), block_len)
+        device = flat_device(at, ctx)
+        remote(dr_ref.at[rows], home_out.at[at], send_sem.at[at], recv_sem.at[at], device).wait()
     length = q_ref.shape[0]
     tiles = length // TILE
     rest = heads + tiles
@@ -1073,15 +1118,16 @@
 
     @pl.when(step == 0)
     def _():
-        greet_line(*scatter.place, scatter.z_size)
+        greet_all(devices, me, ctx)
         scatter.begin(arrays)
         gains_ref[...] = jnp.zeros_like(gains_ref)
 
-    for number in range(scatter.stages()):
-
-        @pl.when(step == 2 + number * (total - 3) // scatter.stages())
-        def _(number=number):
-            scatter.stage(arrays, number)
+    for at_step, acts in middle_plan(scatter.z_size, total).items():
+
+        @pl.when(step == at_step)
+        def _(acts=acts):
+            for act, layer in acts:
+                getattr(scatter, act)(arrays, layer)
 
     @pl.when(step < heads)
     def _():
@@ -1129,6 +1175,8 @@
         d_resid, gain_one = pull_norm(r_ref[...], d_normed, gain_ref[0:1, :])
         dr_ref[rows, :] = (d_resid + dmid_ref[...]).astype(jnp.bfloat16)
         gains_ref[0:1, :] += gain_one
+        first = (step - heads) * near_home
+        each_other(first, first + near_home, me, lambda at: home_copy(at).start())
 
     pairs = (
         (normed_ref, dq_all),
@@ -1143,9 +1191,15 @@
         def _(left=left, right=right):
             grad_ref[...] = dot_w(left[...], right[...]).astype(grad_ref.dtype)
 
+    @pl.when(step == rest)
+    def _():
+        own_home().start()
+
     @pl.when(step == total - 1)
     def _():
         scatter.settle(arrays)
+        each_other(0, devices, me, settle_home)
+        own_home().wait()
 
 
 def middle_all(
@@ -1189,6 +1243,8 @@
     near = pl.BlockSpec(memory_space=pltpu.VMEM)
     once = pl.Buffered(1)
     weights = sum(shape[0] * shape[1] for shape in shapes)
+    devices = lax.axis_size("grp") * lax.axis_size("ctx")
+    dma = pltpu.SemaphoreType.DMA
     return pl.pallas_call(
         functools.partial(middle_kernel, shapes, heads),
         grid=(rest + 5 * tiles,),
@@ -1200,20 +1256,21 @@
         + [whole_block(d_branch)]
         + [anywhere] * len(sums),
         out_specs=[
-            pl.BlockSpec((length, width), lambda i: (0, 0), pipeline_mode=once),
+            anywhere,
             pl.BlockSpec((8, width), lambda i: (0, 0), pipeline_mode=once),
             pl.BlockSpec((TILE, width), lambda i: (jnp.clip(i - rest, 0, 5 * tiles - 1), 0)),
         ]
         + [near] * len(sums),
         out_shape=[
-            jax.ShapeDtypeStruct((length, width), jnp.bfloat16),
+            jax.ShapeDtypeStruct((devices, length // devices, width), jnp.bfloat16),
             jax.ShapeDtypeStruct((8, width), jnp.float32),
             jax.ShapeDtypeStruct((5 * width, width), jnp.bfloat16),
         ]
         + [jax.ShapeDtypeStruct(shape, jnp.float32) for shape in shapes],
-        scratch_shapes=[pltpu.VMEM((length, width), jnp.bfloat16)] * 3
+        scratch_shapes=[pltpu.VMEM((length, width), jnp.bfloat16)] * 4
         + [pltpu.VMEM((length, HEAD_DIM), jnp.float32)] * 2
-        + scatter_scratch(shapes),
+        + scatter_scratch(shapes)
+        + [dma((devices,)), dma((devices,)), dma],
         compiler_params=pltpu.CompilerParams(
             collective_id=collective_id, has_side_effects=True, vmem_limit_bytes=62 * 2**20
         ),
@@ -1242,9 +1299,11 @@
     )
 
 
-def rope_full(positions):
-    cosine, sine = rope_table(positions)
-    return jnp.concatenate([cosine, cosine], 1), jnp.concatenate([-sine, sine], 1)
+def rope_full(length):
+    freq = np.float32(10000.0) ** (np.float32(-2.0 / HEAD_DIM) * np.arange(HEAD_DIM // 2, dtype=np.float32))
+    angle = np.arange(length, dtype=np.float32)[:, None] * freq
+    cosine, sine = np.cos(angle).astype(np.float32), np.sin(angle).astype(np.float32)
+    return jnp.asarray(np.concatenate([cosine, cosine], 1)), jnp.asarray(np.concatenate([-sine, sine], 1))
 
 
 def whole_block(array):
@@ -1283,311 +1342,351 @@
     return jnp.concatenate(parts, 1)
 
 
-def project_heads(resid, gain_ref, wq_ref, wk_ref, wv_ref, cos_ref, sin_ref, q_ref, k_ref, v_ref):
-    normed = (unit_rows(resid)[1] * gain_ref[0:1, :]).astype(jnp.bfloat16)
-    cos, sin = cos_ref[...], sin_ref[...]
+COLUMNS = 256
+
+
+def column_block(rows, column=COLUMNS):
+    return pl.BlockSpec((rows, column), lambda i: (0, i))
+
+
+def write_heads(step_normed, wq_ref, wk_ref, wv_ref, cos, sin, q_ref, k_ref, v_ref):
+    normed = step_normed[...]
     q_ref[...] = turned_heads(dot_n(normed, wq_ref[...]), cos, sin).astype(jnp.bfloat16)
     k_ref[...] = turned_heads(dot_n(normed, wk_ref[...]), cos, sin).astype(jnp.bfloat16)
     v_ref[...] = dot_n(normed, wv_ref[...]).astype(jnp.bfloat16)
-    return normed
-
-
-def first_heads_kernel(r_ref, gain_ref, wq_ref, wk_ref, wv_ref, cos_ref, sin_ref, q_ref, k_ref, v_ref):
-    resid = r_ref[...].astype(jnp.float32)
-    project_heads(resid, gain_ref, wq_ref, wk_ref, wv_ref, cos_ref, sin_ref, q_ref, k_ref, v_ref)
+
+
+def first_heads_kernel(
+    r_ref, gain_ref, cos_ref, sin_ref, wq_ref, wk_ref, wv_ref, q_ref, k_ref, v_ref, normed_sc
+):
+    @pl.when(pl.program_id(0) == 0)
+    def _():
+        resid = r_ref[...].astype(jnp.float32)
+        normed_sc[...] = (unit_rows(resid)[1] * gain_ref[0:1, :]).astype(jnp.bfloat16)
+
+    core = lax.axis_index("ctx") % cos_ref.shape[1]
+    cos, sin = (table[:, core].reshape(-1, HEAD_DIM) for table in (cos_ref, sin_ref))
+    write_heads(normed_sc, wq_ref, wk_ref, wv_ref, cos, sin, q_ref, k_ref, v_ref)
 
 
 def first_heads(resid, gain_float, query_w, key_w, value_w, cos, sin):
     rows, width = resid.shape
-    tile = min(TILE, rows)
-    fixed = (gain_float, query_w, key_w, value_w)
     return pl.pallas_call(
         first_heads_kernel,
-        grid=(rows // tile,),
-        in_specs=[row_block(tile, width)] + [whole_block(a) for a in fixed] + [row_block(tile, HEAD_DIM)] * 2,
-        out_specs=[row_block(tile, width)] * 3,
+        grid=(width // COLUMNS,),
+        in_specs=[whole_block(a) for a in (resid, gain_float, cos, sin)] + [column_block(width)] * 3,
+        out_specs=[column_block(rows)] * 3,
         out_shape=[jax.ShapeDtypeStruct((rows, width), jnp.bfloat16)] * 3,
+        scratch_shapes=[pltpu.VMEM((rows, width), jnp.bfloat16)],
         compiler_params=compute_params(),
         cost_estimate=cost(6 * rows * width * width, 8 * rows * width + 6 * width * width),
         name="first_heads",
-    )(resid, *fixed, cos, sin)
+    )(resid, gain_float, cos, sin, query_w, key_w, value_w)
 
 
 def last_heads_kernel(
-    start_ref, first_ref, wa_ref, gain_ref, wq_ref, wk_ref, wv_ref, cos_ref, sin_ref, r_ref, n_ref, q_ref, k_ref, v_ref
+    start_ref,
+    near_ref,
+    far_ref,
+    wa_ref,
+    gain_ref,
+    cos_ref,
+    sin_ref,
+    wq_ref,
+    wk_ref,
+    wv_ref,
+    r_ref,
+    n_ref,
+    first_ref,
+    q_ref,
+    k_ref,
+    v_ref,
 ):
-    resid = start_ref[...].astype(jnp.float32) + dot_n(first_ref[...], wa_ref[...])
-    r_ref[...] = resid
-    n_ref[...] = project_heads(resid, gain_ref, wq_ref, wk_ref, wv_ref, cos_ref, sin_ref, q_ref, k_ref, v_ref)
-
-
-def last_heads(starting, first_out, adapt_w, gain_float, query_w, key_w, value_w, cos, sin):
+    @pl.when(pl.program_id(0) == 0)
+    def _():
+        owner = lax.axis_index("ctx") % 2 == 0
+        blocks, half, width = near_ref.shape
+        both = jnp.concatenate([near_ref[...], far_ref[...]], 1).reshape(2 * blocks * half, width)
+        first_ref[...] = jnp.where(owner, both, jnp.zeros_like(both))
+        resid = start_ref[...].astype(jnp.float32) + dot_n(first_ref[...], wa_ref[...])
+        r_ref[...] = resid
+        n_ref[...] = (unit_rows(resid)[1] * gain_ref[0:1, :]).astype(jnp.bfloat16)
+
+    write_heads(n_ref, wq_ref, wk_ref, wv_ref, cos_ref[...], sin_ref[...], q_ref, k_ref, v_ref)
+
+
+def last_heads(starting, near_out, far_out, adapt_w, gain_float, query_w, key_w, value_w, cos, sin):
     rows, width = starting.shape
     upper = pl.BlockSpec((width, width), lambda i: (0, 0), pipeline_mode=pl.Buffered(1))
-    fixed = (gain_float, query_w, key_w, value_w)
     like = jax.ShapeDtypeStruct((rows, width), jnp.bfloat16)
+    tall = jax.ShapeDtypeStruct((rows, width), jnp.float32)
     return pl.pallas_call(
         last_heads_kernel,
-        grid=(rows // TILE,),
-        in_specs=[row_block(TILE, width)] * 2
+        grid=(width // COLUMNS,),
+        in_specs=[whole_block(a) for a in (starting, near_out, far_out)]
         + [upper]
-        + [whole_block(a) for a in fixed]
-        + [row_block(TILE, HEAD_DIM)] * 2,
-        out_specs=[row_block(TILE, width)] * 5,
-        out_shape=[jax.ShapeDtypeStruct((rows, width), jnp.float32)] + [like] * 4,
+        + [whole_block(a) for a in (gain_float, cos, sin)]
+        + [column_block(width)] * 3,
+        out_specs=[whole_block(tall)] + [whole_block(like)] * 2 + [column_block(rows)] * 3,
+        out_shape=[tall] + [like] * 5,
         compiler_params=compute_params(),
         cost_estimate=cost(8 * rows * width * width, 16 * rows * width + 8 * width * width),
         name="last_heads",
-    )(starting, first_out, adapt_w, *fixed, cos, sin)
-
-
-def column_chunks(total, chunk=768):
-    return [(at, min(chunk, total - at)) for at in range(0, total, chunk)]
-
-
-def forward_rows(resid, mixed, gain_ref, wo_ref, wg_ref, wu_ref, wd_ref, keep):
-    branch = dot_n(mixed, wo_ref[...])
-    middle = resid + unit_rows(branch)[1] * gain_ref[1:2, :]
-    mlp_in = (unit_rows(middle)[1] * gain_ref[2:3, :]).astype(jnp.bfloat16)
-    down_out = None
-    for at, size in column_chunks(wg_ref.shape[1]):
-        columns = slice(at, at + size)
-        gate_pre = dot_n(mlp_in, wg_ref[:, columns])
-        up_pre = dot_n(mlp_in, wu_ref[:, columns])
-        sigma = 1.0 / (1.0 + jnp.exp(-gate_pre))
-        hidden = (gate_pre * sigma * up_pre).astype(jnp.bfloat16)
-        keep(columns, gate_pre, up_pre, hidden)
-        part = dot_n(hidden, wd_ref[columns, :])
-        down_out = part if down_out is None else down_out + part
-    return branch, middle, mlp_in, down_out
-
-
-def first_rows_kernel(r_ref, mixed_ref, gain_ref, wo_ref, wg_ref, wu_ref, wd_ref, out_ref):
-    resid = r_ref[...].astype(jnp.float32)
-    _, middle, _, down_out = forward_rows(
-        resid, mixed_ref[...], gain_ref, wo_ref, wg_ref, wu_ref, wd_ref, lambda *_: None
-    )
-    out_ref[...] = (middle + unit_rows(down_out)[1] * gain_ref[3:4, :]).astype(jnp.bfloat16)
+    )(starting, near_out, far_out, adapt_w, gain_float, cos, sin, query_w, key_w, value_w)
+
+
+def first_rows_kernel(
+    r_ref, mixed_ref, gain_ref, wo_ref, wg_ref, wu_ref, wd_ref, out_ref, middle_sc, mlp_sc, total_sc
+):
+    step = pl.program_id(0)
+
+    @pl.when(step == 0)
+    def _():
+        branch = dot_n(mixed_ref[...], wo_ref[...])
+        middle = r_ref[...].astype(jnp.float32) + unit_rows(branch)[1] * gain_ref[1:2, :]
+        middle_sc[...] = middle
+        mlp_sc[...] = (unit_rows(middle)[1] * gain_ref[2:3, :]).astype(jnp.bfloat16)
+        total_sc[...] = jnp.zeros_like(total_sc)
+
+    mlp_in = mlp_sc[...]
+    gate_pre = dot_n(mlp_in, wg_ref[...])
+    up_pre = dot_n(mlp_in, wu_ref[...])
+    hidden = (gate_pre / (1.0 + jnp.exp(-gate_pre)) * up_pre).astype(jnp.bfloat16)
+    total_sc[...] += dot_n(hidden, wd_ref[...])
+
+    @pl.when(step == pl.num_programs(0) - 1)
+    def _():
+        out_ref[...] = (middle_sc[...] + unit_rows(total_sc[...])[1] * gain_ref[3:4, :]).astype(jnp.bfloat16)
 
 
 def first_rows(resid, mixed, gain_float, output_w, gate_w, up_w, down_w):
     rows, width = resid.shape
-    tile = min(TILE, rows)
-    fixed = (gain_float, output_w, gate_w, up_w, down_w)
-    weights = output_w.size + gate_w.size + up_w.size + down_w.size
+    inner = gate_w.shape[1]
+    like = jax.ShapeDtypeStruct((rows, width), jnp.bfloat16)
+    weights = output_w.size + 3 * gate_w.size
     return pl.pallas_call(
         first_rows_kernel,
-        grid=(rows // tile,),
-        in_specs=[row_block(tile, width)] * 2 + [whole_block(a) for a in fixed],
-        out_specs=row_block(tile, width),
-        out_shape=jax.ShapeDtypeStruct((rows, width), jnp.bfloat16),
+        grid=(inner // COLUMNS,),
+        in_specs=[whole_block(a) for a in (resid, mixed, gain_float, output_w)]
+        + [column_block(width)] * 2
+        + [row_block(COLUMNS, width)],
+        out_specs=whole_block(like),
+        out_shape=like,
+        scratch_shapes=[
+            pltpu.VMEM((rows, width), jnp.float32),
+            pltpu.VMEM((rows, width), jnp.bfloat16),
+            pltpu.VMEM((rows, width), jnp.float32),
+        ],
         compiler_params=compute_params(),
         cost_estimate=cost(2 * rows * weights, 6 * rows * width + 2 * weights),
         name="first_rows",
-    )(resid, mixed, *fixed)
+    )(resid, mixed, gain_float, output_w, gate_w, up_w, down_w)
 
 
 def last_rows_kernel(
     r_ref,
     mixed_ref,
-    up_ref,
     gain_ref,
     wo_ref,
     wg_ref,
     wu_ref,
     wd_ref,
     out_ref,
+    branch_ref,
+    middle_ref,
+    mlp_ref,
+    down_ref,
+    gate_ref,
+    up_ref,
     hidden_ref,
-    dd_ref,
+):
+    step = pl.program_id(0)
+
+    @pl.when(step == 0)
+    def _():
+        branch = dot_n(mixed_ref[...], wo_ref[...])
+        branch_ref[...] = branch
+        middle = r_ref[...] + unit_rows(branch)[1] * gain_ref[1:2, :]
+        middle_ref[...] = middle
+        mlp_ref[...] = (unit_rows(middle)[1] * gain_ref[2:3, :]).astype(jnp.bfloat16)
+        down_ref[...] = jnp.zeros_like(down_ref)
+
+    mlp_in = mlp_ref[...]
+    gate_pre = dot_n(mlp_in, wg_ref[...])
+    up_pre = dot_n(mlp_in, wu_ref[...])
+    hidden = (gate_pre / (1.0 + jnp.exp(-gate_pre)) * up_pre).astype(jnp.bfloat16)
+    gate_ref[...] = gate_pre.astype(jnp.bfloat16)
+    up_ref[...] = up_pre.astype(jnp.bfloat16)
+    hidden_ref[...] = hidden
+    down_ref[...] += dot_n(hidden, wd_ref[...])
+
+    @pl.when(step == pl.num_programs(0) - 1)
+    def _():
+        out_ref[...] = (middle_ref[...] + unit_rows(down_ref[...])[1] * gain_ref[3:4, :]).astype(jnp.bfloat16)
+
+
+def last_rows(resid, mixed, gain_float, output_w, gate_w, up_w, down_w):
+    rows, width = resid.shape
+    inner = gate_w.shape[1]
+    narrow, wide = (jax.ShapeDtypeStruct((rows, w), jnp.bfloat16) for w in (width, inner))
+    tall = jax.ShapeDtypeStruct((rows, width), jnp.float32)
+    weights = output_w.size + 3 * gate_w.size
+    whole = [narrow, tall, tall, narrow, tall]
+    return pl.pallas_call(
+        last_rows_kernel,
+        grid=(inner // COLUMNS,),
+        in_specs=[whole_block(a) for a in (resid, mixed, gain_float, output_w)]
+        + [column_block(width)] * 2
+        + [row_block(COLUMNS, width)],
+        out_specs=[whole_block(one) for one in whole] + [column_block(rows)] * 3,
+        out_shape=whole + [wide] * 3,
+        compiler_params=compute_params(),
+        cost_estimate=cost(2 * rows * weights, 22 * rows * width + 6 * rows * inner + 2 * weights),
+        name="last_rows",
+    )(resid, mixed, gain_float, output_w, gate_w, up_w, down_w)
+
+
+def back_rows_kernel(
+    down_ref,
+    slope_ref,
+    middle_ref,
+    branch_ref,
     mlp_ref,
-    dg_ref,
-    du_ref,
+    gain_ref,
+    wo_ref,
+    wg_ref,
+    wu_ref,
+    wd_ref,
+    gate_ref,
+    up_ref,
+    hidden_ref,
     dmid_ref,
     db_ref,
     dmix_ref,
     gains_ref,
-    gate_sc,
-    up_sc,
+    dwg_ref,
+    dwu_ref,
+    dwd_ref,
+    dd_sc,
+    total_sc,
 ):
-    def keep(columns, gate_pre, up_pre, hidden):
-        gate_sc[:, columns] = gate_pre
-        up_sc[:, columns] = up_pre
-        hidden_ref[:, columns] = hidden
-
-    branch, middle, mlp_in, down_out = forward_rows(
-        r_ref[...], mixed_ref[...], gain_ref, wo_ref, wg_ref, wu_ref, wd_ref, keep
-    )
-    mlp_ref[...] = mlp_in
-    out_ref[...] = (middle + unit_rows(down_out)[1] * gain_ref[3:4, :]).astype(jnp.bfloat16)
-    d_result = up_ref[...].astype(jnp.float32)
-    d_down, gain_four = pull_norm(down_out, d_result, gain_ref[3:4, :])
-    d_down = d_down.astype(jnp.bfloat16)
-    dd_ref[...] = d_down
-    d_mlp = None
-    for at, size in column_chunks(wg_ref.shape[1]):
-        columns = slice(at, at + size)
-        d_hidden = dot_t(d_down, wd_ref[columns, :])
-        gate_pre, up_pre = gate_sc[:, columns], up_sc[:, columns]
-        sigma = 1.0 / (1.0 + jnp.exp(-gate_pre))
-        d_gate = (d_hidden * up_pre * sigma * (1.0 + gate_pre * (1.0 - sigma))).astype(jnp.bfloat16)
-        d_up = (d_hidden * gate_pre * sigma).astype(jnp.bfloat16)
-        dg_ref[:, columns] = d_gate
-        du_ref[:, columns] = d_up
-        part = dot_t(d_gate, wg_ref[:, columns]) + dot_t(d_up, wu_ref[:, columns])
-        d_mlp = part if d_mlp is None else d_mlp + part
-    d_middle, gain_three = pull_norm(middle, d_mlp, gain_ref[2:3, :])
-    d_middle = d_middle + d_result
-    dmid_ref[...] = d_middle
-    d_branch, gain_two = pull_norm(branch, d_middle, gain_ref[1:2, :])
-    d_branch = d_branch.astype(jnp.bfloat16)
-    db_ref[...] = d_branch
-    dmix_ref[...] = dot_t(d_branch, wo_ref[...]).astype(jnp.bfloat16)
-
-    @pl.when(pl.program_id(0) == 0)
+    step = pl.program_id(0)
+
+    @pl.when(step == 0)
     def _():
         gains_ref[...] = jnp.zeros_like(gains_ref)
-
-    gains_ref[0:1, :] += gain_two
-    gains_ref[1:2, :] += gain_three
-    gains_ref[2:3, :] += gain_four
-
-
-def last_rows(resid, mixed, upstream, gain_float, output_w, gate_w, up_w, down_w):
-    rows, width = resid.shape
+        d_down, gain_four = pull_norm(down_ref[...], slope_ref[...].astype(jnp.float32), gain_ref[3:4, :])
+        gains_ref[2:3, :] = gain_four
+        dd_sc[...] = d_down.astype(jnp.bfloat16)
+        total_sc[...] = jnp.zeros_like(total_sc)
+
+    d_down, mlp_in = dd_sc[...], mlp_ref[...]
+    d_hidden = dot_t(d_down, wd_ref[...])
+    gate_pre, up_pre = gate_ref[...].astype(jnp.float32), up_ref[...].astype(jnp.float32)
+    sigma = 1.0 / (1.0 + jnp.exp(-gate_pre))
+    d_gate = (d_hidden * up_pre * sigma * (1.0 + gate_pre * (1.0 - sigma))).astype(jnp.bfloat16)
+    d_up = (d_hidden * gate_pre * sigma).astype(jnp.bfloat16)
+    dwd_ref[...] = dot_w(hidden_ref[...], d_down).astype(jnp.bfloat16)
+    dwg_ref[...] = dot_w(mlp_in, d_gate).astype(jnp.bfloat16)
+    dwu_ref[...] = dot_w(mlp_in, d_up).astype(jnp.bfloat16)
+    total_sc[...] += dot_t(jnp.concatenate([d_gate, d_up], 1), jnp.concatenate([wg_ref[...], wu_ref[...]], 1))
+
+    @pl.when(step == pl.num_programs(0) - 1)
+    def _():
+        d_middle, gain_three = pull_norm(middle_ref[...], total_sc[...], gain_ref[2:3, :])
+        gains_ref[1:2, :] = gain_three
+        d_middle = d_middle + slope_ref[...].astype(jnp.float32)
+        dmid_ref[...] = d_middle
+        d_branch, gain_two = pull_norm(branch_ref[...], d_middle, gain_ref[1:2, :])
+        gains_ref[0:1, :] = gain_two
+        d_branch = d_branch.astype(jnp.bfloat16)
+        db_ref[...] = d_branch
+        dmix_ref[...] = dot_t(d_branch, wo_ref[...]).astype(jnp.bfloat16)
+
+
+def back_rows(down_out, upstream, middle, branch, mlp_in, gain_float, output_w, gate_w, up_w, down_w, gate_pre, up_pre, hidden):
+    rows, width = middle.shape
     inner = gate_w.shape[1]
-    fixed = (gain_float, output_w, gate_w, up_w, down_w)
-    weights = output_w.size + gate_w.size + up_w.size + down_w.size
-    narrow, wide = (jax.ShapeDtypeStruct((rows, w), jnp.bfloat16) for w in (width, inner))
+    narrow = jax.ShapeDtypeStruct((rows, width), jnp.bfloat16)
     tall = jax.ShapeDtypeStruct((rows, width), jnp.float32)
-    outs = [narrow, wide, narrow, narrow, wide, wide, tall, narrow, narrow]
+    gains = jax.ShapeDtypeStruct((8, width), jnp.float32)
+    wide = jax.ShapeDtypeStruct(gate_w.shape, jnp.bfloat16)
+    whole = [tall, narrow, narrow, gains]
+    fixed = (down_out, upstream, middle, branch, mlp_in, gain_float, output_w)
     return pl.pallas_call(
-        last_rows_kernel,
-        grid=(rows // TILE,),
-        in_specs=[row_block(TILE, width)] * 3 + [whole_block(a) for a in fixed],
-        out_specs=[row_block(TILE, one.shape[1]) for one in outs]
-        + [pl.BlockSpec((8, width), lambda i: (0, 0))],
-        out_shape=outs + [jax.ShapeDtypeStruct((8, width), jnp.float32)],
-        scratch_shapes=[pltpu.VMEM((TILE, inner), jnp.float32)] * 2,
+        back_rows_kernel,
+        grid=(inner // COLUMNS,),
+        in_specs=[whole_block(a) for a in fixed]
+        + [column_block(width)] * 2
+        + [row_block(COLUMNS, width)]
+        + [column_block(rows)] * 3,
+        out_specs=[whole_block(one) for one in whole] + [column_block(width)] * 2 + [row_block(COLUMNS, width)],
+        out_shape=whole + [wide, wide, jax.ShapeDtypeStruct(down_w.shape, jnp.bfloat16)],
+        scratch_shapes=[pltpu.VMEM((rows, width), jnp.bfloat16), pltpu.VMEM((rows, width), jnp.float32)],
         compiler_params=compute_params(),
-        cost_estimate=cost(4 * rows * weights, 30 * rows * width + 2 * weights),
-        name="last_rows",
-    )(resid, mixed, upstream, *fixed)
-
-
-def weight_grad_kernel(left_ref, right_ref, out_ref):
-    out_ref[...] = dot_w(left_ref[...], right_ref[...]).astype(out_ref.dtype)
-
-
-def weight_grad(left, right, tile=256):
-    rows, height = left.shape
-    width = right.shape[1]
-    return pl.pallas_call(
-        weight_grad_kernel,
-        grid=(height // tile,),
-        in_specs=[pl.BlockSpec((rows, tile), lambda i: (0, i)), whole_block(right)],
-        out_specs=row_block(tile, width),
-        out_shape=jax.ShapeDtypeStruct((height, width), jnp.bfloat16),
-        compiler_params=compute_params(),
-        cost_estimate=cost(2 * rows * height * width, 2 * (rows * (height + width) + height * width)),
-        name="weight_grad",
-    )(left, right)
-
-
-def close_kernel(target_ref, final_ref, w_ref, s_ref, e_ref, dr_ref, grad_ref, gain_ref, *refs):
-    _, _, x_size, k_size = grid_sizes()
-    ctx = x_size * k_size
-    parts_count = lax.axis_size("grp") * ctx
-    me = lax.axis_index("grp") * ctx + lax.axis_index("ctx")
+        cost_estimate=cost(12 * rows * gate_w.size, 24 * rows * width + 6 * rows * inner + 12 * gate_w.size),
+        name="back_rows",
+    )(*fixed, gate_w, up_w, down_w, gate_pre, up_pre, hidden)
+
+
+def close_kernel(target_ref, final_ref, w_ref, s_ref, e_ref, home, grad_ref, gain_ref, *refs):
     final_out, ds_ref, de_ref = refs[:3]
     outs, refs = refs[3:9], refs[9:]
-    home, first, total, adapt_part = refs[:4]
-    buffers, refs = refs[4:34], refs[34:]
-    sems, (send_sem, recv_sem, own_sem) = refs[:7], refs[7:]
+    first, total, adapt_part, *refs = refs
+    buffers, sems, own_sem = refs[:30], refs[30:37], refs[37]
     parts = [grad_ref.at[at] for at in range(4)] + [adapt_part, gain_ref]
     scatter = Scatter(row_views([out.shape for out in outs]), parts, outs, buffers, sems)
     early, late = (0, 1, 2, 3, 5), (4,)
     count, width = ds_ref.shape
     tiles = count // TILE
 
-    barrier = pltpu.get_barrier_semaphore()
-
-    def greet(at, carry):
-        @pl.when(at != me)
-        def _():
-            pl.semaphore_signal(barrier, inc=1, device_id=flat_device(at, ctx), device_id_type=MESH)
-
-        return carry
-
-    lax.fori_loop(0, parts_count, greet, 0)
-    pl.semaphore_wait(barrier, parts_count - 1)
-
-    def leave(at, carry):
-        @pl.when(at != me)
-        def _():
-            remote(dr_ref.at[at], home.at[me], send_sem.at[at], recv_sem.at[me], flat_device(at, ctx)).start()
-
-        return carry
-
-    lax.fori_loop(0, parts_count, leave, 0)
-    own = pltpu.make_async_copy(dr_ref.at[me], home.at[me], own_sem.at[0])
-    own_first = pltpu.make_async_copy(grad_ref.at[4], first, own_sem.at[1])
-    own.start()
+    greet_line(*scatter.place, scatter.z_size)
+    scatter.begin(early)
+    own_first = pltpu.make_async_copy(grad_ref.at[4], first, own_sem)
     own_first.start()
-    scatter.begin(early)
 
     def order_rows(tile):
-        rows = pl.ds(pl.multiple_of(tile * TILE, TILE), TILE)
-        at_column = lax.broadcasted_iota(jnp.int32, (TILE, count), 1)
-        return rows, (at_column == target_ref[rows, :]).astype(jnp.bfloat16)
+        rows = pl.ds(tile * TILE, TILE)
+        at_row = lax.broadcasted_iota(jnp.int32, (count, TILE), 0)
+        return rows, (at_row == target_ref[:, rows]).astype(jnp.bfloat16)
 
     def at_home(tile):
         rows, order = order_rows(tile)
-        d_home = dot_n(order, home[...].reshape(count, width)).astype(jnp.bfloat16)
+        d_home = dot_w(order, home[...].reshape(count, width)).astype(jnp.bfloat16)
         ds_ref[rows, :] = dot_t(d_home, w_ref[:width, :]).astype(jnp.bfloat16)
         de_ref[rows, :] = dot_t(d_home, w_ref[width:, :]).astype(jnp.bfloat16)
         upper, lower = dot_w(s_ref[rows, :], d_home), dot_w(e_ref[rows, :], d_home)
         if tile == 0:
+            own_first.wait()
             total[:width, :] = upper + first[...].reshape(width, width).astype(jnp.float32)
             total[width:, :] = lower
         else:
             total[:width, :] += upper
             total[width:, :] += lower
 
-    for number in range(4):
-        scatter.stage(early, number)
-        if number < tiles:
-            rows, order = order_rows(number)
-            final_out[rows, :] = dot_n(order, final_ref[...]).astype(jnp.bfloat16)
-
-    def arrive(at, carry):
-        @pl.when(at != me)
-        def _():
-            remote(dr_ref.at[at], home.at[at], send_sem.at[at], recv_sem.at[at], flat_device(at, ctx)).wait()
-
-        return carry
-
-    lax.fori_loop(0, parts_count, arrive, 0)
-    own.wait()
-    own_first.wait()
     for tile in range(tiles):
         at_home(tile)
-        if tile < scatter.stages() - 4:
-            scatter.stage(early, 4 + tile)
+        if tile < scatter.z_size:
+            scatter.stage(early, tile)
     adapt_part[...] = total[...].reshape(adapt_part.shape).astype(adapt_part.dtype)
     scatter.begin(late)
     for number in range(scatter.stages()):
+        if number >= tiles:
+            scatter.stage(early, number)
         scatter.stage(late, number)
+        if number < tiles:
+            rows, order = order_rows(number)
+            final_out[rows, :] = dot_w(order, final_ref[...]).astype(jnp.bfloat16)
     scatter.settle(early)
     scatter.settle(late)
 
 
 def close_all(
-    target, final_slots, adapt_w, once, embeds, d_resid, weight_parts, gain_part, block_len, collective_id
+    target, final_slots, adapt_w, once, embeds, d_home, weight_parts, gain_part, collective_id
 ):
     sizes = grid_sizes()
     parts = lax.axis_size("grp") * lax.axis_size("ctx")
-    width = weight_parts.shape[1]
-    count = target.shape[0]
+    count, width = embeds.shape
     side = width // parts
     square = weight_parts.reshape((5,) + sizes + (side, width))
     gain = gain_part.reshape(sizes + gain_part.shape[1:])
@@ -1598,22 +1697,21 @@
     like = jax.ShapeDtypeStruct((count, width), jnp.bfloat16)
     return pl.pallas_call(
         close_kernel,
-        in_specs=[near] * 5 + [anywhere] * 3,
+        in_specs=[near] * 6 + [anywhere] * 2,
         out_specs=[near] * (3 + len(shapes)),
         out_shape=[like] * 3 + [jax.ShapeDtypeStruct(shape, jnp.float32) for shape in shapes],
         scratch_shapes=[
-            pltpu.VMEM((parts, block_len, width), jnp.bfloat16),
             pltpu.VMEM(sizes + (side, width), jnp.bfloat16),
             pltpu.VMEM((2 * width, width), jnp.float32),
             pltpu.VMEM(sizes + (2 * side, width), jnp.bfloat16),
         ]
         + scatter_scratch(shapes)
-        + [dma((parts,)), dma((parts,)), dma((2,))],
+        + [dma],
         compiler_params=pltpu.CompilerParams(
             collective_id=collective_id, has_side_effects=True, vmem_limit_bytes=62 * 2**20
         ),
         name="close_all",
-    )(target, final_slots, adapt_w, once, embeds, d_resid, square, gain)
+    )(target, final_slots, adapt_w, once, embeds, d_home, square, gain)
 
 
 def paired_on_device(
@@ -1623,7 +1721,6 @@
     parts = lax.axis_size("grp") * lax.axis_size("ctx")
     length = block_len * parts
     core = grid_place()[3]
-    owner = core == 0
 
     twice = counts == 2
     slot = jnp.where(
@@ -1657,38 +1754,54 @@
     shared = shared.reshape(length // 2, width)
     starting = exchange(starting).reshape(length, width)
 
-    resid = shared
-    local = jnp.arange(length // 2, dtype=jnp.int32)
-    cos_half, sin_half = rope_full((local // half * 2 + core) * half + local % half)
-    queries, keys_in, values_in = first_heads(resid, gain_float, query_w, key_w, value_w, cos_half, sin_half)
+    cos_full, sin_full = rope_full(length)
+    cos_half, sin_half = (table.reshape(parts, 2, half, HEAD_DIM) for table in (cos_full, sin_full))
+    queries, keys_in, values_in = first_heads(shared, gain_float, query_w, key_w, value_w, cos_half, sin_half)
     far_keys, far_values = send(keys_in, 3), send(values_in, 3)
     mixed = attend_shared(core, half, queries, keys_in, values_in, far_keys, far_values)
-    first_out = first_rows(resid, mixed, gain_float, output_w, gate_w, up_w, down_w)
-    first_out, upstream = lax.optimization_barrier((first_out, upstream))
+    near_out = first_rows(shared, mixed, gain_float, output_w, gate_w, up_w, down_w)
+    near_out, upstream = lax.optimization_barrier((near_out, upstream))
     upstream = exchange(upstream.reshape(parts, block_len, width)).reshape(length, width)
-    far_out = send(first_out, 3, -1)
-    first_out = jnp.stack(
-        [first_out.reshape(-1, half, width), far_out.reshape(-1, half, width)], 1
-    ).reshape(length, width)
-    first_out = jnp.where(owner, first_out, jnp.zeros_like(first_out))
-
-    cos_full, sin_full = rope_full(jnp.arange(length, dtype=jnp.int32))
-    resid, normed, queries, keys_in, values_in = last_heads(
-        starting, first_out, adapt_w, gain_float, query_w, key_w, value_w, cos_full, sin_full
+    far_out = send(near_out, 3, -1)
+
+    resid, normed, first_out, queries, keys_in, values_in = last_heads(
+        starting,
+        near_out.reshape(parts, half, width),
+        far_out.reshape(parts, half, width),
+        adapt_w,
+        gain_float,
+        query_w,
+        key_w,
+        value_w,
+        cos_full,
+        sin_full,
     )
     mixed, log_total = attend_whole(queries, keys_in, values_in)
-    result, hidden, d_down, mlp_in, d_gate, d_up, d_middle, d_branch, d_mixed, gain_rest = last_rows(
-        resid, mixed, upstream, gain_float, output_w, gate_w, up_w, down_w
-    )
+    result, branch, middle, mlp_in, down_out, gate_pre, up_pre, hidden = last_rows(
+        resid, mixed, gain_float, output_w, gate_w, up_w, down_w
+    )
+    d_middle, d_branch, d_mixed, gain_rest, gate_part, up_part, down_part = back_rows(
+        down_out,
+        upstream,
+        middle,
+        branch,
+        mlp_in,
+        gain_float,
+        output_w,
+        gate_w,
+        up_w,
+        down_w,
+        gate_pre,
+        up_pre,
+        hidden,
+    )
+    result, upstream = lax.optimization_barrier((result, upstream))
     final_back = exchange(result.reshape(parts, block_len, width))
-    down_part = weight_grad(hidden, d_down)
-    gate_part = weight_grad(mlp_in, d_gate)
-    up_part = weight_grad(mlp_in, d_up)
 
     def blocks(part):
         return part.reshape(parts, -1, part.shape[-1])
 
-    d_resid, gain_one, weight_parts, gate_grad, up_grad, down_grad = middle_all(
+    d_home, gain_one, weight_parts, gate_grad, up_grad, down_grad = middle_all(
         queries,
         keys_in,
         values_in,
@@ -1715,15 +1828,14 @@
         gain_part.reshape(parts, 1, gains.size).astype(jnp.bfloat16), ((0, 0), (0, 15), (0, 0))
     )
     final_back, latent_back, embed_back, query_grad, key_grad, value_grad, out_grad, adapt_grad, gain_grad = close_all(
-        target.reshape(row_count, 1),
+        target.reshape(1, row_count),
         final_back.reshape(row_count, width),
         adapt_w,
         jnp.where(twice[None, :, None], jnp.zeros_like(latents), latents).reshape(row_count, width),
         embed_rows,
-        blocks(d_resid),
+        d_home,
         weight_parts,
         gain_part,
-        block_len,
         2,
     )
     gain_grad = gain_grad[0].reshape(gains.shape)

time: 659 us -> 587 us (0.89); the launches traced: 656 us -> 577 us
  Pallas kernels: 575 us -> 524 us
  starting transfers between devices: 31.7 us -> 15.5 us
  local copies, waits for them, and re-layouts: 34.4 us -> 22.5 us
  other arithmetic: 9.99 us -> 3.1 us
    pallas_call x8 -> x6, Pallas kernels: 254 us -> 215 us  [the longest x1 74.3 us: close_all(): pl.pallas_call(close_kernel, in_specs=[near] * 6 + [anywhere] * 2, out_sp...]
    pallas_call x1, Pallas kernels: 181 us -> 157 us  [open_all(): pl.pallas_call(functools.partial(open_kernel, views, count, block_len), i...]
    ppermute x3, starting transfers between devices: 16.5 us -> 2.01 us  [send(): return lax.ppermute(values, BOTH, pairs)]
    pallas_call x1, Pallas kernels: 115 us -> 126 us  [middle_all(): pl.pallas_call(functools.partial(middle_kernel, shapes, heads), grid=(res...]
    unnamed x55 -> x41, local copies, waits for them, and re-layouts: 25.4 us -> 14.9 us
  transfers between devices with their start and end apart: 6 -> 6, of which waited for: 2 -> 4; matrix products, arithmetic and copies ran while one was open for 2% -> 1% of each run, Pallas kernels for 33% -> 51%
where the time goes in v5:
time: 587 us; the launch traced here: 577 us
  Pallas kernels  524 us (89%)
  local copies, waits for them, and re-layouts  22.5 us (4%)
  starting transfers between devices  15.5 us (3%)
  waiting for transfers between devices  10.3 us (2%)
    pallas_call x1, Pallas kernels, open_all(): pl.pallas_call(functools.partial(open_kernel, views, count, block_len), i...  157 us
    pallas_call x1, Pallas kernels, middle_all(): pl.pallas_call(functools.partial(middle_kernel, shapes, heads), grid=(res...  126 us
    pallas_call x1, Pallas kernels, close_all(): pl.pallas_call(close_kernel, in_specs=[near] * 6 + [anywhere] * 2, out_sp...  74.3 us
    pallas_call x1, Pallas kernels, back_rows(): pl.pallas_call(back_rows_kernel, grid=(inner // COLUMNS,), in_specs=[whol...  60.9 us
    pallas_call x1, Pallas kernels, last_rows(): pl.pallas_call(last_rows_kernel, grid=(inner // COLUMNS,), in_specs=[whol...  36.1 us
    pallas_call x1, Pallas kernels, first_rows(): pl.pallas_call(first_rows_kernel, grid=(inner // COLUMNS,), in_specs=[who...  19.3 us
    pallas_call x1, Pallas kernels, last_heads(): pl.pallas_call(last_heads_kernel, grid=(width // COLUMNS,), in_specs=[who...  16.6 us
    pallas_call x1, Pallas kernels, attend_whole(): pl.pallas_call(whole_attend, grid=(width // HEAD_DIM,), in_specs=[head_bl...  15.8 us
  transfers between devices with their start and end apart: 6, of which 4 were waited for; matrix products, arithmetic and copies ran while one was open for 1% of the time, Pallas kernels for 51%

profile of v5, /device:TPU:0, one launch (start us, length us, event | category | flops | bytes accessed | tf_op | source)
XLA Modules:
  0.0 576.6 jit_solution(11121590218925761664)
XLA Ops:
  0.6 0.7 broadcast_compare_fusion
  1.6 0.1 add_reduce_fusion
  1.7 0.7 select_multiply_fusion
  2.4 0.7 add.46.refs_0_.target_ref
  3.1 0.8 reshape.225
  3.8 0.6 pad.8.refs_12_
  4.4 156.6 %open_all.1 = (bf16[4,2,2,2,64,1024]{5,4,3,2,1,0:T(8,128)(2,1)}, bf16[4,2,2,2,32,1024]{5,4,3,2,1,0:T(8,128)(2,1)}, bf16[4,2,2,2,32,1024]{5,4,3,2,1,0:T(8,128)(2,...) custom-call(s32[1,1024]{1,0:T(1,128)} %add.46.refs_0_.target_ref, ...), custom_call_target="tpu_custom_call" | custom-call | tf_op jit(solution)/shard_map/open_all/pallas_call | solution.py:718
  161.0 3.0 all-to-all-start
  164.0 0.9 slice.18
  165.0 0.7 reshape.254.gain_ref
  165.7 8.3 %first_heads.1 = (bf16[512,1024]{1,0:T(8,128)(2,1)}, bf16[512,1024]{1,0:T(8,128)(2,1)}, bf16[512,1024]{1,0:T(8,128)(2,1)}) custom-call(bf16[512,1024]{1,0:T(8,128)(2,1)} %bitcast.79, f32[4,1024]{1,0:T(4,128)} %reshape.254.gain_ref, f32[32,2,16,128]{3,2,1,0:T(8,128)} %constant.43.cos_ref, f32[32,2,16,128]{3,2,1,0:T(8,128)} %constant.44.sin_ref, ...), custom_call_target="tpu_custom_call" | custom-call | flops 3221225472 | bytes 10485760 | tf_op jit(solution)/shard_map/first_heads/pallas_call | solution.py:1374
  174.0 0.3 collective-permute-start
  174.3 0.2 collective-permute-start.1
  174.5 2.4 collective-permute-done.ok_ref
  176.9 1.6 collective-permute-done.1.ov_ref
  178.5 10.3 %attend_shared.1.mixed_ref = bf16[512,1024]{1,0:T(8,128)(2,1)} custom-call(s32[1]{0:T(128)} %bitcast.7.core_ref, bf16[512,1024]{1,0:T(8,128)(2,1)} %get-tuple-element.74.q_ref, bf16[512,1024]{1,0:T(8,128)(2,1)} %get-tuple-element.75.k_ref, bf16[512,1024]{1,0:T(8,128)(2,1)} %get-tuple-element.76.v_ref, bf16[512,1024]{1,0:T(8,128)(2,1)} %copy-done.4, ...), custom_call_target="tpu_custom_call" | custom-call | flops 1073741824 | bytes 6291456 | tf_op jit(solution)/shard_map/attend_shared/pallas_call | solution.py:1033
  188.9 19.3 %first_rows.1 = bf16[512,1024]{1,0:T(8,128)(2,1)} custom-call(bf16[512,1024]{1,0:T(8,128)(2,1)} %bitcast.80, bf16[512,1024]{1,0:T(8,128)(2,1)} %attend_shared.1.mixed_ref, f32[4,1024]{1,0:T(4,128)} %reshape.254.gain_ref, bf16[1024,1024]{1,0:T(8,128)(2,1)} %bitcast.76, bf16[1024,2816]{1,0:T(8,128)(2,1)} %bitcast.58, bf16[1024,2816]{1,0:T(8,128)(2,1)} %bitcast.61, ...), custom_call_target="tpu_custom_call" | custom-call | flops 9932111872 | bytes 22544384 | tf_op jit(solution)/shard_map/first_rows/pallas_call | solution.py:1467
  208.2 4.8 all-to-all-done
  212.9 1.3 copy-done.1
  214.2 4.1 all-to-all-start.1
  218.4 1.5 collective-permute-start.2
  219.9 1.5 broadcast_select_fusion
  221.4 1.5 collective-permute-done.2
  222.9 1.0 copy-done.14
  223.9 16.6 %last_heads.1 = (f32[1024,1024]{1,0:T(8,128)}, bf16[1024,1024]{1,0:T(8,128)(2,1)}, bf16[1024,1024]{1,0:T(8,128)(2,1)}, bf16[1024,1024]{1,0:T(8,128)(2,1)}, bf16[...) custom-call(bf16[1024,1024]{1,0:T(8,128)(2,1)} %bitcast.48, bf16[32,16,1024]{2,1,0:T(8,128)(2,1)} %bitcast.81, ...), custom_call_target="tpu_custom_call" | custom-call | flops 8589934592 | bytes 25165824 | tf_op jit(solution)/shard_map/last_heads/pallas_call | solution.py:1423
  240.5 15.8 %attend_whole.1 = (bf16[1024,1024]{1,0:T(8,128)(2,1)}, f32[1024,128]{1,0:T(8,128)}) custom-call(bf16[1024,1024]{1,0:T(8,128)(2,1)} %get-tuple-element.85.q_ref, bf16[1024,1024]{1,0:T(8,128)(2,1)} %get-tuple-element.86.k_ref, bf16[1024,1024]{1,0:T(8,128)(2,1)} %get-tuple-element.87.v_ref), custom_call_target="tpu_custom_call" | custom-call | flops 2147483648 | bytes 8388608 | tf_op jit(solution)/shard_map/attend_whole/pallas_call | solution.py:988
  256.2 36.1 %last_rows.1 = (bf16[1024,1024]{1,0:T(8,128)(2,1)}, f32[1024,1024]{1,0:T(8,128)}, f32[1024,1024]{1,0:T(8,128)}, bf16[1024,1024]{1,0:T(8,128)(2,1)}, f32[1024,102...) custom-call(f32[1024,1024]{1,0:T(8,128)} %get-tuple-element.84.r_ref, ...), custom_call_target="tpu_custom_call" | custom-call | flops 19864223744 | bytes 59768832 | tf_op jit(solution)/shard_map/last_rows/pallas_call | solution.py:1535
  292.3 6.3 %all-to-all-start.2 = ((bf16[32,32,1024]{2,1,0:T(8,128)(2,1)}), bf16[32,32,1024]{2,1,0:T(8,128)(2,1)}, u32[]{:S(2)}, u32[]{:S(2)}) async-start(bf16[32,32,1024]{2,1,0:T(8,128)(2,1)} %bitcast.49), calls=%async_computation.2 | async-start | bytes 4194304 | tf_op jit(solution)/shard_map/all_to_all | solution.py:1736
  298.6 60.9 %back_rows.1 = (f32[1024,1024]{1,0:T(8,128)}, bf16[1024,1024]{1,0:T(8,128)(2,1)}, bf16[1024,1024]{1,0:T(8,128)(2,1)}, f32[8,1024]{1,0:T(8,128)}, bf16[1024,2816]...) custom-call(f32[1024,1024]{1,0:T(8,128)} %get-tuple-element.92.down_ref, ...), custom_call_target="tpu_custom_call" | custom-call | flops 35433480192 | bytes 77070336 | tf_op jit(solution)/shard_map/back_rows/pallas_call | solution.py:1616
  359.5 125.9 %middle_all.1 = (bf16[32,32,1024]{2,1,0:T(8,128)(2,1)}, f32[8,1024]{1,0:T(8,128)}, bf16[5120,1024]{1,0:T(8,128)(2,1)}, f32[32,2816]{1,0:T(8,128)}, f32[32,2816]{1,0:T(8,128)}, /*index=5*/f32[88,1024]{1,0:T(8,128)}) custom-call(bf16[1024,1024]{1,0:T(8,128)(2,1)} %get-tuple-element.85.q_ref, bf16[1024,1024]{1,0:T(8,128)(2,1)} %get-tuple-element.86.k_ref, ...), custom_call_target="tpu_custom_call" | custom-call | flops 25769803776 | bytes 84410368 | tf_op jit(solution)/shard_map/middle_all/pallas_call | solution.py:1248
  485.4 0.8 slice.25
  486.2 0.8 slice.24
  487.2 0.7 pad.9.clone
  487.9 74.3 %close_all.1 = (bf16[1024,1024]{1,0:T(8,128)(2,1)}, bf16[1024,1024]{1,0:T(8,128)(2,1)}, bf16[1024,1024]{1,0:T(8,128)(2,1)}, f32[32,1024]{1,0:T(8,128)}, f32[32,1...) custom-call(s32[1,1024]{1,0:T(1,128)} %add.46.refs_0_.target_ref, ...), custom_call_target="tpu_custom_call" | custom-call | tf_op jit(solution)/shard_map/close_all/pallas_call | solution.py:1698
  562.2 0.7 slice_reduce_fusion
  562.9 0.7 reshape_squeeze.4
  563.5 3.3 copy.52
  566.9 1.3 copy.53
  568.2 1.0 copy-done.2
  569.2 1.3 copy.54
  570.6 0.7 copy.55
  571.3 0.7 copy.56
  571.9 0.7 copy.57
  572.6 0.7 copy.58
  573.3 0.7 copy.59
  573.9 0.7 copy.60
  574.7 0.7 copy.61
  575.4 0.7 copy.62
  (41 shorter events, 0.7 us)
Async XLA Ops:
  161.0 51.9 %all-to-all-start = ((bf16[32,32,1024]{2,1,0:T(8,128)(2,1)}), bf16[32,32,1024]{2,1,0:T(8,128)(2,1)S(1)}, u32[]{:S(2)}, u32[]{:S(2)}) async-start(bf16[32,32,1024]{2,1,0:T(8,128)(2,1)} %get-tuple-element.68), calls=%async_computation | async-start | bytes 4194304 | tf_op jit(solution)/shard_map/all_to_all | solution.py:1736
  174.0 2.9 collective-permute-start
  174.3 4.2 collective-permute-start.1
  176.9 1.6 copy-start.4
  212.9 1.3 copy-start.1
  214.2 4.2 copy-start.13
  214.2 5.7 copy-start
  214.2 78.1 %all-to-all-start.1 = ((bf16[32,32,1024]{2,1,0:T(8,128)(2,1)}), bf16[32,32,1024]{2,1,0:T(8,128)(2,1)}, u32[]{:S(2)}, u32[]{:S(2)}) async-start(bf16[32,32,1024]{2,1,0:T(8,128)(2,1)} %bitcast.47), calls=%async_computation.1 | async-start | bytes 4194304 | tf_op jit(solution)/shard_map/all_to_all | solution.py:1736
  218.4 4.6 collective-permute-start.2
  222.9 1.0 copy-start.14
  292.3 195.5 %all-to-all-start.2 = ((bf16[32,32,1024]{2,1,0:T(8,128)(2,1)}), bf16[32,32,1024]{2,1,0:T(8,128)(2,1)}, u32[]{:S(2)}, u32[]{:S(2)}) async-start(bf16[32,32,1024]{2,1,0:T(8,128)(2,1)} %bitcast.49), calls=%async_computation.2 | async-start | bytes 4194304 | tf_op jit(solution)/shard_map/all_to_all | solution.py:1736
  563.5 3.3 copy-start.3
  566.9 2.3 copy-start.2
  569.2 1.4 copy-start.8
  569.2 2.1 copy-start.12
  569.2 2.7 copy-start.11
  569.2 3.4 copy-start.10
  569.2 4.0 copy-start.9
  569.2 4.7 copy-start.7
  570.6 4.1 copy-start.6
  570.6 4.8 copy-start.5

commit v6 on v5

--- a/solution.py
+++ b/solution.py
@@ -1172,8 +1172,8 @@
             + dot_t(dk_all[rows, :], wk_ref[...])
             + dot_t(dv_all[rows, :], wv_ref[...])
         )
-        d_resid, gain_one = pull_norm(r_ref[...], d_normed, gain_ref[0:1, :])
-        dr_ref[rows, :] = (d_resid + dmid_ref[...]).astype(jnp.bfloat16)
+        d_resid, gain_one = pull_norm(r_ref[...].astype(jnp.float32), d_normed, gain_ref[0:1, :])
+        dr_ref[rows, :] = (d_resid + dmid_ref[...].astype(jnp.float32)).astype(jnp.bfloat16)
         gains_ref[0:1, :] += gain_one
         first = (step - heads) * near_home
         each_other(first, first + near_home, me, lambda at: home_copy(at).start())
@@ -1409,7 +1409,7 @@
         both = jnp.concatenate([near_ref[...], far_ref[...]], 1).reshape(2 * blocks * half, width)
         first_ref[...] = jnp.where(owner, both, jnp.zeros_like(both))
         resid = start_ref[...].astype(jnp.float32) + dot_n(first_ref[...], wa_ref[...])
-        r_ref[...] = resid
+        r_ref[...] = resid.astype(jnp.bfloat16)
         n_ref[...] = (unit_rows(resid)[1] * gain_ref[0:1, :]).astype(jnp.bfloat16)
 
     write_heads(n_ref, wq_ref, wk_ref, wv_ref, cos_ref[...], sin_ref[...], q_ref, k_ref, v_ref)
@@ -1419,7 +1419,6 @@
     rows, width = starting.shape
     upper = pl.BlockSpec((width, width), lambda i: (0, 0), pipeline_mode=pl.Buffered(1))
     like = jax.ShapeDtypeStruct((rows, width), jnp.bfloat16)
-    tall = jax.ShapeDtypeStruct((rows, width), jnp.float32)
     return pl.pallas_call(
         last_heads_kernel,
         grid=(width // COLUMNS,),
@@ -1427,8 +1426,8 @@
         + [upper]
         + [whole_block(a) for a in (gain_float, cos, sin)]
         + [column_block(width)] * 3,
-        out_specs=[whole_block(tall)] + [whole_block(like)] * 2 + [column_block(rows)] * 3,
-        out_shape=[tall] + [like] * 5,
+        out_specs=[whole_block(like)] * 3 + [column_block(rows)] * 3,
+        out_shape=[like] * 6,
         compiler_params=compute_params(),
         cost_estimate=cost(8 * rows * width * width, 16 * rows * width + 8 * width * width),
         name="last_heads",
@@ -1492,56 +1491,76 @@
     wu_ref,
     wd_ref,
     out_ref,
-    branch_ref,
-    middle_ref,
-    mlp_ref,
+    branch_out,
+    middle_out,
+    mlp_out,
     down_ref,
     gate_ref,
     up_ref,
     hidden_ref,
+    branch_sc,
+    middle_sc,
+    middle_low,
+    mlp_sc,
+    total_sc,
+    sems,
 ):
     step = pl.program_id(0)
+    copies = [
+        pltpu.make_async_copy(source, target, sems.at[at])
+        for at, (source, target) in enumerate(
+            ((branch_sc, branch_out), (middle_low, middle_out), (mlp_sc, mlp_out))
+        )
+    ]
 
     @pl.when(step == 0)
     def _():
         branch = dot_n(mixed_ref[...], wo_ref[...])
-        branch_ref[...] = branch
-        middle = r_ref[...] + unit_rows(branch)[1] * gain_ref[1:2, :]
-        middle_ref[...] = middle
-        mlp_ref[...] = (unit_rows(middle)[1] * gain_ref[2:3, :]).astype(jnp.bfloat16)
-        down_ref[...] = jnp.zeros_like(down_ref)
-
-    mlp_in = mlp_ref[...]
+        branch_sc[...] = branch.astype(jnp.bfloat16)
+        middle = r_ref[...].astype(jnp.float32) + unit_rows(branch)[1] * gain_ref[1:2, :]
+        middle_sc[...] = middle
+        middle_low[...] = middle.astype(jnp.bfloat16)
+        mlp_sc[...] = (unit_rows(middle)[1] * gain_ref[2:3, :]).astype(jnp.bfloat16)
+        total_sc[...] = jnp.zeros_like(total_sc)
+        for copy in copies:
+            copy.start()
+
+    mlp_in = mlp_sc[...]
     gate_pre = dot_n(mlp_in, wg_ref[...])
     up_pre = dot_n(mlp_in, wu_ref[...])
     hidden = (gate_pre / (1.0 + jnp.exp(-gate_pre)) * up_pre).astype(jnp.bfloat16)
     gate_ref[...] = gate_pre.astype(jnp.bfloat16)
     up_ref[...] = up_pre.astype(jnp.bfloat16)
     hidden_ref[...] = hidden
-    down_ref[...] += dot_n(hidden, wd_ref[...])
+    total_sc[...] += dot_n(hidden, wd_ref[...])
 
     @pl.when(step == pl.num_programs(0) - 1)
     def _():
-        out_ref[...] = (middle_ref[...] + unit_rows(down_ref[...])[1] * gain_ref[3:4, :]).astype(jnp.bfloat16)
+        down_out = total_sc[...]
+        down_ref[...] = down_out.astype(jnp.bfloat16)
+        out_ref[...] = (middle_sc[...] + unit_rows(down_out)[1] * gain_ref[3:4, :]).astype(jnp.bfloat16)
+        for copy in copies:
+            copy.wait()
 
 
 def last_rows(resid, mixed, gain_float, output_w, gate_w, up_w, down_w):
     rows, width = resid.shape
     inner = gate_w.shape[1]
     narrow, wide = (jax.ShapeDtypeStruct((rows, w), jnp.bfloat16) for w in (width, inner))
-    tall = jax.ShapeDtypeStruct((rows, width), jnp.float32)
     weights = output_w.size + 3 * gate_w.size
-    whole = [narrow, tall, tall, narrow, tall]
+    low, tall = pltpu.VMEM((rows, width), jnp.bfloat16), pltpu.VMEM((rows, width), jnp.float32)
+    anywhere = pl.BlockSpec(memory_space=pl.ANY)
     return pl.pallas_call(
         last_rows_kernel,
         grid=(inner // COLUMNS,),
         in_specs=[whole_block(a) for a in (resid, mixed, gain_float, output_w)]
         + [column_block(width)] * 2
         + [row_block(COLUMNS, width)],
-        out_specs=[whole_block(one) for one in whole] + [column_block(rows)] * 3,
-        out_shape=whole + [wide] * 3,
+        out_specs=[whole_block(narrow)] + [anywhere] * 3 + [whole_block(narrow)] + [column_block(rows)] * 3,
+        out_shape=[narrow] * 5 + [wide] * 3,
+        scratch_shapes=[low, tall, low, low, tall, pltpu.SemaphoreType.DMA((3,))],
         compiler_params=compute_params(),
-        cost_estimate=cost(2 * rows * weights, 22 * rows * width + 6 * rows * inner + 2 * weights),
+        cost_estimate=cost(2 * rows * weights, 14 * rows * width + 6 * rows * inner + 2 * weights),
         name="last_rows",
     )(resid, mixed, gain_float, output_w, gate_w, up_w, down_w)
 
@@ -1549,11 +1568,11 @@
 def back_rows_kernel(
     down_ref,
     slope_ref,
-    middle_ref,
-    branch_ref,
     mlp_ref,
     gain_ref,
-    wo_ref,
+    middle_in,
+    branch_in,
+    wo_in,
     wg_ref,
     wu_ref,
     wd_ref,
@@ -1569,13 +1588,25 @@
     dwd_ref,
     dd_sc,
     total_sc,
+    middle_sc,
+    branch_sc,
+    wo_sc,
+    sems,
 ):
     step = pl.program_id(0)
+    copies = [
+        pltpu.make_async_copy(source, target, sems.at[at])
+        for at, (source, target) in enumerate(((middle_in, middle_sc), (branch_in, branch_sc), (wo_in, wo_sc)))
+    ]
 
     @pl.when(step == 0)
     def _():
+        for copy in copies:
+            copy.start()
         gains_ref[...] = jnp.zeros_like(gains_ref)
-        d_down, gain_four = pull_norm(down_ref[...], slope_ref[...].astype(jnp.float32), gain_ref[3:4, :])
+        d_down, gain_four = pull_norm(
+            down_ref[...].astype(jnp.float32), slope_ref[...].astype(jnp.float32), gain_ref[3:4, :]
+        )
         gains_ref[2:3, :] = gain_four
         dd_sc[...] = d_down.astype(jnp.bfloat16)
         total_sc[...] = jnp.zeros_like(total_sc)
@@ -1593,40 +1624,52 @@
 
     @pl.when(step == pl.num_programs(0) - 1)
     def _():
-        d_middle, gain_three = pull_norm(middle_ref[...], total_sc[...], gain_ref[2:3, :])
+        for copy in copies:
+            copy.wait()
+        d_middle, gain_three = pull_norm(middle_sc[...].astype(jnp.float32), total_sc[...], gain_ref[2:3, :])
         gains_ref[1:2, :] = gain_three
         d_middle = d_middle + slope_ref[...].astype(jnp.float32)
-        dmid_ref[...] = d_middle
-        d_branch, gain_two = pull_norm(branch_ref[...], d_middle, gain_ref[1:2, :])
+        dmid_ref[...] = d_middle.astype(jnp.bfloat16)
+        d_branch, gain_two = pull_norm(branch_sc[...].astype(jnp.float32), d_middle, gain_ref[1:2, :])
         gains_ref[0:1, :] = gain_two
         d_branch = d_branch.astype(jnp.bfloat16)
         db_ref[...] = d_branch
-        dmix_ref[...] = dot_t(d_branch, wo_ref[...]).astype(jnp.bfloat16)
-
-
-def back_rows(down_out, upstream, middle, branch, mlp_in, gain_float, output_w, gate_w, up_w, down_w, gate_pre, up_pre, hidden):
+        dmix_ref[...] = dot_t(d_branch, wo_sc[...]).astype(jnp.bfloat16)
+
+
+def back_rows(
+    down_out, upstream, middle, branch, mlp_in, gain_float, output_w, gate_w, up_w, down_w, gate_pre, up_pre, hidden
+):
     rows, width = middle.shape
     inner = gate_w.shape[1]
     narrow = jax.ShapeDtypeStruct((rows, width), jnp.bfloat16)
-    tall = jax.ShapeDtypeStruct((rows, width), jnp.float32)
     gains = jax.ShapeDtypeStruct((8, width), jnp.float32)
     wide = jax.ShapeDtypeStruct(gate_w.shape, jnp.bfloat16)
-    whole = [tall, narrow, narrow, gains]
-    fixed = (down_out, upstream, middle, branch, mlp_in, gain_float, output_w)
+    whole = [narrow] * 3 + [gains]
+    near = (down_out, upstream, mlp_in, gain_float)
+    low = pltpu.VMEM((rows, width), jnp.bfloat16)
     return pl.pallas_call(
         back_rows_kernel,
         grid=(inner // COLUMNS,),
-        in_specs=[whole_block(a) for a in fixed]
+        in_specs=[whole_block(a) for a in near]
+        + [pl.BlockSpec(memory_space=pl.ANY)] * 3
         + [column_block(width)] * 2
         + [row_block(COLUMNS, width)]
         + [column_block(rows)] * 3,
         out_specs=[whole_block(one) for one in whole] + [column_block(width)] * 2 + [row_block(COLUMNS, width)],
         out_shape=whole + [wide, wide, jax.ShapeDtypeStruct(down_w.shape, jnp.bfloat16)],
-        scratch_shapes=[pltpu.VMEM((rows, width), jnp.bfloat16), pltpu.VMEM((rows, width), jnp.float32)],
+        scratch_shapes=[
+            low,
+            pltpu.VMEM((rows, width), jnp.float32),
+            low,
+            low,
+            pltpu.VMEM(output_w.shape, jnp.bfloat16),
+            pltpu.SemaphoreType.DMA((3,)),
+        ],
         compiler_params=compute_params(),
-        cost_estimate=cost(12 * rows * gate_w.size, 24 * rows * width + 6 * rows * inner + 12 * gate_w.size),
+        cost_estimate=cost(12 * rows * gate_w.size, 18 * rows * width + 6 * rows * inner + 12 * gate_w.size),
         name="back_rows",
-    )(*fixed, gate_w, up_w, down_w, gate_pre, up_pre, hidden)
+    )(*near, middle, branch, output_w, gate_w, up_w, down_w, gate_pre, up_pre, hidden)
 
 
 def close_kernel(target_ref, final_ref, w_ref, s_ref, e_ref, home, grad_ref, gain_ref, *refs):
@@ -1639,6 +1682,7 @@
     early, late = (0, 1, 2, 3, 5), (4,)
     count, width = ds_ref.shape
     tiles = count // TILE
+    block_len = home.shape[1]
 
     greet_line(*scatter.place, scatter.z_size)
     scatter.begin(early)
@@ -1652,10 +1696,14 @@
 
     def at_home(tile):
         rows, order = order_rows(tile)
-        d_home = dot_w(order, home[...].reshape(count, width)).astype(jnp.bfloat16)
+        d_slots = home[...].reshape(count, width)
+        d_home = dot_w(order, d_slots).astype(jnp.bfloat16)
+        at_row = lax.broadcasted_iota(jnp.int32, (count, TILE), 0)
+        once = jnp.where(at_row // block_len % 2 == 1, order, jnp.zeros_like(order))
+        d_once = dot_w(once, d_slots).astype(jnp.bfloat16)
         ds_ref[rows, :] = dot_t(d_home, w_ref[:width, :]).astype(jnp.bfloat16)
         de_ref[rows, :] = dot_t(d_home, w_ref[width:, :]).astype(jnp.bfloat16)
-        upper, lower = dot_w(s_ref[rows, :], d_home), dot_w(e_ref[rows, :], d_home)
+        upper, lower = dot_w(s_ref[rows, :], d_once), dot_w(e_ref[rows, :], d_home)
         if tile == 0:
             own_first.wait()
             total[:width, :] = upper + first[...].reshape(width, width).astype(jnp.float32)
@@ -1714,6 +1762,24 @@
     )(target, final_slots, adapt_w, once, embeds, d_home, square, gain)
 
 
+def finish_kernel(count, *refs):
+    for source, target in zip(refs[:count], refs[count:]):
+        target[...] = source[...]
+
+
+def finish_all(results):
+    count = len(results)
+    near = pl.BlockSpec(memory_space=pltpu.VMEM)
+    return pl.pallas_call(
+        functools.partial(finish_kernel, count),
+        in_specs=[near] * count,
+        out_specs=[near] * count,
+        out_shape=[jax.ShapeDtypeStruct(one.shape, one.dtype) for one in results],
+        compiler_params=compute_params(),
+        name="finish_all",
+    )(*results)
+
+
 def paired_on_device(
     latents, embeds, cotangent, counts, w_adapt, w_query, w_key, w_value, w_out, w_gate, w_up, w_down, gains
 ):
@@ -1831,28 +1897,30 @@
         target.reshape(1, row_count),
         final_back.reshape(row_count, width),
         adapt_w,
-        jnp.where(twice[None, :, None], jnp.zeros_like(latents), latents).reshape(row_count, width),
+        latent_rows,
         embed_rows,
         d_home,
         weight_parts,
         gain_part,
         2,
     )
+    results = finish_all(
+        [
+            final_back,
+            latent_back,
+            embed_back,
+            adapt_grad,
+            query_grad,
+            key_grad,
+            value_grad,
+            out_grad,
+            gate_grad,
+            up_grad,
+            down_grad,
+        ]
+    )
     gain_grad = gain_grad[0].reshape(gains.shape)
-    return (
-        final_back.reshape(latents.shape),
-        latent_back.reshape(latents.shape),
-        embed_back.reshape(latents.shape),
-        adapt_grad,
-        query_grad,
-        key_grad,
-        value_grad,
-        out_grad,
-        gate_grad,
-        up_grad,
-        down_grad,
-        gain_grad,
-    )
+    return tuple(one.reshape(latents.shape) for one in results[:3]) + tuple(results[3:]) + (gain_grad,)
 
 
 def on_device(latents, *others):

time: 587 us -> 573 us (0.976)
  local copies, waits for them, and re-layouts: 22.5 us -> 9.93 us
    unnamed x41 -> x8, local copies, waits for them, and re-layouts: 14.9 us -> 2.29 us
    pallas_call x0 -> x1, Pallas kernels: none -> 6.67 us  [finish_all(): pl.pallas_call(functools.partial(finish_kernel, count), in_specs=[near] *...]
where the time goes in v6:
time: 573 us; the launch traced here: 563 us
  Pallas kernels  523 us (91%)
  starting transfers between devices  15.5 us (3%)
  waiting for transfers between devices  11.8 us (2%)
  local copies, waits for them, and re-layouts  9.93 us (2%)
    pallas_call x1, Pallas kernels, open_all(): pl.pallas_call(functools.partial(open_kernel, views, count, block_len), i...  157 us
    pallas_call x1, Pallas kernels, middle_all(): pl.pallas_call(functools.partial(middle_kernel, shapes, heads), grid=(res...  126 us
    pallas_call x1, Pallas kernels, close_all(): pl.pallas_call(close_kernel, in_specs=[near] * 6 + [anywhere] * 2, out_sp...  75.2 us
    pallas_call x1, Pallas kernels, back_rows(): pl.pallas_call(back_rows_kernel, grid=(inner // COLUMNS,), in_specs=[whol...  56.9 us
    pallas_call x1, Pallas kernels, last_rows(): pl.pallas_call(last_rows_kernel, grid=(inner // COLUMNS,), in_specs=[whol...  32.1 us
    pallas_call x1, Pallas kernels, first_rows(): pl.pallas_call(first_rows_kernel, grid=(inner // COLUMNS,), in_specs=[who...  19.3 us
    pallas_call x1, Pallas kernels, last_heads(): pl.pallas_call(last_heads_kernel, grid=(width // COLUMNS,), in_specs=[who...  16.1 us
    pallas_call x1, Pallas kernels, attend_whole(): pl.pallas_call(whole_attend, grid=(width // HEAD_DIM,), in_specs=[head_bl...  15.8 us
  transfers between devices with their start and end apart: 6, of which 4 were waited for; matrix products, arithmetic and copies ran while one was open for 1% of the time, Pallas kernels for 51%

profile of v6, /device:TPU:0, one launch (start us, length us, event | category | flops | bytes accessed | tf_op | source)
XLA Modules:
  0.0 562.8 jit_solution(11092075295755218672)
XLA Ops:
  0.6 0.8 reshape.221
  1.4 0.7 fusion
  2.1 0.1 copy.31
  2.2 0.1 copy.30
  2.2 0.1 reduce-window.19
  2.3 0.1 reduce-window.18
  2.4 0.1 add_reduce_fusion
  2.5 0.7 select_multiply_fusion
  3.1 0.7 add.46.refs_0_.target_ref
  3.8 0.6 pad.8.refs_12_
  4.4 156.6 %open_all.1 = (bf16[4,2,2,2,64,1024]{5,4,3,2,1,0:T(8,128)(2,1)}, bf16[4,2,2,2,32,1024]{5,4,3,2,1,0:T(8,128)(2,1)}, bf16[4,2,2,2,32,1024]{5,4,3,2,1,0:T(8,128)(2,...) custom-call(s32[1,1024]{1,0:T(1,128)} %add.46.refs_0_.target_ref, ...), custom_call_target="tpu_custom_call" | custom-call | tf_op jit(solution)/shard_map/open_all/pallas_call | solution.py:718
  161.0 3.0 all-to-all-start
  164.0 0.9 slice.18
  164.9 0.1 reshape.250
  165.0 0.7 reshape.249.gain_ref
  165.7 8.3 %first_heads.1 = (bf16[512,1024]{1,0:T(8,128)(2,1)}, bf16[512,1024]{1,0:T(8,128)(2,1)}, bf16[512,1024]{1,0:T(8,128)(2,1)}) custom-call(bf16[512,1024]{1,0:T(8,128)(2,1)} %bitcast.77, f32[4,1024]{1,0:T(4,128)} %reshape.249.gain_ref, f32[32,2,16,128]{3,2,1,0:T(8,128)} %constant.42.cos_ref, f32[32,2,16,128]{3,2,1,0:T(8,128)} %constant.43.sin_ref, ...), custom_call_target="tpu_custom_call" | custom-call | flops 3221225472 | bytes 10485760 | tf_op jit(solution)/shard_map/first_heads/pallas_call | solution.py:1374
  174.0 0.3 collective-permute-start
  174.3 0.2 collective-permute-start.1
  174.5 2.4 collective-permute-done.ok_ref
  176.9 0.0 copy-start.1
  176.9 1.6 collective-permute-done.1.ov_ref
  178.5 0.0 copy-done.1
  178.5 10.3 %attend_shared.1.mixed_ref = bf16[512,1024]{1,0:T(8,128)(2,1)} custom-call(s32[1]{0:T(128)} %bitcast.7.core_ref, bf16[512,1024]{1,0:T(8,128)(2,1)} %get-tuple-element.85.q_ref, bf16[512,1024]{1,0:T(8,128)(2,1)} %get-tuple-element.86.k_ref, bf16[512,1024]{1,0:T(8,128)(2,1)} %get-tuple-element.87.v_ref, bf16[512,1024]{1,0:T(8,128)(2,1)} %copy-done.1, ...), custom_call_target="tpu_custom_call" | custom-call | flops 1073741824 | bytes 6291456 | tf_op jit(solution)/shard_map/attend_shared/pallas_call | solution.py:1033
  188.9 19.3 %first_rows.1 = bf16[512,1024]{1,0:T(8,128)(2,1)} custom-call(bf16[512,1024]{1,0:T(8,128)(2,1)} %bitcast.78, bf16[512,1024]{1,0:T(8,128)(2,1)} %attend_shared.1.mixed_ref, f32[4,1024]{1,0:T(4,128)} %reshape.249.gain_ref, bf16[1024,1024]{1,0:T(8,128)(2,1)} %bitcast.71, bf16[1024,2816]{1,0:T(8,128)(2,1)} %bitcast.53, bf16[1024,2816]{1,0:T(8,128)(2,1)} %bitcast.56, ...), custom_call_target="tpu_custom_call" | custom-call | flops 9932111872 | bytes 22544384 | tf_op jit(solution)/shard_map/first_rows/pallas_call | solution.py:1466
  208.1 4.8 all-to-all-done
  212.9 1.3 copy-done
  214.2 4.1 all-to-all-start.1
  218.4 0.0 copy-done.2
  218.4 1.5 collective-permute-start.2
  219.9 3.0 collective-permute-done.2
  223.0 1.0 copy-done.3
  223.9 16.1 %last_heads.1 = (bf16[1024,1024]{1,0:T(8,128)(2,1)}, bf16[1024,1024]{1,0:T(8,128)(2,1)}, bf16[1024,1024]{1,0:T(8,128)(2,1)}, bf16[1024,1024]{1,0:T(8,128)(2,1)},...) custom-call(bf16[1024,1024]{1,0:T(8,128)(2,1)} %bitcast.46, bf16[32,16,1024]{2,1,0:T(8,128)(2,1)} %bitcast.79, ...), custom_call_target="tpu_custom_call" | custom-call | flops 8589934592 | bytes 25165824 | tf_op jit(solution)/shard_map/last_heads/pallas_call | solution.py:1422
  240.0 15.8 %attend_whole.1 = (bf16[1024,1024]{1,0:T(8,128)(2,1)}, f32[1024,128]{1,0:T(8,128)}) custom-call(bf16[1024,1024]{1,0:T(8,128)(2,1)} %get-tuple-element.96.q_ref, bf16[1024,1024]{1,0:T(8,128)(2,1)} %get-tuple-element.97.k_ref, bf16[1024,1024]{1,0:T(8,128)(2,1)} %get-tuple-element.98.v_ref), custom_call_target="tpu_custom_call" | custom-call | flops 2147483648 | bytes 8388608 | tf_op jit(solution)/shard_map/attend_whole/pallas_call | solution.py:988
  255.7 32.1 %last_rows.1 = (bf16[1024,1024]{1,0:T(8,128)(2,1)}, bf16[1024,1024]{1,0:T(8,128)(2,1)}, bf16[1024,1024]{1,0:T(8,128)(2,1)}, bf16[1024,1024]{1,0:T(8,128)(2,1)}, ...) custom-call(bf16[1024,1024]{1,0:T(8,128)(2,1)} %get-tuple-element.95, ...), custom_call_target="tpu_custom_call" | custom-call | flops 19864223744 | bytes 51380224 | tf_op jit(solution)/shard_map/last_rows/pallas_call | solution.py:1553
  287.8 0.0 all-to-all-done.1
  287.8 6.3 %all-to-all-start.2 = ((bf16[32,32,1024]{2,1,0:T(8,128)(2,1)}), bf16[32,32,1024]{2,1,0:T(8,128)(2,1)}, u32[]{:S(2)}, u32[]{:S(2)}) async-start(bf16[32,32,1024]{2,1,0:T(8,128)(2,1)} %bitcast.47), calls=%async_computation.2 | async-start | bytes 4194304 | tf_op jit(solution)/shard_map/all_to_all | solution.py:1802
  294.2 56.9 %back_rows.1 = (bf16[1024,1024]{1,0:T(8,128)(2,1)}, bf16[1024,1024]{1,0:T(8,128)(2,1)}, bf16[1024,1024]{1,0:T(8,128)(2,1)}, f32[8,1024]{1,0:T(8,128)}, bf16[1024...) custom-call(bf16[1024,1024]{1,0:T(8,128)(2,1)} %get-tuple-element.103.down_ref, ...), custom_call_target="tpu_custom_call" | custom-call | flops 35433480192 | bytes 70778880 | tf_op jit(solution)/shard_map/back_rows/pallas_call | solution.py:1651
  351.1 125.6 %middle_all.1 = (bf16[32,32,1024]{2,1,0:T(8,128)(2,1)}, f32[8,1024]{1,0:T(8,128)}, bf16[5120,1024]{1,0:T(8,128)(2,1)}, f32[32,2816]{1,0:T(8,128)}, f32[32,2816]{1,0:T(8,128)}, /*index=5*/f32[88,1024]{1,0:T(8,128)}) custom-call(bf16[1024,1024]{1,0:T(8,128)(2,1)} %get-tuple-element.96.q_ref, bf16[1024,1024]{1,0:T(8,128)(2,1)} %get-tuple-element.97.k_ref, ...), custom_call_target="tpu_custom_call" | custom-call | flops 25769803776 | bytes 84410368 | tf_op jit(solution)/shard_map/middle_all/pallas_call | solution.py:1248
  476.7 0.8 slice.25
  477.5 0.8 slice.24
  478.3 0.1 convert_element_type.37
  478.4 0.1 convert_element_type.43
  478.5 0.7 pad.9.clone
  479.2 0.0 all-to-all-done.2
  479.2 75.2 %close_all.1 = (bf16[1024,1024]{1,0:T(8,128)(2,1)}, bf16[1024,1024]{1,0:T(8,128)(2,1)}, bf16[1024,1024]{1,0:T(8,128)(2,1)}, f32[32,1024]{1,0:T(8,128)}, f32[32,1...) custom-call(s32[1,1024]{1,0:T(1,128)} %add.46.refs_0_.target_ref, ...), custom_call_target="tpu_custom_call" | custom-call | tf_op jit(solution)/shard_map/close_all/pallas_call | solution.py:1746
  554.3 0.7 slice_reduce_fusion
  555.0 0.7 reshape_squeeze.4
  555.7 6.7 %finish_all.1 = (bf16[1024,1024]{1,0:T(8,128)(2,1)}, bf16[1024,1024]{1,0:T(8,128)(2,1)}, bf16[1024,1024]{1,0:T(8,128)(2,1)}, f32[64,1024]{1,0:T(8,128)}, f32[32,...) custom-call(bf16[1024,1024]{1,0:T(8,128)(2,1)} %get-tuple-element.12, ...), custom_call_target="tpu_custom_call" | custom-call | tf_op jit(solution)/shard_map/finish_all/pallas_call | solution.py:1773
  (8 shorter events, 0.1 us)
Async XLA Ops:
  161.0 51.9 %all-to-all-start = ((bf16[32,32,1024]{2,1,0:T(8,128)(2,1)}), bf16[32,32,1024]{2,1,0:T(8,128)(2,1)S(1)}, u32[]{:S(2)}, u32[]{:S(2)}) async-start(bf16[32,32,1024]{2,1,0:T(8,128)(2,1)} %get-tuple-element.79), calls=%async_computation | async-start | bytes 4194304 | tf_op jit(solution)/shard_map/all_to_all | solution.py:1802
  174.0 2.9 collective-permute-start
  174.3 4.2 collective-permute-start.1
  176.9 1.6 copy-start.1
  212.9 1.3 copy-start
  212.9 5.5 copy-start.2
  214.2 73.6 %all-to-all-start.1 = ((bf16[32,32,1024]{2,1,0:T(8,128)(2,1)}), bf16[32,32,1024]{2,1,0:T(8,128)(2,1)}, u32[]{:S(2)}, u32[]{:S(2)}) async-start(bf16[32,32,1024]{2,1,0:T(8,128)(2,1)} %bitcast.20), calls=%async_computation.1 | async-start | bytes 4194304 | tf_op jit(solution)/shard_map/all_to_all | solution.py:1802
  218.4 4.6 collective-permute-start.2
  223.0 1.0 copy-start.3
  287.8 191.3 %all-to-all-start.2 = ((bf16[32,32,1024]{2,1,0:T(8,128)(2,1)}), bf16[32,32,1024]{2,1,0:T(8,128)(2,1)}, u32[]{:S(2)}, u32[]{:S(2)}) async-start(bf16[32,32,1024]{2,1,0:T(8,128)(2,1)} %bitcast.47), calls=%async_computation.2 | async-start | bytes 4194304 | tf_op jit(solution)/shard_map/all_to_all | solution.py:1802
